TPU v7x, 32 devices: a whole 2x2x4 slice. The times are simulated.
32 devices in a mesh: dp: 8 (over y, x, core), vox: 4 (over z).
Axes of the slice: x: 2, y: 2, z: 4, core: 2. Of those that a mesh axis runs over, the one named last changes fastest.
Arguments:
- kernels: bfloat16 [384, 16384], P('dp', 'vox'), may hold values from -0.046875 to 0.046875
- observed: float32 [8, 384], P(None, 'dp'), may hold values from -6 to 6
- initial: float32 [8, 16384], P(None, 'vox'), may hold values from -6 to 6
- threshold: float32 [8, 16, 2], replicated, may hold values from 0.05 to 0.5
Outputs:
- coefficients: float32 [8, 16384], P(None, 'vox')
- residual: float32 [8, 384], P(None, 'dp')
All inputs are finite; a program needn't handle non-finite values.
Results may differ from a plain program's by a relative error of at most 0.0043.
Values may be sent and summed in bfloat16 or wider, within the bound.
No kernel may reach another device: no remote copies, remote signals or barrier semaphores. Data moves between devices by JAX's collectives and lax.ppermute only.
A program may use at most 64 MiB of HBM per device.

v0:
```python
import jax
import jax.numpy as jnp
from jax import lax
from jax.sharding import PartitionSpec as P

ITERS = 2


step_size = 0.5


def passed_along(block, axis, distance):
    devices = range(lax.axis_size(axis))
    route = [((i - distance) % len(devices), i) for i in devices]
    return lax.ppermute(block, axis, route)


def from_right(edge):
    return passed_along(edge, "vox", -1)


def from_left(edge):
    return passed_along(edge, "vox", 1)


def forward_wave(arranged):
    even_part = arranged[..., 0, :]
    odd_part = arranged[..., 1, :]
    even_next = jnp.concatenate([even_part[..., 1:], from_right(even_part[..., :1])], axis=-1)
    detail = odd_part - 0.5 * (even_part + even_next)
    detail_prev = jnp.concatenate([from_left(detail[..., -1:]), detail[..., :-1]], axis=-1)
    smooth = even_part + 0.25 * (detail_prev + detail)
    return jnp.stack([smooth, detail], axis=-2)


def inverse_wave(arranged):
    smooth = arranged[..., 0, :]
    detail = arranged[..., 1, :]
    detail_prev = jnp.concatenate([from_left(detail[..., -1:]), detail[..., :-1]], axis=-1)
    even_part = smooth - 0.25 * (detail_prev + detail)
    even_next = jnp.concatenate([even_part[..., 1:], from_right(even_part[..., :1])], axis=-1)
    odd_part = detail + 0.5 * (even_part + even_next)
    return jnp.stack([even_part, odd_part], axis=-2)


def shrink(values, thresholds):
    return jnp.sign(values) * jnp.maximum(jnp.abs(values) - thresholds, 0.0)


def body(kernels, observed, initial, threshold):
    models_count = initial.shape[0]
    block_width = initial.shape[1]
    layer_count = threshold.shape[1]
    half_cells = block_width // (2 * layer_count)
    wavelets = initial.reshape(models_count, layer_count, 2, half_cells)
    voxel_model = inverse_wave(wavelets).reshape(models_count, block_width).astype(jnp.bfloat16)
    cutoff = threshold[..., None]
    residual = observed
    for iteration in range(ITERS):
        partial_pred = lax.dot_general(
            voxel_model, kernels, (((1,), (1,)), ((), ())), preferred_element_type=jnp.float32
        )
        predicted = lax.psum(partial_pred, "vox")
        residual = observed - predicted
        partial_grad = jnp.dot(
            residual.astype(jnp.bfloat16), kernels, preferred_element_type=jnp.float32
        )
        final_turn = iteration + 1 == ITERS
        gradient = lax.psum(partial_grad, "dp").reshape(models_count, layer_count, 2, half_cells)
        wavelets = shrink(wavelets + step_size * forward_wave(gradient), cutoff)
        if not final_turn:
            voxel_model = (
                inverse_wave(wavelets).reshape(models_count, block_width).astype(jnp.bfloat16)
            )
    coefficients = wavelets.reshape(models_count, block_width)
    return (coefficients, residual)


def solution(mesh):
    return jax.shard_map(
        body,
        mesh=mesh,
        in_specs=(P("dp", "vox"), P(None, "dp"), P(None, "vox"), P()),
        out_specs=(P(None, "vox"), P(None, "dp")),
        check_vma=False,
    )
```

profile of v0, /device:TPU:0, one launch (start us, length us, event | category | flops | bytes accessed | tf_op | source)
XLA Modules:
  0.0 193.4 jit_solution(17878899734470123063)
XLA Ops:
  7.2 1.1 reshape.51
  8.3 0.1 fusion.35
  8.5 3.0 %collective-permute-start = (f32[8,16,1]{2,1,0:T(8,128)S(1)}, f32[8,16,1]{2,1,0:T(8,128)S(1)}, u32[]{:S(2)}, u32[]{:S(2)}) collective-permute-start(f32[8,16,1]{2,1,0:T(8,128)S(1)} %slice.98), channel_id=1, source_target_pairs={{3,0},{0,1},{1,2},{2,3},{7,4},{4,5},{5,6},{6,7},{11,8},{8,9},{9,10... | collective-permute-start | bytes 1544 | tf_op jit(solution)/shard_map/ppermute | solution.py:15
  11.6 4.3 %collective-permute-done = f32[8,16,1]{2,1,0:T(8,128)S(1)} collective-permute-done((f32[8,16,1]{2,1,0:T(8,128)S(1)}, f32[8,16,1]{2,1,0:T(8,128)S(1)}, u32[]{:S(2)}, u32[]{:S(2)}) %collective-permute-start) | collective-permute-done | bytes 544 | tf_op jit(solution)/shard_map/ppermute | solution.py:15
  15.8 0.1 fusion.6
  15.9 2.1 %collective-permute-start.1 = (f32[8,16,1]{2,1,0:T(8,128)S(1)}, f32[8,16,1]{2,1,0:T(8,128)S(1)}, u32[]{:S(2)}, u32[]{:S(2)}) collective-permute-start(f32[8,16,1]{2,1,0:T(8,128)S(1)} %bitcast.105), channel_id=1, source_target_pairs={{1,0},{2,1},{3,2},{0,3},{5,4},{6,5},{7,6},{4,7},{9,8},{10,9},{11,1... | collective-permute-start | bytes 1544 | tf_op jit(solution)/shard_map/ppermute | solution.py:15
  18.1 2.2 %collective-permute-done.1 = f32[8,16,1]{2,1,0:T(8,128)S(1)} collective-permute-done((f32[8,16,1]{2,1,0:T(8,128)S(1)}, f32[8,16,1]{2,1,0:T(8,128)S(1)}, u32[]{:S(2)}, u32[]{:S(2)}) %collective-permute-start.1) | collective-permute-done | bytes 544 | tf_op jit(solution)/shard_map/ppermute | solution.py:15
  20.2 0.1 fusion.30
  20.5 0.2 fusion.37
  20.7 12.3 %psum.28 = f32[8,48]{1,0:T(8,128)S(1)} all-reduce(f32[8,48]{1,0:T(8,128)S(1)} %fusion.37), channel_id=1, replica_groups=mesh['dp'=8,'vox'=4] {'vox'}, use_global_device_ids=true, to_apply=%region_0.0 | all-reduce | flops 384 | bytes 3072 | tf_op jit(solution)/shard_map/psum | solution.py:63
  33.0 0.2 fusion.27
  33.2 0.1 reshape.52
  33.3 0.7 copy.100
  34.0 51.2 %all-reduce.3.cloned.1.call-done = f32[8,16,2,128]{3,1,0,2:T(8,128)} async-done(((f32[8,16,2,128]{3,1,0,2:T(8,128)}), f32[8,16,2,128]{3,1,0,2:T(8,128)}) %all-reduce.3.cloned.1.call-update) | async-done | bytes 131088 | tf_op jit(solution)/shard_map/psum | solution.py:69
  85.3 0.8 slice_bitcast_fusion.6
  86.1 3.3 %collective-permute-start.2 = (f32[8,16,1]{2,1,0:T(8,128)S(1)}, f32[8,16,1]{2,1,0:T(8,128)S(1)}, u32[]{:S(2)}, u32[]{:S(2)}) collective-permute-start(f32[8,16,1]{2,1,0:T(8,128)S(1)} %bitcast.103), channel_id=1, source_target_pairs={{1,0},{2,1},{3,2},{0,3},{5,4},{6,5},{7,6},{4,7},{9,8},{10,9},{11,1... | collective-permute-start | bytes 1544 | tf_op jit(solution)/shard_map/ppermute | solution.py:15
  89.5 2.0 %collective-permute-done.2 = f32[8,16,1]{2,1,0:T(8,128)S(1)} collective-permute-done((f32[8,16,1]{2,1,0:T(8,128)S(1)}, f32[8,16,1]{2,1,0:T(8,128)S(1)}, u32[]{:S(2)}, u32[]{:S(2)}) %collective-permute-start.2) | collective-permute-done | bytes 544 | tf_op jit(solution)/shard_map/ppermute | solution.py:15
  91.6 0.1 fusion.8
  91.7 0.3 collective-permute-start.3
  92.1 6.2 %collective-permute-done.3 = f32[8,16,1]{2,1,0:T(8,128)S(1)} collective-permute-done((f32[8,16,1]{2,1,0:T(8,128)S(1)}, f32[8,16,1]{2,1,0:T(8,128)S(1)}, u32[]{:S(2)}, u32[]{:S(2)}) %collective-permute-start.3) | collective-permute-done | bytes 544 | tf_op jit(solution)/shard_map/ppermute | solution.py:15
  98.3 0.1 fusion.10
  98.4 0.6 copy-done.4
  99.0 0.1 copy_multiply_fusion
  99.2 6.0 %collective-permute-done.4 = f32[8,16,1]{2,1,0:T(8,128)S(1)} collective-permute-done((f32[8,16,1]{2,1,0:T(8,128)S(1)}, f32[8,16,1]{2,1,0:T(8,128)S(1)}, u32[]{:S(2)}, u32[]{:S(2)}) %collective-permute-start.4) | collective-permute-done | bytes 544 | tf_op jit(solution)/shard_map/ppermute | solution.py:15
  105.4 0.4 collective-permute-start.5
  105.7 0.1 fusion.32
  105.9 3.8 %collective-permute-done.5 = f32[8,16,1]{2,1,0:T(8,128)S(1)} collective-permute-done((f32[8,16,1]{2,1,0:T(8,128)S(1)}, f32[8,16,1]{2,1,0:T(8,128)S(1)}, u32[]{:S(2)}, u32[]{:S(2)}) %collective-permute-start.5) | collective-permute-done | bytes 544 | tf_op jit(solution)/shard_map/ppermute | solution.py:15
  109.7 0.1 fusion.18
  109.9 0.2 fusion.38
  110.1 10.4 %psum.30 = f32[8,48]{1,0:T(8,128)S(1)} all-reduce(f32[8,48]{1,0:T(8,128)S(1)} %fusion.38), channel_id=1, replica_groups=mesh['dp'=8,'vox'=4] {'vox'}, use_global_device_ids=true, to_apply=%region_2.0 | all-reduce | flops 384 | bytes 3072 | tf_op jit(solution)/shard_map/psum | solution.py:63
  120.6 0.2 fusion.28
  120.7 0.4 copy-done.6
  121.2 0.1 reshape.53
  121.3 0.7 copy.115
  122.0 0.1 copy.126
  122.1 0.2 sub.59.clone
  122.3 0.1 sub.60
  122.5 0.1 mul.75
  122.6 49.1 %all-reduce.5.cloned.1.call-done = f32[8,16,2,128]{3,1,0,2:T(8,128)} async-done(((f32[8,16,2,128]{3,1,0,2:T(8,128)}), f32[8,16,2,128]{3,1,0,2:T(8,128)}) %all-reduce.5.cloned.1.call-update) | async-done | bytes 131088 | tf_op jit(solution)/shard_map/psum | solution.py:69
  171.7 0.8 slice_bitcast_fusion.4
  172.5 3.3 %collective-permute-start.6 = (f32[8,16,1]{2,1,0:T(8,128)S(1)}, f32[8,16,1]{2,1,0:T(8,128)S(1)}, u32[]{:S(2)}, u32[]{:S(2)}) collective-permute-start(f32[8,16,1]{2,1,0:T(8,128)S(1)} %bitcast.104), channel_id=1, source_target_pairs={{1,0},{2,1},{3,2},{0,3},{5,4},{6,5},{7,6},{4,7},{9,8},{10,9},{11,1... | collective-permute-start | bytes 1544 | tf_op jit(solution)/shard_map/ppermute | solution.py:15
  176.0 2.0 %collective-permute-done.6 = f32[8,16,1]{2,1,0:T(8,128)S(1)} collective-permute-done((f32[8,16,1]{2,1,0:T(8,128)S(1)}, f32[8,16,1]{2,1,0:T(8,128)S(1)}, u32[]{:S(2)}, u32[]{:S(2)}) %collective-permute-start.6) | collective-permute-done | bytes 544 | tf_op jit(solution)/shard_map/ppermute | solution.py:15
  178.2 0.3 collective-permute-start.7
  178.5 6.2 %collective-permute-done.7 = f32[8,16,1]{2,1,0:T(8,128)S(1)} collective-permute-done((f32[8,16,1]{2,1,0:T(8,128)S(1)}, f32[8,16,1]{2,1,0:T(8,128)S(1)}, u32[]{:S(2)}, u32[]{:S(2)}) %collective-permute-start.7) | collective-permute-done | bytes 544 | tf_op jit(solution)/shard_map/ppermute | solution.py:15
  184.7 0.1 fusion.23
  184.9 0.1 mul.85
  185.0 0.8 copy-done.3
  185.8 0.8 maximum_multiply_fusion.1
  (41 shorter events, 1.4 us)
Async XLA Ops:
  7.2 13.3 %copy-start = (bf16[48,4096]{1,0:T(8,128)(2,1)S(1)}, bf16[48,4096]{1,0:T(8,128)(2,1)}, u32[]{:S(2)}) copy-start(bf16[48,4096]{1,0:T(8,128)(2,1)} %param.4) | copy-start | bytes 1179652
  7.2 78.1 %all-reduce.3.cloned.1.call-start = ((), (), s32[]{:S(2)}) async-start(), calls=%async_computation | async-start | bytes 262144 | tf_op jit(solution)/shard_map/psum | solution.py:69
  8.5 7.3 %collective-permute-start = (f32[8,16,1]{2,1,0:T(8,128)S(1)}, f32[8,16,1]{2,1,0:T(8,128)S(1)}, u32[]{:S(2)}, u32[]{:S(2)}) collective-permute-start(f32[8,16,1]{2,1,0:T(8,128)S(1)} %slice.98), channel_id=1, source_target_pairs={{3,0},{0,1},{1,2},{2,3},{7,4},{4,5},{5,6},{6,7},{11,8},{8,9},{9,10... | collective-permute-start | bytes 1544 | tf_op jit(solution)/shard_map/ppermute | solution.py:15
  15.9 4.3 %collective-permute-start.1 = (f32[8,16,1]{2,1,0:T(8,128)S(1)}, f32[8,16,1]{2,1,0:T(8,128)S(1)}, u32[]{:S(2)}, u32[]{:S(2)}) collective-permute-start(f32[8,16,1]{2,1,0:T(8,128)S(1)} %bitcast.105), channel_id=1, source_target_pairs={{1,0},{2,1},{3,2},{0,3},{5,4},{6,5},{7,6},{4,7},{9,8},{10,9},{11,1... | collective-permute-start | bytes 1544 | tf_op jit(solution)/shard_map/ppermute | solution.py:15
  20.7 12.3 %copy-start.5 = (f32[8,48]{1,0:T(8,128)S(1)}, f32[8,48]{1,0:T(8,128)}, u32[]{:S(2)}) copy-start(f32[8,48]{1,0:T(8,128)} %param.5) | copy-start | bytes 4612
  34.0 137.7 %all-reduce.5.cloned.1.call-start = ((), (), s32[]{:S(2)}) async-start(), calls=%async_computation.1 | async-start | bytes 262144 | tf_op jit(solution)/shard_map/psum | solution.py:69
  86.1 5.5 %copy-start.2 = (f32[8,16,2,128]{3,1,0,2:T(8,128)S(1)}, f32[8,16,2,128]{3,1,0,2:T(8,128)}, u32[]{:S(2)}) copy-start(f32[8,16,2,128]{3,1,0,2:T(8,128)} %all-reduce.3.cloned.1.call-done) | copy-start | bytes 393220
  86.1 5.4 %collective-permute-start.2 = (f32[8,16,1]{2,1,0:T(8,128)S(1)}, f32[8,16,1]{2,1,0:T(8,128)S(1)}, u32[]{:S(2)}, u32[]{:S(2)}) collective-permute-start(f32[8,16,1]{2,1,0:T(8,128)S(1)} %bitcast.103), channel_id=1, source_target_pairs={{1,0},{2,1},{3,2},{0,3},{5,4},{6,5},{7,6},{4,7},{9,8},{10,9},{11,1... | collective-permute-start | bytes 1544 | tf_op jit(solution)/shard_map/ppermute | solution.py:15
  91.7 6.6 %collective-permute-start.3 = (f32[8,16,1]{2,1,0:T(8,128)S(1)}, f32[8,16,1]{2,1,0:T(8,128)S(1)}, u32[]{:S(2)}, u32[]{:S(2)}) collective-permute-start(f32[8,16,1]{2,1,0:T(8,128)S(1)} %slice.106), channel_id=1, source_target_pairs={{3,0},{0,1},{1,2},{2,3},{7,4},{4,5},{5,6},{6,7},{11,8},{8,9},{9,10... | collective-permute-start | bytes 1544 | tf_op jit(solution)/shard_map/ppermute | solution.py:15
  98.3 0.7 copy-start.4
  99.2 6.1 %collective-permute-start.4 = (f32[8,16,1]{2,1,0:T(8,128)S(1)}, f32[8,16,1]{2,1,0:T(8,128)S(1)}, u32[]{:S(2)}, u32[]{:S(2)}) collective-permute-start(f32[8,16,1]{2,1,0:T(8,128)S(1)} %slice.110), channel_id=1, source_target_pairs={{3,0},{0,1},{1,2},{2,3},{7,4},{4,5},{5,6},{6,7},{11,8},{8,9},{9,10... | collective-permute-start | bytes 1544 | tf_op jit(solution)/shard_map/ppermute | solution.py:15
  105.4 4.3 %collective-permute-start.5 = (f32[8,16,1]{2,1,0:T(8,128)S(1)}, f32[8,16,1]{2,1,0:T(8,128)S(1)}, u32[]{:S(2)}, u32[]{:S(2)}) collective-permute-start(f32[8,16,1]{2,1,0:T(8,128)S(1)} %bitcast.102), channel_id=1, source_target_pairs={{1,0},{2,1},{3,2},{0,3},{5,4},{6,5},{7,6},{4,7},{9,8},{10,9},{11,1... | collective-permute-start | bytes 1544 | tf_op jit(solution)/shard_map/ppermute | solution.py:15
  120.6 0.6 copy-start.6
  172.5 5.5 %copy-start.1 = (f32[8,16,2,128]{3,1,0,2:T(8,128)S(1)}, f32[8,16,2,128]{3,1,0,2:T(8,128)}, u32[]{:S(2)}) copy-start(f32[8,16,2,128]{3,1,0,2:T(8,128)} %all-reduce.5.cloned.1.call-done) | copy-start | bytes 393220
  172.5 5.4 %collective-permute-start.6 = (f32[8,16,1]{2,1,0:T(8,128)S(1)}, f32[8,16,1]{2,1,0:T(8,128)S(1)}, u32[]{:S(2)}, u32[]{:S(2)}) collective-permute-start(f32[8,16,1]{2,1,0:T(8,128)S(1)} %bitcast.104), channel_id=1, source_target_pairs={{1,0},{2,1},{3,2},{0,3},{5,4},{6,5},{7,6},{4,7},{9,8},{10,9},{11,1... | collective-permute-start | bytes 1544 | tf_op jit(solution)/shard_map/ppermute | solution.py:15
  178.2 6.6 %collective-permute-start.7 = (f32[8,16,1]{2,1,0:T(8,128)S(1)}, f32[8,16,1]{2,1,0:T(8,128)S(1)}, u32[]{:S(2)}, u32[]{:S(2)}) collective-permute-start(f32[8,16,1]{2,1,0:T(8,128)S(1)} %slice.118), channel_id=1, source_target_pairs={{3,0},{0,1},{1,2},{2,3},{7,4},{4,5},{5,6},{6,7},{11,8},{8,9},{9,10... | collective-permute-start | bytes 1544 | tf_op jit(solution)/shard_map/ppermute | solution.py:15
  184.9 0.9 copy-start.3
Sparse Core Ops, SparseCore 0:
  34.1 51.1 all-reduce.2
  122.1 49.5 all-reduce.4
where the time goes:
time: 194 us; the launch traced here: 193 us
  waiting for transfers between devices  133 us (69%)
  blocking collectives  22.7 us (12%)
  between operations  14.3 us (7%)
  starting transfers between devices  12.9 us (7%)
  local copies, waits for them, and re-layouts  7.88 us (4%)
    psum x2, waiting for transfers between devices, body(): lax.psum(partial_grad, 'dp')  100 us
    ppermute x8, waiting for transfers between devices, passed_along(): return lax.ppermute(block, axis, route)  32.7 us
    psum x2, blocking collectives, body(): predicted = lax.psum(partial_pred, 'vox')  22.7 us
    ppermute x8, starting transfers between devices, passed_along(): return lax.ppermute(block, axis, route)  12.8 us
  transfers between devices with their start and end apart: 10, of which 10 were waited for; matrix products, arithmetic and copies ran while one was open for 1% of the time, Pallas kernels for 0%

commit v1 on v0

v1 whole, which is shorter than its diff:
```python
import functools

import jax
import jax.numpy as jnp
from jax import lax
from jax.experimental import pallas as pl
from jax.experimental.pallas import tpu as pltpu
from jax.sharding import PartitionSpec as P

step_size = 0.5
LANES = 128
F32 = jnp.float32
BF16 = jnp.bfloat16

E_LAST, E_FIRST, E_SECOND, O_LAST, O_FIRST = range(5)
KINDS = 5


def lanes_of(shape):
    return lax.broadcasted_iota(jnp.int32, shape, len(shape) - 1)


def turned(x, by):
    return pltpu.roll(x, by % LANES, x.ndim - 1)


def shifted_in(x, by, edge):
    free = 0 if by == 1 else LANES - 1
    return jnp.where(lanes_of(x.shape) == free, edge, turned(x, by))


def column(x, lane):
    return jnp.broadcast_to(x[:, lane : lane + 1], x.shape)


def edge_tile(pair_of, layers, base):
    tile = None
    for layer in reversed(range(layers)):
        even, odd = pair_of(layer)
        lane = lanes_of(even.shape)
        fresh = jnp.where((lane >= LANES - 1) | (lane <= 1), even, turned(odd, 3))
        if tile is None:
            tile = jnp.zeros_like(fresh)
        tile = jnp.where((lane >= LANES - 1) | (lane <= 3), fresh, turned(tile, KINDS))
    lane = lanes_of(tile.shape)
    tile = turned(tile, base + 1)
    return jnp.where((lane >= base) & (lane < base + KINDS * layers), tile, 0.0)


def kind_lane(lane, base, kind):
    return lax.rem(lane - base + KINDS * LANES, KINDS) == kind


def shrink(values, cutoff):
    return values - jnp.clip(values, -cutoff, cutoff)


def layer_tiles(ref, layer):
    start = layer * 2 * LANES
    return ref[:, start : start + LANES], ref[:, start + LANES : start + 2 * LANES]


def nt_dot(a, b):
    return lax.dot_general(a, b, (((1,), (1,)), ((), ())), preferred_element_type=F32)


def first_kernel(layers, wave_ref, k_ref, packet_ref, tile):
    rows = k_ref.shape[0]
    models = wave_ref.shape[0]
    parts = []
    for layer in range(layers):
        smooth, detail = layer_tiles(wave_ref, layer)
        even = smooth - 0.25 * (shifted_in(detail, 1, 0.0) + detail)
        odd = detail + 0.5 * (even + shifted_in(even, -1, 0.0))
        parts += [even, odd]
    model = jnp.concatenate(parts, axis=1).astype(BF16)
    tile[...] = edge_tile(lambda l: layer_tiles(wave_ref, l), layers, rows)
    tile[:, :rows] = nt_dot(model, k_ref[...])
    whole = tile[...]
    high = whole.astype(BF16).astype(F32)
    packet_ref[rows:, :] = jnp.concatenate([high, whole - high], axis=0).astype(BF16)
    edges = edge_tile(lambda l: tuple(t.astype(F32) for t in layer_tiles(k_ref, l)), layers, rows)
    packet_ref[:rows, :] = edges.astype(BF16)


def second_kernel(layers, n_vox, *refs):
    (observed_ref, *packets, out_ref, halo_ref, held) = refs
    models, rows = observed_ref.shape
    me = lax.axis_index("vox")
    for distance, packet in enumerate(packets):
        held[me ^ distance] = packet[...]
    lane = lanes_of((models, LANES))

    def edge_values(which):
        both = held[which, rows:, :].astype(F32)
        return both[:models] + both[models:]

    def mixed(from_left, from_right):
        at = lanes_of(from_left.shape)
        left = kind_lane(at, rows, E_LAST) | kind_lane(at, rows, O_LAST)
        return jnp.where(left, from_left, from_right)

    edge = [edge_values(z) for z in range(n_vox)]
    terms, columns = [], []
    for z in range(n_vox):
        before, after = edge[z - 1], edge[(z + 1) % n_vox]
        last = turned(before, E_FIRST - O_LAST)
        last_odd = turned(before, O_FIRST - O_LAST)
        next_smooth = turned(after, O_LAST - E_FIRST)
        next_detail = turned(after, O_LAST - O_FIRST)
        next_even = next_smooth - 0.25 * (edge[z] + next_detail)
        term = jnp.where(
            kind_lane(lane, rows, E_FIRST),
            -0.25 * last,
            jnp.where(
                kind_lane(lane, rows, O_FIRST),
                -0.125 * last_odd,
                jnp.where(kind_lane(lane, rows, O_LAST), 0.5 * next_even, 0.0),
            ),
        )
        inside = (lane >= rows) & (lane < rows + KINDS * layers)
        terms.append(jnp.where(inside, term, 0.0).astype(BF16))
        columns.append(held[z, :rows, :])
    predicted = nt_dot(jnp.concatenate(terms, axis=1), jnp.concatenate(columns, axis=1))
    shares = edge[0]
    for z in range(1, n_vox):
        shares = shares + edge[z]
    predicted = predicted + shares[:, :rows]
    left, right = lax.rem(me + n_vox - 1, n_vox), lax.rem(me + 1, n_vox)
    out_ref[:rows, :] = mixed(held[left, :rows, :].astype(F32), held[right, :rows, :].astype(F32))
    out_ref[rows:, :] = jnp.zeros((2 * models, LANES), F32)
    out_ref[rows : rows + models, :rows] = observed_ref[...] - predicted
    out_ref[rows + models :, :rows] = observed_ref[...]
    halo_ref[...] = mixed(edge_values(left), edge_values(right))


def back_projected(residual, k_ref, halo_columns, g_ref):
    width = k_ref.shape[1]
    sent = residual.astype(BF16)
    g_ref[:, :width] = jnp.dot(sent, k_ref[...], preferred_element_type=F32).astype(BF16)
    g_ref[:, width:] = jnp.dot(sent, halo_columns, preferred_element_type=F32).astype(BF16)


def third_kernel(mine_ref, other_ref, k_ref, g_ref, columns_ref, observed_ref, held, lhs):
    core = lax.rem(lax.axis_index("dp"), 2)
    models = g_ref.shape[0]
    rows = mine_ref.shape[0] - 2 * models
    held[core] = mine_ref[...]
    held[1 - core] = other_ref[...]
    lhs[...] = jnp.zeros_like(lhs)
    observed_ref[...] = jnp.zeros_like(observed_ref)
    for c in range(2):
        lhs[:, c * rows : (c + 1) * rows] = held[c, rows : rows + models, :rows]
        observed_ref[:, c * rows : (c + 1) * rows] = held[c, rows + models :, :rows]
    columns = jnp.concatenate([held[c, :rows, :] for c in range(2)], axis=0).astype(BF16)
    columns_ref[...] = columns
    back_projected(lhs[:, : 2 * rows], k_ref, columns, g_ref)


def tree_sum(values):
    while len(values) > 1:
        values = [a + b for a, b in zip(values[::2], values[1::2])]
    return values[0]


def stepped_layer(layer, base, gradient, wave_ref, cut_ref, halo, full):
    even, odd = gradient(layer)
    edge = gradient(None)
    lane = base + KINDS * layer

    def at(tile, kind):
        return column(tile, lane + kind)

    cut_s, cut_d = column(cut_ref, 2 * layer), column(cut_ref, 2 * layer + 1)
    smooth, detail = layer_tiles(wave_ref, layer)
    even_next = at(edge, E_FIRST)
    detail_g = odd - 0.5 * (even + shifted_in(even, -1, even_next))
    before_g = at(edge, O_LAST) - 0.5 * (at(edge, E_LAST) + column(even, 0))
    smooth_g = even + 0.25 * (shifted_in(detail_g, 1, before_g) + detail_g)
    smooth = shrink(smooth + step_size * smooth_g, cut_s)
    detail = shrink(detail + step_size * detail_g, cut_d)
    if not full:
        return smooth, detail
    after_g = at(edge, O_FIRST) - 0.5 * (even_next + at(edge, E_SECOND))
    next_g = even_next + 0.25 * (column(detail_g, LANES - 1) + after_g)
    before = shrink(at(halo, O_LAST) + step_size * before_g, cut_d)
    next_s = shrink(at(halo, E_FIRST) + step_size * next_g, cut_s)
    after = shrink(at(halo, O_FIRST) + step_size * after_g, cut_d)
    return smooth, detail, before, next_s, after


def gradient_reader(refs):
    width = refs[0].shape[1]

    def read(layer):
        if layer is None:
            return tree_sum([r[:, width - LANES :].astype(F32) for r in refs])
        start = 2 * LANES * layer
        return tuple(
            tree_sum([r[:, s : s + LANES].astype(F32) for r in refs]) for s in (start, start + LANES)
        )

    return functools.lru_cache(None)(read)


def fourth_kernel(layers, base, wave_ref, cut_ref, halo_ref, k_ref, *refs):
    *g_refs, new_ref, pred_ref = refs
    gradient = gradient_reader(g_refs)
    cut, halo = cut_ref[...], halo_ref[...]
    parts = []
    for layer in range(layers):
        smooth, detail, before, next_s, after = stepped_layer(layer, base, gradient, wave_ref, cut, halo, True)
        start = 2 * LANES * layer
        new_ref[:, start : start + LANES] = smooth
        new_ref[:, start + LANES : start + 2 * LANES] = detail
        even = smooth - 0.25 * (shifted_in(detail, 1, before) + detail)
        even_next = next_s - 0.25 * (column(detail, LANES - 1) + after)
        odd = detail + 0.5 * (even + shifted_in(even, -1, even_next))
        parts += [even, odd]
    model = jnp.concatenate(parts, axis=1).astype(BF16)
    pred_ref[...] = jnp.zeros_like(pred_ref)
    pred_ref[:, : k_ref.shape[0]] = nt_dot(model, k_ref[...])


def fifth_kernel(k_ref, columns_ref, observed_ref, *refs):
    *shares, g_ref, residual_ref = refs
    core = lax.rem(lax.axis_index("dp"), 2)
    rows = residual_ref.shape[1]
    residual = observed_ref[...] - tree_sum([s[...] for s in shares])
    back_projected(residual[:, : 2 * rows], k_ref, columns_ref[...], g_ref)
    residual_ref[...] = jnp.where(core == 0, residual[:, :rows], residual[:, rows : 2 * rows])


def sixth_kernel(layers, base, wave_ref, cut_ref, *refs):
    *g_refs, new_ref = refs
    gradient = gradient_reader(g_refs)
    cut = cut_ref[...]
    for layer in range(layers):
        smooth, detail = stepped_layer(layer, base, gradient, wave_ref, cut, None, False)
        start = 2 * LANES * layer
        new_ref[:, start : start + LANES] = smooth
        new_ref[:, start + LANES : start + 2 * LANES] = detail


def from_partner(x, axis, distance):
    return lax.ppermute(x, axis, [(i, i ^ distance) for i in range(lax.axis_size(axis))])


def shares_of(x, axis, lowest):
    size = lax.axis_size(axis) // lowest
    while size > 4:
        parts = [x] + [from_partner(x, axis, lowest * d) for d in range(1, 4)]
        x = tree_sum([p.astype(F32) for p in parts]).astype(x.dtype)
        lowest, size = lowest * 4, size // 4
    return [x] + [from_partner(x, axis, lowest * d) for d in range(1, size)]


def call(kernel, out_shape, scratch=(), *args):
    return pl.pallas_call(
        kernel,
        out_shape=out_shape,
        in_specs=[pl.BlockSpec(memory_space=pltpu.VMEM)] * len(args),
        out_specs=jax.tree.map(lambda _: pl.BlockSpec(memory_space=pltpu.VMEM), out_shape),
        scratch_shapes=list(scratch),
    )(*args)


def body(kernels, observed, initial, threshold):
    models, width = initial.shape
    rows = kernels.shape[0]
    layers = threshold.shape[1]
    n_vox = lax.axis_size("vox")
    assert width == 2 * layers * LANES and rows + KINDS * layers <= LANES and 2 * rows <= LANES
    shape = jax.ShapeDtypeStruct
    cut = threshold.reshape(models, layers * 2)
    cut = jnp.pad(cut, ((0, 0), (0, LANES - 2 * layers)))

    packet_rows = rows + 2 * models
    packet = call(
        functools.partial(first_kernel, layers),
        shape((packet_rows, LANES), BF16),
        [pltpu.VMEM((models, LANES), F32)],
        initial,
        kernels,
    )
    packets = [packet] + [from_partner(packet, "vox", d) for d in range(1, n_vox)]

    other = from_partner(kernels, "dp", 1)
    first_core = lax.rem(lax.axis_index("dp"), 2) == 0
    both = jnp.where(first_core, jnp.concatenate([kernels, other]), jnp.concatenate([other, kernels]))

    mine, halo = call(
        functools.partial(second_kernel, layers, n_vox),
        (shape((packet_rows, LANES), F32), shape((models, LANES), F32)),
        [pltpu.VMEM((n_vox, packet_rows, LANES), BF16)],
        observed,
        *packets,
    )
    theirs = from_partner(mine, "dp", 1)
    g, columns, observed_both = call(
        third_kernel,
        (
            shape((models, width + LANES), BF16),
            shape((2 * rows, LANES), BF16),
            shape((models, LANES), F32),
        ),
        [pltpu.VMEM((2, packet_rows, LANES), F32), pltpu.VMEM((models, LANES), F32)],
        mine,
        theirs,
        both,
    )
    wavelets, predicted = call(
        functools.partial(fourth_kernel, layers, rows),
        (shape((models, width), F32), shape((models, LANES), F32)),
        (),
        initial,
        cut,
        halo,
        both,
        *shares_of(g, "dp", 2),
    )
    g, residual = call(
        fifth_kernel,
        (shape((models, width + LANES), BF16), shape((models, rows), F32)),
        (),
        both,
        columns,
        observed_both,
        *shares_of(predicted, "vox", 1),
    )
    coefficients = call(
        functools.partial(sixth_kernel, layers, rows),
        shape((models, width), F32),
        (),
        wavelets,
        cut,
        *shares_of(g, "dp", 2),
    )
    return coefficients, residual


def solution(mesh):
    return jax.shard_map(
        body,
        mesh=mesh,
        in_specs=(P("dp", "vox"), P(None, "dp"), P(None, "vox"), P()),
        out_specs=(P(None, "vox"), P(None, "dp")),
        check_vma=False,
    )
```

time: 194 us -> 51.5 us (0.27)
  waiting for transfers between devices: 133 us -> 15 us
  blocking collectives: 22.7 us -> 0 us
  between operations: 14.3 us -> 0.68 us
  Pallas kernels: 0 us -> 13.5 us
  starting transfers between devices: 12.9 us -> 17.1 us
  local copies, waits for them, and re-layouts: 7.88 us -> 3.79 us
    psum x2 -> x0, waiting for transfers between devices: 100 us -> none  [body(): lax.psum(partial_grad, 'dp')]
    psum x2 -> x0, blocking collectives: 22.7 us -> none  [body(): predicted = lax.psum(partial_pred, 'vox')]
    ppermute x8 -> x14, waiting for transfers between devices: 32.7 us -> 15 us  [from_partner(): lax.ppermute(x, axis, [(i, i ^ distance) for i in range(lax.axis_size(axi...]
    pallas_call x0 -> x6, Pallas kernels: none -> 13.5 us  [call(): pl.pallas_call(kernel, out_shape=out_shape, in_specs=[pl.BlockSpec(memory...]
    ppermute x8 -> x14, starting transfers between devices: 12.8 us -> 17.1 us  [from_partner(): lax.ppermute(x, axis, [(i, i ^ distance) for i in range(lax.axis_size(axi...]
    reshape x5 -> x1, local copies, waits for them, and re-layouts: 2.66 us -> 0.07 us  [body(): cut = threshold.reshape(models, layers * 2)]
  transfers between devices with their start and end apart: 10 -> 14, of which waited for: 10 -> 11; matrix products, arithmetic and copies ran while one was open for 1% -> 4% of each run, Pallas kernels for 0% -> 9%
where the time goes in v1:
time: 51.5 us; the launch traced here: 51.2 us
  starting transfers between devices  17.1 us (33%)
  waiting for transfers between devices  15 us (29%)
  Pallas kernels  13.5 us (26%)
  local copies, waits for them, and re-layouts  3.79 us (7%)
  other arithmetic  1.06 us (2%)
  between operations  0.68 us (1%)
    ppermute x14, starting transfers between devices, from_partner(): lax.ppermute(x, axis, [(i, i ^ distance) for i in range(lax.axis_size(axi...  17.1 us
    ppermute x14, waiting for transfers between devices, from_partner(): lax.ppermute(x, axis, [(i, i ^ distance) for i in range(lax.axis_size(axi...  15 us
    pallas_call x6, Pallas kernels, call(): pl.pallas_call(kernel, out_shape=out_shape, in_specs=[pl.BlockSpec(memory...  13.5 us
    unnamed x31, local copies, waits for them, and re-layouts  3.13 us
    select_n x1, other arithmetic, body(): jnp.where(first_core, jnp.concatenate([kernels, other]), jnp.concatenate(...  1.06 us
  transfers between devices with their start and end apart: 14, of which 11 were waited for; matrix products, arithmetic and copies ran while one was open for 4% of the time, Pallas kernels for 9%

profile of v1, /device:TPU:0, one launch (start us, length us, event | category | flops | bytes accessed | tf_op | source)
XLA Modules:
  0.0 51.2 jit_solution(17644177064764049452)
XLA Ops:
  0.6 0.0 copy-start
  0.6 0.5 %collective-permute-start.3 = (bf16[48,4096]{1,0:T(8,128)(2,1)}, bf16[48,4096]{1,0:T(8,128)(2,1)S(1)}, u32[]{:S(2)}, u32[]{:S(2)}) collective-permute-start(bf16[48,4096]{1,0:T(8,128)(2,1)} %k_ref.1), channel_id=1, source_target_pairs={{0,4},{4,0},{8,12},{12,8},{16,20},{20,16},{24,28},{28,24},{1,5},{5... | collective-permute-start | bytes 1179656 | tf_op jit(solution)/shard_map/ppermute | solution.py:246
  1.2 2.9 %shard_map.59.refs_1_ = bf16[64,128]{1,0:T(8,128)(2,1)} custom-call(f32[8,4096]{1,0:T(8,128)} %wave_ref.3, bf16[48,4096]{1,0:T(8,128)(2,1)} %k_ref.1), custom_call_target="tpu_custom_call" | custom-call | tf_op jit(solution)/shard_map/pallas_call | solution.py:259
  4.0 2.6 %collective-permute-start = (bf16[64,128]{1,0:T(8,128)(2,1)}, bf16[64,128]{1,0:T(8,128)(2,1)S(1)}, u32[]{:S(2)}, u32[]{:S(2)}) collective-permute-start(bf16[64,128]{1,0:T(8,128)(2,1)} %shard_map.59.refs_1_), channel_id=1, source_target_pairs={{0,1},{1,0},{2,3},{3,2},{4,5},{5,4},{6,7},{7,6},{8,9},{9,8},{10,11... | collective-permute-start | bytes 49160 | tf_op jit(solution)/shard_map/ppermute | solution.py:246
  6.6 2.6 %collective-permute-start.1 = (bf16[64,128]{1,0:T(8,128)(2,1)}, bf16[64,128]{1,0:T(8,128)(2,1)S(1)}, u32[]{:S(2)}, u32[]{:S(2)}) collective-permute-start(bf16[64,128]{1,0:T(8,128)(2,1)} %shard_map.59.refs_1_), channel_id=1, source_target_pairs={{0,2},{1,3},{2,0},{3,1},{4,6},{5,7},{6,4},{7,5},{8,10},{9,11},{10,... | collective-permute-start | bytes 49160 | tf_op jit(solution)/shard_map/ppermute | solution.py:246
  9.2 0.0 collective-permute-start.2
  9.2 0.0 collective-permute-done.refs_2_
  9.2 2.2 %collective-permute-done.1.refs_3_ = bf16[64,128]{1,0:T(8,128)(2,1)S(1)} collective-permute-done((bf16[64,128]{1,0:T(8,128)(2,1)}, bf16[64,128]{1,0:T(8,128)(2,1)S(1)}, u32[]{:S(2)}, u32[]{:S(2)}) %collective-permute-start.1) | collective-permute-done | bytes 16416 | tf_op jit(solution)/shard_map/ppermute | solution.py:246
  11.5 3.5 %collective-permute-done.2.refs_4_ = bf16[64,128]{1,0:T(8,128)(2,1)S(1)} collective-permute-done((bf16[64,128]{1,0:T(8,128)(2,1)}, bf16[64,128]{1,0:T(8,128)(2,1)S(1)}, u32[]{:S(2)}, u32[]{:S(2)}) %collective-permute-start.2) | collective-permute-done | bytes 16416 | tf_op jit(solution)/shard_map/ppermute | solution.py:246
  15.0 0.0 copy-done.8
  15.0 0.6 %copy-done.10 = bf16[64,128]{1,0:T(8,128)(2,1)} copy-done((bf16[64,128]{1,0:T(8,128)(2,1)}, bf16[64,128]{1,0:T(8,128)(2,1)S(1)}, u32[]{:S(2)}) %copy-start.10) | copy-done | bytes 16408
  15.6 1.6 %shard_map.60 = (f32[64,128]{1,0:T(8,128)}, f32[8,128]{1,0:T(8,128)}) custom-call(f32[8,48]{1,0:T(8,128)} %refs_0_.1, bf16[64,128]{1,0:T(8,128)(2,1)} %shard_map.59.refs_1_, bf16[64,128]{1,0:T(8,128)(2,1)} %copy-done.8, bf16[64,128]{1,0:T(8,128)(2,1)} %copy-done.9, bf16[64,128]{1,0:T(8,128)(2,1)} %copy-done.10), custom_call_target="tpu_custom_call" | custom-call | tf_op jit(solution)/shard_map/pallas_call | solution.py:259
  17.2 0.0 collective-permute-start.4
  17.2 0.0 collective-permute-done.3
  17.2 1.1 %maximum_select_fusion.k_ref = bf16[96,4096]{1,0:T(8,128)(2,1)} fusion(bf16[48,4096]{1,0:T(8,128)(2,1)S(1)} %collective-permute-done.3, bf16[48,4096]{1,0:T(8,128)(2,1)S(1)} %copy-done, pred[]{:T(512)S(6)} %eq.3), kind=kLoop, calls=%fused_computation | loop fusion | flops 3538944 | bytes 1572865 | tf_op jit(solution)/shard_map/jit(_where)/select_n | solution.py:290
  18.3 0.3 collective-permute-done.4.other_ref
  18.6 0.6 %copy-done.7 = f32[64,128]{1,0:T(8,128)} copy-done((f32[64,128]{1,0:T(8,128)}, f32[64,128]{1,0:T(8,128)S(1)}, u32[]{:S(2)}) %copy-start.7) | copy-done | bytes 32792
  19.2 2.1 %shard_map.61 = (bf16[8,4224]{1,0:T(8,128)(2,1)}, bf16[96,128]{1,0:T(8,128)(2,1)}, f32[8,128]{1,0:T(8,128)}) custom-call(f32[64,128]{1,0:T(8,128)} %get-tuple-element.12.mine_ref, f32[64,128]{1,0:T(8,128)} %copy-done.7, bf16[96,4096]{1,0:T(8,128)(2,1)} %maximum_select_fusion.k_ref), custom_call_target="tpu_custom_call" | custom-call | tf_op jit(solution)/shard_map/pallas_call | solution.py:259
  21.3 1.5 %collective-permute-start.5 = (bf16[8,4224]{1,0:T(8,128)(2,1)}, bf16[8,4224]{1,0:T(8,128)(2,1)S(1)}, u32[]{:S(2)}, u32[]{:S(2)}) collective-permute-start(bf16[8,4224]{1,0:T(8,128)(2,1)} %get-tuple-element.13.refs_0_), channel_id=1, source_target_pairs={{0,8},{4,12},{8,0},{12,4},{16,24},{20,28},{24,16},{28,20},{1,9},{5... | collective-permute-start | bytes 202760 | tf_op jit(solution)/shard_map/ppermute | solution.py:246
  22.8 1.5 %collective-permute-start.6 = (bf16[8,4224]{1,0:T(8,128)(2,1)}, bf16[8,4224]{1,0:T(8,128)(2,1)S(1)}, u32[]{:S(2)}, u32[]{:S(2)}) collective-permute-start(bf16[8,4224]{1,0:T(8,128)(2,1)} %get-tuple-element.13.refs_0_), channel_id=1, source_target_pairs={{0,16},{4,20},{8,24},{12,28},{16,0},{20,4},{24,8},{28,12},{1,17},{... | collective-permute-start | bytes 202760 | tf_op jit(solution)/shard_map/ppermute | solution.py:246
  24.3 0.5 collective-permute-start.7
  24.8 0.1 copy.7
  24.9 0.1 copy.8
  25.0 0.6 %pad.4.cut_ref = f32[8,128]{1,0:T(8,128)} pad(f32[8,32]{1,0:T(8,128)S(1)} %copy.8, f32[]{:T(128)} %constant.9.clone.1), padding=0_0x0_96 | pad | bytes 5124 | tf_op jit(solution)/shard_map/jit(_pad)/pad | solution.py:276
  25.6 0.3 collective-permute-done.5.refs_1_
  25.8 1.5 %collective-permute-done.6.refs_2_ = bf16[8,4224]{1,0:T(8,128)(2,1)S(1)} collective-permute-done((bf16[8,4224]{1,0:T(8,128)(2,1)}, bf16[8,4224]{1,0:T(8,128)(2,1)S(1)}, u32[]{:S(2)}, u32[]{:S(2)}) %collective-permute-start.6) | collective-permute-done | bytes 67616 | tf_op jit(solution)/shard_map/ppermute | solution.py:246
  27.3 2.4 %collective-permute-done.7.refs_3_ = bf16[8,4224]{1,0:T(8,128)(2,1)S(1)} collective-permute-done((bf16[8,4224]{1,0:T(8,128)(2,1)}, bf16[8,4224]{1,0:T(8,128)(2,1)S(1)}, u32[]{:S(2)}, u32[]{:S(2)}) %collective-permute-start.7) | collective-permute-done | bytes 67616 | tf_op jit(solution)/shard_map/ppermute | solution.py:246
  29.7 0.0 copy-done.2
  29.7 0.6 %copy-done.3 = bf16[8,4224]{1,0:T(8,128)(2,1)} copy-done((bf16[8,4224]{1,0:T(8,128)(2,1)}, bf16[8,4224]{1,0:T(8,128)(2,1)S(1)}, u32[]{:S(2)}) %copy-start.3) | copy-done | bytes 67608
  30.4 2.6 %shard_map.62 = (f32[8,4096]{1,0:T(8,128)}, f32[8,128]{1,0:T(8,128)}) custom-call(f32[8,4096]{1,0:T(8,128)} %wave_ref.3, f32[8,128]{1,0:T(8,128)} %pad.4.cut_ref, f32[8,128]{1,0:T(8,128)} %get-tuple-element.11.halo_ref, bf16[96,4096]{1,0:T(8,128)(2,1)} %maximum_select_fusion.k_ref, bf16[8,4224]{1,0:T(8,128)(2,1)} %get-tuple-element.13.refs_0_, ...), custom_call_target="tpu_custom_call" | custom-call | tf_op jit(solution)/shard_map/pallas_call | solution.py:259
  33.0 0.2 collective-permute-start.10
  33.2 0.0 collective-permute-start.8
  33.3 4.1 %collective-permute-start.9 = (f32[8,128]{1,0:T(8,128)}, f32[8,128]{1,0:T(8,128)S(1)}, u32[]{:S(2)}, u32[]{:S(2)}) collective-permute-start(f32[8,128]{1,0:T(8,128)} %get-tuple-element.17.refs_0_), channel_id=1, source_target_pairs={{0,2},{1,3},{2,0},{3,1},{4,6},{5,7},{6,4},{7,5},{8,10},{9,11},{10,... | collective-permute-start | bytes 12296 | tf_op jit(solution)/shard_map/ppermute | solution.py:246
  37.4 1.2 %collective-permute-done.10.refs_3_ = f32[8,128]{1,0:T(8,128)S(1)} collective-permute-done((f32[8,128]{1,0:T(8,128)}, f32[8,128]{1,0:T(8,128)S(1)}, u32[]{:S(2)}, u32[]{:S(2)}) %collective-permute-start.10) | collective-permute-done | bytes 4128 | tf_op jit(solution)/shard_map/ppermute | solution.py:246
  38.6 0.0 collective-permute-done.8.refs_1_
  38.6 0.6 %collective-permute-done.9.refs_2_ = f32[8,128]{1,0:T(8,128)S(1)} collective-permute-done((f32[8,128]{1,0:T(8,128)}, f32[8,128]{1,0:T(8,128)S(1)}, u32[]{:S(2)}, u32[]{:S(2)}) %collective-permute-start.9) | collective-permute-done | bytes 4128 | tf_op jit(solution)/shard_map/ppermute | solution.py:246
  39.2 0.0 copy-done.13
  39.2 0.6 %copy-done.14 = f32[8,128]{1,0:T(8,128)} copy-done((f32[8,128]{1,0:T(8,128)}, f32[8,128]{1,0:T(8,128)S(1)}, u32[]{:S(2)}) %copy-start.14) | copy-done | bytes 4120
  39.8 2.0 %shard_map.63 = (bf16[8,4224]{1,0:T(8,128)(2,1)}, f32[8,48]{1,0:T(8,128)}) custom-call(bf16[96,4096]{1,0:T(8,128)(2,1)} %maximum_select_fusion.k_ref, bf16[96,128]{1,0:T(8,128)(2,1)} %get-tuple-element.15.columns_ref, f32[8,128]{1,0:T(8,128)} %get-tuple-element.16.observed_ref, f32[8,128]{1,0:T(8,128)} %get-tuple-element.17.refs_0_, f32[8,128]{1,0:T(8,128)} %copy-done.13, ...), custom_call_target="tpu_custom_call" | custom-call | tf_op jit(solution)/shard_map/pallas_call | solution.py:259
  41.8 0.5 %collective-permute-start.11 = (bf16[8,4224]{1,0:T(8,128)(2,1)}, bf16[8,4224]{1,0:T(8,128)(2,1)S(1)}, u32[]{:S(2)}, u32[]{:S(2)}) collective-permute-start(bf16[8,4224]{1,0:T(8,128)(2,1)} %get-tuple-element.18.refs_0_), channel_id=1, source_target_pairs={{0,8},{4,12},{8,0},{12,4},{16,24},{20,28},{24,16},{28,20},{1,9},{5... | collective-permute-start | bytes 202760 | tf_op jit(solution)/shard_map/ppermute | solution.py:246
  42.4 0.5 %collective-permute-start.12 = (bf16[8,4224]{1,0:T(8,128)(2,1)}, bf16[8,4224]{1,0:T(8,128)(2,1)S(1)}, u32[]{:S(2)}, u32[]{:S(2)}) collective-permute-start(bf16[8,4224]{1,0:T(8,128)(2,1)} %get-tuple-element.18.refs_0_), channel_id=1, source_target_pairs={{0,16},{4,20},{8,24},{12,28},{16,0},{20,4},{24,8},{28,12},{1,17},{... | collective-permute-start | bytes 202760 | tf_op jit(solution)/shard_map/ppermute | solution.py:246
  42.9 2.4 %collective-permute-start.13 = (bf16[8,4224]{1,0:T(8,128)(2,1)}, bf16[8,4224]{1,0:T(8,128)(2,1)S(1)}, u32[]{:S(2)}, u32[]{:S(2)}) collective-permute-start(bf16[8,4224]{1,0:T(8,128)(2,1)} %get-tuple-element.18.refs_0_), channel_id=1, source_target_pairs={{0,24},{4,28},{8,16},{12,20},{16,8},{20,12},{24,0},{28,4},{1,25},{... | collective-permute-start | bytes 202760 | tf_op jit(solution)/shard_map/ppermute | solution.py:246
  45.3 1.0 %collective-permute-done.11.refs_1_ = bf16[8,4224]{1,0:T(8,128)(2,1)S(1)} collective-permute-done((bf16[8,4224]{1,0:T(8,128)(2,1)}, bf16[8,4224]{1,0:T(8,128)(2,1)S(1)}, u32[]{:S(2)}, u32[]{:S(2)}) %collective-permute-start.11) | collective-permute-done | bytes 67616 | tf_op jit(solution)/shard_map/ppermute | solution.py:246
  46.3 0.5 %collective-permute-done.12.refs_2_ = bf16[8,4224]{1,0:T(8,128)(2,1)S(1)} collective-permute-done((bf16[8,4224]{1,0:T(8,128)(2,1)}, bf16[8,4224]{1,0:T(8,128)(2,1)S(1)}, u32[]{:S(2)}, u32[]{:S(2)}) %collective-permute-start.12) | collective-permute-done | bytes 67616 | tf_op jit(solution)/shard_map/ppermute | solution.py:246
  46.9 1.4 %collective-permute-done.13.refs_3_ = bf16[8,4224]{1,0:T(8,128)(2,1)S(1)} collective-permute-done((bf16[8,4224]{1,0:T(8,128)(2,1)}, bf16[8,4224]{1,0:T(8,128)(2,1)S(1)}, u32[]{:S(2)}, u32[]{:S(2)}) %collective-permute-start.13) | collective-permute-done | bytes 67616 | tf_op jit(solution)/shard_map/ppermute | solution.py:246
  48.3 0.0 copy-done.4
  48.3 0.6 %copy-done.6 = bf16[8,4224]{1,0:T(8,128)(2,1)} copy-done((bf16[8,4224]{1,0:T(8,128)(2,1)}, bf16[8,4224]{1,0:T(8,128)(2,1)S(1)}, u32[]{:S(2)}) %copy-start.6) | copy-done | bytes 67608
  48.9 2.2 %shard_map.64 = f32[8,4096]{1,0:T(8,128)} custom-call(f32[8,4096]{1,0:T(8,128)} %get-tuple-element.14.wave_ref, f32[8,128]{1,0:T(8,128)} %pad.4.cut_ref, bf16[8,4224]{1,0:T(8,128)(2,1)} %get-tuple-element.18.refs_0_, bf16[8,4224]{1,0:T(8,128)(2,1)} %copy-done.4, bf16[8,4224]{1,0:T(8,128)(2,1)} %copy-done.5, bf16[8,4224]{1,0:T(8,128)(2,1)} %copy-done.6), custom_call_target="tpu_custom_call" | custom-call | tf_op jit(solution)/shard_map/pallas_call | solution.py:259
  (20 shorter events, 0.0 us)
Async XLA Ops:
  0.6 16.6 %copy-start = (bf16[48,4096]{1,0:T(8,128)(2,1)S(1)}, bf16[48,4096]{1,0:T(8,128)(2,1)}, u32[]{:S(2)}) copy-start(bf16[48,4096]{1,0:T(8,128)(2,1)} %k_ref.1) | copy-start | bytes 1179652
  0.6 16.6 %collective-permute-start.3 = (bf16[48,4096]{1,0:T(8,128)(2,1)}, bf16[48,4096]{1,0:T(8,128)(2,1)S(1)}, u32[]{:S(2)}, u32[]{:S(2)}) collective-permute-start(bf16[48,4096]{1,0:T(8,128)(2,1)} %k_ref.1), channel_id=1, source_target_pairs={{0,4},{4,0},{8,12},{12,8},{16,20},{20,16},{24,28},{28,24},{1,5},{5... | collective-permute-start | bytes 1179656 | tf_op jit(solution)/shard_map/ppermute | solution.py:246
  4.0 5.2 %collective-permute-start = (bf16[64,128]{1,0:T(8,128)(2,1)}, bf16[64,128]{1,0:T(8,128)(2,1)S(1)}, u32[]{:S(2)}, u32[]{:S(2)}) collective-permute-start(bf16[64,128]{1,0:T(8,128)(2,1)} %shard_map.59.refs_1_), channel_id=1, source_target_pairs={{0,1},{1,0},{2,3},{3,2},{4,5},{5,4},{6,7},{7,6},{8,9},{9,8},{10,11... | collective-permute-start | bytes 49160 | tf_op jit(solution)/shard_map/ppermute | solution.py:246
  6.6 4.8 %collective-permute-start.1 = (bf16[64,128]{1,0:T(8,128)(2,1)}, bf16[64,128]{1,0:T(8,128)(2,1)S(1)}, u32[]{:S(2)}, u32[]{:S(2)}) collective-permute-start(bf16[64,128]{1,0:T(8,128)(2,1)} %shard_map.59.refs_1_), channel_id=1, source_target_pairs={{0,2},{1,3},{2,0},{3,1},{4,6},{5,7},{6,4},{7,5},{8,10},{9,11},{10,... | collective-permute-start | bytes 49160 | tf_op jit(solution)/shard_map/ppermute | solution.py:246
  9.2 5.7 %collective-permute-start.2 = (bf16[64,128]{1,0:T(8,128)(2,1)}, bf16[64,128]{1,0:T(8,128)(2,1)S(1)}, u32[]{:S(2)}, u32[]{:S(2)}) collective-permute-start(bf16[64,128]{1,0:T(8,128)(2,1)} %shard_map.59.refs_1_), channel_id=1, source_target_pairs={{0,3},{1,2},{2,1},{3,0},{4,7},{5,6},{6,5},{7,4},{8,11},{9,10},{10,... | collective-permute-start | bytes 49160 | tf_op jit(solution)/shard_map/ppermute | solution.py:246
  9.2 5.7 %copy-start.8 = (bf16[64,128]{1,0:T(8,128)(2,1)}, bf16[64,128]{1,0:T(8,128)(2,1)S(1)}, u32[]{:S(2)}) copy-start(bf16[64,128]{1,0:T(8,128)(2,1)S(1)} %collective-permute-done.refs_2_) | copy-start | bytes 49156
  11.5 3.5 %copy-start.9 = (bf16[64,128]{1,0:T(8,128)(2,1)}, bf16[64,128]{1,0:T(8,128)(2,1)S(1)}, u32[]{:S(2)}) copy-start(bf16[64,128]{1,0:T(8,128)(2,1)S(1)} %collective-permute-done.1.refs_3_) | copy-start | bytes 49156
  15.0 0.6 %copy-start.10 = (bf16[64,128]{1,0:T(8,128)(2,1)}, bf16[64,128]{1,0:T(8,128)(2,1)S(1)}, u32[]{:S(2)}) copy-start(bf16[64,128]{1,0:T(8,128)(2,1)S(1)} %collective-permute-done.2.refs_4_) | copy-start | bytes 49156
  17.2 1.4 %collective-permute-start.4 = (f32[64,128]{1,0:T(8,128)}, f32[64,128]{1,0:T(8,128)S(1)}, u32[]{:S(2)}, u32[]{:S(2)}) collective-permute-start(f32[64,128]{1,0:T(8,128)} %get-tuple-element.12.mine_ref), channel_id=1, source_target_pairs={{0,4},{4,0},{8,12},{12,8},{16,20},{20,16},{24,28},{28,24},{1,5},{5... | collective-permute-start | bytes 98312 | tf_op jit(solution)/shard_map/ppermute | solution.py:246
  18.3 6.5 %copy-start.11 = (f32[8,16,2]{1,2,0:T(2,128)S(1)}, f32[8,16,2]{1,2,0:T(2,128)}, u32[]{:S(2)}) copy-start(f32[8,16,2]{1,2,0:T(2,128)} %param.7) | copy-start | bytes 3076
  18.6 0.6 %copy-start.7 = (f32[64,128]{1,0:T(8,128)}, f32[64,128]{1,0:T(8,128)S(1)}, u32[]{:S(2)}) copy-start(f32[64,128]{1,0:T(8,128)S(1)} %collective-permute-done.4.other_ref) | copy-start | bytes 98308
  21.3 4.5 %collective-permute-start.5 = (bf16[8,4224]{1,0:T(8,128)(2,1)}, bf16[8,4224]{1,0:T(8,128)(2,1)S(1)}, u32[]{:S(2)}, u32[]{:S(2)}) collective-permute-start(bf16[8,4224]{1,0:T(8,128)(2,1)} %get-tuple-element.13.refs_0_), channel_id=1, source_target_pairs={{0,8},{4,12},{8,0},{12,4},{16,24},{20,28},{24,16},{28,20},{1,9},{5... | collective-permute-start | bytes 202760 | tf_op jit(solution)/shard_map/ppermute | solution.py:246
  22.8 4.5 %collective-permute-start.6 = (bf16[8,4224]{1,0:T(8,128)(2,1)}, bf16[8,4224]{1,0:T(8,128)(2,1)S(1)}, u32[]{:S(2)}, u32[]{:S(2)}) collective-permute-start(bf16[8,4224]{1,0:T(8,128)(2,1)} %get-tuple-element.13.refs_0_), channel_id=1, source_target_pairs={{0,16},{4,20},{8,24},{12,28},{16,0},{20,4},{24,8},{28,12},{1,17},{... | collective-permute-start | bytes 202760 | tf_op jit(solution)/shard_map/ppermute | solution.py:246
  24.3 5.4 %collective-permute-start.7 = (bf16[8,4224]{1,0:T(8,128)(2,1)}, bf16[8,4224]{1,0:T(8,128)(2,1)S(1)}, u32[]{:S(2)}, u32[]{:S(2)}) collective-permute-start(bf16[8,4224]{1,0:T(8,128)(2,1)} %get-tuple-element.13.refs_0_), channel_id=1, source_target_pairs={{0,24},{4,28},{8,16},{12,20},{16,8},{20,12},{24,0},{28,4},{1,25},{... | collective-permute-start | bytes 202760 | tf_op jit(solution)/shard_map/ppermute | solution.py:246
  25.8 3.9 %copy-start.1 = (bf16[8,4224]{1,0:T(8,128)(2,1)}, bf16[8,4224]{1,0:T(8,128)(2,1)S(1)}, u32[]{:S(2)}) copy-start(bf16[8,4224]{1,0:T(8,128)(2,1)S(1)} %collective-permute-done.5.refs_1_) | copy-start | bytes 202756
  27.3 2.4 %copy-start.2 = (bf16[8,4224]{1,0:T(8,128)(2,1)}, bf16[8,4224]{1,0:T(8,128)(2,1)S(1)}, u32[]{:S(2)}) copy-start(bf16[8,4224]{1,0:T(8,128)(2,1)S(1)} %collective-permute-done.6.refs_2_) | copy-start | bytes 202756
  29.7 0.6 %copy-start.3 = (bf16[8,4224]{1,0:T(8,128)(2,1)}, bf16[8,4224]{1,0:T(8,128)(2,1)S(1)}, u32[]{:S(2)}) copy-start(bf16[8,4224]{1,0:T(8,128)(2,1)S(1)} %collective-permute-done.7.refs_3_) | copy-start | bytes 202756
  33.0 5.6 %collective-permute-start.10 = (f32[8,128]{1,0:T(8,128)}, f32[8,128]{1,0:T(8,128)S(1)}, u32[]{:S(2)}, u32[]{:S(2)}) collective-permute-start(f32[8,128]{1,0:T(8,128)} %get-tuple-element.17.refs_0_), channel_id=1, source_target_pairs={{0,3},{1,2},{2,1},{3,0},{4,7},{5,6},{6,5},{7,4},{8,11},{9,10},{10,... | collective-permute-start | bytes 12296 | tf_op jit(solution)/shard_map/ppermute | solution.py:246
  33.2 5.4 %collective-permute-start.8 = (f32[8,128]{1,0:T(8,128)}, f32[8,128]{1,0:T(8,128)S(1)}, u32[]{:S(2)}, u32[]{:S(2)}) collective-permute-start(f32[8,128]{1,0:T(8,128)} %get-tuple-element.17.refs_0_), channel_id=1, source_target_pairs={{0,1},{1,0},{2,3},{3,2},{4,5},{5,4},{6,7},{7,6},{8,9},{9,8},{10,11... | collective-permute-start | bytes 12296 | tf_op jit(solution)/shard_map/ppermute | solution.py:246
  33.3 6.0 %collective-permute-start.9 = (f32[8,128]{1,0:T(8,128)}, f32[8,128]{1,0:T(8,128)S(1)}, u32[]{:S(2)}, u32[]{:S(2)}) collective-permute-start(f32[8,128]{1,0:T(8,128)} %get-tuple-element.17.refs_0_), channel_id=1, source_target_pairs={{0,2},{1,3},{2,0},{3,1},{4,6},{5,7},{6,4},{7,5},{8,10},{9,11},{10,... | collective-permute-start | bytes 12296 | tf_op jit(solution)/shard_map/ppermute | solution.py:246
  38.6 0.6 %copy-start.12 = (f32[8,128]{1,0:T(8,128)}, f32[8,128]{1,0:T(8,128)S(1)}, u32[]{:S(2)}) copy-start(f32[8,128]{1,0:T(8,128)S(1)} %collective-permute-done.10.refs_3_) | copy-start | bytes 12292
  38.6 0.6 %copy-start.13 = (f32[8,128]{1,0:T(8,128)}, f32[8,128]{1,0:T(8,128)S(1)}, u32[]{:S(2)}) copy-start(f32[8,128]{1,0:T(8,128)S(1)} %collective-permute-done.8.refs_1_) | copy-start | bytes 12292
  39.2 0.6 %copy-start.14 = (f32[8,128]{1,0:T(8,128)}, f32[8,128]{1,0:T(8,128)S(1)}, u32[]{:S(2)}) copy-start(f32[8,128]{1,0:T(8,128)S(1)} %collective-permute-done.9.refs_2_) | copy-start | bytes 12292
  41.8 4.5 %collective-permute-start.11 = (bf16[8,4224]{1,0:T(8,128)(2,1)}, bf16[8,4224]{1,0:T(8,128)(2,1)S(1)}, u32[]{:S(2)}, u32[]{:S(2)}) collective-permute-start(bf16[8,4224]{1,0:T(8,128)(2,1)} %get-tuple-element.18.refs_0_), channel_id=1, source_target_pairs={{0,8},{4,12},{8,0},{12,4},{16,24},{20,28},{24,16},{28,20},{1,9},{5... | collective-permute-start | bytes 202760 | tf_op jit(solution)/shard_map/ppermute | solution.py:246
  42.4 4.5 %collective-permute-start.12 = (bf16[8,4224]{1,0:T(8,128)(2,1)}, bf16[8,4224]{1,0:T(8,128)(2,1)S(1)}, u32[]{:S(2)}, u32[]{:S(2)}) collective-permute-start(bf16[8,4224]{1,0:T(8,128)(2,1)} %get-tuple-element.18.refs_0_), channel_id=1, source_target_pairs={{0,16},{4,20},{8,24},{12,28},{16,0},{20,4},{24,8},{28,12},{1,17},{... | collective-permute-start | bytes 202760 | tf_op jit(solution)/shard_map/ppermute | solution.py:246
  42.9 5.4 %collective-permute-start.13 = (bf16[8,4224]{1,0:T(8,128)(2,1)}, bf16[8,4224]{1,0:T(8,128)(2,1)S(1)}, u32[]{:S(2)}, u32[]{:S(2)}) collective-permute-start(bf16[8,4224]{1,0:T(8,128)(2,1)} %get-tuple-element.18.refs_0_), channel_id=1, source_target_pairs={{0,24},{4,28},{8,16},{12,20},{16,8},{20,12},{24,0},{28,4},{1,25},{... | collective-permute-start | bytes 202760 | tf_op jit(solution)/shard_map/ppermute | solution.py:246
  46.3 2.0 %copy-start.4 = (bf16[8,4224]{1,0:T(8,128)(2,1)}, bf16[8,4224]{1,0:T(8,128)(2,1)S(1)}, u32[]{:S(2)}) copy-start(bf16[8,4224]{1,0:T(8,128)(2,1)S(1)} %collective-permute-done.11.refs_1_) | copy-start | bytes 202756
  46.9 1.5 %copy-start.5 = (bf16[8,4224]{1,0:T(8,128)(2,1)}, bf16[8,4224]{1,0:T(8,128)(2,1)S(1)}, u32[]{:S(2)}) copy-start(bf16[8,4224]{1,0:T(8,128)(2,1)S(1)} %collective-permute-done.12.refs_2_) | copy-start | bytes 202756
  48.3 0.6 %copy-start.6 = (bf16[8,4224]{1,0:T(8,128)(2,1)}, bf16[8,4224]{1,0:T(8,128)(2,1)S(1)}, u32[]{:S(2)}) copy-start(bf16[8,4224]{1,0:T(8,128)(2,1)S(1)} %collective-permute-done.13.refs_3_) | copy-start | bytes 202756

commit v2 on v1

v2 whole, which is shorter than its diff:
```python
import functools

import jax
import jax.numpy as jnp
from jax import lax
from jax.experimental import pallas as pl
from jax.experimental.pallas import tpu as pltpu
from jax.sharding import PartitionSpec as P

step_size = 0.5
LANES = 128
F32 = jnp.float32
BF16 = jnp.bfloat16

E_LAST, E_FIRST, E_SECOND, O_LAST, O_FIRST = range(5)
KINDS = 5


def lanes_of(shape):
    return lax.broadcasted_iota(jnp.int32, shape, len(shape) - 1)


def turned(x, by):
    return pltpu.roll(x, by % LANES, x.ndim - 1)


def shifted_in(x, by, edge):
    free = 0 if by == 1 else LANES - 1
    return jnp.where(lanes_of(x.shape) == free, edge, turned(x, by))


def column(x, lane):
    return jnp.broadcast_to(x[:, lane : lane + 1], x.shape)


def edge_tile(pair_of, layers, base):
    tile = None
    for layer in range(layers):
        even, odd = pair_of(layer)
        start = base + KINDS * layer
        lane = lanes_of(even.shape)
        if tile is None:
            tile = jnp.zeros_like(even)
        tile = jnp.where((lane >= start) & (lane < start + 3), turned(even, start + 1), tile)
        tile = jnp.where((lane >= start + 3) & (lane < start + 5), turned(odd, start + 4), tile)
    return tile


def kind_lane(lane, base, kind):
    return lax.rem(lane - base + KINDS * LANES, KINDS) == kind


def shrink(values, cutoff):
    return values - jnp.clip(values, -cutoff, cutoff)


def layer_tiles(ref, layer):
    start = layer * 2 * LANES
    return ref[:, start : start + LANES], ref[:, start + LANES : start + 2 * LANES]


def stacked(ref, layers):
    tiles = [layer_tiles(ref, layer) for layer in range(layers)]
    return tuple(jnp.concatenate([t[p] for t in tiles], axis=0).astype(F32) for p in range(2))


def stacked_lane(tile, lanes):
    return jnp.concatenate([tile[:, lane : lane + 1] for lane in lanes], axis=0)


def unstacked(even, odd, models):
    rows = [slice(start, start + models) for start in range(0, even.shape[0], models)]
    return jnp.concatenate([t[r] for r in rows for t in (even, odd)], axis=1)


def nt_dot(a, b):
    return lax.dot_general(a, b, (((1,), (1,)), ((), ())), preferred_element_type=F32)


def inverse_wave(smooth, detail, before, next_even_of):
    even = smooth - 0.25 * (shifted_in(detail, 1, before) + detail)
    odd = detail + 0.5 * (even + shifted_in(even, -1, next_even_of(detail)))
    return even, odd


def first_kernel(layers, wave_ref, k_ref, packet_ref, tile):
    rows = k_ref.shape[0]
    models = wave_ref.shape[0]
    even, odd = inverse_wave(*stacked(wave_ref, layers), 0.0, lambda detail: 0.0)
    tile[...] = edge_tile(lambda l: layer_tiles(wave_ref, l), layers, rows)
    edges = edge_tile(lambda l: tuple(t.astype(F32) for t in layer_tiles(k_ref, l)), layers, rows)
    packet_ref[:rows, :] = edges.astype(BF16)
    tile[:, :rows] = nt_dot(unstacked(even, odd, models).astype(BF16), k_ref[...])
    whole = tile[...]
    high = whole.astype(BF16).astype(F32)
    packet_ref[rows:, :] = jnp.concatenate([high, whole - high], axis=0).astype(BF16)


def second_kernel(layers, n_vox, *refs):
    (observed_ref, *packets, out_ref, halo_ref, held) = refs
    models, rows = observed_ref.shape
    me = lax.axis_index("vox")
    for distance, packet in enumerate(packets):
        held[me ^ distance] = packet[...]
    lane = lanes_of((models, LANES))

    def edge_values(which):
        both = held[which, rows:, :].astype(F32)
        return both[:models] + both[models:]

    def mixed(from_left, from_right):
        at = lanes_of(from_left.shape)
        left = kind_lane(at, rows, E_LAST) | kind_lane(at, rows, O_LAST)
        return jnp.where(left, from_left, from_right)

    edge = [edge_values(z) for z in range(n_vox)]
    terms, columns = [], []
    for z in range(n_vox):
        before, after = edge[z - 1], edge[(z + 1) % n_vox]
        last = turned(before, E_FIRST - O_LAST)
        last_odd = turned(before, O_FIRST - O_LAST)
        next_smooth = turned(after, O_LAST - E_FIRST)
        next_detail = turned(after, O_LAST - O_FIRST)
        next_even = next_smooth - 0.25 * (edge[z] + next_detail)
        term = jnp.where(
            kind_lane(lane, rows, E_FIRST),
            -0.25 * last,
            jnp.where(
                kind_lane(lane, rows, O_FIRST),
                -0.125 * last_odd,
                jnp.where(kind_lane(lane, rows, O_LAST), 0.5 * next_even, 0.0),
            ),
        )
        inside = (lane >= rows) & (lane < rows + KINDS * layers)
        terms.append(jnp.where(inside, term, 0.0).astype(BF16))
        columns.append(held[z, :rows, :])
    predicted = nt_dot(jnp.concatenate(terms, axis=1), jnp.concatenate(columns, axis=1))
    shares = edge[0]
    for z in range(1, n_vox):
        shares = shares + edge[z]
    predicted = predicted + shares[:, :rows]
    left, right = lax.rem(me + n_vox - 1, n_vox), lax.rem(me + 1, n_vox)
    out_ref[:rows, :] = mixed(held[left, :rows, :].astype(F32), held[right, :rows, :].astype(F32))
    out_ref[rows:, :] = jnp.zeros((2 * models, LANES), F32)
    out_ref[rows : rows + models, :rows] = observed_ref[...] - predicted
    out_ref[rows + models :, :rows] = observed_ref[...]
    halo_ref[...] = mixed(edge_values(left), edge_values(right))


def in_core_order(mine, other, work):
    core = lax.rem(lax.axis_index("dp"), 2)

    @pl.when(core == 0)
    def _():
        work(mine, other)

    @pl.when(core == 1)
    def _():
        work(other, mine)


def back_projected(mine, other, g_ref):
    width = mine[1].shape[1]

    def work(*cores):
        sent = [residual.astype(BF16) for residual, _, _ in cores]
        g_ref[:, :width] = sum(
            jnp.dot(r, k[...], preferred_element_type=F32) for r, (_, k, _) in zip(sent, cores)
        ).astype(BF16)
        g_ref[:, width:] = sum(
            jnp.dot(r, h[...].astype(BF16), preferred_element_type=F32) for r, (_, _, h) in zip(sent, cores)
        ).astype(BF16)

    in_core_order(mine, other, work)


def third_kernel(mine_ref, other_ref, k_ref, k_other_ref, g_ref):
    rows = k_ref.shape[0]
    models = g_ref.shape[0]

    def core(ref, k):
        return ref[rows : rows + models, :rows], k, ref.at[:rows]

    back_projected(core(mine_ref, k_ref), core(other_ref, k_other_ref), g_ref)


def tree_sum(values):
    while len(values) > 1:
        values = [a + b for a, b in zip(values[::2], values[1::2])]
    return values[0]


def stepped(layers, base, wave_ref, cut_ref, g_refs, halo_ref=None):
    models, width = wave_ref.shape
    gradients = [stacked(g, layers) for g in g_refs]
    even, odd = (tree_sum([g[p] for g in gradients]) for p in range(2))
    edge = tree_sum([g[:, width:].astype(F32) for g in g_refs])
    cut_s, cut_d = (stacked_lane(cut_ref[:, p, :], range(layers)) for p in range(2))

    def at(tile, kind):
        return stacked_lane(tile, [base + KINDS * layer + kind for layer in range(layers)])

    even_next = at(edge, E_FIRST)
    detail_g = odd - 0.5 * (even + shifted_in(even, -1, even_next))
    before_g = at(edge, O_LAST) - 0.5 * (at(edge, E_LAST) + even[:, :1])
    smooth_g = even + 0.25 * (shifted_in(detail_g, 1, before_g) + detail_g)
    smooth, detail = stacked(wave_ref, layers)
    smooth = shrink(smooth + step_size * smooth_g, cut_s)
    detail = shrink(detail + step_size * detail_g, cut_d)
    if halo_ref is None:
        return smooth, detail
    halo = halo_ref[...]
    after_g = at(edge, O_FIRST) - 0.5 * (even_next + at(edge, E_SECOND))
    next_g = even_next + 0.25 * (detail_g[:, LANES - 1 :] + after_g)
    before = shrink(at(halo, O_LAST) + step_size * before_g, cut_d)
    next_smooth = shrink(at(halo, E_FIRST) + step_size * next_g, cut_s)
    after = shrink(at(halo, O_FIRST) + step_size * after_g, cut_d)
    return smooth, detail, before, next_smooth, after


def fourth_kernel(layers, base, wave_ref, cut_ref, halo_ref, k_ref, k_other_ref, *refs):
    *g_refs, new_ref, pred_ref = refs
    models = wave_ref.shape[0]
    rows = k_ref.shape[0]
    smooth, detail, before, next_smooth, after = stepped(layers, base, wave_ref, cut_ref, g_refs, halo_ref)
    new_ref[...] = unstacked(smooth, detail, models)

    def next_even_of(detail):
        return next_smooth - 0.25 * (detail[:, LANES - 1 :] + after)

    model = unstacked(*inverse_wave(smooth, detail, before, next_even_of), models).astype(BF16)
    pred_ref[...] = jnp.zeros_like(pred_ref)
    pred_ref[:, :rows] = nt_dot(model, k_ref[...])
    pred_ref[:, rows : 2 * rows] = nt_dot(model, k_other_ref[...])


def fifth_kernel(mine_ref, other_ref, k_ref, k_other_ref, *refs):
    *shares, g_ref, residual_ref = refs
    models, rows = residual_ref.shape
    predicted = tree_sum([s[...] for s in shares])

    def core(ref, k, start):
        residual = ref[rows + models :, :rows] - predicted[:, start : start + rows]
        return residual, k, ref.at[:rows]

    mine = core(mine_ref, k_ref, 0)
    residual_ref[...] = mine[0]
    back_projected(mine, core(other_ref, k_other_ref, rows), g_ref)


def sixth_kernel(layers, base, wave_ref, cut_ref, *refs):
    *g_refs, new_ref = refs
    new_ref[...] = unstacked(*stepped(layers, base, wave_ref, cut_ref, g_refs), wave_ref.shape[0])


def from_partner(x, axis, distance):
    return lax.ppermute(x, axis, [(i, i ^ distance) for i in range(lax.axis_size(axis))])


def shares_of(x, axis, lowest):
    size = lax.axis_size(axis) // lowest
    while size > 4:
        parts = [x] + [from_partner(x, axis, lowest * d) for d in range(1, 4)]
        x = tree_sum([p.astype(F32) for p in parts]).astype(x.dtype)
        lowest, size = lowest * 4, size // 4
    return [x] + [from_partner(x, axis, lowest * d) for d in range(1, size)]


def call(kernel, out_shape, *args, scratch=()):
    return pl.pallas_call(
        kernel,
        out_shape=out_shape,
        in_specs=[pl.BlockSpec(memory_space=pltpu.VMEM)] * len(args),
        out_specs=jax.tree.map(lambda _: pl.BlockSpec(memory_space=pltpu.VMEM), out_shape),
        scratch_shapes=list(scratch),
    )(*[pltpu.with_memory_space_constraint(arg, pltpu.VMEM) for arg in args])


def body(kernels, observed, initial, threshold):
    models, width = initial.shape
    rows = kernels.shape[0]
    layers = threshold.shape[1]
    n_vox = lax.axis_size("vox")
    assert width == 2 * layers * LANES and rows + KINDS * layers <= LANES and 2 * rows <= LANES
    cut = jnp.swapaxes(threshold, 1, 2)
    packet_rows = rows + 2 * models

    packet = call(
        functools.partial(first_kernel, layers),
        pltpu.VMEM((packet_rows, LANES), BF16),
        initial,
        kernels,
        scratch=[pltpu.VMEM((models, LANES), F32)],
    )
    packets = [packet] + [from_partner(packet, "vox", d) for d in range(1, n_vox)]
    k_other = from_partner(kernels, "dp", 1)
    mine, halo = call(
        functools.partial(second_kernel, layers, n_vox),
        (pltpu.VMEM((packet_rows, LANES), F32), pltpu.VMEM((models, LANES), F32)),
        observed,
        *packets,
        scratch=[pltpu.VMEM((n_vox, packet_rows, LANES), BF16)],
    )
    other = from_partner(mine, "dp", 1)
    g = call(third_kernel, pltpu.VMEM((models, width + LANES), BF16), mine, other, kernels, k_other)
    wavelets, predicted = call(
        functools.partial(fourth_kernel, layers, rows),
        (pltpu.VMEM((models, width), F32), pltpu.VMEM((models, LANES), F32)),
        initial,
        cut,
        halo,
        kernels,
        k_other,
        *shares_of(g, "dp", 2),
    )
    g, residual = call(
        fifth_kernel,
        (pltpu.VMEM((models, width + LANES), BF16), jax.ShapeDtypeStruct((models, rows), F32)),
        mine,
        other,
        kernels,
        k_other,
        *shares_of(predicted, "vox", 1),
    )
    coefficients = call(
        functools.partial(sixth_kernel, layers, rows),
        jax.ShapeDtypeStruct((models, width), F32),
        wavelets,
        cut,
        *shares_of(g, "dp", 2),
    )
    return coefficients, residual


def solution(mesh):
    return jax.shard_map(
        body,
        mesh=mesh,
        in_specs=(P("dp", "vox"), P(None, "dp"), P(None, "vox"), P()),
        out_specs=(P(None, "vox"), P(None, "dp")),
        check_vma=False,
    )
```

time: 51.5 us -> 37.8 us (0.73)
  Pallas kernels: 13.5 us -> 4.08 us
  local copies, waits for them, and re-layouts: 3.79 us -> 1.91 us
  waiting for transfers between devices: 15 us -> 13.7 us
  other arithmetic: 1.06 us -> 0 us
    pallas_call x6, Pallas kernels: 13.5 us -> 4.08 us  [call(): pl.pallas_call(kernel, out_shape=out_shape, in_specs=[pl.BlockSpec(memory...]
    ppermute x14, waiting for transfers between devices: 15 us -> 13.7 us  [from_partner(): lax.ppermute(x, axis, [(i, i ^ distance) for i in range(lax.axis_size(axi...]
    unnamed x31 -> x12, local copies, waits for them, and re-layouts: 3.13 us -> 1.91 us
    select_n x1 -> x0, other arithmetic: 1.06 us -> none  [body(): jnp.where(first_core, jnp.concatenate([kernels, other]), jnp.concatenate(...]
    pad x1 -> x0, local copies, waits for them, and re-layouts: 0.6 us -> none  [body(): cut = jnp.pad(cut, ((0, 0), (0, LANES - 2 * layers)))]
  transfers between devices with their start and end apart: 14 -> 14, of which waited for: 11 -> 11; matrix products, arithmetic and copies ran while one was open for 4% -> 0% of each run, Pallas kernels for 9% -> 2%
where the time goes in v2:
time: 37.8 us; the launch traced here: 37.6 us
  starting transfers between devices  17.2 us (46%)
  waiting for transfers between devices  13.7 us (36%)
  Pallas kernels  4.08 us (11%)
  local copies, waits for them, and re-layouts  1.91 us (5%)
  between operations  0.67 us (2%)
    ppermute x14, starting transfers between devices, from_partner(): lax.ppermute(x, axis, [(i, i ^ distance) for i in range(lax.axis_size(axi...  17.2 us
    ppermute x14, waiting for transfers between devices, from_partner(): lax.ppermute(x, axis, [(i, i ^ distance) for i in range(lax.axis_size(axi...  13.7 us
    pallas_call x6, Pallas kernels, call(): pl.pallas_call(kernel, out_shape=out_shape, in_specs=[pl.BlockSpec(memory...  4.08 us
    unnamed x12, local copies, waits for them, and re-layouts  1.91 us
  transfers between devices with their start and end apart: 14, of which 11 were waited for; matrix products, arithmetic and copies ran while one was open for 0% of the time, Pallas kernels for 2%

profile of v2, /device:TPU:0, one launch (start us, length us, event | category | flops | bytes accessed | tf_op | source)
XLA Modules:
  0.0 37.6 jit_solution(848141530779553767)
XLA Ops:
  0.6 0.5 %collective-permute-start.3 = (bf16[48,4096]{1,0:T(8,128)(2,1)}, bf16[48,4096]{1,0:T(8,128)(2,1)S(1)}, u32[]{:S(2)}, u32[]{:S(2)}) collective-permute-start(bf16[48,4096]{1,0:T(8,128)(2,1)} %k_ref.7), channel_id=1, source_target_pairs={{0,4},{4,0},{8,12},{12,8},{16,20},{20,16},{24,28},{28,24},{1,5},{5... | collective-permute-start | bytes 1179656 | tf_op jit(solution)/shard_map/ppermute | solution.py:257
  1.1 0.0 copy-start
  1.1 1.0 %copy-done = bf16[48,4096]{1,0:T(8,128)(2,1)S(1)} copy-done((bf16[48,4096]{1,0:T(8,128)(2,1)S(1)}, bf16[48,4096]{1,0:T(8,128)(2,1)}, u32[]{:S(2)}) %copy-start) | copy-done | bytes 393240
  2.1 0.0 copy-start.2
  2.1 0.9 %copy-done.2 = f32[8,4096]{1,0:T(8,128)S(1)} copy-done((f32[8,4096]{1,0:T(8,128)S(1)}, f32[8,4096]{1,0:T(8,128)}, u32[]{:S(2)}) %copy-start.2) | copy-done | bytes 131096
  3.0 0.0 copy-start.5
  3.1 0.0 copy-start.1
  3.1 0.4 shard_map.59.refs_1_
  3.4 4.6 %collective-permute-start.2 = (bf16[64,128]{1,0:T(8,128)(2,1)S(1)}, bf16[64,128]{1,0:T(8,128)(2,1)S(1)}, u32[]{:S(2)}, u32[]{:S(2)}) collective-permute-start(bf16[64,128]{1,0:T(8,128)(2,1)S(1)} %shard_map.59.refs_1_), channel_id=1, source_target_pairs={{0,3},{1,2},{2,1},{3,0},{4,7},{5,6},{6,5},{7,4},{8,11},{9,10},{10,... | collective-permute-start | bytes 49160 | tf_op jit(solution)/shard_map/ppermute | solution.py:257
  8.0 0.0 collective-permute-start.1
  8.0 0.6 %collective-permute-start = (bf16[64,128]{1,0:T(8,128)(2,1)S(1)}, bf16[64,128]{1,0:T(8,128)(2,1)S(1)}, u32[]{:S(2)}, u32[]{:S(2)}) collective-permute-start(bf16[64,128]{1,0:T(8,128)(2,1)S(1)} %shard_map.59.refs_1_), channel_id=1, source_target_pairs={{0,1},{1,0},{2,3},{3,2},{4,5},{5,4},{6,7},{7,6},{8,9},{9,8},{10,11... | collective-permute-start | bytes 49160 | tf_op jit(solution)/shard_map/ppermute | solution.py:257
  8.7 1.1 %collective-permute-done.2.refs_4_ = bf16[64,128]{1,0:T(8,128)(2,1)S(1)} collective-permute-done((bf16[64,128]{1,0:T(8,128)(2,1)S(1)}, bf16[64,128]{1,0:T(8,128)(2,1)S(1)}, u32[]{:S(2)}, u32[]{:S(2)}) %collective-permute-start.2) | collective-permute-done | bytes 16416 | tf_op jit(solution)/shard_map/ppermute | solution.py:257
  9.8 2.9 %collective-permute-done.1.refs_3_ = bf16[64,128]{1,0:T(8,128)(2,1)S(1)} collective-permute-done((bf16[64,128]{1,0:T(8,128)(2,1)S(1)}, bf16[64,128]{1,0:T(8,128)(2,1)S(1)}, u32[]{:S(2)}, u32[]{:S(2)}) %collective-permute-start.1) | collective-permute-done | bytes 16416 | tf_op jit(solution)/shard_map/ppermute | solution.py:257
  12.7 0.0 collective-permute-done.refs_2_
  12.7 0.0 copy-done.5
  12.7 0.2 shard_map.60
  12.9 0.0 copy-start.3
  12.9 0.0 collective-permute-start.4
  12.9 1.2 %collective-permute-done.4.other_ref = f32[64,128]{1,0:T(8,128)S(1)} collective-permute-done((f32[64,128]{1,0:T(8,128)S(1)}, f32[64,128]{1,0:T(8,128)S(1)}, u32[]{:S(2)}, u32[]{:S(2)}) %collective-permute-start.4) | collective-permute-done | bytes 32800 | tf_op jit(solution)/shard_map/ppermute | solution.py:257
  14.1 0.0 collective-permute-done.3.k_other_ref
  14.1 0.0 copy-done.1
  14.1 0.0 copy-start.4
  14.1 0.3 shard_map.61.refs_0_
  14.4 2.5 %collective-permute-start.7 = (bf16[8,4224]{1,0:T(8,128)(2,1)S(1)}, bf16[8,4224]{1,0:T(8,128)(2,1)S(1)}, u32[]{:S(2)}, u32[]{:S(2)}) collective-permute-start(bf16[8,4224]{1,0:T(8,128)(2,1)S(1)} %shard_map.61.refs_0_), channel_id=1, source_target_pairs={{0,24},{4,28},{8,16},{12,20},{16,8},{20,12},{24,0},{28,4},{1,25},{... | collective-permute-start | bytes 202760 | tf_op jit(solution)/shard_map/ppermute | solution.py:257
  16.9 0.5 %collective-permute-start.6 = (bf16[8,4224]{1,0:T(8,128)(2,1)S(1)}, bf16[8,4224]{1,0:T(8,128)(2,1)S(1)}, u32[]{:S(2)}, u32[]{:S(2)}) collective-permute-start(bf16[8,4224]{1,0:T(8,128)(2,1)S(1)} %shard_map.61.refs_0_), channel_id=1, source_target_pairs={{0,16},{4,20},{8,24},{12,28},{16,0},{20,4},{24,8},{28,12},{1,17},{... | collective-permute-start | bytes 202760 | tf_op jit(solution)/shard_map/ppermute | solution.py:257
  17.4 0.5 %collective-permute-start.5 = (bf16[8,4224]{1,0:T(8,128)(2,1)S(1)}, bf16[8,4224]{1,0:T(8,128)(2,1)S(1)}, u32[]{:S(2)}, u32[]{:S(2)}) collective-permute-start(bf16[8,4224]{1,0:T(8,128)(2,1)S(1)} %shard_map.61.refs_0_), channel_id=1, source_target_pairs={{0,8},{4,12},{8,0},{12,4},{16,24},{20,28},{24,16},{28,20},{1,9},{5... | collective-permute-start | bytes 202760 | tf_op jit(solution)/shard_map/ppermute | solution.py:257
  17.9 1.7 %collective-permute-done.7.refs_3_ = bf16[8,4224]{1,0:T(8,128)(2,1)S(1)} collective-permute-done((bf16[8,4224]{1,0:T(8,128)(2,1)S(1)}, bf16[8,4224]{1,0:T(8,128)(2,1)S(1)}, u32[]{:S(2)}, u32[]{:S(2)}) %collective-permute-start.7) | collective-permute-done | bytes 67616 | tf_op jit(solution)/shard_map/ppermute | solution.py:257
  19.7 1.5 %collective-permute-done.6.refs_2_ = bf16[8,4224]{1,0:T(8,128)(2,1)S(1)} collective-permute-done((bf16[8,4224]{1,0:T(8,128)(2,1)S(1)}, bf16[8,4224]{1,0:T(8,128)(2,1)S(1)}, u32[]{:S(2)}, u32[]{:S(2)}) %collective-permute-start.6) | collective-permute-done | bytes 67616 | tf_op jit(solution)/shard_map/ppermute | solution.py:257
  21.2 0.5 %collective-permute-done.5.refs_1_ = bf16[8,4224]{1,0:T(8,128)(2,1)S(1)} collective-permute-done((bf16[8,4224]{1,0:T(8,128)(2,1)S(1)}, bf16[8,4224]{1,0:T(8,128)(2,1)S(1)}, u32[]{:S(2)}, u32[]{:S(2)}) %collective-permute-start.5) | collective-permute-done | bytes 67616 | tf_op jit(solution)/shard_map/ppermute | solution.py:257
  21.7 0.0 copy-done.3
  21.7 0.0 copy-done.4
  21.7 1.3 %shard_map.62 = (f32[8,4096]{1,0:T(8,128)S(1)}, f32[8,128]{1,0:T(8,128)S(1)}) custom-call(f32[8,4096]{1,0:T(8,128)S(1)} %copy-done.3, f32[8,2,16]{2,1,0:T(2,128)S(1)} %bitcast.1, f32[8,128]{1,0:T(8,128)S(1)} %get-tuple-element.8.halo_ref, bf16[48,4096]{1,0:T(8,128)(2,1)S(1)} %copy-done.1, bf16[48,4096]{1,0:T(8,128)(2,1)S(1)} %collective-permute-done.3.k_other_ref, ...), custom_call_target="tpu_custom_call" | custom-call | tf_op jit(solution)/shard_map/pallas_call | solution.py:270
  23.0 1.5 %collective-permute-start.10 = (f32[8,128]{1,0:T(8,128)S(1)}, f32[8,128]{1,0:T(8,128)S(1)}, u32[]{:S(2)}, u32[]{:S(2)}) collective-permute-start(f32[8,128]{1,0:T(8,128)S(1)} %get-tuple-element.11.refs_0_), channel_id=1, source_target_pairs={{0,3},{1,2},{2,1},{3,0},{4,7},{5,6},{6,5},{7,4},{8,11},{9,10},{10,... | collective-permute-start | bytes 12296 | tf_op jit(solution)/shard_map/ppermute | solution.py:257
  24.4 0.6 %collective-permute-start.9 = (f32[8,128]{1,0:T(8,128)S(1)}, f32[8,128]{1,0:T(8,128)S(1)}, u32[]{:S(2)}, u32[]{:S(2)}) collective-permute-start(f32[8,128]{1,0:T(8,128)S(1)} %get-tuple-element.11.refs_0_), channel_id=1, source_target_pairs={{0,2},{1,3},{2,0},{3,1},{4,6},{5,7},{6,4},{7,5},{8,10},{9,11},{10,... | collective-permute-start | bytes 12296 | tf_op jit(solution)/shard_map/ppermute | solution.py:257
  25.0 2.4 %collective-permute-start.8 = (f32[8,128]{1,0:T(8,128)S(1)}, f32[8,128]{1,0:T(8,128)S(1)}, u32[]{:S(2)}, u32[]{:S(2)}) collective-permute-start(f32[8,128]{1,0:T(8,128)S(1)} %get-tuple-element.11.refs_0_), channel_id=1, source_target_pairs={{0,1},{1,0},{2,3},{3,2},{4,5},{5,4},{6,7},{7,6},{8,9},{9,8},{10,11... | collective-permute-start | bytes 12296 | tf_op jit(solution)/shard_map/ppermute | solution.py:257
  27.4 1.0 %collective-permute-done.10.refs_3_ = f32[8,128]{1,0:T(8,128)S(1)} collective-permute-done((f32[8,128]{1,0:T(8,128)S(1)}, f32[8,128]{1,0:T(8,128)S(1)}, u32[]{:S(2)}, u32[]{:S(2)}) %collective-permute-start.10) | collective-permute-done | bytes 4128 | tf_op jit(solution)/shard_map/ppermute | solution.py:257
  28.4 0.6 %collective-permute-done.9.refs_2_ = f32[8,128]{1,0:T(8,128)S(1)} collective-permute-done((f32[8,128]{1,0:T(8,128)S(1)}, f32[8,128]{1,0:T(8,128)S(1)}, u32[]{:S(2)}, u32[]{:S(2)}) %collective-permute-start.9) | collective-permute-done | bytes 4128 | tf_op jit(solution)/shard_map/ppermute | solution.py:257
  29.0 0.0 collective-permute-done.8.refs_1_
  29.0 0.9 %shard_map.63 = (bf16[8,4224]{1,0:T(8,128)(2,1)S(1)}, f32[8,48]{1,0:T(8,128)}) custom-call(f32[64,128]{1,0:T(8,128)S(1)} %get-tuple-element.9.mine_ref, f32[64,128]{1,0:T(8,128)S(1)} %collective-permute-done.4.other_ref, bf16[48,4096]{1,0:T(8,128)(2,1)S(1)} %copy-done.1, bf16[48,4096]{1,0:T(8,128)(2,1)S(1)} %collective-permute-done.3.k_other_ref, ...), custom_call_target="tpu_custom_call" | custom-call | tf_op jit(solution)/shard_map/pallas_call | solution.py:270
  29.9 1.5 %collective-permute-start.13 = (bf16[8,4224]{1,0:T(8,128)(2,1)S(1)}, bf16[8,4224]{1,0:T(8,128)(2,1)S(1)}, u32[]{:S(2)}, u32[]{:S(2)}) collective-permute-start(bf16[8,4224]{1,0:T(8,128)(2,1)S(1)} %get-tuple-element.12.refs_0_), channel_id=1, source_target_pairs={{0,24},{4,28},{8,16},{12,20},{16,8},{20,12},{24,0},{28,4},{1,25},{... | collective-permute-start | bytes 202760 | tf_op jit(solution)/shard_map/ppermute | solution.py:257
  31.4 0.8 %collective-permute-start.12 = (bf16[8,4224]{1,0:T(8,128)(2,1)S(1)}, bf16[8,4224]{1,0:T(8,128)(2,1)S(1)}, u32[]{:S(2)}, u32[]{:S(2)}) collective-permute-start(bf16[8,4224]{1,0:T(8,128)(2,1)S(1)} %get-tuple-element.12.refs_0_), channel_id=1, source_target_pairs={{0,16},{4,20},{8,24},{12,28},{16,0},{20,4},{24,8},{28,12},{1,17},{... | collective-permute-start | bytes 202760 | tf_op jit(solution)/shard_map/ppermute | solution.py:257
  32.2 1.2 %collective-permute-start.11 = (bf16[8,4224]{1,0:T(8,128)(2,1)S(1)}, bf16[8,4224]{1,0:T(8,128)(2,1)S(1)}, u32[]{:S(2)}, u32[]{:S(2)}) collective-permute-start(bf16[8,4224]{1,0:T(8,128)(2,1)S(1)} %get-tuple-element.12.refs_0_), channel_id=1, source_target_pairs={{0,8},{4,12},{8,0},{12,4},{16,24},{20,28},{24,16},{28,20},{1,9},{5... | collective-permute-start | bytes 202760 | tf_op jit(solution)/shard_map/ppermute | solution.py:257
  33.4 1.7 %collective-permute-done.13.refs_3_ = bf16[8,4224]{1,0:T(8,128)(2,1)S(1)} collective-permute-done((bf16[8,4224]{1,0:T(8,128)(2,1)S(1)}, bf16[8,4224]{1,0:T(8,128)(2,1)S(1)}, u32[]{:S(2)}, u32[]{:S(2)}) %collective-permute-start.13) | collective-permute-done | bytes 67616 | tf_op jit(solution)/shard_map/ppermute | solution.py:257
  35.1 0.7 %collective-permute-done.12.refs_2_ = bf16[8,4224]{1,0:T(8,128)(2,1)S(1)} collective-permute-done((bf16[8,4224]{1,0:T(8,128)(2,1)S(1)}, bf16[8,4224]{1,0:T(8,128)(2,1)S(1)}, u32[]{:S(2)}, u32[]{:S(2)}) %collective-permute-start.12) | collective-permute-done | bytes 67616 | tf_op jit(solution)/shard_map/ppermute | solution.py:257
  35.8 0.7 %collective-permute-done.11.refs_1_ = bf16[8,4224]{1,0:T(8,128)(2,1)S(1)} collective-permute-done((bf16[8,4224]{1,0:T(8,128)(2,1)S(1)}, bf16[8,4224]{1,0:T(8,128)(2,1)S(1)}, u32[]{:S(2)}, u32[]{:S(2)}) %collective-permute-start.11) | collective-permute-done | bytes 67616 | tf_op jit(solution)/shard_map/ppermute | solution.py:257
  36.5 1.1 %shard_map.64 = f32[8,4096]{1,0:T(8,128)} custom-call(f32[8,4096]{1,0:T(8,128)S(1)} %get-tuple-element.10.wave_ref, f32[8,2,16]{2,1,0:T(2,128)S(1)} %bitcast.2, bf16[8,4224]{1,0:T(8,128)(2,1)S(1)} %get-tuple-element.12.refs_0_, bf16[8,4224]{1,0:T(8,128)(2,1)S(1)} %collective-permute-done.11.refs_1_, bf16[8,4224]{1,0:T(8,128)(2,1)S(1)} %collective-permute-done.12.refs_2_, ...), custom_call_target="tpu_custom_call" | custom-call | tf_op jit(solution)/shard_map/pallas_call | solution.py:270
Async XLA Ops:
  0.6 13.5 %collective-permute-start.3 = (bf16[48,4096]{1,0:T(8,128)(2,1)}, bf16[48,4096]{1,0:T(8,128)(2,1)S(1)}, u32[]{:S(2)}, u32[]{:S(2)}) collective-permute-start(bf16[48,4096]{1,0:T(8,128)(2,1)} %k_ref.7), channel_id=1, source_target_pairs={{0,4},{4,0},{8,12},{12,8},{16,20},{20,16},{24,28},{28,24},{1,5},{5... | collective-permute-start | bytes 1179656 | tf_op jit(solution)/shard_map/ppermute | solution.py:257
  1.1 1.0 %copy-start = (bf16[48,4096]{1,0:T(8,128)(2,1)S(1)}, bf16[48,4096]{1,0:T(8,128)(2,1)}, u32[]{:S(2)}) copy-start(bf16[48,4096]{1,0:T(8,128)(2,1)} %k_ref.7) | copy-start | bytes 1179652
  2.1 0.9 %copy-start.2 = (f32[8,4096]{1,0:T(8,128)S(1)}, f32[8,4096]{1,0:T(8,128)}, u32[]{:S(2)}) copy-start(f32[8,4096]{1,0:T(8,128)} %wave_ref.3) | copy-start | bytes 393220
  3.0 9.6 %copy-start.5 = (f32[8,48]{1,0:T(8,128)S(1)}, f32[8,48]{1,0:T(8,128)}, u32[]{:S(2)}) copy-start(f32[8,48]{1,0:T(8,128)} %refs_0_.1) | copy-start | bytes 4612
  3.1 11.1 %copy-start.1 = (bf16[48,4096]{1,0:T(8,128)(2,1)S(1)}, bf16[48,4096]{1,0:T(8,128)(2,1)}, u32[]{:S(2)}) copy-start(bf16[48,4096]{1,0:T(8,128)(2,1)} %k_ref.7) | copy-start | bytes 1179652
  3.4 6.3 %collective-permute-start.2 = (bf16[64,128]{1,0:T(8,128)(2,1)S(1)}, bf16[64,128]{1,0:T(8,128)(2,1)S(1)}, u32[]{:S(2)}, u32[]{:S(2)}) collective-permute-start(bf16[64,128]{1,0:T(8,128)(2,1)S(1)} %shard_map.59.refs_1_), channel_id=1, source_target_pairs={{0,3},{1,2},{2,1},{3,0},{4,7},{5,6},{6,5},{7,4},{8,11},{9,10},{10,... | collective-permute-start | bytes 49160 | tf_op jit(solution)/shard_map/ppermute | solution.py:257
  8.0 4.6 %collective-permute-start.1 = (bf16[64,128]{1,0:T(8,128)(2,1)S(1)}, bf16[64,128]{1,0:T(8,128)(2,1)S(1)}, u32[]{:S(2)}, u32[]{:S(2)}) collective-permute-start(bf16[64,128]{1,0:T(8,128)(2,1)S(1)} %shard_map.59.refs_1_), channel_id=1, source_target_pairs={{0,2},{1,3},{2,0},{3,1},{4,6},{5,7},{6,4},{7,5},{8,10},{9,11},{10,... | collective-permute-start | bytes 49160 | tf_op jit(solution)/shard_map/ppermute | solution.py:257
  8.0 4.6 %collective-permute-start = (bf16[64,128]{1,0:T(8,128)(2,1)S(1)}, bf16[64,128]{1,0:T(8,128)(2,1)S(1)}, u32[]{:S(2)}, u32[]{:S(2)}) collective-permute-start(bf16[64,128]{1,0:T(8,128)(2,1)S(1)} %shard_map.59.refs_1_), channel_id=1, source_target_pairs={{0,1},{1,0},{2,3},{3,2},{4,5},{5,4},{6,7},{7,6},{8,9},{9,8},{10,11... | collective-permute-start | bytes 49160 | tf_op jit(solution)/shard_map/ppermute | solution.py:257
  12.9 8.8 %copy-start.3 = (f32[8,4096]{1,0:T(8,128)S(1)}, f32[8,4096]{1,0:T(8,128)}, u32[]{:S(2)}) copy-start(f32[8,4096]{1,0:T(8,128)} %wave_ref.3) | copy-start | bytes 393220
  12.9 1.2 %collective-permute-start.4 = (f32[64,128]{1,0:T(8,128)S(1)}, f32[64,128]{1,0:T(8,128)S(1)}, u32[]{:S(2)}, u32[]{:S(2)}) collective-permute-start(f32[64,128]{1,0:T(8,128)S(1)} %get-tuple-element.9.mine_ref), channel_id=1, source_target_pairs={{0,4},{4,0},{8,12},{12,8},{16,20},{20,16},{24,28},{28,24},{1,5},{5... | collective-permute-start | bytes 98312 | tf_op jit(solution)/shard_map/ppermute | solution.py:257
  14.1 7.6 %copy-start.4 = (f32[8,16,2]{1,2,0:T(2,128)S(1)}, f32[8,16,2]{1,2,0:T(2,128)}, u32[]{:S(2)}) copy-start(f32[8,16,2]{1,2,0:T(2,128)} %param.7) | copy-start | bytes 3076
  14.4 5.3 %collective-permute-start.7 = (bf16[8,4224]{1,0:T(8,128)(2,1)S(1)}, bf16[8,4224]{1,0:T(8,128)(2,1)S(1)}, u32[]{:S(2)}, u32[]{:S(2)}) collective-permute-start(bf16[8,4224]{1,0:T(8,128)(2,1)S(1)} %shard_map.61.refs_0_), channel_id=1, source_target_pairs={{0,24},{4,28},{8,16},{12,20},{16,8},{20,12},{24,0},{28,4},{1,25},{... | collective-permute-start | bytes 202760 | tf_op jit(solution)/shard_map/ppermute | solution.py:257
  16.9 4.3 %collective-permute-start.6 = (bf16[8,4224]{1,0:T(8,128)(2,1)S(1)}, bf16[8,4224]{1,0:T(8,128)(2,1)S(1)}, u32[]{:S(2)}, u32[]{:S(2)}) collective-permute-start(bf16[8,4224]{1,0:T(8,128)(2,1)S(1)} %shard_map.61.refs_0_), channel_id=1, source_target_pairs={{0,16},{4,20},{8,24},{12,28},{16,0},{20,4},{24,8},{28,12},{1,17},{... | collective-permute-start | bytes 202760 | tf_op jit(solution)/shard_map/ppermute | solution.py:257
  17.4 4.3 %collective-permute-start.5 = (bf16[8,4224]{1,0:T(8,128)(2,1)S(1)}, bf16[8,4224]{1,0:T(8,128)(2,1)S(1)}, u32[]{:S(2)}, u32[]{:S(2)}) collective-permute-start(bf16[8,4224]{1,0:T(8,128)(2,1)S(1)} %shard_map.61.refs_0_), channel_id=1, source_target_pairs={{0,8},{4,12},{8,0},{12,4},{16,24},{20,28},{24,16},{28,20},{1,9},{5... | collective-permute-start | bytes 202760 | tf_op jit(solution)/shard_map/ppermute | solution.py:257
  23.0 5.4 %collective-permute-start.10 = (f32[8,128]{1,0:T(8,128)S(1)}, f32[8,128]{1,0:T(8,128)S(1)}, u32[]{:S(2)}, u32[]{:S(2)}) collective-permute-start(f32[8,128]{1,0:T(8,128)S(1)} %get-tuple-element.11.refs_0_), channel_id=1, source_target_pairs={{0,3},{1,2},{2,1},{3,0},{4,7},{5,6},{6,5},{7,4},{8,11},{9,10},{10,... | collective-permute-start | bytes 12296 | tf_op jit(solution)/shard_map/ppermute | solution.py:257
  24.4 4.5 %collective-permute-start.9 = (f32[8,128]{1,0:T(8,128)S(1)}, f32[8,128]{1,0:T(8,128)S(1)}, u32[]{:S(2)}, u32[]{:S(2)}) collective-permute-start(f32[8,128]{1,0:T(8,128)S(1)} %get-tuple-element.11.refs_0_), channel_id=1, source_target_pairs={{0,2},{1,3},{2,0},{3,1},{4,6},{5,7},{6,4},{7,5},{8,10},{9,11},{10,... | collective-permute-start | bytes 12296 | tf_op jit(solution)/shard_map/ppermute | solution.py:257
  25.0 4.0 %collective-permute-start.8 = (f32[8,128]{1,0:T(8,128)S(1)}, f32[8,128]{1,0:T(8,128)S(1)}, u32[]{:S(2)}, u32[]{:S(2)}) collective-permute-start(f32[8,128]{1,0:T(8,128)S(1)} %get-tuple-element.11.refs_0_), channel_id=1, source_target_pairs={{0,1},{1,0},{2,3},{3,2},{4,5},{5,4},{6,7},{7,6},{8,9},{9,8},{10,11... | collective-permute-start | bytes 12296 | tf_op jit(solution)/shard_map/ppermute | solution.py:257
  29.9 5.2 %collective-permute-start.13 = (bf16[8,4224]{1,0:T(8,128)(2,1)S(1)}, bf16[8,4224]{1,0:T(8,128)(2,1)S(1)}, u32[]{:S(2)}, u32[]{:S(2)}) collective-permute-start(bf16[8,4224]{1,0:T(8,128)(2,1)S(1)} %get-tuple-element.12.refs_0_), channel_id=1, source_target_pairs={{0,24},{4,28},{8,16},{12,20},{16,8},{20,12},{24,0},{28,4},{1,25},{... | collective-permute-start | bytes 202760 | tf_op jit(solution)/shard_map/ppermute | solution.py:257
  31.4 4.4 %collective-permute-start.12 = (bf16[8,4224]{1,0:T(8,128)(2,1)S(1)}, bf16[8,4224]{1,0:T(8,128)(2,1)S(1)}, u32[]{:S(2)}, u32[]{:S(2)}) collective-permute-start(bf16[8,4224]{1,0:T(8,128)(2,1)S(1)} %get-tuple-element.12.refs_0_), channel_id=1, source_target_pairs={{0,16},{4,20},{8,24},{12,28},{16,0},{20,4},{24,8},{28,12},{1,17},{... | collective-permute-start | bytes 202760 | tf_op jit(solution)/shard_map/ppermute | solution.py:257
  32.2 4.3 %collective-permute-start.11 = (bf16[8,4224]{1,0:T(8,128)(2,1)S(1)}, bf16[8,4224]{1,0:T(8,128)(2,1)S(1)}, u32[]{:S(2)}, u32[]{:S(2)}) collective-permute-start(bf16[8,4224]{1,0:T(8,128)(2,1)S(1)} %get-tuple-element.12.refs_0_), channel_id=1, source_target_pairs={{0,8},{4,12},{8,0},{12,4},{16,24},{20,28},{24,16},{28,20},{1,9},{5... | collective-permute-start | bytes 202760 | tf_op jit(solution)/shard_map/ppermute | solution.py:257

commit v3 on v2

v3 whole, which is shorter than its diff:
```python
import functools

import jax
import jax.numpy as jnp
from jax import lax
from jax.experimental import pallas as pl
from jax.experimental.pallas import tpu as pltpu
from jax.sharding import PartitionSpec as P

step_size = 0.5
LANES = 128
F32 = jnp.float32
BF16 = jnp.bfloat16

E_LAST, E_FIRST, E_SECOND, O_LAST, O_FIRST = range(5)
E_NEXT, D_BEFORE, S_NEXT, D_LAST, D_NEXT = range(5)
KINDS = 5


def lanes_of(shape):
    return lax.broadcasted_iota(jnp.int32, shape, len(shape) - 1)


def turned(x, by):
    return pltpu.roll(x, by % LANES, x.ndim - 1)


def shifted_in(x, by, edge):
    free = 0 if by == 1 else LANES - 1
    return jnp.where(lanes_of(x.shape) == free, edge, turned(x, by))


def edge_tile(pair_of, layers, base):
    tile = None
    for layer in range(layers):
        even, odd = pair_of(layer)
        start = base + KINDS * layer
        lane = lanes_of(even.shape)
        if tile is None:
            tile = jnp.zeros_like(even)
        tile = jnp.where((lane >= start) & (lane < start + 3), turned(even, start + 1), tile)
        tile = jnp.where((lane >= start + 3) & (lane < start + 5), turned(odd, start + 4), tile)
    return tile


def kind_lane(lane, base, kind):
    return lax.rem(lane - base + KINDS * LANES, KINDS) == kind


def shrink(values, cutoff):
    return values - jnp.clip(values, -cutoff, cutoff)


def layer_tiles(ref, layer):
    start = layer * 2 * LANES
    return ref[:, start : start + LANES], ref[:, start + LANES : start + 2 * LANES]


def stacked(ref, layers):
    tiles = [layer_tiles(ref, layer) for layer in range(layers)]
    return tuple(jnp.concatenate([t[p] for t in tiles], axis=0).astype(F32) for p in range(2))


def unstacked(even, odd, models):
    rows = [slice(start, start + models) for start in range(0, even.shape[0], models)]
    return jnp.concatenate([t[r] for r in rows for t in (even, odd)], axis=1)


def nt_dot(a, b):
    return lax.dot_general(a, b, (((1,), (1,)), ((), ())), preferred_element_type=F32)


def inverse_wave(smooth, detail, edge):
    even = smooth - 0.25 * (shifted_in(detail, 1, edge) + detail)
    odd = detail + 0.5 * (even + shifted_in(even, -1, edge))
    return even, odd


def forward_wave(even, odd):
    detail = odd - 0.5 * (even + shifted_in(even, -1, 0.0))
    smooth = even + 0.25 * (shifted_in(detail, 1, 0.0) + detail)
    return smooth, detail


def by_kind(lane, base, *values):
    kind = lax.rem(lane - base + KINDS * LANES, KINDS)
    result = values[0]
    for k, value in enumerate(values[1:], 1):
        result = jnp.where(kind == k, value, result)
    return result


def first_kernel(layers, wave_hbm, k_hbm, packet_ref, wave_ref, k_ref, tile, arrived):
    loads = [
        pltpu.make_async_copy(wave_hbm, wave_ref, arrived.at[0]),
        pltpu.make_async_copy(k_hbm, k_ref, arrived.at[1]),
    ]
    for load in loads:
        load.start()
    rows = k_ref.shape[0]
    models = wave_ref.shape[0]
    loads[0].wait()
    even, odd = inverse_wave(*stacked(wave_ref, layers), 0.0)
    model = unstacked(even, odd, models).astype(BF16)
    tile[...] = edge_tile(lambda l: layer_tiles(wave_ref, l), layers, rows)
    loads[1].wait()
    edges = edge_tile(lambda l: tuple(t.astype(F32) for t in layer_tiles(k_ref, l)), layers, rows)
    packet_ref[:rows, :] = edges.astype(BF16)
    tile[:, :rows] = nt_dot(model, k_ref[...])
    whole = tile[...]
    high = whole.astype(BF16).astype(F32)
    packet_ref[rows:, :] = jnp.concatenate([high, whole - high], axis=0).astype(BF16)


def preparing_kernel(layers, base, k_ref, k_other_ref, threshold_ref, kw_ref, kw_other_ref, cut_ref, cut_halo_ref):
    rows = k_ref.shape[0]
    models, width = cut_ref.shape
    for source, target in ((k_ref, kw_ref), (k_other_ref, kw_other_ref)):
        target[...] = unstacked(*forward_wave(*stacked(source, layers)), rows).astype(BF16)
    lane = lanes_of((models, LANES))
    halo = jnp.zeros((models, LANES), F32)
    for layer in range(layers):
        smooth, detail = (
            jnp.broadcast_to(threshold_ref[:, p, layer : layer + 1], (models, LANES)) for p in range(2)
        )
        start = 2 * LANES * layer
        cut_ref[:, start : start + LANES] = smooth
        cut_ref[:, start + LANES : start + 2 * LANES] = detail
        start = base + KINDS * layer
        here = (lane >= start) & (lane < start + KINDS)
        halo = jnp.where(here, jnp.where(lane == start + S_NEXT, smooth, detail), halo)
    cut_halo_ref[...] = halo


def second_kernel(layers, n_vox, *refs):
    (observed_ref, *packets, out_ref, halo_ref, held) = refs
    models, rows = observed_ref.shape
    me = lax.axis_index("vox")
    for distance, packet in enumerate(packets):
        held[me ^ distance] = packet[...]
    left, right = lax.rem(me + n_vox - 1, n_vox), lax.rem(me + 1, n_vox)
    lane = lanes_of((models, LANES))
    inside = (lane >= rows) & (lane < rows + KINDS * layers)

    def edge_values(which):
        both = held[which, rows:, :].astype(F32)
        return both[:models] + both[models:]

    edge = [edge_values(z) for z in range(n_vox)]
    terms, columns = [], []
    for z in range(n_vox):
        before, after = edge[z - 1], edge[(z + 1) % n_vox]
        next_smooth = turned(after, O_LAST - E_FIRST)
        next_detail = turned(after, O_LAST - O_FIRST)
        next_even = next_smooth - 0.25 * (edge[z] + next_detail)
        term = by_kind(
            lane,
            rows,
            0.0,
            -0.25 * turned(before, E_FIRST - O_LAST),
            0.0,
            0.5 * next_even,
            -0.125 * turned(before, O_FIRST - O_LAST),
        )
        terms.append(jnp.where(inside, term, 0.0).astype(BF16))
        columns.append(held[z, :rows, :])
    predicted = nt_dot(jnp.concatenate(terms, axis=1), jnp.concatenate(columns, axis=1))
    shares = edge[0]
    for z in range(1, n_vox):
        shares = shares + edge[z]
    predicted = predicted + shares[:, :rows]

    before, own, after = (held[z, :rows, :].astype(F32) for z in (left, me, right))
    details = by_kind(
        lanes_of(own.shape),
        rows,
        0.0,
        0.0,
        0.0,
        own - 0.5 * (turned(own, O_LAST - E_LAST) + turned(after, O_LAST - E_FIRST)),
        after - 0.5 * (turned(after, O_FIRST - E_FIRST) + turned(after, O_FIRST - E_SECOND)),
    )
    out_ref[:rows, :] = by_kind(
        lanes_of(own.shape),
        rows,
        turned(after, E_NEXT - E_FIRST),
        turned(before, D_BEFORE - O_LAST) - 0.5 * (turned(before, D_BEFORE - E_LAST) + own),
        turned(after, S_NEXT - E_FIRST) + 0.25 * (turned(details, S_NEXT - D_LAST) + turned(details, S_NEXT - D_NEXT)),
        details,
        details,
    )
    out_ref[rows:, :] = jnp.zeros((2 * models, LANES), F32)
    out_ref[rows : rows + models, :rows] = observed_ref[...] - predicted
    out_ref[rows + models :, :rows] = observed_ref[...]
    before, own, after = (edge_values(z) for z in (left, me, right))
    halo_ref[...] = by_kind(
        lane, rows, 0.0, turned(before, D_BEFORE - O_LAST), turned(after, S_NEXT - E_FIRST), own, after
    )


def in_core_order(mine, other, work):
    core = lax.rem(lax.axis_index("dp"), 2)

    @pl.when(core == 0)
    def _():
        work(mine, other)

    @pl.when(core == 1)
    def _():
        work(other, mine)


def back_projected(mine, other, g_ref):
    width = mine[1].shape[1]

    def work(*cores):
        sent = [residual.astype(BF16) for residual, _, _ in cores]
        g_ref[:, :width] = sum(
            jnp.dot(r, k[...], preferred_element_type=F32) for r, (_, k, _) in zip(sent, cores)
        ).astype(BF16)
        g_ref[:, width:] = sum(
            jnp.dot(r, h[...].astype(BF16), preferred_element_type=F32) for r, (_, _, h) in zip(sent, cores)
        ).astype(BF16)

    in_core_order(mine, other, work)


def third_kernel(mine_ref, other_ref, kw_ref, kw_other_ref, g_ref):
    rows = kw_ref.shape[0]
    models = g_ref.shape[0]

    def core(ref, k):
        return ref[rows : rows + models, :rows], k, ref.at[:rows]

    back_projected(core(mine_ref, kw_ref), core(other_ref, kw_other_ref), g_ref)


def tree_sum(values):
    while len(values) > 1:
        values = [a + b for a, b in zip(values[::2], values[1::2])]
    return values[0]


def at_ends(tile, layers, base):
    return jnp.concatenate([turned(tile, -(base + KINDS * layer + 1)) for layer in range(layers)], axis=0)


def stepped(layers, base, wave_ref, cut_ref, g_refs):
    width = wave_ref.shape[1]
    gradients = [stacked(g, layers) for g in g_refs]
    smooth_g, detail_g = (tree_sum([g[p] for g in gradients]) for p in range(2))
    edge = tree_sum([g[:, width:].astype(F32) for g in g_refs])
    ends = at_ends(edge, layers, base)
    lane = lanes_of(ends.shape)
    smooth_g += jnp.where(lane == 0, 0.25 * ends, jnp.where(lane == LANES - 1, -0.125 * ends, 0.0))
    detail_g += jnp.where(lane == LANES - 1, -0.5 * ends, 0.0)
    smooth, detail = (
        shrink(w + step_size * g, cut)
        for w, g, cut in zip(stacked(wave_ref, layers), (smooth_g, detail_g), stacked(cut_ref, layers))
    )
    return smooth, detail, edge


def fourth_kernel(layers, base, wave_ref, cut_ref, halo_ref, cut_halo_ref, k_ref, k_other_ref, *refs):
    *g_refs, new_ref, pred_ref = refs
    models = wave_ref.shape[0]
    rows = k_ref.shape[0]
    smooth, detail, edge = stepped(layers, base, wave_ref, cut_ref, g_refs)
    new_ref[...] = unstacked(smooth, detail, models)
    halo = shrink(halo_ref[...] + step_size * edge, cut_halo_ref[...])
    next_even = turned(halo, E_NEXT - S_NEXT) - 0.25 * (turned(halo, E_NEXT - D_LAST) + turned(halo, E_NEXT - D_NEXT))
    ends = at_ends(by_kind(lanes_of(halo.shape), base, next_even, halo), layers, base)
    model = unstacked(*inverse_wave(smooth, detail, ends), models).astype(BF16)
    pred_ref[...] = jnp.zeros_like(pred_ref)
    pred_ref[:, :rows] = nt_dot(model, k_ref[...])
    pred_ref[:, rows : 2 * rows] = nt_dot(model, k_other_ref[...])


def fifth_kernel(mine_ref, other_ref, kw_ref, kw_other_ref, *refs):
    *shares, g_ref, residual_ref = refs
    models, rows = residual_ref.shape
    predicted = tree_sum([s[...] for s in shares])

    def core(ref, k, start):
        residual = ref[rows + models :, :rows] - predicted[:, start : start + rows]
        return residual, k, ref.at[:rows]

    mine = core(mine_ref, kw_ref, 0)
    residual_ref[...] = mine[0]
    back_projected(mine, core(other_ref, kw_other_ref, rows), g_ref)


def sixth_kernel(layers, base, wave_ref, cut_ref, *refs):
    *g_refs, new_ref = refs
    smooth, detail, _ = stepped(layers, base, wave_ref, cut_ref, g_refs)
    new_ref[...] = unstacked(smooth, detail, wave_ref.shape[0])


def from_partner(x, axis, distance):
    return lax.ppermute(x, axis, [(i, i ^ distance) for i in range(lax.axis_size(axis))])


def shares_of(x, axis, lowest):
    size = lax.axis_size(axis) // lowest
    while size > 4:
        parts = [x] + [from_partner(x, axis, lowest * d) for d in range(1, 4)]
        x = tree_sum([p.astype(F32) for p in parts]).astype(x.dtype)
        lowest, size = lowest * 4, size // 4
    return [x] + [from_partner(x, axis, lowest * d) for d in range(1, size)]


def call(kernel, out_shape, *args, scratch=(), space=pltpu.VMEM):
    return pl.pallas_call(
        kernel,
        out_shape=out_shape,
        in_specs=[pl.BlockSpec(memory_space=space)] * len(args),
        out_specs=jax.tree.map(lambda _: pl.BlockSpec(memory_space=pltpu.VMEM), out_shape),
        scratch_shapes=list(scratch),
    )(*[pltpu.with_memory_space_constraint(arg, space) for arg in args])


def body(kernels, observed, initial, threshold):
    models, width = initial.shape
    rows = kernels.shape[0]
    layers = threshold.shape[1]
    n_vox = lax.axis_size("vox")
    assert width == 2 * layers * LANES and rows + KINDS * layers <= LANES and 2 * rows <= LANES
    packet_rows = rows + 2 * models
    g_shape = pltpu.VMEM((models, width + LANES), BF16)

    packet, wavelets, k_mine = call(
        functools.partial(first_kernel, layers),
        (pltpu.VMEM((packet_rows, LANES), BF16), pltpu.VMEM((models, width), F32), pltpu.VMEM((rows, width), BF16)),
        initial,
        kernels,
        scratch=[pltpu.VMEM((models, LANES), F32), pltpu.SemaphoreType.DMA((2,))],
        space=pltpu.HBM,
    )
    packets = [packet] + [from_partner(packet, "vox", d) for d in range(1, n_vox)]
    k_other = from_partner(k_mine, "dp", 1)
    kw, kw_other, cut, cut_halo = call(
        functools.partial(preparing_kernel, layers, rows),
        (
            pltpu.VMEM((rows, width), BF16),
            pltpu.VMEM((rows, width), BF16),
            pltpu.VMEM((models, width), F32),
            pltpu.VMEM((models, LANES), F32),
        ),
        k_mine,
        k_other,
        jnp.swapaxes(threshold, 1, 2),
    )
    mine, halo = call(
        functools.partial(second_kernel, layers, n_vox),
        (pltpu.VMEM((packet_rows, LANES), F32), pltpu.VMEM((models, LANES), F32)),
        observed,
        *packets,
        scratch=[pltpu.VMEM((n_vox, packet_rows, LANES), BF16)],
    )
    other = from_partner(mine, "dp", 1)
    g = call(third_kernel, g_shape, mine, other, kw, kw_other)
    wavelets, predicted = call(
        functools.partial(fourth_kernel, layers, rows),
        (pltpu.VMEM((models, width), F32), pltpu.VMEM((models, LANES), F32)),
        wavelets,
        cut,
        halo,
        cut_halo,
        k_mine,
        k_other,
        *shares_of(g, "dp", 2),
    )
    g, residual = call(
        fifth_kernel,
        (g_shape, pltpu.VMEM((models, rows), F32)),
        mine,
        other,
        kw,
        kw_other,
        *shares_of(predicted, "vox", 1),
    )
    coefficients = call(
        functools.partial(sixth_kernel, layers, rows),
        jax.ShapeDtypeStruct((models, width), F32),
        wavelets,
        cut,
        *shares_of(g, "dp", 2),
    )
    return coefficients, residual


def solution(mesh):
    return jax.shard_map(
        body,
        mesh=mesh,
        in_specs=(P("dp", "vox"), P(None, "dp"), P(None, "vox"), P()),
        out_specs=(P(None, "vox"), P(None, "dp")),
        check_vma=False,
    )
```

time: 37.8 us -> 35.5 us (0.939)
  waiting for transfers between devices: 13.7 us -> 11.9 us
  local copies, waits for them, and re-layouts: 1.91 us -> 0.99 us
    ppermute x14, waiting for transfers between devices: 13.7 us -> 11.9 us  [from_partner(): lax.ppermute(x, axis, [(i, i ^ distance) for i in range(lax.axis_size(axi...]
    unnamed x12 -> x5, local copies, waits for them, and re-layouts: 1.91 us -> 0.99 us
    pallas_call x6 -> x7, Pallas kernels: 4.08 us -> 4.28 us  [call(): pl.pallas_call(kernel, out_shape=out_shape, in_specs=[pl.BlockSpec(memory...]
  transfers between devices with their start and end apart: 14 -> 14, of which waited for: 11 -> 10; matrix products, arithmetic and copies ran while one was open for 0% -> 2% of each run, Pallas kernels for 2% -> 3%
where the time goes in v3:
time: 35.5 us; the launch traced here: 35.3 us
  starting transfers between devices  17.4 us (49%)
  waiting for transfers between devices  11.9 us (34%)
  Pallas kernels  4.28 us (12%)
  local copies, waits for them, and re-layouts  0.99 us (3%)
  between operations  0.7 us (2%)
    ppermute x14, starting transfers between devices, from_partner(): lax.ppermute(x, axis, [(i, i ^ distance) for i in range(lax.axis_size(axi...  17.4 us
    ppermute x14, waiting for transfers between devices, from_partner(): lax.ppermute(x, axis, [(i, i ^ distance) for i in range(lax.axis_size(axi...  11.9 us
    pallas_call x7, Pallas kernels, call(): pl.pallas_call(kernel, out_shape=out_shape, in_specs=[pl.BlockSpec(memory...  4.28 us
    unnamed x5, local copies, waits for them, and re-layouts  0.99 us
  transfers between devices with their start and end apart: 14, of which 10 were waited for; matrix products, arithmetic and copies ran while one was open for 2% of the time, Pallas kernels for 3%

profile of v3, /device:TPU:0, one launch (start us, length us, event | category | flops | bytes accessed | tf_op | source)
XLA Modules:
  0.0 35.3 jit_solution(8798621636658241247)
XLA Ops:
  0.6 0.0 copy-start.1
  0.6 1.3 %shard_map.59 = (bf16[64,128]{1,0:T(8,128)(2,1)S(1)}, f32[8,4096]{1,0:T(8,128)S(1)}, bf16[48,4096]{1,0:T(8,128)(2,1)S(1)}) custom-call(f32[8,4096]{1,0:T(8,128)} %wave_hbm.1, bf16[48,4096]{1,0:T(8,128)(2,1)} %k_hbm.1), custom_call_target="tpu_custom_call" | custom-call | tf_op jit(solution)/shard_map/pallas_call | solution.py:313
  2.0 0.5 %collective-permute-start = (bf16[48,4096]{1,0:T(8,128)(2,1)S(1)}, bf16[48,4096]{1,0:T(8,128)(2,1)S(1)}, u32[]{:S(2)}, u32[]{:S(2)}) collective-permute-start(bf16[48,4096]{1,0:T(8,128)(2,1)S(1)} %get-tuple-element.16.k_ref), channel_id=1, source_target_pairs={{0,4},{4,0},{8,12},{12,8},{16,20},{20,16},{24,28},{28,24},{1,5},{5... | collective-permute-start | bytes 1179656 | tf_op jit(solution)/shard_map/ppermute | solution.py:300
  2.5 4.7 %collective-permute-start.3 = (bf16[64,128]{1,0:T(8,128)(2,1)S(1)}, bf16[64,128]{1,0:T(8,128)(2,1)S(1)}, u32[]{:S(2)}, u32[]{:S(2)}) collective-permute-start(bf16[64,128]{1,0:T(8,128)(2,1)S(1)} %get-tuple-element.18.refs_1_), channel_id=1, source_target_pairs={{0,3},{1,2},{2,1},{3,0},{4,7},{5,6},{6,5},{7,4},{8,11},{9,10},{10,... | collective-permute-start | bytes 49160 | tf_op jit(solution)/shard_map/ppermute | solution.py:300
  7.2 0.0 collective-permute-start.2
  7.2 0.6 %collective-permute-start.1 = (bf16[64,128]{1,0:T(8,128)(2,1)S(1)}, bf16[64,128]{1,0:T(8,128)(2,1)S(1)}, u32[]{:S(2)}, u32[]{:S(2)}) collective-permute-start(bf16[64,128]{1,0:T(8,128)(2,1)S(1)} %get-tuple-element.18.refs_1_), channel_id=1, source_target_pairs={{0,1},{1,0},{2,3},{3,2},{4,5},{5,4},{6,7},{7,6},{8,9},{9,8},{10,11... | collective-permute-start | bytes 49160 | tf_op jit(solution)/shard_map/ppermute | solution.py:300
  7.8 1.1 %collective-permute-done.3.refs_4_ = bf16[64,128]{1,0:T(8,128)(2,1)S(1)} collective-permute-done((bf16[64,128]{1,0:T(8,128)(2,1)S(1)}, bf16[64,128]{1,0:T(8,128)(2,1)S(1)}, u32[]{:S(2)}, u32[]{:S(2)}) %collective-permute-start.3) | collective-permute-done | bytes 16416 | tf_op jit(solution)/shard_map/ppermute | solution.py:300
  8.9 2.9 %collective-permute-done.2.refs_3_ = bf16[64,128]{1,0:T(8,128)(2,1)S(1)} collective-permute-done((bf16[64,128]{1,0:T(8,128)(2,1)S(1)}, bf16[64,128]{1,0:T(8,128)(2,1)S(1)}, u32[]{:S(2)}, u32[]{:S(2)}) %collective-permute-start.2) | collective-permute-done | bytes 16416 | tf_op jit(solution)/shard_map/ppermute | solution.py:300
  11.8 0.0 collective-permute-done.1.refs_2_
  11.8 0.0 copy-done.1
  11.8 0.0 copy-start
  11.8 0.2 shard_map.61
  12.0 0.1 collective-permute-start.4
  12.1 0.0 collective-permute-done.k_other_ref
  12.1 0.4 %copy-done = f32[8,16,2]{1,2,0:T(2,128)S(1)} copy-done((f32[8,16,2]{1,2,0:T(2,128)S(1)}, f32[8,16,2]{1,2,0:T(2,128)}, u32[]{:S(2)}) %copy-start) | copy-done | bytes 1048
  12.5 0.8 %shard_map.60 = (bf16[48,4096]{1,0:T(8,128)(2,1)S(1)}, bf16[48,4096]{1,0:T(8,128)(2,1)S(1)}, f32[8,4096]{1,0:T(8,128)S(1)}, f32[8,128]{1,0:T(8,128)S(1)}) custom-call(bf16[48,4096]{1,0:T(8,128)(2,1)S(1)} %get-tuple-element.16.k_ref, bf16[48,4096]{1,0:T(8,128)(2,1)S(1)} %collective-permute-done.k_other_ref, f32[8,2,16]{2,1,0:T(2,128)S(1)} %bitcast.1), custom_call_target="tpu_custom_call" | custom-call | tf_op jit(solution)/shard_map/pallas_call | solution.py:313
  13.3 0.0 collective-permute-done.4.other_ref
  13.3 0.2 shard_map.62.refs_0_
  13.5 2.5 %collective-permute-start.7 = (bf16[8,4224]{1,0:T(8,128)(2,1)S(1)}, bf16[8,4224]{1,0:T(8,128)(2,1)S(1)}, u32[]{:S(2)}, u32[]{:S(2)}) collective-permute-start(bf16[8,4224]{1,0:T(8,128)(2,1)S(1)} %shard_map.62.refs_0_), channel_id=1, source_target_pairs={{0,24},{4,28},{8,16},{12,20},{16,8},{20,12},{24,0},{28,4},{1,25},{... | collective-permute-start | bytes 202760 | tf_op jit(solution)/shard_map/ppermute | solution.py:300
  16.1 0.5 %collective-permute-start.6 = (bf16[8,4224]{1,0:T(8,128)(2,1)S(1)}, bf16[8,4224]{1,0:T(8,128)(2,1)S(1)}, u32[]{:S(2)}, u32[]{:S(2)}) collective-permute-start(bf16[8,4224]{1,0:T(8,128)(2,1)S(1)} %shard_map.62.refs_0_), channel_id=1, source_target_pairs={{0,16},{4,20},{8,24},{12,28},{16,0},{20,4},{24,8},{28,12},{1,17},{... | collective-permute-start | bytes 202760 | tf_op jit(solution)/shard_map/ppermute | solution.py:300
  16.6 0.5 %collective-permute-start.5 = (bf16[8,4224]{1,0:T(8,128)(2,1)S(1)}, bf16[8,4224]{1,0:T(8,128)(2,1)S(1)}, u32[]{:S(2)}, u32[]{:S(2)}) collective-permute-start(bf16[8,4224]{1,0:T(8,128)(2,1)S(1)} %shard_map.62.refs_0_), channel_id=1, source_target_pairs={{0,8},{4,12},{8,0},{12,4},{16,24},{20,28},{24,16},{28,20},{1,9},{5... | collective-permute-start | bytes 202760 | tf_op jit(solution)/shard_map/ppermute | solution.py:300
  17.1 1.7 %collective-permute-done.7.refs_3_ = bf16[8,4224]{1,0:T(8,128)(2,1)S(1)} collective-permute-done((bf16[8,4224]{1,0:T(8,128)(2,1)S(1)}, bf16[8,4224]{1,0:T(8,128)(2,1)S(1)}, u32[]{:S(2)}, u32[]{:S(2)}) %collective-permute-start.7) | collective-permute-done | bytes 67616 | tf_op jit(solution)/shard_map/ppermute | solution.py:300
  18.8 1.5 %collective-permute-done.6.refs_2_ = bf16[8,4224]{1,0:T(8,128)(2,1)S(1)} collective-permute-done((bf16[8,4224]{1,0:T(8,128)(2,1)S(1)}, bf16[8,4224]{1,0:T(8,128)(2,1)S(1)}, u32[]{:S(2)}, u32[]{:S(2)}) %collective-permute-start.6) | collective-permute-done | bytes 67616 | tf_op jit(solution)/shard_map/ppermute | solution.py:300
  20.3 0.5 %collective-permute-done.5.refs_1_ = bf16[8,4224]{1,0:T(8,128)(2,1)S(1)} collective-permute-done((bf16[8,4224]{1,0:T(8,128)(2,1)S(1)}, bf16[8,4224]{1,0:T(8,128)(2,1)S(1)}, u32[]{:S(2)}, u32[]{:S(2)}) %collective-permute-start.5) | collective-permute-done | bytes 67616 | tf_op jit(solution)/shard_map/ppermute | solution.py:300
  20.9 0.7 %shard_map.63 = (f32[8,4096]{1,0:T(8,128)S(1)}, f32[8,128]{1,0:T(8,128)S(1)}) custom-call(f32[8,4096]{1,0:T(8,128)S(1)} %get-tuple-element.15.wave_ref, f32[8,4096]{1,0:T(8,128)S(1)} %get-tuple-element.17.cut_ref, f32[8,128]{1,0:T(8,128)S(1)} %get-tuple-element.19.halo_ref, f32[8,128]{1,0:T(8,128)S(1)} %get-tuple-element.20.cut_halo_ref, ...), custom_call_target="tpu_custom_call" | custom-call | tf_op jit(solution)/shard_map/pallas_call | solution.py:313
  21.5 1.5 %collective-permute-start.10 = (f32[8,128]{1,0:T(8,128)S(1)}, f32[8,128]{1,0:T(8,128)S(1)}, u32[]{:S(2)}, u32[]{:S(2)}) collective-permute-start(f32[8,128]{1,0:T(8,128)S(1)} %get-tuple-element.25.refs_0_), channel_id=1, source_target_pairs={{0,3},{1,2},{2,1},{3,0},{4,7},{5,6},{6,5},{7,4},{8,11},{9,10},{10,... | collective-permute-start | bytes 12296 | tf_op jit(solution)/shard_map/ppermute | solution.py:300
  23.0 0.6 %collective-permute-start.9 = (f32[8,128]{1,0:T(8,128)S(1)}, f32[8,128]{1,0:T(8,128)S(1)}, u32[]{:S(2)}, u32[]{:S(2)}) collective-permute-start(f32[8,128]{1,0:T(8,128)S(1)} %get-tuple-element.25.refs_0_), channel_id=1, source_target_pairs={{0,2},{1,3},{2,0},{3,1},{4,6},{5,7},{6,4},{7,5},{8,10},{9,11},{10,... | collective-permute-start | bytes 12296 | tf_op jit(solution)/shard_map/ppermute | solution.py:300
  23.6 2.4 %collective-permute-start.8 = (f32[8,128]{1,0:T(8,128)S(1)}, f32[8,128]{1,0:T(8,128)S(1)}, u32[]{:S(2)}, u32[]{:S(2)}) collective-permute-start(f32[8,128]{1,0:T(8,128)S(1)} %get-tuple-element.25.refs_0_), channel_id=1, source_target_pairs={{0,1},{1,0},{2,3},{3,2},{4,5},{5,4},{6,7},{7,6},{8,9},{9,8},{10,11... | collective-permute-start | bytes 12296 | tf_op jit(solution)/shard_map/ppermute | solution.py:300
  25.9 1.0 %collective-permute-done.10.refs_3_ = f32[8,128]{1,0:T(8,128)S(1)} collective-permute-done((f32[8,128]{1,0:T(8,128)S(1)}, f32[8,128]{1,0:T(8,128)S(1)}, u32[]{:S(2)}, u32[]{:S(2)}) %collective-permute-start.10) | collective-permute-done | bytes 4128 | tf_op jit(solution)/shard_map/ppermute | solution.py:300
  27.0 0.6 %collective-permute-done.9.refs_2_ = f32[8,128]{1,0:T(8,128)S(1)} collective-permute-done((f32[8,128]{1,0:T(8,128)S(1)}, f32[8,128]{1,0:T(8,128)S(1)}, u32[]{:S(2)}, u32[]{:S(2)}) %collective-permute-start.9) | collective-permute-done | bytes 4128 | tf_op jit(solution)/shard_map/ppermute | solution.py:300
  27.5 0.0 collective-permute-done.8.refs_1_
  27.5 0.3 shard_map.64
  27.9 1.6 %collective-permute-start.13 = (bf16[8,4224]{1,0:T(8,128)(2,1)S(1)}, bf16[8,4224]{1,0:T(8,128)(2,1)S(1)}, u32[]{:S(2)}, u32[]{:S(2)}) collective-permute-start(bf16[8,4224]{1,0:T(8,128)(2,1)S(1)} %get-tuple-element.26.refs_0_), channel_id=1, source_target_pairs={{0,24},{4,28},{8,16},{12,20},{16,8},{20,12},{24,0},{28,4},{1,25},{... | collective-permute-start | bytes 202760 | tf_op jit(solution)/shard_map/ppermute | solution.py:300
  29.4 0.8 %collective-permute-start.12 = (bf16[8,4224]{1,0:T(8,128)(2,1)S(1)}, bf16[8,4224]{1,0:T(8,128)(2,1)S(1)}, u32[]{:S(2)}, u32[]{:S(2)}) collective-permute-start(bf16[8,4224]{1,0:T(8,128)(2,1)S(1)} %get-tuple-element.26.refs_0_), channel_id=1, source_target_pairs={{0,16},{4,20},{8,24},{12,28},{16,0},{20,4},{24,8},{28,12},{1,17},{... | collective-permute-start | bytes 202760 | tf_op jit(solution)/shard_map/ppermute | solution.py:300
  30.2 1.2 %collective-permute-start.11 = (bf16[8,4224]{1,0:T(8,128)(2,1)S(1)}, bf16[8,4224]{1,0:T(8,128)(2,1)S(1)}, u32[]{:S(2)}, u32[]{:S(2)}) collective-permute-start(bf16[8,4224]{1,0:T(8,128)(2,1)S(1)} %get-tuple-element.26.refs_0_), channel_id=1, source_target_pairs={{0,8},{4,12},{8,0},{12,4},{16,24},{20,28},{24,16},{28,20},{1,9},{5... | collective-permute-start | bytes 202760 | tf_op jit(solution)/shard_map/ppermute | solution.py:300
  31.4 0.6 %copy.6 = f32[8,48]{1,0:T(8,128)} copy(f32[8,48]{1,0:T(8,128)S(1)} %get-tuple-element.29) | data formatting | bytes 3072
  32.0 1.1 %collective-permute-done.13.refs_3_ = bf16[8,4224]{1,0:T(8,128)(2,1)S(1)} collective-permute-done((bf16[8,4224]{1,0:T(8,128)(2,1)S(1)}, bf16[8,4224]{1,0:T(8,128)(2,1)S(1)}, u32[]{:S(2)}, u32[]{:S(2)}) %collective-permute-start.13) | collective-permute-done | bytes 67616 | tf_op jit(solution)/shard_map/ppermute | solution.py:300
  33.1 0.7 %collective-permute-done.12.refs_2_ = bf16[8,4224]{1,0:T(8,128)(2,1)S(1)} collective-permute-done((bf16[8,4224]{1,0:T(8,128)(2,1)S(1)}, bf16[8,4224]{1,0:T(8,128)(2,1)S(1)}, u32[]{:S(2)}, u32[]{:S(2)}) %collective-permute-start.12) | collective-permute-done | bytes 67616 | tf_op jit(solution)/shard_map/ppermute | solution.py:300
  33.8 0.7 %collective-permute-done.11.refs_1_ = bf16[8,4224]{1,0:T(8,128)(2,1)S(1)} collective-permute-done((bf16[8,4224]{1,0:T(8,128)(2,1)S(1)}, bf16[8,4224]{1,0:T(8,128)(2,1)S(1)}, u32[]{:S(2)}, u32[]{:S(2)}) %collective-permute-start.11) | collective-permute-done | bytes 67616 | tf_op jit(solution)/shard_map/ppermute | solution.py:300
  34.5 0.8 %shard_map.65 = f32[8,4096]{1,0:T(8,128)} custom-call(f32[8,4096]{1,0:T(8,128)S(1)} %get-tuple-element.24.wave_ref, f32[8,4096]{1,0:T(8,128)S(1)} %get-tuple-element.17.cut_ref, bf16[8,4224]{1,0:T(8,128)(2,1)S(1)} %get-tuple-element.26.refs_0_, bf16[8,4224]{1,0:T(8,128)(2,1)S(1)} %collective-permute-done.11.refs_1_, ...), custom_call_target="tpu_custom_call" | custom-call | tf_op jit(solution)/shard_map/pallas_call | solution.py:313
Async XLA Ops:
  0.6 11.2 %copy-start.1 = (f32[8,48]{1,0:T(8,128)S(1)}, f32[8,48]{1,0:T(8,128)}, u32[]{:S(2)}) copy-start(f32[8,48]{1,0:T(8,128)} %refs_0_.1) | copy-start | bytes 4612
  2.0 10.1 %collective-permute-start = (bf16[48,4096]{1,0:T(8,128)(2,1)S(1)}, bf16[48,4096]{1,0:T(8,128)(2,1)S(1)}, u32[]{:S(2)}, u32[]{:S(2)}) collective-permute-start(bf16[48,4096]{1,0:T(8,128)(2,1)S(1)} %get-tuple-element.16.k_ref), channel_id=1, source_target_pairs={{0,4},{4,0},{8,12},{12,8},{16,20},{20,16},{24,28},{28,24},{1,5},{5... | collective-permute-start | bytes 1179656 | tf_op jit(solution)/shard_map/ppermute | solution.py:300
  2.5 6.4 %collective-permute-start.3 = (bf16[64,128]{1,0:T(8,128)(2,1)S(1)}, bf16[64,128]{1,0:T(8,128)(2,1)S(1)}, u32[]{:S(2)}, u32[]{:S(2)}) collective-permute-start(bf16[64,128]{1,0:T(8,128)(2,1)S(1)} %get-tuple-element.18.refs_1_), channel_id=1, source_target_pairs={{0,3},{1,2},{2,1},{3,0},{4,7},{5,6},{6,5},{7,4},{8,11},{9,10},{10,... | collective-permute-start | bytes 49160 | tf_op jit(solution)/shard_map/ppermute | solution.py:300
  7.2 4.6 %collective-permute-start.2 = (bf16[64,128]{1,0:T(8,128)(2,1)S(1)}, bf16[64,128]{1,0:T(8,128)(2,1)S(1)}, u32[]{:S(2)}, u32[]{:S(2)}) collective-permute-start(bf16[64,128]{1,0:T(8,128)(2,1)S(1)} %get-tuple-element.18.refs_1_), channel_id=1, source_target_pairs={{0,2},{1,3},{2,0},{3,1},{4,6},{5,7},{6,4},{7,5},{8,10},{9,11},{10,... | collective-permute-start | bytes 49160 | tf_op jit(solution)/shard_map/ppermute | solution.py:300
  7.2 4.6 %collective-permute-start.1 = (bf16[64,128]{1,0:T(8,128)(2,1)S(1)}, bf16[64,128]{1,0:T(8,128)(2,1)S(1)}, u32[]{:S(2)}, u32[]{:S(2)}) collective-permute-start(bf16[64,128]{1,0:T(8,128)(2,1)S(1)} %get-tuple-element.18.refs_1_), channel_id=1, source_target_pairs={{0,1},{1,0},{2,3},{3,2},{4,5},{5,4},{6,7},{7,6},{8,9},{9,8},{10,11... | collective-permute-start | bytes 49160 | tf_op jit(solution)/shard_map/ppermute | solution.py:300
  11.8 0.7 %copy-start = (f32[8,16,2]{1,2,0:T(2,128)S(1)}, f32[8,16,2]{1,2,0:T(2,128)}, u32[]{:S(2)}) copy-start(f32[8,16,2]{1,2,0:T(2,128)} %param.7) | copy-start | bytes 3076
  12.0 1.3 %collective-permute-start.4 = (f32[64,128]{1,0:T(8,128)S(1)}, f32[64,128]{1,0:T(8,128)S(1)}, u32[]{:S(2)}, u32[]{:S(2)}) collective-permute-start(f32[64,128]{1,0:T(8,128)S(1)} %get-tuple-element.21.mine_ref), channel_id=1, source_target_pairs={{0,4},{4,0},{8,12},{12,8},{16,20},{20,16},{24,28},{28,24},{1,5},{5... | collective-permute-start | bytes 98312 | tf_op jit(solution)/shard_map/ppermute | solution.py:300
  13.5 5.3 %collective-permute-start.7 = (bf16[8,4224]{1,0:T(8,128)(2,1)S(1)}, bf16[8,4224]{1,0:T(8,128)(2,1)S(1)}, u32[]{:S(2)}, u32[]{:S(2)}) collective-permute-start(bf16[8,4224]{1,0:T(8,128)(2,1)S(1)} %shard_map.62.refs_0_), channel_id=1, source_target_pairs={{0,24},{4,28},{8,16},{12,20},{16,8},{20,12},{24,0},{28,4},{1,25},{... | collective-permute-start | bytes 202760 | tf_op jit(solution)/shard_map/ppermute | solution.py:300
  16.1 4.3 %collective-permute-start.6 = (bf16[8,4224]{1,0:T(8,128)(2,1)S(1)}, bf16[8,4224]{1,0:T(8,128)(2,1)S(1)}, u32[]{:S(2)}, u32[]{:S(2)}) collective-permute-start(bf16[8,4224]{1,0:T(8,128)(2,1)S(1)} %shard_map.62.refs_0_), channel_id=1, source_target_pairs={{0,16},{4,20},{8,24},{12,28},{16,0},{20,4},{24,8},{28,12},{1,17},{... | collective-permute-start | bytes 202760 | tf_op jit(solution)/shard_map/ppermute | solution.py:300
  16.6 4.3 %collective-permute-start.5 = (bf16[8,4224]{1,0:T(8,128)(2,1)S(1)}, bf16[8,4224]{1,0:T(8,128)(2,1)S(1)}, u32[]{:S(2)}, u32[]{:S(2)}) collective-permute-start(bf16[8,4224]{1,0:T(8,128)(2,1)S(1)} %shard_map.62.refs_0_), channel_id=1, source_target_pairs={{0,8},{4,12},{8,0},{12,4},{16,24},{20,28},{24,16},{28,20},{1,9},{5... | collective-permute-start | bytes 202760 | tf_op jit(solution)/shard_map/ppermute | solution.py:300
  21.5 5.4 %collective-permute-start.10 = (f32[8,128]{1,0:T(8,128)S(1)}, f32[8,128]{1,0:T(8,128)S(1)}, u32[]{:S(2)}, u32[]{:S(2)}) collective-permute-start(f32[8,128]{1,0:T(8,128)S(1)} %get-tuple-element.25.refs_0_), channel_id=1, source_target_pairs={{0,3},{1,2},{2,1},{3,0},{4,7},{5,6},{6,5},{7,4},{8,11},{9,10},{10,... | collective-permute-start | bytes 12296 | tf_op jit(solution)/shard_map/ppermute | solution.py:300
  23.0 4.5 %collective-permute-start.9 = (f32[8,128]{1,0:T(8,128)S(1)}, f32[8,128]{1,0:T(8,128)S(1)}, u32[]{:S(2)}, u32[]{:S(2)}) collective-permute-start(f32[8,128]{1,0:T(8,128)S(1)} %get-tuple-element.25.refs_0_), channel_id=1, source_target_pairs={{0,2},{1,3},{2,0},{3,1},{4,6},{5,7},{6,4},{7,5},{8,10},{9,11},{10,... | collective-permute-start | bytes 12296 | tf_op jit(solution)/shard_map/ppermute | solution.py:300
  23.6 4.0 %collective-permute-start.8 = (f32[8,128]{1,0:T(8,128)S(1)}, f32[8,128]{1,0:T(8,128)S(1)}, u32[]{:S(2)}, u32[]{:S(2)}) collective-permute-start(f32[8,128]{1,0:T(8,128)S(1)} %get-tuple-element.25.refs_0_), channel_id=1, source_target_pairs={{0,1},{1,0},{2,3},{3,2},{4,5},{5,4},{6,7},{7,6},{8,9},{9,8},{10,11... | collective-permute-start | bytes 12296 | tf_op jit(solution)/shard_map/ppermute | solution.py:300
  27.9 5.3 %collective-permute-start.13 = (bf16[8,4224]{1,0:T(8,128)(2,1)S(1)}, bf16[8,4224]{1,0:T(8,128)(2,1)S(1)}, u32[]{:S(2)}, u32[]{:S(2)}) collective-permute-start(bf16[8,4224]{1,0:T(8,128)(2,1)S(1)} %get-tuple-element.26.refs_0_), channel_id=1, source_target_pairs={{0,24},{4,28},{8,16},{12,20},{16,8},{20,12},{24,0},{28,4},{1,25},{... | collective-permute-start | bytes 202760 | tf_op jit(solution)/shard_map/ppermute | solution.py:300
  29.4 4.4 %collective-permute-start.12 = (bf16[8,4224]{1,0:T(8,128)(2,1)S(1)}, bf16[8,4224]{1,0:T(8,128)(2,1)S(1)}, u32[]{:S(2)}, u32[]{:S(2)}) collective-permute-start(bf16[8,4224]{1,0:T(8,128)(2,1)S(1)} %get-tuple-element.26.refs_0_), channel_id=1, source_target_pairs={{0,16},{4,20},{8,24},{12,28},{16,0},{20,4},{24,8},{28,12},{1,17},{... | collective-permute-start | bytes 202760 | tf_op jit(solution)/shard_map/ppermute | solution.py:300
  30.2 4.3 %collective-permute-start.11 = (bf16[8,4224]{1,0:T(8,128)(2,1)S(1)}, bf16[8,4224]{1,0:T(8,128)(2,1)S(1)}, u32[]{:S(2)}, u32[]{:S(2)}) collective-permute-start(bf16[8,4224]{1,0:T(8,128)(2,1)S(1)} %get-tuple-element.26.refs_0_), channel_id=1, source_target_pairs={{0,8},{4,12},{8,0},{12,4},{16,24},{20,28},{24,16},{28,20},{1,9},{5... | collective-permute-start | bytes 202760 | tf_op jit(solution)/shard_map/ppermute | solution.py:300

commit v4 on v3

--- a/solution.py
+++ b/solution.py
@@ -272,22 +272,27 @@
     ends = at_ends(by_kind(lanes_of(halo.shape), base, next_even, halo), layers, base)
     model = unstacked(*inverse_wave(smooth, detail, ends), models).astype(BF16)
     pred_ref[...] = jnp.zeros_like(pred_ref)
-    pred_ref[:, :rows] = nt_dot(model, k_ref[...])
-    pred_ref[:, rows : 2 * rows] = nt_dot(model, k_other_ref[...])
+
+    def work(first, second):
+        pred_ref[:, :rows] = nt_dot(model, first[...])
+        pred_ref[:, rows : 2 * rows] = nt_dot(model, second[...])
+
+    in_core_order(k_ref, k_other_ref, work)
 
 
 def fifth_kernel(mine_ref, other_ref, kw_ref, kw_other_ref, *refs):
     *shares, g_ref, residual_ref = refs
     models, rows = residual_ref.shape
     predicted = tree_sum([s[...] for s in shares])
-
-    def core(ref, k, start):
-        residual = ref[rows + models :, :rows] - predicted[:, start : start + rows]
-        return residual, k, ref.at[:rows]
-
-    mine = core(mine_ref, kw_ref, 0)
+    first, second = predicted[:, :rows], predicted[:, rows : 2 * rows]
+    is_first = lax.rem(lax.axis_index("dp"), 2) == 0
+
+    def core(ref, k, predicted):
+        return ref[rows + models :, :rows] - predicted, k, ref.at[:rows]
+
+    mine = core(mine_ref, kw_ref, jnp.where(is_first, first, second))
     residual_ref[...] = mine[0]
-    back_projected(mine, core(other_ref, kw_other_ref, rows), g_ref)
+    back_projected(mine, core(other_ref, kw_other_ref, jnp.where(is_first, second, first)), g_ref)
 
 
 def sixth_kernel(layers, base, wave_ref, cut_ref, *refs):
@@ -300,13 +305,28 @@
     return lax.ppermute(x, axis, [(i, i ^ distance) for i in range(lax.axis_size(axis))])
 
 
-def shares_of(x, axis, lowest):
-    size = lax.axis_size(axis) // lowest
+def from_other_core(x, chips, vox):
+    n_vox = lax.axis_size("vox")
+    places = [(d, z) for d in range(lax.axis_size("dp")) for z in range(n_vox)]
+    route = [(d * n_vox + z, (d ^ (2 * chips + 1)) * n_vox + (z ^ vox)) for d, z in places]
+    return lax.ppermute(x, ("dp", "vox"), route)
+
+
+def shares_of(x, size, fetch):
+    lowest = 1
     while size > 4:
-        parts = [x] + [from_partner(x, axis, lowest * d) for d in range(1, 4)]
+        parts = [x] + [fetch(x, lowest * d) for d in range(1, 4)]
         x = tree_sum([p.astype(F32) for p in parts]).astype(x.dtype)
         lowest, size = lowest * 4, size // 4
-    return [x] + [from_partner(x, axis, lowest * d) for d in range(1, size)]
+    return [x] + [fetch(x, lowest * d) for d in range(1, size)]
+
+
+def over_chips(x):
+    return shares_of(x, lax.axis_size("dp") // 2, lambda x, d: from_other_core(x, d, 0))
+
+
+def over_vox(x):
+    return shares_of(x, lax.axis_size("vox"), lambda x, d: from_other_core(x, 0, d))
 
 
 def call(kernel, out_shape, *args, scratch=(), space=pltpu.VMEM):
@@ -327,10 +347,11 @@
     assert width == 2 * layers * LANES and rows + KINDS * layers <= LANES and 2 * rows <= LANES
     packet_rows = rows + 2 * models
     g_shape = pltpu.VMEM((models, width + LANES), BF16)
+    k_shape = pltpu.VMEM((rows, width), BF16)
 
     packet, wavelets, k_mine = call(
         functools.partial(first_kernel, layers),
-        (pltpu.VMEM((packet_rows, LANES), BF16), pltpu.VMEM((models, width), F32), pltpu.VMEM((rows, width), BF16)),
+        (pltpu.VMEM((packet_rows, LANES), BF16), pltpu.VMEM((models, width), F32), k_shape),
         initial,
         kernels,
         scratch=[pltpu.VMEM((models, LANES), F32), pltpu.SemaphoreType.DMA((2,))],
@@ -341,8 +362,8 @@
     kw, kw_other, cut, cut_halo = call(
         functools.partial(preparing_kernel, layers, rows),
         (
-            pltpu.VMEM((rows, width), BF16),
-            pltpu.VMEM((rows, width), BF16),
+            k_shape,
+            k_shape,
             pltpu.VMEM((models, width), F32),
             pltpu.VMEM((models, LANES), F32),
         ),
@@ -368,7 +389,7 @@
         cut_halo,
         k_mine,
         k_other,
-        *shares_of(g, "dp", 2),
+        *over_chips(g),
     )
     g, residual = call(
         fifth_kernel,
@@ -377,14 +398,14 @@
         other,
         kw,
         kw_other,
-        *shares_of(predicted, "vox", 1),
+        *over_vox(predicted),
     )
     coefficients = call(
         functools.partial(sixth_kernel, layers, rows),
         jax.ShapeDtypeStruct((models, width), F32),
         wavelets,
         cut,
-        *shares_of(g, "dp", 2),
+        *over_chips(g),
     )
     return coefficients, residual
 

time: 35.5 us -> 34.5 us (0.972)
  starting transfers between devices: 17.4 us -> 16 us
    ppermute x14 -> x5, starting transfers between devices: 17.4 us -> 5.9 us  [from_partner(): lax.ppermute(x, axis, [(i, i ^ distance) for i in range(lax.axis_size(axi...]
    ppermute x0 -> x9, starting transfers between devices: none -> 10.1 us  [from_other_core(): return lax.ppermute(x, ('dp', 'vox'), route)]
    ppermute x0 -> x9, waiting for transfers between devices: none -> 8.2 us  [from_other_core(): return lax.ppermute(x, ('dp', 'vox'), route)]
    ppermute x14 -> x5, waiting for transfers between devices: 11.9 us -> 4.03 us  [from_partner(): lax.ppermute(x, axis, [(i, i ^ distance) for i in range(lax.axis_size(axi...]
where the time goes in v4:
time: 34.5 us; the launch traced here: 34.3 us
  starting transfers between devices  16 us (46%)
  waiting for transfers between devices  12.2 us (35%)
  Pallas kernels  4.31 us (12%)
  local copies, waits for them, and re-layouts  0.99 us (3%)
  between operations  0.7 us (2%)
    ppermute x9, starting transfers between devices, from_other_core(): return lax.ppermute(x, ('dp', 'vox'), route)  10.1 us
    ppermute x9, waiting for transfers between devices, from_other_core(): return lax.ppermute(x, ('dp', 'vox'), route)  8.2 us
    ppermute x5, starting transfers between devices, from_partner(): lax.ppermute(x, axis, [(i, i ^ distance) for i in range(lax.axis_size(axi...  5.9 us
    pallas_call x7, Pallas kernels, call(): pl.pallas_call(kernel, out_shape=out_shape, in_specs=[pl.BlockSpec(memory...  4.31 us
    ppermute x5, waiting for transfers between devices, from_partner(): lax.ppermute(x, axis, [(i, i ^ distance) for i in range(lax.axis_size(axi...  4.03 us
    unnamed x5, local copies, waits for them, and re-layouts  0.99 us
  transfers between devices with their start and end apart: 14, of which 10 were waited for; matrix products, arithmetic and copies ran while one was open for 2% of the time, Pallas kernels for 3%

profile of v4, /device:TPU:0, one launch (start us, length us, event | category | flops | bytes accessed | tf_op | source)
XLA Modules:
  0.0 34.3 jit_solution(10101076353283553472)
XLA Ops:
  0.6 0.0 copy-start.1
  0.6 1.3 %shard_map.59 = (bf16[64,128]{1,0:T(8,128)(2,1)S(1)}, f32[8,4096]{1,0:T(8,128)S(1)}, bf16[48,4096]{1,0:T(8,128)(2,1)S(1)}) custom-call(f32[8,4096]{1,0:T(8,128)} %wave_hbm.1, bf16[48,4096]{1,0:T(8,128)(2,1)} %k_hbm.1), custom_call_target="tpu_custom_call" | custom-call | tf_op jit(solution)/shard_map/pallas_call | solution.py:333
  2.0 0.5 %collective-permute-start = (bf16[48,4096]{1,0:T(8,128)(2,1)S(1)}, bf16[48,4096]{1,0:T(8,128)(2,1)S(1)}, u32[]{:S(2)}, u32[]{:S(2)}) collective-permute-start(bf16[48,4096]{1,0:T(8,128)(2,1)S(1)} %get-tuple-element.16.k_ref), channel_id=1, source_target_pairs={{0,4},{4,0},{8,12},{12,8},{16,20},{20,16},{24,28},{28,24},{1,5},{5... | collective-permute-start | bytes 1179656 | tf_op jit(solution)/shard_map/ppermute | solution.py:305
  2.5 4.7 %collective-permute-start.3 = (bf16[64,128]{1,0:T(8,128)(2,1)S(1)}, bf16[64,128]{1,0:T(8,128)(2,1)S(1)}, u32[]{:S(2)}, u32[]{:S(2)}) collective-permute-start(bf16[64,128]{1,0:T(8,128)(2,1)S(1)} %get-tuple-element.18.refs_1_), channel_id=1, source_target_pairs={{0,3},{1,2},{2,1},{3,0},{4,7},{5,6},{6,5},{7,4},{8,11},{9,10},{10,... | collective-permute-start | bytes 49160 | tf_op jit(solution)/shard_map/ppermute | solution.py:305
  7.2 0.0 collective-permute-start.2
  7.2 0.6 %collective-permute-start.1 = (bf16[64,128]{1,0:T(8,128)(2,1)S(1)}, bf16[64,128]{1,0:T(8,128)(2,1)S(1)}, u32[]{:S(2)}, u32[]{:S(2)}) collective-permute-start(bf16[64,128]{1,0:T(8,128)(2,1)S(1)} %get-tuple-element.18.refs_1_), channel_id=1, source_target_pairs={{0,1},{1,0},{2,3},{3,2},{4,5},{5,4},{6,7},{7,6},{8,9},{9,8},{10,11... | collective-permute-start | bytes 49160 | tf_op jit(solution)/shard_map/ppermute | solution.py:305
  7.8 1.1 %collective-permute-done.3.refs_4_ = bf16[64,128]{1,0:T(8,128)(2,1)S(1)} collective-permute-done((bf16[64,128]{1,0:T(8,128)(2,1)S(1)}, bf16[64,128]{1,0:T(8,128)(2,1)S(1)}, u32[]{:S(2)}, u32[]{:S(2)}) %collective-permute-start.3) | collective-permute-done | bytes 16416 | tf_op jit(solution)/shard_map/ppermute | solution.py:305
  8.9 2.9 %collective-permute-done.2.refs_3_ = bf16[64,128]{1,0:T(8,128)(2,1)S(1)} collective-permute-done((bf16[64,128]{1,0:T(8,128)(2,1)S(1)}, bf16[64,128]{1,0:T(8,128)(2,1)S(1)}, u32[]{:S(2)}, u32[]{:S(2)}) %collective-permute-start.2) | collective-permute-done | bytes 16416 | tf_op jit(solution)/shard_map/ppermute | solution.py:305
  11.8 0.0 collective-permute-done.1.refs_2_
  11.8 0.0 copy-done.1
  11.8 0.0 copy-start
  11.8 0.2 shard_map.61
  12.0 0.1 collective-permute-start.4
  12.1 0.0 collective-permute-done.k_other_ref
  12.1 0.4 %copy-done = f32[8,16,2]{1,2,0:T(2,128)S(1)} copy-done((f32[8,16,2]{1,2,0:T(2,128)S(1)}, f32[8,16,2]{1,2,0:T(2,128)}, u32[]{:S(2)}) %copy-start) | copy-done | bytes 1048
  12.5 0.8 %shard_map.60 = (bf16[48,4096]{1,0:T(8,128)(2,1)S(1)}, bf16[48,4096]{1,0:T(8,128)(2,1)S(1)}, f32[8,4096]{1,0:T(8,128)S(1)}, f32[8,128]{1,0:T(8,128)S(1)}) custom-call(bf16[48,4096]{1,0:T(8,128)(2,1)S(1)} %get-tuple-element.16.k_ref, bf16[48,4096]{1,0:T(8,128)(2,1)S(1)} %collective-permute-done.k_other_ref, f32[8,2,16]{2,1,0:T(2,128)S(1)} %bitcast.1), custom_call_target="tpu_custom_call" | custom-call | tf_op jit(solution)/shard_map/pallas_call | solution.py:333
  13.3 0.0 collective-permute-done.4.other_ref
  13.3 0.2 shard_map.62.refs_0_
  13.5 2.3 %collective-permute-start.7 = (bf16[8,4224]{1,0:T(8,128)(2,1)S(1)}, bf16[8,4224]{1,0:T(8,128)(2,1)S(1)}, u32[]{:S(2)}, u32[]{:S(2)}) collective-permute-start(bf16[8,4224]{1,0:T(8,128)(2,1)S(1)} %shard_map.62.refs_0_), channel_id=1, source_target_pairs={{0,28},{1,29},{2,30},{3,31},{4,24},{5,25},{6,26},{7,27},{8,20},{9,... | collective-permute-start | bytes 202760 | tf_op jit(solution)/shard_map/ppermute | solution.py:312
  15.8 0.5 %collective-permute-start.6 = (bf16[8,4224]{1,0:T(8,128)(2,1)S(1)}, bf16[8,4224]{1,0:T(8,128)(2,1)S(1)}, u32[]{:S(2)}, u32[]{:S(2)}) collective-permute-start(bf16[8,4224]{1,0:T(8,128)(2,1)S(1)} %shard_map.62.refs_0_), channel_id=1, source_target_pairs={{0,20},{1,21},{2,22},{3,23},{4,16},{5,17},{6,18},{7,19},{8,28},{9,... | collective-permute-start | bytes 202760 | tf_op jit(solution)/shard_map/ppermute | solution.py:312
  16.3 0.3 collective-permute-start.5
  16.6 2.0 %collective-permute-done.7.refs_3_ = bf16[8,4224]{1,0:T(8,128)(2,1)S(1)} collective-permute-done((bf16[8,4224]{1,0:T(8,128)(2,1)S(1)}, bf16[8,4224]{1,0:T(8,128)(2,1)S(1)}, u32[]{:S(2)}, u32[]{:S(2)}) %collective-permute-start.7) | collective-permute-done | bytes 67616 | tf_op jit(solution)/shard_map/ppermute | solution.py:312
  18.6 1.5 %collective-permute-done.6.refs_2_ = bf16[8,4224]{1,0:T(8,128)(2,1)S(1)} collective-permute-done((bf16[8,4224]{1,0:T(8,128)(2,1)S(1)}, bf16[8,4224]{1,0:T(8,128)(2,1)S(1)}, u32[]{:S(2)}, u32[]{:S(2)}) %collective-permute-start.6) | collective-permute-done | bytes 67616 | tf_op jit(solution)/shard_map/ppermute | solution.py:312
  20.1 0.3 collective-permute-done.5.refs_1_
  20.4 0.6 %shard_map.63 = (f32[8,4096]{1,0:T(8,128)S(1)}, f32[8,128]{1,0:T(8,128)S(1)}) custom-call(f32[8,4096]{1,0:T(8,128)S(1)} %get-tuple-element.15.wave_ref, f32[8,4096]{1,0:T(8,128)S(1)} %get-tuple-element.17.cut_ref, f32[8,128]{1,0:T(8,128)S(1)} %get-tuple-element.19.halo_ref, f32[8,128]{1,0:T(8,128)S(1)} %get-tuple-element.20.cut_halo_ref, ...), custom_call_target="tpu_custom_call" | custom-call | tf_op jit(solution)/shard_map/pallas_call | solution.py:333
  21.0 1.2 %collective-permute-start.10 = (f32[8,128]{1,0:T(8,128)S(1)}, f32[8,128]{1,0:T(8,128)S(1)}, u32[]{:S(2)}, u32[]{:S(2)}) collective-permute-start(f32[8,128]{1,0:T(8,128)S(1)} %get-tuple-element.25.refs_0_), channel_id=1, source_target_pairs={{0,7},{1,6},{2,5},{3,4},{4,3},{5,2},{6,1},{7,0},{8,15},{9,14},{10,... | collective-permute-start | bytes 12296 | tf_op jit(solution)/shard_map/ppermute | solution.py:312
  22.3 0.6 %collective-permute-start.9 = (f32[8,128]{1,0:T(8,128)S(1)}, f32[8,128]{1,0:T(8,128)S(1)}, u32[]{:S(2)}, u32[]{:S(2)}) collective-permute-start(f32[8,128]{1,0:T(8,128)S(1)} %get-tuple-element.25.refs_0_), channel_id=1, source_target_pairs={{0,6},{1,7},{2,4},{3,5},{4,2},{5,3},{6,0},{7,1},{8,14},{9,15},{10,... | collective-permute-start | bytes 12296 | tf_op jit(solution)/shard_map/ppermute | solution.py:312
  22.8 2.1 %collective-permute-start.8 = (f32[8,128]{1,0:T(8,128)S(1)}, f32[8,128]{1,0:T(8,128)S(1)}, u32[]{:S(2)}, u32[]{:S(2)}) collective-permute-start(f32[8,128]{1,0:T(8,128)S(1)} %get-tuple-element.25.refs_0_), channel_id=1, source_target_pairs={{0,5},{1,4},{2,7},{3,6},{4,1},{5,0},{6,3},{7,2},{8,13},{9,12},{10,... | collective-permute-start | bytes 12296 | tf_op jit(solution)/shard_map/ppermute | solution.py:312
  24.9 1.0 %collective-permute-done.10.refs_3_ = f32[8,128]{1,0:T(8,128)S(1)} collective-permute-done((f32[8,128]{1,0:T(8,128)S(1)}, f32[8,128]{1,0:T(8,128)S(1)}, u32[]{:S(2)}, u32[]{:S(2)}) %collective-permute-start.10) | collective-permute-done | bytes 4128 | tf_op jit(solution)/shard_map/ppermute | solution.py:312
  25.9 0.3 collective-permute-done.9.refs_2_
  26.2 0.1 collective-permute-done.8.refs_1_
  26.3 0.4 %shard_map.64 = (bf16[8,4224]{1,0:T(8,128)(2,1)S(1)}, f32[8,48]{1,0:T(8,128)S(1)}) custom-call(f32[64,128]{1,0:T(8,128)S(1)} %get-tuple-element.21.mine_ref, f32[64,128]{1,0:T(8,128)S(1)} %collective-permute-done.4.other_ref, bf16[48,4096]{1,0:T(8,128)(2,1)S(1)} %get-tuple-element.22.kw_ref, bf16[48,4096]{1,0:T(8,128)(2,1)S(1)} %get-tuple-element.23.kw_other_ref, ...), custom_call_target="tpu_custom_call" | custom-call | tf_op jit(solution)/shard_map/pallas_call | solution.py:333
  26.7 1.5 %collective-permute-start.13 = (bf16[8,4224]{1,0:T(8,128)(2,1)S(1)}, bf16[8,4224]{1,0:T(8,128)(2,1)S(1)}, u32[]{:S(2)}, u32[]{:S(2)}) collective-permute-start(bf16[8,4224]{1,0:T(8,128)(2,1)S(1)} %get-tuple-element.26.refs_0_), channel_id=1, source_target_pairs={{0,28},{1,29},{2,30},{3,31},{4,24},{5,25},{6,26},{7,27},{8,20},{9,... | collective-permute-start | bytes 202760 | tf_op jit(solution)/shard_map/ppermute | solution.py:312
  28.1 1.2 %collective-permute-start.12 = (bf16[8,4224]{1,0:T(8,128)(2,1)S(1)}, bf16[8,4224]{1,0:T(8,128)(2,1)S(1)}, u32[]{:S(2)}, u32[]{:S(2)}) collective-permute-start(bf16[8,4224]{1,0:T(8,128)(2,1)S(1)} %get-tuple-element.26.refs_0_), channel_id=1, source_target_pairs={{0,20},{1,21},{2,22},{3,23},{4,16},{5,17},{6,18},{7,19},{8,28},{9,... | collective-permute-start | bytes 202760 | tf_op jit(solution)/shard_map/ppermute | solution.py:312
  29.3 0.5 %collective-permute-start.11 = (bf16[8,4224]{1,0:T(8,128)(2,1)S(1)}, bf16[8,4224]{1,0:T(8,128)(2,1)S(1)}, u32[]{:S(2)}, u32[]{:S(2)}) collective-permute-start(bf16[8,4224]{1,0:T(8,128)(2,1)S(1)} %get-tuple-element.26.refs_0_), channel_id=1, source_target_pairs={{0,12},{1,13},{2,14},{3,15},{4,8},{5,9},{6,10},{7,11},{8,4},{9,5},... | collective-permute-start | bytes 202760 | tf_op jit(solution)/shard_map/ppermute | solution.py:312
  29.8 0.6 %copy.6 = f32[8,48]{1,0:T(8,128)} copy(f32[8,48]{1,0:T(8,128)S(1)} %get-tuple-element.29) | data formatting | bytes 3072
  30.4 1.3 %collective-permute-done.13.refs_3_ = bf16[8,4224]{1,0:T(8,128)(2,1)S(1)} collective-permute-done((bf16[8,4224]{1,0:T(8,128)(2,1)S(1)}, bf16[8,4224]{1,0:T(8,128)(2,1)S(1)}, u32[]{:S(2)}, u32[]{:S(2)}) %collective-permute-start.13) | collective-permute-done | bytes 67616 | tf_op jit(solution)/shard_map/ppermute | solution.py:312
  31.7 1.8 %collective-permute-done.12.refs_2_ = bf16[8,4224]{1,0:T(8,128)(2,1)S(1)} collective-permute-done((bf16[8,4224]{1,0:T(8,128)(2,1)S(1)}, bf16[8,4224]{1,0:T(8,128)(2,1)S(1)}, u32[]{:S(2)}, u32[]{:S(2)}) %collective-permute-start.12) | collective-permute-done | bytes 67616 | tf_op jit(solution)/shard_map/ppermute | solution.py:312
  33.5 0.0 collective-permute-done.11.refs_1_
  33.5 0.8 %shard_map.65 = f32[8,4096]{1,0:T(8,128)} custom-call(f32[8,4096]{1,0:T(8,128)S(1)} %get-tuple-element.24.wave_ref, f32[8,4096]{1,0:T(8,128)S(1)} %get-tuple-element.17.cut_ref, bf16[8,4224]{1,0:T(8,128)(2,1)S(1)} %get-tuple-element.26.refs_0_, bf16[8,4224]{1,0:T(8,128)(2,1)S(1)} %collective-permute-done.11.refs_1_, ...), custom_call_target="tpu_custom_call" | custom-call | tf_op jit(solution)/shard_map/pallas_call | solution.py:333
Async XLA Ops:
  0.6 11.2 %copy-start.1 = (f32[8,48]{1,0:T(8,128)S(1)}, f32[8,48]{1,0:T(8,128)}, u32[]{:S(2)}) copy-start(f32[8,48]{1,0:T(8,128)} %refs_0_.1) | copy-start | bytes 4612
  2.0 10.1 %collective-permute-start = (bf16[48,4096]{1,0:T(8,128)(2,1)S(1)}, bf16[48,4096]{1,0:T(8,128)(2,1)S(1)}, u32[]{:S(2)}, u32[]{:S(2)}) collective-permute-start(bf16[48,4096]{1,0:T(8,128)(2,1)S(1)} %get-tuple-element.16.k_ref), channel_id=1, source_target_pairs={{0,4},{4,0},{8,12},{12,8},{16,20},{20,16},{24,28},{28,24},{1,5},{5... | collective-permute-start | bytes 1179656 | tf_op jit(solution)/shard_map/ppermute | solution.py:305
  2.5 6.4 %collective-permute-start.3 = (bf16[64,128]{1,0:T(8,128)(2,1)S(1)}, bf16[64,128]{1,0:T(8,128)(2,1)S(1)}, u32[]{:S(2)}, u32[]{:S(2)}) collective-permute-start(bf16[64,128]{1,0:T(8,128)(2,1)S(1)} %get-tuple-element.18.refs_1_), channel_id=1, source_target_pairs={{0,3},{1,2},{2,1},{3,0},{4,7},{5,6},{6,5},{7,4},{8,11},{9,10},{10,... | collective-permute-start | bytes 49160 | tf_op jit(solution)/shard_map/ppermute | solution.py:305
  7.2 4.6 %collective-permute-start.2 = (bf16[64,128]{1,0:T(8,128)(2,1)S(1)}, bf16[64,128]{1,0:T(8,128)(2,1)S(1)}, u32[]{:S(2)}, u32[]{:S(2)}) collective-permute-start(bf16[64,128]{1,0:T(8,128)(2,1)S(1)} %get-tuple-element.18.refs_1_), channel_id=1, source_target_pairs={{0,2},{1,3},{2,0},{3,1},{4,6},{5,7},{6,4},{7,5},{8,10},{9,11},{10,... | collective-permute-start | bytes 49160 | tf_op jit(solution)/shard_map/ppermute | solution.py:305
  7.2 4.6 %collective-permute-start.1 = (bf16[64,128]{1,0:T(8,128)(2,1)S(1)}, bf16[64,128]{1,0:T(8,128)(2,1)S(1)}, u32[]{:S(2)}, u32[]{:S(2)}) collective-permute-start(bf16[64,128]{1,0:T(8,128)(2,1)S(1)} %get-tuple-element.18.refs_1_), channel_id=1, source_target_pairs={{0,1},{1,0},{2,3},{3,2},{4,5},{5,4},{6,7},{7,6},{8,9},{9,8},{10,11... | collective-permute-start | bytes 49160 | tf_op jit(solution)/shard_map/ppermute | solution.py:305
  11.8 0.7 %copy-start = (f32[8,16,2]{1,2,0:T(2,128)S(1)}, f32[8,16,2]{1,2,0:T(2,128)}, u32[]{:S(2)}) copy-start(f32[8,16,2]{1,2,0:T(2,128)} %param.7) | copy-start | bytes 3076
  12.0 1.3 %collective-permute-start.4 = (f32[64,128]{1,0:T(8,128)S(1)}, f32[64,128]{1,0:T(8,128)S(1)}, u32[]{:S(2)}, u32[]{:S(2)}) collective-permute-start(f32[64,128]{1,0:T(8,128)S(1)} %get-tuple-element.21.mine_ref), channel_id=1, source_target_pairs={{0,4},{4,0},{8,12},{12,8},{16,20},{20,16},{24,28},{28,24},{1,5},{5... | collective-permute-start | bytes 98312 | tf_op jit(solution)/shard_map/ppermute | solution.py:305
  13.5 5.1 %collective-permute-start.7 = (bf16[8,4224]{1,0:T(8,128)(2,1)S(1)}, bf16[8,4224]{1,0:T(8,128)(2,1)S(1)}, u32[]{:S(2)}, u32[]{:S(2)}) collective-permute-start(bf16[8,4224]{1,0:T(8,128)(2,1)S(1)} %shard_map.62.refs_0_), channel_id=1, source_target_pairs={{0,28},{1,29},{2,30},{3,31},{4,24},{5,25},{6,26},{7,27},{8,20},{9,... | collective-permute-start | bytes 202760 | tf_op jit(solution)/shard_map/ppermute | solution.py:312
  15.8 4.2 %collective-permute-start.6 = (bf16[8,4224]{1,0:T(8,128)(2,1)S(1)}, bf16[8,4224]{1,0:T(8,128)(2,1)S(1)}, u32[]{:S(2)}, u32[]{:S(2)}) collective-permute-start(bf16[8,4224]{1,0:T(8,128)(2,1)S(1)} %shard_map.62.refs_0_), channel_id=1, source_target_pairs={{0,20},{1,21},{2,22},{3,23},{4,16},{5,17},{6,18},{7,19},{8,28},{9,... | collective-permute-start | bytes 202760 | tf_op jit(solution)/shard_map/ppermute | solution.py:312
  16.3 4.1 %collective-permute-start.5 = (bf16[8,4224]{1,0:T(8,128)(2,1)S(1)}, bf16[8,4224]{1,0:T(8,128)(2,1)S(1)}, u32[]{:S(2)}, u32[]{:S(2)}) collective-permute-start(bf16[8,4224]{1,0:T(8,128)(2,1)S(1)} %shard_map.62.refs_0_), channel_id=1, source_target_pairs={{0,12},{1,13},{2,14},{3,15},{4,8},{5,9},{6,10},{7,11},{8,4},{9,5},... | collective-permute-start | bytes 202760 | tf_op jit(solution)/shard_map/ppermute | solution.py:312
  21.0 4.8 %collective-permute-start.10 = (f32[8,128]{1,0:T(8,128)S(1)}, f32[8,128]{1,0:T(8,128)S(1)}, u32[]{:S(2)}, u32[]{:S(2)}) collective-permute-start(f32[8,128]{1,0:T(8,128)S(1)} %get-tuple-element.25.refs_0_), channel_id=1, source_target_pairs={{0,7},{1,6},{2,5},{3,4},{4,3},{5,2},{6,1},{7,0},{8,15},{9,14},{10,... | collective-permute-start | bytes 12296 | tf_op jit(solution)/shard_map/ppermute | solution.py:312
  22.3 3.9 %collective-permute-start.9 = (f32[8,128]{1,0:T(8,128)S(1)}, f32[8,128]{1,0:T(8,128)S(1)}, u32[]{:S(2)}, u32[]{:S(2)}) collective-permute-start(f32[8,128]{1,0:T(8,128)S(1)} %get-tuple-element.25.refs_0_), channel_id=1, source_target_pairs={{0,6},{1,7},{2,4},{3,5},{4,2},{5,3},{6,0},{7,1},{8,14},{9,15},{10,... | collective-permute-start | bytes 12296 | tf_op jit(solution)/shard_map/ppermute | solution.py:312
  22.8 3.5 %collective-permute-start.8 = (f32[8,128]{1,0:T(8,128)S(1)}, f32[8,128]{1,0:T(8,128)S(1)}, u32[]{:S(2)}, u32[]{:S(2)}) collective-permute-start(f32[8,128]{1,0:T(8,128)S(1)} %get-tuple-element.25.refs_0_), channel_id=1, source_target_pairs={{0,5},{1,4},{2,7},{3,6},{4,1},{5,0},{6,3},{7,2},{8,13},{9,12},{10,... | collective-permute-start | bytes 12296 | tf_op jit(solution)/shard_map/ppermute | solution.py:312
  26.7 5.0 %collective-permute-start.13 = (bf16[8,4224]{1,0:T(8,128)(2,1)S(1)}, bf16[8,4224]{1,0:T(8,128)(2,1)S(1)}, u32[]{:S(2)}, u32[]{:S(2)}) collective-permute-start(bf16[8,4224]{1,0:T(8,128)(2,1)S(1)} %get-tuple-element.26.refs_0_), channel_id=1, source_target_pairs={{0,28},{1,29},{2,30},{3,31},{4,24},{5,25},{6,26},{7,27},{8,20},{9,... | collective-permute-start | bytes 202760 | tf_op jit(solution)/shard_map/ppermute | solution.py:312
  28.1 5.3 %collective-permute-start.12 = (bf16[8,4224]{1,0:T(8,128)(2,1)S(1)}, bf16[8,4224]{1,0:T(8,128)(2,1)S(1)}, u32[]{:S(2)}, u32[]{:S(2)}) collective-permute-start(bf16[8,4224]{1,0:T(8,128)(2,1)S(1)} %get-tuple-element.26.refs_0_), channel_id=1, source_target_pairs={{0,20},{1,21},{2,22},{3,23},{4,16},{5,17},{6,18},{7,19},{8,28},{9,... | collective-permute-start | bytes 202760 | tf_op jit(solution)/shard_map/ppermute | solution.py:312
  29.3 4.1 %collective-permute-start.11 = (bf16[8,4224]{1,0:T(8,128)(2,1)S(1)}, bf16[8,4224]{1,0:T(8,128)(2,1)S(1)}, u32[]{:S(2)}, u32[]{:S(2)}) collective-permute-start(bf16[8,4224]{1,0:T(8,128)(2,1)S(1)} %get-tuple-element.26.refs_0_), channel_id=1, source_target_pairs={{0,12},{1,13},{2,14},{3,15},{4,8},{5,9},{6,10},{7,11},{8,4},{9,5},... | collective-permute-start | bytes 202760 | tf_op jit(solution)/shard_map/ppermute | solution.py:312

commit v5 on v4

--- a/solution.py
+++ b/solution.py
@@ -90,33 +90,51 @@
     return result
 
 
-def first_kernel(layers, wave_hbm, k_hbm, packet_ref, wave_ref, k_ref, tile, arrived):
+def pieces(x, count):
+    result = []
+    for _ in range(count):
+        result.append(x.astype(BF16).astype(F32))
+        x = x - result[-1]
+    return result
+
+
+def first_kernel(layers, wave_hbm, k_hbm, observed_hbm, packet_ref, wave_ref, block_ref, observed_ref, tile, arrived):
+    rows = k_hbm.shape[0]
+    models = wave_ref.shape[0]
     loads = [
-        pltpu.make_async_copy(wave_hbm, wave_ref, arrived.at[0]),
-        pltpu.make_async_copy(k_hbm, k_ref, arrived.at[1]),
+        pltpu.make_async_copy(source, target, arrived.at[i])
+        for i, (source, target) in enumerate(
+            ((wave_hbm, wave_ref), (k_hbm, block_ref.at[:rows]), (observed_hbm, observed_ref))
+        )
     ]
     for load in loads:
         load.start()
-    rows = k_ref.shape[0]
-    models = wave_ref.shape[0]
     loads[0].wait()
     even, odd = inverse_wave(*stacked(wave_ref, layers), 0.0)
     model = unstacked(even, odd, models).astype(BF16)
     tile[...] = edge_tile(lambda l: layer_tiles(wave_ref, l), layers, rows)
     loads[1].wait()
-    edges = edge_tile(lambda l: tuple(t.astype(F32) for t in layer_tiles(k_ref, l)), layers, rows)
+    loads[2].wait()
+    edges = edge_tile(lambda l: tuple(t[:rows].astype(F32) for t in layer_tiles(block_ref, l)), layers, rows)
     packet_ref[:rows, :] = edges.astype(BF16)
-    tile[:, :rows] = nt_dot(model, k_ref[...])
-    whole = tile[...]
-    high = whole.astype(BF16).astype(F32)
-    packet_ref[rows:, :] = jnp.concatenate([high, whole - high], axis=0).astype(BF16)
-
-
-def preparing_kernel(layers, base, k_ref, k_other_ref, threshold_ref, kw_ref, kw_other_ref, cut_ref, cut_halo_ref):
-    rows = k_ref.shape[0]
-    models, width = cut_ref.shape
-    for source, target in ((k_ref, kw_ref), (k_other_ref, kw_other_ref)):
-        target[...] = unstacked(*forward_wave(*stacked(source, layers)), rows).astype(BF16)
+    tile[:, :rows] = nt_dot(model, block_ref[:rows, :])
+    packet_ref[rows:, :] = jnp.concatenate(pieces(tile[...], 2), axis=0).astype(BF16)
+    tile[...] = jnp.zeros_like(tile)
+    tile[:, :rows] = observed_ref[...]
+    below = pieces(tile[...], 3) + [jnp.zeros_like(tile)]
+    below = [jnp.concatenate(below[i : i + 2], axis=0).astype(BF16) for i in (0, 2)]
+    packed = [packet_ref[i : i + 2 * models, :] for i in range(0, packet_ref.shape[0], 2 * models)] + below
+    for i, part in enumerate(packed):
+        block_ref[rows:, i * LANES : (i + 1) * LANES] = part
+
+
+def applied_kernel(layers, block_ref, kw_ref):
+    rows = kw_ref.shape[0]
+    kw_ref[...] = unstacked(*forward_wave(*stacked(block_ref.at[:rows], layers)), rows).astype(BF16)
+
+
+def spread_kernel(layers, base, threshold_ref, cut_ref, cut_halo_ref):
+    models = cut_ref.shape[0]
     lane = lanes_of((models, LANES))
     halo = jnp.zeros((models, LANES), F32)
     for layer in range(layers):
@@ -132,12 +150,18 @@
     cut_halo_ref[...] = halo
 
 
-def second_kernel(layers, n_vox, *refs):
-    (observed_ref, *packets, out_ref, halo_ref, held) = refs
-    models, rows = observed_ref.shape
+def second_kernel(layers, n_vox, models, *refs):
+    (block_ref, *packets, out_ref, halo_ref, held) = refs
+    rows = held.shape[1] - 2 * models
     me = lax.axis_index("vox")
-    for distance, packet in enumerate(packets):
+    for distance, packet in enumerate(packets, 1):
         held[me ^ distance] = packet[...]
+    chunks = held.shape[1] // (2 * models)
+    below = [block_ref[rows:, i * LANES : (i + 1) * LANES] for i in range(chunks + 2)]
+    for i in range(chunks):
+        held[me, i * 2 * models : (i + 1) * 2 * models] = below[i]
+    high, low = below[chunks].astype(F32), below[chunks + 1].astype(F32)
+    observed = ((high[:models] + high[models:]) + low[:models])[:, :rows]
     left, right = lax.rem(me + n_vox - 1, n_vox), lax.rem(me + 1, n_vox)
     lane = lanes_of((models, LANES))
     inside = (lane >= rows) & (lane < rows + KINDS * layers)
@@ -190,8 +214,8 @@
         details,
     )
     out_ref[rows:, :] = jnp.zeros((2 * models, LANES), F32)
-    out_ref[rows : rows + models, :rows] = observed_ref[...] - predicted
-    out_ref[rows + models :, :rows] = observed_ref[...]
+    out_ref[rows : rows + models, :rows] = observed - predicted
+    out_ref[rows + models :, :rows] = observed
     before, own, after = (edge_values(z) for z in (left, me, right))
     halo_ref[...] = by_kind(
         lane, rows, 0.0, turned(before, D_BEFORE - O_LAST), turned(after, S_NEXT - E_FIRST), own, after
@@ -261,10 +285,10 @@
     return smooth, detail, edge
 
 
-def fourth_kernel(layers, base, wave_ref, cut_ref, halo_ref, cut_halo_ref, k_ref, k_other_ref, *refs):
+def fourth_kernel(layers, base, wave_ref, cut_ref, halo_ref, cut_halo_ref, block_ref, block_other_ref, *refs):
     *g_refs, new_ref, pred_ref = refs
     models = wave_ref.shape[0]
-    rows = k_ref.shape[0]
+    rows = base
     smooth, detail, edge = stepped(layers, base, wave_ref, cut_ref, g_refs)
     new_ref[...] = unstacked(smooth, detail, models)
     halo = shrink(halo_ref[...] + step_size * edge, cut_halo_ref[...])
@@ -274,10 +298,10 @@
     pred_ref[...] = jnp.zeros_like(pred_ref)
 
     def work(first, second):
-        pred_ref[:, :rows] = nt_dot(model, first[...])
-        pred_ref[:, rows : 2 * rows] = nt_dot(model, second[...])
-
-    in_core_order(k_ref, k_other_ref, work)
+        pred_ref[:, :rows] = nt_dot(model, first[:rows, :])
+        pred_ref[:, rows : 2 * rows] = nt_dot(model, second[:rows, :])
+
+    in_core_order(block_ref, block_other_ref, work)
 
 
 def fifth_kernel(mine_ref, other_ref, kw_ref, kw_other_ref, *refs):
@@ -344,41 +368,45 @@
     rows = kernels.shape[0]
     layers = threshold.shape[1]
     n_vox = lax.axis_size("vox")
+    packet_rows = rows + 2 * models
     assert width == 2 * layers * LANES and rows + KINDS * layers <= LANES and 2 * rows <= LANES
-    packet_rows = rows + 2 * models
+    assert packet_rows % (2 * models) == 0 and packet_rows // (2 * models) + 2 <= 2 * layers
     g_shape = pltpu.VMEM((models, width + LANES), BF16)
     k_shape = pltpu.VMEM((rows, width), BF16)
 
-    packet, wavelets, k_mine = call(
+    packet, wavelets, block = call(
         functools.partial(first_kernel, layers),
-        (pltpu.VMEM((packet_rows, LANES), BF16), pltpu.VMEM((models, width), F32), k_shape),
+        (
+            pltpu.VMEM((packet_rows, LANES), BF16),
+            pltpu.VMEM((models, width), F32),
+            pltpu.VMEM((rows + 2 * models, width), BF16),
+        ),
         initial,
         kernels,
-        scratch=[pltpu.VMEM((models, LANES), F32), pltpu.SemaphoreType.DMA((2,))],
+        observed,
+        scratch=[
+            pltpu.VMEM((models, rows), F32),
+            pltpu.VMEM((models, LANES), F32),
+            pltpu.SemaphoreType.DMA((3,)),
+        ],
         space=pltpu.HBM,
     )
-    packets = [packet] + [from_partner(packet, "vox", d) for d in range(1, n_vox)]
-    k_other = from_partner(k_mine, "dp", 1)
-    kw, kw_other, cut, cut_halo = call(
-        functools.partial(preparing_kernel, layers, rows),
-        (
-            k_shape,
-            k_shape,
-            pltpu.VMEM((models, width), F32),
-            pltpu.VMEM((models, LANES), F32),
-        ),
-        k_mine,
-        k_other,
+    block_other = from_partner(block, "dp", 1)
+    packets = [from_other_core(packet, 0, d) for d in range(1, n_vox)]
+    kw, kw_other = (call(functools.partial(applied_kernel, layers), k_shape, b) for b in (block, block_other))
+    cut, cut_halo = call(
+        functools.partial(spread_kernel, layers, rows),
+        (pltpu.VMEM((models, width), F32), pltpu.VMEM((models, LANES), F32)),
         jnp.swapaxes(threshold, 1, 2),
     )
-    mine, halo = call(
-        functools.partial(second_kernel, layers, n_vox),
+    other, halo = call(
+        functools.partial(second_kernel, layers, n_vox, models),
         (pltpu.VMEM((packet_rows, LANES), F32), pltpu.VMEM((models, LANES), F32)),
-        observed,
+        block_other,
         *packets,
         scratch=[pltpu.VMEM((n_vox, packet_rows, LANES), BF16)],
     )
-    other = from_partner(mine, "dp", 1)
+    mine = from_partner(other, "dp", 1)
     g = call(third_kernel, g_shape, mine, other, kw, kw_other)
     wavelets, predicted = call(
         functools.partial(fourth_kernel, layers, rows),
@@ -387,8 +415,8 @@
         cut,
         halo,
         cut_halo,
-        k_mine,
-        k_other,
+        block,
+        block_other,
         *over_chips(g),
     )
     g, residual = call(

time: 34.5 us -> 35.2 us (1.020)
  local copies, waits for them, and re-layouts: 0.99 us -> 1.64 us
    ppermute x5 -> x2, starting transfers between devices: 5.9 us -> 0.69 us  [from_partner(): lax.ppermute(x, axis, [(i, i ^ distance) for i in range(lax.axis_size(axi...]
    ppermute x9 -> x12, starting transfers between devices: 10.1 us -> 15.2 us  [from_other_core(): return lax.ppermute(x, ('dp', 'vox'), route)]
    ppermute x9 -> x12, waiting for transfers between devices: 8.2 us -> 11.8 us  [from_other_core(): return lax.ppermute(x, ('dp', 'vox'), route)]
    ppermute x5 -> x2, waiting for transfers between devices: 4.03 us -> 0.55 us  [from_partner(): lax.ppermute(x, axis, [(i, i ^ distance) for i in range(lax.axis_size(axi...]
    unnamed x5 -> x7, local copies, waits for them, and re-layouts: 0.99 us -> 1.64 us
    pallas_call x7 -> x9, Pallas kernels: 4.31 us -> 4.46 us  [call(): pl.pallas_call(kernel, out_shape=out_shape, in_specs=[pl.BlockSpec(memory...]
  transfers between devices with their start and end apart: 14 -> 14, of which waited for: 10 -> 10; matrix products, arithmetic and copies ran while one was open for 2% -> 2% of each run, Pallas kernels for 3% -> 2%
where the time goes in v5:
time: 35.2 us; the launch traced here: 35 us
  starting transfers between devices  15.9 us (45%)
  waiting for transfers between devices  12.3 us (35%)
  Pallas kernels  4.46 us (13%)
  local copies, waits for them, and re-layouts  1.64 us (5%)
  between operations  0.71 us (2%)
    ppermute x12, starting transfers between devices, from_other_core(): return lax.ppermute(x, ('dp', 'vox'), route)  15.2 us
    ppermute x12, waiting for transfers between devices, from_other_core(): return lax.ppermute(x, ('dp', 'vox'), route)  11.8 us
    pallas_call x9, Pallas kernels, call(): pl.pallas_call(kernel, out_shape=out_shape, in_specs=[pl.BlockSpec(memory...  4.46 us
    unnamed x7, local copies, waits for them, and re-layouts  1.64 us
  transfers between devices with their start and end apart: 14, of which 10 were waited for; matrix products, arithmetic and copies ran while one was open for 2% of the time, Pallas kernels for 2%

profile of v5, /device:TPU:0, one launch (start us, length us, event | category | flops | bytes accessed | tf_op | source)
XLA Modules:
  0.0 35.0 jit_solution(6379790401734170900)
XLA Ops:
  0.6 1.3 %shard_map.59 = (bf16[64,128]{1,0:T(8,128)(2,1)S(1)}, f32[8,4096]{1,0:T(8,128)S(1)}, bf16[64,4096]{1,0:T(8,128)(2,1)S(1)}) custom-call(f32[8,4096]{1,0:T(8,128)} %wave_hbm.1, bf16[48,4096]{1,0:T(8,128)(2,1)} %k_hbm.1, f32[8,48]{1,0:T(8,128)} %observed_hbm.1), custom_call_target="tpu_custom_call" | custom-call | tf_op jit(solution)/shard_map/pallas_call | solution.py:357
  2.0 0.0 copy-start
  2.0 0.5 %collective-permute-start = (bf16[64,4096]{1,0:T(8,128)(2,1)S(1)}, bf16[64,4096]{1,0:T(8,128)(2,1)S(1)}, u32[]{:S(2)}, u32[]{:S(2)}) collective-permute-start(bf16[64,4096]{1,0:T(8,128)(2,1)S(1)} %get-tuple-element.15.block_ref), channel_id=1, source_target_pairs={{0,4},{4,0},{8,12},{12,8},{16,20},{20,16},{24,28},{28,24},{1,5},{5... | collective-permute-start | bytes 1572872 | tf_op jit(solution)/shard_map/ppermute | solution.py:329
  2.5 4.7 %collective-permute-start.3 = (bf16[64,128]{1,0:T(8,128)(2,1)S(1)}, bf16[64,128]{1,0:T(8,128)(2,1)S(1)}, u32[]{:S(2)}, u32[]{:S(2)}) collective-permute-start(bf16[64,128]{1,0:T(8,128)(2,1)S(1)} %get-tuple-element.16), channel_id=1, source_target_pairs={{0,7},{1,6},{2,5},{3,4},{4,3},{5,2},{6,1},{7,0},{8,15},{9,14},{10,... | collective-permute-start | bytes 49160 | tf_op jit(solution)/shard_map/ppermute | solution.py:336
  7.2 0.0 collective-permute-start.2
  7.2 0.3 collective-permute-start.1
  7.5 1.1 %collective-permute-done.3.refs_3_ = bf16[64,128]{1,0:T(8,128)(2,1)S(1)} collective-permute-done((bf16[64,128]{1,0:T(8,128)(2,1)S(1)}, bf16[64,128]{1,0:T(8,128)(2,1)S(1)}, u32[]{:S(2)}, u32[]{:S(2)}) %collective-permute-start.3) | collective-permute-done | bytes 16416 | tf_op jit(solution)/shard_map/ppermute | solution.py:336
  8.7 2.6 %collective-permute-done.2.refs_2_ = bf16[64,128]{1,0:T(8,128)(2,1)S(1)} collective-permute-done((bf16[64,128]{1,0:T(8,128)(2,1)S(1)}, bf16[64,128]{1,0:T(8,128)(2,1)S(1)}, u32[]{:S(2)}, u32[]{:S(2)}) %collective-permute-start.2) | collective-permute-done | bytes 16416 | tf_op jit(solution)/shard_map/ppermute | solution.py:336
  11.3 0.0 collective-permute-done.1.refs_1_
  11.3 0.0 collective-permute-done.refs_0_.block_ref.block_other_ref
  11.3 0.2 shard_map.61
  11.5 0.2 collective-permute-start.4
  11.7 0.3 shard_map.62.kw_ref
  12.0 0.0 copy-done
  12.0 0.3 shard_map.63.kw_other_ref
  12.2 0.0 copy-start.2
  12.2 0.6 %collective-permute-done.4.mine_ref = f32[64,128]{1,0:T(8,128)S(1)} collective-permute-done((f32[64,128]{1,0:T(8,128)S(1)}, f32[64,128]{1,0:T(8,128)S(1)}, u32[]{:S(2)}, u32[]{:S(2)}) %collective-permute-start.4) | collective-permute-done | bytes 32800 | tf_op jit(solution)/shard_map/ppermute | solution.py:329
  12.8 0.2 shard_map.64.refs_0_
  13.0 2.3 %collective-permute-start.7 = (bf16[8,4224]{1,0:T(8,128)(2,1)S(1)}, bf16[8,4224]{1,0:T(8,128)(2,1)S(1)}, u32[]{:S(2)}, u32[]{:S(2)}) collective-permute-start(bf16[8,4224]{1,0:T(8,128)(2,1)S(1)} %shard_map.64.refs_0_), channel_id=1, source_target_pairs={{0,28},{1,29},{2,30},{3,31},{4,24},{5,25},{6,26},{7,27},{8,20},{9,... | collective-permute-start | bytes 202760 | tf_op jit(solution)/shard_map/ppermute | solution.py:336
  15.3 0.5 %collective-permute-start.6 = (bf16[8,4224]{1,0:T(8,128)(2,1)S(1)}, bf16[8,4224]{1,0:T(8,128)(2,1)S(1)}, u32[]{:S(2)}, u32[]{:S(2)}) collective-permute-start(bf16[8,4224]{1,0:T(8,128)(2,1)S(1)} %shard_map.64.refs_0_), channel_id=1, source_target_pairs={{0,20},{1,21},{2,22},{3,23},{4,16},{5,17},{6,18},{7,19},{8,28},{9,... | collective-permute-start | bytes 202760 | tf_op jit(solution)/shard_map/ppermute | solution.py:336
  15.8 0.3 collective-permute-start.5
  16.1 0.0 copy-done.2
  16.1 0.4 %shard_map.60 = (f32[8,4096]{1,0:T(8,128)S(1)}, f32[8,128]{1,0:T(8,128)S(1)}) custom-call(f32[8,2,16]{2,1,0:T(2,128)S(1)} %bitcast.1), custom_call_target="tpu_custom_call" | custom-call | tf_op jit(solution)/shard_map/pallas_call | solution.py:357
  16.4 1.7 %collective-permute-done.7.refs_3_ = bf16[8,4224]{1,0:T(8,128)(2,1)S(1)} collective-permute-done((bf16[8,4224]{1,0:T(8,128)(2,1)S(1)}, bf16[8,4224]{1,0:T(8,128)(2,1)S(1)}, u32[]{:S(2)}, u32[]{:S(2)}) %collective-permute-start.7) | collective-permute-done | bytes 67616 | tf_op jit(solution)/shard_map/ppermute | solution.py:336
  18.1 1.5 %collective-permute-done.6.refs_2_ = bf16[8,4224]{1,0:T(8,128)(2,1)S(1)} collective-permute-done((bf16[8,4224]{1,0:T(8,128)(2,1)S(1)}, bf16[8,4224]{1,0:T(8,128)(2,1)S(1)}, u32[]{:S(2)}, u32[]{:S(2)}) %collective-permute-start.6) | collective-permute-done | bytes 67616 | tf_op jit(solution)/shard_map/ppermute | solution.py:336
  19.6 0.4 %collective-permute-done.5.refs_1_ = bf16[8,4224]{1,0:T(8,128)(2,1)S(1)} collective-permute-done((bf16[8,4224]{1,0:T(8,128)(2,1)S(1)}, bf16[8,4224]{1,0:T(8,128)(2,1)S(1)}, u32[]{:S(2)}, u32[]{:S(2)}) %collective-permute-start.5) | collective-permute-done | bytes 67616 | tf_op jit(solution)/shard_map/ppermute | solution.py:336
  20.0 0.0 copy-start.1
  20.0 1.0 %copy-done.1 = bf16[64,4096]{1,0:T(8,128)(2,1)S(1)} copy-done((bf16[64,4096]{1,0:T(8,128)(2,1)S(1)}, bf16[64,4096]{1,0:T(8,128)(2,1)}, u32[]{:S(2)}) %copy-start.1) | copy-done | bytes 524312
  21.0 0.6 %shard_map.65 = (f32[8,4096]{1,0:T(8,128)S(1)}, f32[8,128]{1,0:T(8,128)S(1)}) custom-call(f32[8,4096]{1,0:T(8,128)S(1)} %get-tuple-element.13.wave_ref, f32[8,4096]{1,0:T(8,128)S(1)} %get-tuple-element.14.cut_ref, f32[8,128]{1,0:T(8,128)S(1)} %get-tuple-element.17.halo_ref, f32[8,128]{1,0:T(8,128)S(1)} %get-tuple-element.18.cut_halo_ref, ...), custom_call_target="tpu_custom_call" | custom-call | tf_op jit(solution)/shard_map/pallas_call | solution.py:357
  21.6 1.4 %collective-permute-start.10 = (f32[8,128]{1,0:T(8,128)S(1)}, f32[8,128]{1,0:T(8,128)S(1)}, u32[]{:S(2)}, u32[]{:S(2)}) collective-permute-start(f32[8,128]{1,0:T(8,128)S(1)} %get-tuple-element.21.refs_0_), channel_id=1, source_target_pairs={{0,7},{1,6},{2,5},{3,4},{4,3},{5,2},{6,1},{7,0},{8,15},{9,14},{10,... | collective-permute-start | bytes 12296 | tf_op jit(solution)/shard_map/ppermute | solution.py:336
  23.1 0.1 collective-permute-start.9
  23.1 2.4 %collective-permute-start.8 = (f32[8,128]{1,0:T(8,128)S(1)}, f32[8,128]{1,0:T(8,128)S(1)}, u32[]{:S(2)}, u32[]{:S(2)}) collective-permute-start(f32[8,128]{1,0:T(8,128)S(1)} %get-tuple-element.21.refs_0_), channel_id=1, source_target_pairs={{0,5},{1,4},{2,7},{3,6},{4,1},{5,0},{6,3},{7,2},{8,13},{9,12},{10,... | collective-permute-start | bytes 12296 | tf_op jit(solution)/shard_map/ppermute | solution.py:336
  25.5 1.0 %collective-permute-done.10.refs_3_ = f32[8,128]{1,0:T(8,128)S(1)} collective-permute-done((f32[8,128]{1,0:T(8,128)S(1)}, f32[8,128]{1,0:T(8,128)S(1)}, u32[]{:S(2)}, u32[]{:S(2)}) %collective-permute-start.10) | collective-permute-done | bytes 4128 | tf_op jit(solution)/shard_map/ppermute | solution.py:336
  26.5 0.5 %collective-permute-done.9.refs_2_ = f32[8,128]{1,0:T(8,128)S(1)} collective-permute-done((f32[8,128]{1,0:T(8,128)S(1)}, f32[8,128]{1,0:T(8,128)S(1)}, u32[]{:S(2)}, u32[]{:S(2)}) %collective-permute-start.9) | collective-permute-done | bytes 4128 | tf_op jit(solution)/shard_map/ppermute | solution.py:336
  27.0 0.0 collective-permute-done.8.refs_1_
  27.0 0.4 %shard_map.66 = (bf16[8,4224]{1,0:T(8,128)(2,1)S(1)}, f32[8,48]{1,0:T(8,128)S(1)}) custom-call(f32[64,128]{1,0:T(8,128)S(1)} %collective-permute-done.4.mine_ref, f32[64,128]{1,0:T(8,128)S(1)} %get-tuple-element.19.other_ref, bf16[48,4096]{1,0:T(8,128)(2,1)S(1)} %shard_map.62.kw_ref, bf16[48,4096]{1,0:T(8,128)(2,1)S(1)} %shard_map.63.kw_other_ref, ...), custom_call_target="tpu_custom_call" | custom-call | tf_op jit(solution)/shard_map/pallas_call | solution.py:357
  27.4 1.4 %collective-permute-start.13 = (bf16[8,4224]{1,0:T(8,128)(2,1)S(1)}, bf16[8,4224]{1,0:T(8,128)(2,1)S(1)}, u32[]{:S(2)}, u32[]{:S(2)}) collective-permute-start(bf16[8,4224]{1,0:T(8,128)(2,1)S(1)} %get-tuple-element.22.refs_0_), channel_id=1, source_target_pairs={{0,28},{1,29},{2,30},{3,31},{4,24},{5,25},{6,26},{7,27},{8,20},{9,... | collective-permute-start | bytes 202760 | tf_op jit(solution)/shard_map/ppermute | solution.py:336
  28.8 1.2 %collective-permute-start.12 = (bf16[8,4224]{1,0:T(8,128)(2,1)S(1)}, bf16[8,4224]{1,0:T(8,128)(2,1)S(1)}, u32[]{:S(2)}, u32[]{:S(2)}) collective-permute-start(bf16[8,4224]{1,0:T(8,128)(2,1)S(1)} %get-tuple-element.22.refs_0_), channel_id=1, source_target_pairs={{0,20},{1,21},{2,22},{3,23},{4,16},{5,17},{6,18},{7,19},{8,28},{9,... | collective-permute-start | bytes 202760 | tf_op jit(solution)/shard_map/ppermute | solution.py:336
  30.0 0.6 %collective-permute-start.11 = (bf16[8,4224]{1,0:T(8,128)(2,1)S(1)}, bf16[8,4224]{1,0:T(8,128)(2,1)S(1)}, u32[]{:S(2)}, u32[]{:S(2)}) collective-permute-start(bf16[8,4224]{1,0:T(8,128)(2,1)S(1)} %get-tuple-element.22.refs_0_), channel_id=1, source_target_pairs={{0,12},{1,13},{2,14},{3,15},{4,8},{5,9},{6,10},{7,11},{8,4},{9,5},... | collective-permute-start | bytes 202760 | tf_op jit(solution)/shard_map/ppermute | solution.py:336
  30.6 0.6 %copy.6 = f32[8,48]{1,0:T(8,128)} copy(f32[8,48]{1,0:T(8,128)S(1)} %get-tuple-element.25) | data formatting | bytes 3072
  31.2 1.2 %collective-permute-done.13.refs_3_ = bf16[8,4224]{1,0:T(8,128)(2,1)S(1)} collective-permute-done((bf16[8,4224]{1,0:T(8,128)(2,1)S(1)}, bf16[8,4224]{1,0:T(8,128)(2,1)S(1)}, u32[]{:S(2)}, u32[]{:S(2)}) %collective-permute-start.13) | collective-permute-done | bytes 67616 | tf_op jit(solution)/shard_map/ppermute | solution.py:336
  32.4 1.8 %collective-permute-done.12.refs_2_ = bf16[8,4224]{1,0:T(8,128)(2,1)S(1)} collective-permute-done((bf16[8,4224]{1,0:T(8,128)(2,1)S(1)}, bf16[8,4224]{1,0:T(8,128)(2,1)S(1)}, u32[]{:S(2)}, u32[]{:S(2)}) %collective-permute-start.12) | collective-permute-done | bytes 67616 | tf_op jit(solution)/shard_map/ppermute | solution.py:336
  34.2 0.0 collective-permute-done.11.refs_1_
  34.2 0.8 %shard_map.67 = f32[8,4096]{1,0:T(8,128)} custom-call(f32[8,4096]{1,0:T(8,128)S(1)} %get-tuple-element.20.wave_ref, f32[8,4096]{1,0:T(8,128)S(1)} %get-tuple-element.14.cut_ref, bf16[8,4224]{1,0:T(8,128)(2,1)S(1)} %get-tuple-element.22.refs_0_, bf16[8,4224]{1,0:T(8,128)(2,1)S(1)} %collective-permute-done.11.refs_1_, ...), custom_call_target="tpu_custom_call" | custom-call | tf_op jit(solution)/shard_map/pallas_call | solution.py:357
Async XLA Ops:
  2.0 10.0 %copy-start = (bf16[64,4096]{1,0:T(8,128)(2,1)}, bf16[64,4096]{1,0:T(8,128)(2,1)S(1)}, u32[]{:S(2)}) copy-start(bf16[64,4096]{1,0:T(8,128)(2,1)S(1)} %get-tuple-element.15.block_ref) | copy-start | bytes 1572868
  2.0 9.3 %collective-permute-start = (bf16[64,4096]{1,0:T(8,128)(2,1)S(1)}, bf16[64,4096]{1,0:T(8,128)(2,1)S(1)}, u32[]{:S(2)}, u32[]{:S(2)}) collective-permute-start(bf16[64,4096]{1,0:T(8,128)(2,1)S(1)} %get-tuple-element.15.block_ref), channel_id=1, source_target_pairs={{0,4},{4,0},{8,12},{12,8},{16,20},{20,16},{24,28},{28,24},{1,5},{5... | collective-permute-start | bytes 1572872 | tf_op jit(solution)/shard_map/ppermute | solution.py:329
  2.5 6.2 %collective-permute-start.3 = (bf16[64,128]{1,0:T(8,128)(2,1)S(1)}, bf16[64,128]{1,0:T(8,128)(2,1)S(1)}, u32[]{:S(2)}, u32[]{:S(2)}) collective-permute-start(bf16[64,128]{1,0:T(8,128)(2,1)S(1)} %get-tuple-element.16), channel_id=1, source_target_pairs={{0,7},{1,6},{2,5},{3,4},{4,3},{5,2},{6,1},{7,0},{8,15},{9,14},{10,... | collective-permute-start | bytes 49160 | tf_op jit(solution)/shard_map/ppermute | solution.py:336
  7.2 4.1 %collective-permute-start.2 = (bf16[64,128]{1,0:T(8,128)(2,1)S(1)}, bf16[64,128]{1,0:T(8,128)(2,1)S(1)}, u32[]{:S(2)}, u32[]{:S(2)}) collective-permute-start(bf16[64,128]{1,0:T(8,128)(2,1)S(1)} %get-tuple-element.16), channel_id=1, source_target_pairs={{0,6},{1,7},{2,4},{3,5},{4,2},{5,3},{6,0},{7,1},{8,14},{9,15},{10,... | collective-permute-start | bytes 49160 | tf_op jit(solution)/shard_map/ppermute | solution.py:336
  7.2 4.1 %collective-permute-start.1 = (bf16[64,128]{1,0:T(8,128)(2,1)S(1)}, bf16[64,128]{1,0:T(8,128)(2,1)S(1)}, u32[]{:S(2)}, u32[]{:S(2)}) collective-permute-start(bf16[64,128]{1,0:T(8,128)(2,1)S(1)} %get-tuple-element.16), channel_id=1, source_target_pairs={{0,5},{1,4},{2,7},{3,6},{4,1},{5,0},{6,3},{7,2},{8,13},{9,12},{10,... | collective-permute-start | bytes 49160 | tf_op jit(solution)/shard_map/ppermute | solution.py:336
  11.5 1.3 %collective-permute-start.4 = (f32[64,128]{1,0:T(8,128)S(1)}, f32[64,128]{1,0:T(8,128)S(1)}, u32[]{:S(2)}, u32[]{:S(2)}) collective-permute-start(f32[64,128]{1,0:T(8,128)S(1)} %get-tuple-element.19.other_ref), channel_id=1, source_target_pairs={{0,4},{4,0},{8,12},{12,8},{16,20},{20,16},{24,28},{28,24},{1,5},{5... | collective-permute-start | bytes 98312 | tf_op jit(solution)/shard_map/ppermute | solution.py:329
  12.2 3.8 %copy-start.2 = (f32[8,16,2]{1,2,0:T(2,128)S(1)}, f32[8,16,2]{1,2,0:T(2,128)}, u32[]{:S(2)}) copy-start(f32[8,16,2]{1,2,0:T(2,128)} %param.7) | copy-start | bytes 3076
  13.0 5.1 %collective-permute-start.7 = (bf16[8,4224]{1,0:T(8,128)(2,1)S(1)}, bf16[8,4224]{1,0:T(8,128)(2,1)S(1)}, u32[]{:S(2)}, u32[]{:S(2)}) collective-permute-start(bf16[8,4224]{1,0:T(8,128)(2,1)S(1)} %shard_map.64.refs_0_), channel_id=1, source_target_pairs={{0,28},{1,29},{2,30},{3,31},{4,24},{5,25},{6,26},{7,27},{8,20},{9,... | collective-permute-start | bytes 202760 | tf_op jit(solution)/shard_map/ppermute | solution.py:336
  15.3 4.3 %collective-permute-start.6 = (bf16[8,4224]{1,0:T(8,128)(2,1)S(1)}, bf16[8,4224]{1,0:T(8,128)(2,1)S(1)}, u32[]{:S(2)}, u32[]{:S(2)}) collective-permute-start(bf16[8,4224]{1,0:T(8,128)(2,1)S(1)} %shard_map.64.refs_0_), channel_id=1, source_target_pairs={{0,20},{1,21},{2,22},{3,23},{4,16},{5,17},{6,18},{7,19},{8,28},{9,... | collective-permute-start | bytes 202760 | tf_op jit(solution)/shard_map/ppermute | solution.py:336
  15.8 4.2 %collective-permute-start.5 = (bf16[8,4224]{1,0:T(8,128)(2,1)S(1)}, bf16[8,4224]{1,0:T(8,128)(2,1)S(1)}, u32[]{:S(2)}, u32[]{:S(2)}) collective-permute-start(bf16[8,4224]{1,0:T(8,128)(2,1)S(1)} %shard_map.64.refs_0_), channel_id=1, source_target_pairs={{0,12},{1,13},{2,14},{3,15},{4,8},{5,9},{6,10},{7,11},{8,4},{9,5},... | collective-permute-start | bytes 202760 | tf_op jit(solution)/shard_map/ppermute | solution.py:336
  20.0 1.0 %copy-start.1 = (bf16[64,4096]{1,0:T(8,128)(2,1)S(1)}, bf16[64,4096]{1,0:T(8,128)(2,1)}, u32[]{:S(2)}) copy-start(bf16[64,4096]{1,0:T(8,128)(2,1)} %copy-done) | copy-start | bytes 1572868
  21.6 4.8 %collective-permute-start.10 = (f32[8,128]{1,0:T(8,128)S(1)}, f32[8,128]{1,0:T(8,128)S(1)}, u32[]{:S(2)}, u32[]{:S(2)}) collective-permute-start(f32[8,128]{1,0:T(8,128)S(1)} %get-tuple-element.21.refs_0_), channel_id=1, source_target_pairs={{0,7},{1,6},{2,5},{3,4},{4,3},{5,2},{6,1},{7,0},{8,15},{9,14},{10,... | collective-permute-start | bytes 12296 | tf_op jit(solution)/shard_map/ppermute | solution.py:336
  23.1 4.0 %collective-permute-start.9 = (f32[8,128]{1,0:T(8,128)S(1)}, f32[8,128]{1,0:T(8,128)S(1)}, u32[]{:S(2)}, u32[]{:S(2)}) collective-permute-start(f32[8,128]{1,0:T(8,128)S(1)} %get-tuple-element.21.refs_0_), channel_id=1, source_target_pairs={{0,6},{1,7},{2,4},{3,5},{4,2},{5,3},{6,0},{7,1},{8,14},{9,15},{10,... | collective-permute-start | bytes 12296 | tf_op jit(solution)/shard_map/ppermute | solution.py:336
  23.1 3.9 %collective-permute-start.8 = (f32[8,128]{1,0:T(8,128)S(1)}, f32[8,128]{1,0:T(8,128)S(1)}, u32[]{:S(2)}, u32[]{:S(2)}) collective-permute-start(f32[8,128]{1,0:T(8,128)S(1)} %get-tuple-element.21.refs_0_), channel_id=1, source_target_pairs={{0,5},{1,4},{2,7},{3,6},{4,1},{5,0},{6,3},{7,2},{8,13},{9,12},{10,... | collective-permute-start | bytes 12296 | tf_op jit(solution)/shard_map/ppermute | solution.py:336
  27.4 5.0 %collective-permute-start.13 = (bf16[8,4224]{1,0:T(8,128)(2,1)S(1)}, bf16[8,4224]{1,0:T(8,128)(2,1)S(1)}, u32[]{:S(2)}, u32[]{:S(2)}) collective-permute-start(bf16[8,4224]{1,0:T(8,128)(2,1)S(1)} %get-tuple-element.22.refs_0_), channel_id=1, source_target_pairs={{0,28},{1,29},{2,30},{3,31},{4,24},{5,25},{6,26},{7,27},{8,20},{9,... | collective-permute-start | bytes 202760 | tf_op jit(solution)/shard_map/ppermute | solution.py:336
  28.8 5.4 %collective-permute-start.12 = (bf16[8,4224]{1,0:T(8,128)(2,1)S(1)}, bf16[8,4224]{1,0:T(8,128)(2,1)S(1)}, u32[]{:S(2)}, u32[]{:S(2)}) collective-permute-start(bf16[8,4224]{1,0:T(8,128)(2,1)S(1)} %get-tuple-element.22.refs_0_), channel_id=1, source_target_pairs={{0,20},{1,21},{2,22},{3,23},{4,16},{5,17},{6,18},{7,19},{8,28},{9,... | collective-permute-start | bytes 202760 | tf_op jit(solution)/shard_map/ppermute | solution.py:336
  30.0 4.2 %collective-permute-start.11 = (bf16[8,4224]{1,0:T(8,128)(2,1)S(1)}, bf16[8,4224]{1,0:T(8,128)(2,1)S(1)}, u32[]{:S(2)}, u32[]{:S(2)}) collective-permute-start(bf16[8,4224]{1,0:T(8,128)(2,1)S(1)} %get-tuple-element.22.refs_0_), channel_id=1, source_target_pairs={{0,12},{1,13},{2,14},{3,15},{4,8},{5,9},{6,10},{7,11},{8,4},{9,5},... | collective-permute-start | bytes 202760 | tf_op jit(solution)/shard_map/ppermute | solution.py:336

commit v6 on v5

--- a/solution.py
+++ b/solution.py
@@ -9,6 +9,7 @@
 
 step_size = 0.5
 LANES = 128
+KERNEL_BYTES = 8 * 2**20
 F32 = jnp.float32
 BF16 = jnp.bfloat16
 
@@ -360,6 +361,7 @@
         in_specs=[pl.BlockSpec(memory_space=space)] * len(args),
         out_specs=jax.tree.map(lambda _: pl.BlockSpec(memory_space=pltpu.VMEM), out_shape),
         scratch_shapes=list(scratch),
+        compiler_params=pltpu.CompilerParams(vmem_limit_bytes=KERNEL_BYTES),
     )(*[pltpu.with_memory_space_constraint(arg, space) for arg in args])
 
 

time: 35.2 us -> 34 us (0.966)
  local copies, waits for them, and re-layouts: 1.64 us -> 0.6 us
    unnamed x7 -> x3, local copies, waits for them, and re-layouts: 1.64 us -> 0.6 us
  transfers between devices with their start and end apart: 14 -> 14, of which waited for: 10 -> 10; matrix products, arithmetic and copies ran while one was open for 2% -> 2% of each run, Pallas kernels for 2% -> 3%
where the time goes in v6:
time: 34 us; the launch traced here: 33.9 us
  starting transfers between devices  15.9 us (47%)
  waiting for transfers between devices  12.2 us (36%)
  Pallas kernels  4.45 us (13%)
  between operations  0.69 us (2%)
  local copies, waits for them, and re-layouts  0.6 us (2%)
    ppermute x12, starting transfers between devices, from_other_core(): return lax.ppermute(x, ('dp', 'vox'), route)  15.2 us
    ppermute x12, waiting for transfers between devices, from_other_core(): return lax.ppermute(x, ('dp', 'vox'), route)  11.7 us
    pallas_call x9, Pallas kernels, call(): pl.pallas_call(kernel, out_shape=out_shape, in_specs=[pl.BlockSpec(memory...  4.45 us
    ppermute x2, starting transfers between devices, from_partner(): lax.ppermute(x, axis, [(i, i ^ distance) for i in range(lax.axis_size(axi...  0.69 us
  transfers between devices with their start and end apart: 14, of which 10 were waited for; matrix products, arithmetic and copies ran while one was open for 2% of the time, Pallas kernels for 3%

profile of v6, /device:TPU:0, one launch (start us, length us, event | category | flops | bytes accessed | tf_op | source)
XLA Modules:
  0.0 33.9 jit_solution(10704619184238278148)
XLA Ops:
  0.6 1.3 %shard_map.59 = (bf16[64,128]{1,0:T(8,128)(2,1)S(1)}, f32[8,4096]{1,0:T(8,128)S(1)}, bf16[64,4096]{1,0:T(8,128)(2,1)S(1)}) custom-call(f32[8,4096]{1,0:T(8,128)} %wave_hbm.1, bf16[48,4096]{1,0:T(8,128)(2,1)} %k_hbm.1, f32[8,48]{1,0:T(8,128)} %observed_hbm.1), custom_call_target="tpu_custom_call" | custom-call | tf_op jit(solution)/shard_map/pallas_call | solution.py:358
  2.0 0.5 %collective-permute-start = (bf16[64,4096]{1,0:T(8,128)(2,1)S(1)}, bf16[64,4096]{1,0:T(8,128)(2,1)S(1)}, u32[]{:S(2)}, u32[]{:S(2)}) collective-permute-start(bf16[64,4096]{1,0:T(8,128)(2,1)S(1)} %get-tuple-element.15.block_ref), channel_id=1, source_target_pairs={{0,4},{4,0},{8,12},{12,8},{16,20},{20,16},{24,28},{28,24},{1,5},{5... | collective-permute-start | bytes 1572872 | tf_op jit(solution)/shard_map/ppermute | solution.py:330
  2.5 4.7 %collective-permute-start.3 = (bf16[64,128]{1,0:T(8,128)(2,1)S(1)}, bf16[64,128]{1,0:T(8,128)(2,1)S(1)}, u32[]{:S(2)}, u32[]{:S(2)}) collective-permute-start(bf16[64,128]{1,0:T(8,128)(2,1)S(1)} %get-tuple-element.16), channel_id=1, source_target_pairs={{0,7},{1,6},{2,5},{3,4},{4,3},{5,2},{6,1},{7,0},{8,15},{9,14},{10,... | collective-permute-start | bytes 49160 | tf_op jit(solution)/shard_map/ppermute | solution.py:337
  7.2 0.0 collective-permute-start.2
  7.2 0.3 collective-permute-start.1
  7.5 1.1 %collective-permute-done.3.refs_3_ = bf16[64,128]{1,0:T(8,128)(2,1)S(1)} collective-permute-done((bf16[64,128]{1,0:T(8,128)(2,1)S(1)}, bf16[64,128]{1,0:T(8,128)(2,1)S(1)}, u32[]{:S(2)}, u32[]{:S(2)}) %collective-permute-start.3) | collective-permute-done | bytes 16416 | tf_op jit(solution)/shard_map/ppermute | solution.py:337
  8.7 2.6 %collective-permute-done.2.refs_2_ = bf16[64,128]{1,0:T(8,128)(2,1)S(1)} collective-permute-done((bf16[64,128]{1,0:T(8,128)(2,1)S(1)}, bf16[64,128]{1,0:T(8,128)(2,1)S(1)}, u32[]{:S(2)}, u32[]{:S(2)}) %collective-permute-start.2) | collective-permute-done | bytes 16416 | tf_op jit(solution)/shard_map/ppermute | solution.py:337
  11.3 0.0 collective-permute-done.1.refs_1_
  11.3 0.0 collective-permute-done.refs_0_.block_ref.block_other_ref
  11.3 0.2 shard_map.61
  11.5 0.2 collective-permute-start.4
  11.7 0.3 shard_map.62.kw_ref
  11.9 0.3 shard_map.63.kw_other_ref
  12.2 0.0 copy-start
  12.2 0.6 %collective-permute-done.4.mine_ref = f32[64,128]{1,0:T(8,128)S(1)} collective-permute-done((f32[64,128]{1,0:T(8,128)S(1)}, f32[64,128]{1,0:T(8,128)S(1)}, u32[]{:S(2)}, u32[]{:S(2)}) %collective-permute-start.4) | collective-permute-done | bytes 32800 | tf_op jit(solution)/shard_map/ppermute | solution.py:330
  12.8 0.2 shard_map.64.refs_0_
  13.0 2.3 %collective-permute-start.7 = (bf16[8,4224]{1,0:T(8,128)(2,1)S(1)}, bf16[8,4224]{1,0:T(8,128)(2,1)S(1)}, u32[]{:S(2)}, u32[]{:S(2)}) collective-permute-start(bf16[8,4224]{1,0:T(8,128)(2,1)S(1)} %shard_map.64.refs_0_), channel_id=1, source_target_pairs={{0,28},{1,29},{2,30},{3,31},{4,24},{5,25},{6,26},{7,27},{8,20},{9,... | collective-permute-start | bytes 202760 | tf_op jit(solution)/shard_map/ppermute | solution.py:337
  15.3 0.5 %collective-permute-start.6 = (bf16[8,4224]{1,0:T(8,128)(2,1)S(1)}, bf16[8,4224]{1,0:T(8,128)(2,1)S(1)}, u32[]{:S(2)}, u32[]{:S(2)}) collective-permute-start(bf16[8,4224]{1,0:T(8,128)(2,1)S(1)} %shard_map.64.refs_0_), channel_id=1, source_target_pairs={{0,20},{1,21},{2,22},{3,23},{4,16},{5,17},{6,18},{7,19},{8,28},{9,... | collective-permute-start | bytes 202760 | tf_op jit(solution)/shard_map/ppermute | solution.py:337
  15.8 0.3 collective-permute-start.5
  16.1 0.0 copy-done
  16.1 0.4 %shard_map.60 = (f32[8,4096]{1,0:T(8,128)S(1)}, f32[8,128]{1,0:T(8,128)S(1)}) custom-call(f32[8,2,16]{2,1,0:T(2,128)S(1)} %bitcast.1), custom_call_target="tpu_custom_call" | custom-call | tf_op jit(solution)/shard_map/pallas_call | solution.py:358
  16.4 1.6 %collective-permute-done.7.refs_3_ = bf16[8,4224]{1,0:T(8,128)(2,1)S(1)} collective-permute-done((bf16[8,4224]{1,0:T(8,128)(2,1)S(1)}, bf16[8,4224]{1,0:T(8,128)(2,1)S(1)}, u32[]{:S(2)}, u32[]{:S(2)}) %collective-permute-start.7) | collective-permute-done | bytes 67616 | tf_op jit(solution)/shard_map/ppermute | solution.py:337
  18.1 1.5 %collective-permute-done.6.refs_2_ = bf16[8,4224]{1,0:T(8,128)(2,1)S(1)} collective-permute-done((bf16[8,4224]{1,0:T(8,128)(2,1)S(1)}, bf16[8,4224]{1,0:T(8,128)(2,1)S(1)}, u32[]{:S(2)}, u32[]{:S(2)}) %collective-permute-start.6) | collective-permute-done | bytes 67616 | tf_op jit(solution)/shard_map/ppermute | solution.py:337
  19.5 0.3 collective-permute-done.5.refs_1_
  19.9 0.6 %shard_map.65 = (f32[8,4096]{1,0:T(8,128)S(1)}, f32[8,128]{1,0:T(8,128)S(1)}) custom-call(f32[8,4096]{1,0:T(8,128)S(1)} %get-tuple-element.13.wave_ref, f32[8,4096]{1,0:T(8,128)S(1)} %get-tuple-element.14.cut_ref, f32[8,128]{1,0:T(8,128)S(1)} %get-tuple-element.17.halo_ref, f32[8,128]{1,0:T(8,128)S(1)} %get-tuple-element.18.cut_halo_ref, ...), custom_call_target="tpu_custom_call" | custom-call | tf_op jit(solution)/shard_map/pallas_call | solution.py:358
  20.5 1.5 %collective-permute-start.10 = (f32[8,128]{1,0:T(8,128)S(1)}, f32[8,128]{1,0:T(8,128)S(1)}, u32[]{:S(2)}, u32[]{:S(2)}) collective-permute-start(f32[8,128]{1,0:T(8,128)S(1)} %get-tuple-element.21.refs_0_), channel_id=1, source_target_pairs={{0,7},{1,6},{2,5},{3,4},{4,3},{5,2},{6,1},{7,0},{8,15},{9,14},{10,... | collective-permute-start | bytes 12296 | tf_op jit(solution)/shard_map/ppermute | solution.py:337
  22.0 0.1 collective-permute-start.9
  22.1 2.3 %collective-permute-start.8 = (f32[8,128]{1,0:T(8,128)S(1)}, f32[8,128]{1,0:T(8,128)S(1)}, u32[]{:S(2)}, u32[]{:S(2)}) collective-permute-start(f32[8,128]{1,0:T(8,128)S(1)} %get-tuple-element.21.refs_0_), channel_id=1, source_target_pairs={{0,5},{1,4},{2,7},{3,6},{4,1},{5,0},{6,3},{7,2},{8,13},{9,12},{10,... | collective-permute-start | bytes 12296 | tf_op jit(solution)/shard_map/ppermute | solution.py:337
  24.4 1.0 %collective-permute-done.10.refs_3_ = f32[8,128]{1,0:T(8,128)S(1)} collective-permute-done((f32[8,128]{1,0:T(8,128)S(1)}, f32[8,128]{1,0:T(8,128)S(1)}, u32[]{:S(2)}, u32[]{:S(2)}) %collective-permute-start.10) | collective-permute-done | bytes 4128 | tf_op jit(solution)/shard_map/ppermute | solution.py:337
  25.3 0.5 %collective-permute-done.9.refs_2_ = f32[8,128]{1,0:T(8,128)S(1)} collective-permute-done((f32[8,128]{1,0:T(8,128)S(1)}, f32[8,128]{1,0:T(8,128)S(1)}, u32[]{:S(2)}, u32[]{:S(2)}) %collective-permute-start.9) | collective-permute-done | bytes 4128 | tf_op jit(solution)/shard_map/ppermute | solution.py:337
  25.9 0.0 collective-permute-done.8.refs_1_
  25.9 0.4 %shard_map.66 = (bf16[8,4224]{1,0:T(8,128)(2,1)S(1)}, f32[8,48]{1,0:T(8,128)S(1)}) custom-call(f32[64,128]{1,0:T(8,128)S(1)} %collective-permute-done.4.mine_ref, f32[64,128]{1,0:T(8,128)S(1)} %get-tuple-element.19.other_ref, bf16[48,4096]{1,0:T(8,128)(2,1)S(1)} %shard_map.62.kw_ref, bf16[48,4096]{1,0:T(8,128)(2,1)S(1)} %shard_map.63.kw_other_ref, ...), custom_call_target="tpu_custom_call" | custom-call | tf_op jit(solution)/shard_map/pallas_call | solution.py:358
  26.3 1.5 %collective-permute-start.13 = (bf16[8,4224]{1,0:T(8,128)(2,1)S(1)}, bf16[8,4224]{1,0:T(8,128)(2,1)S(1)}, u32[]{:S(2)}, u32[]{:S(2)}) collective-permute-start(bf16[8,4224]{1,0:T(8,128)(2,1)S(1)} %get-tuple-element.22.refs_0_), channel_id=1, source_target_pairs={{0,28},{1,29},{2,30},{3,31},{4,24},{5,25},{6,26},{7,27},{8,20},{9,... | collective-permute-start | bytes 202760 | tf_op jit(solution)/shard_map/ppermute | solution.py:337
  27.8 1.2 %collective-permute-start.12 = (bf16[8,4224]{1,0:T(8,128)(2,1)S(1)}, bf16[8,4224]{1,0:T(8,128)(2,1)S(1)}, u32[]{:S(2)}, u32[]{:S(2)}) collective-permute-start(bf16[8,4224]{1,0:T(8,128)(2,1)S(1)} %get-tuple-element.22.refs_0_), channel_id=1, source_target_pairs={{0,20},{1,21},{2,22},{3,23},{4,16},{5,17},{6,18},{7,19},{8,28},{9,... | collective-permute-start | bytes 202760 | tf_op jit(solution)/shard_map/ppermute | solution.py:337
  29.0 0.6 %collective-permute-start.11 = (bf16[8,4224]{1,0:T(8,128)(2,1)S(1)}, bf16[8,4224]{1,0:T(8,128)(2,1)S(1)}, u32[]{:S(2)}, u32[]{:S(2)}) collective-permute-start(bf16[8,4224]{1,0:T(8,128)(2,1)S(1)} %get-tuple-element.22.refs_0_), channel_id=1, source_target_pairs={{0,12},{1,13},{2,14},{3,15},{4,8},{5,9},{6,10},{7,11},{8,4},{9,5},... | collective-permute-start | bytes 202760 | tf_op jit(solution)/shard_map/ppermute | solution.py:337
  29.5 0.6 %copy.6 = f32[8,48]{1,0:T(8,128)} copy(f32[8,48]{1,0:T(8,128)S(1)} %get-tuple-element.25) | data formatting | bytes 3072
  30.1 1.1 %collective-permute-done.13.refs_3_ = bf16[8,4224]{1,0:T(8,128)(2,1)S(1)} collective-permute-done((bf16[8,4224]{1,0:T(8,128)(2,1)S(1)}, bf16[8,4224]{1,0:T(8,128)(2,1)S(1)}, u32[]{:S(2)}, u32[]{:S(2)}) %collective-permute-start.13) | collective-permute-done | bytes 67616 | tf_op jit(solution)/shard_map/ppermute | solution.py:337
  31.3 1.8 %collective-permute-done.12.refs_2_ = bf16[8,4224]{1,0:T(8,128)(2,1)S(1)} collective-permute-done((bf16[8,4224]{1,0:T(8,128)(2,1)S(1)}, bf16[8,4224]{1,0:T(8,128)(2,1)S(1)}, u32[]{:S(2)}, u32[]{:S(2)}) %collective-permute-start.12) | collective-permute-done | bytes 67616 | tf_op jit(solution)/shard_map/ppermute | solution.py:337
  33.1 0.0 collective-permute-done.11.refs_1_
  33.1 0.8 %shard_map.67 = f32[8,4096]{1,0:T(8,128)} custom-call(f32[8,4096]{1,0:T(8,128)S(1)} %get-tuple-element.20.wave_ref, f32[8,4096]{1,0:T(8,128)S(1)} %get-tuple-element.14.cut_ref, bf16[8,4224]{1,0:T(8,128)(2,1)S(1)} %get-tuple-element.22.refs_0_, bf16[8,4224]{1,0:T(8,128)(2,1)S(1)} %collective-permute-done.11.refs_1_, ...), custom_call_target="tpu_custom_call" | custom-call | tf_op jit(solution)/shard_map/pallas_call | solution.py:358
Async XLA Ops:
  2.0 9.3 %collective-permute-start = (bf16[64,4096]{1,0:T(8,128)(2,1)S(1)}, bf16[64,4096]{1,0:T(8,128)(2,1)S(1)}, u32[]{:S(2)}, u32[]{:S(2)}) collective-permute-start(bf16[64,4096]{1,0:T(8,128)(2,1)S(1)} %get-tuple-element.15.block_ref), channel_id=1, source_target_pairs={{0,4},{4,0},{8,12},{12,8},{16,20},{20,16},{24,28},{28,24},{1,5},{5... | collective-permute-start | bytes 1572872 | tf_op jit(solution)/shard_map/ppermute | solution.py:330
  2.5 6.2 %collective-permute-start.3 = (bf16[64,128]{1,0:T(8,128)(2,1)S(1)}, bf16[64,128]{1,0:T(8,128)(2,1)S(1)}, u32[]{:S(2)}, u32[]{:S(2)}) collective-permute-start(bf16[64,128]{1,0:T(8,128)(2,1)S(1)} %get-tuple-element.16), channel_id=1, source_target_pairs={{0,7},{1,6},{2,5},{3,4},{4,3},{5,2},{6,1},{7,0},{8,15},{9,14},{10,... | collective-permute-start | bytes 49160 | tf_op jit(solution)/shard_map/ppermute | solution.py:337
  7.2 4.1 %collective-permute-start.2 = (bf16[64,128]{1,0:T(8,128)(2,1)S(1)}, bf16[64,128]{1,0:T(8,128)(2,1)S(1)}, u32[]{:S(2)}, u32[]{:S(2)}) collective-permute-start(bf16[64,128]{1,0:T(8,128)(2,1)S(1)} %get-tuple-element.16), channel_id=1, source_target_pairs={{0,6},{1,7},{2,4},{3,5},{4,2},{5,3},{6,0},{7,1},{8,14},{9,15},{10,... | collective-permute-start | bytes 49160 | tf_op jit(solution)/shard_map/ppermute | solution.py:337
  7.2 4.1 %collective-permute-start.1 = (bf16[64,128]{1,0:T(8,128)(2,1)S(1)}, bf16[64,128]{1,0:T(8,128)(2,1)S(1)}, u32[]{:S(2)}, u32[]{:S(2)}) collective-permute-start(bf16[64,128]{1,0:T(8,128)(2,1)S(1)} %get-tuple-element.16), channel_id=1, source_target_pairs={{0,5},{1,4},{2,7},{3,6},{4,1},{5,0},{6,3},{7,2},{8,13},{9,12},{10,... | collective-permute-start | bytes 49160 | tf_op jit(solution)/shard_map/ppermute | solution.py:337
  11.5 1.3 %collective-permute-start.4 = (f32[64,128]{1,0:T(8,128)S(1)}, f32[64,128]{1,0:T(8,128)S(1)}, u32[]{:S(2)}, u32[]{:S(2)}) collective-permute-start(f32[64,128]{1,0:T(8,128)S(1)} %get-tuple-element.19.other_ref), channel_id=1, source_target_pairs={{0,4},{4,0},{8,12},{12,8},{16,20},{20,16},{24,28},{28,24},{1,5},{5... | collective-permute-start | bytes 98312 | tf_op jit(solution)/shard_map/ppermute | solution.py:330
  12.2 3.9 %copy-start = (f32[8,16,2]{1,2,0:T(2,128)S(1)}, f32[8,16,2]{1,2,0:T(2,128)}, u32[]{:S(2)}) copy-start(f32[8,16,2]{1,2,0:T(2,128)} %param.7) | copy-start | bytes 3076
  13.0 5.1 %collective-permute-start.7 = (bf16[8,4224]{1,0:T(8,128)(2,1)S(1)}, bf16[8,4224]{1,0:T(8,128)(2,1)S(1)}, u32[]{:S(2)}, u32[]{:S(2)}) collective-permute-start(bf16[8,4224]{1,0:T(8,128)(2,1)S(1)} %shard_map.64.refs_0_), channel_id=1, source_target_pairs={{0,28},{1,29},{2,30},{3,31},{4,24},{5,25},{6,26},{7,27},{8,20},{9,... | collective-permute-start | bytes 202760 | tf_op jit(solution)/shard_map/ppermute | solution.py:337
  15.3 4.2 %collective-permute-start.6 = (bf16[8,4224]{1,0:T(8,128)(2,1)S(1)}, bf16[8,4224]{1,0:T(8,128)(2,1)S(1)}, u32[]{:S(2)}, u32[]{:S(2)}) collective-permute-start(bf16[8,4224]{1,0:T(8,128)(2,1)S(1)} %shard_map.64.refs_0_), channel_id=1, source_target_pairs={{0,20},{1,21},{2,22},{3,23},{4,16},{5,17},{6,18},{7,19},{8,28},{9,... | collective-permute-start | bytes 202760 | tf_op jit(solution)/shard_map/ppermute | solution.py:337
  15.8 4.1 %collective-permute-start.5 = (bf16[8,4224]{1,0:T(8,128)(2,1)S(1)}, bf16[8,4224]{1,0:T(8,128)(2,1)S(1)}, u32[]{:S(2)}, u32[]{:S(2)}) collective-permute-start(bf16[8,4224]{1,0:T(8,128)(2,1)S(1)} %shard_map.64.refs_0_), channel_id=1, source_target_pairs={{0,12},{1,13},{2,14},{3,15},{4,8},{5,9},{6,10},{7,11},{8,4},{9,5},... | collective-permute-start | bytes 202760 | tf_op jit(solution)/shard_map/ppermute | solution.py:337
  20.5 4.8 %collective-permute-start.10 = (f32[8,128]{1,0:T(8,128)S(1)}, f32[8,128]{1,0:T(8,128)S(1)}, u32[]{:S(2)}, u32[]{:S(2)}) collective-permute-start(f32[8,128]{1,0:T(8,128)S(1)} %get-tuple-element.21.refs_0_), channel_id=1, source_target_pairs={{0,7},{1,6},{2,5},{3,4},{4,3},{5,2},{6,1},{7,0},{8,15},{9,14},{10,... | collective-permute-start | bytes 12296 | tf_op jit(solution)/shard_map/ppermute | solution.py:337
  22.0 3.9 %collective-permute-start.9 = (f32[8,128]{1,0:T(8,128)S(1)}, f32[8,128]{1,0:T(8,128)S(1)}, u32[]{:S(2)}, u32[]{:S(2)}) collective-permute-start(f32[8,128]{1,0:T(8,128)S(1)} %get-tuple-element.21.refs_0_), channel_id=1, source_target_pairs={{0,6},{1,7},{2,4},{3,5},{4,2},{5,3},{6,0},{7,1},{8,14},{9,15},{10,... | collective-permute-start | bytes 12296 | tf_op jit(solution)/shard_map/ppermute | solution.py:337
  22.1 3.8 %collective-permute-start.8 = (f32[8,128]{1,0:T(8,128)S(1)}, f32[8,128]{1,0:T(8,128)S(1)}, u32[]{:S(2)}, u32[]{:S(2)}) collective-permute-start(f32[8,128]{1,0:T(8,128)S(1)} %get-tuple-element.21.refs_0_), channel_id=1, source_target_pairs={{0,5},{1,4},{2,7},{3,6},{4,1},{5,0},{6,3},{7,2},{8,13},{9,12},{10,... | collective-permute-start | bytes 12296 | tf_op jit(solution)/shard_map/ppermute | solution.py:337
  26.3 5.0 %collective-permute-start.13 = (bf16[8,4224]{1,0:T(8,128)(2,1)S(1)}, bf16[8,4224]{1,0:T(8,128)(2,1)S(1)}, u32[]{:S(2)}, u32[]{:S(2)}) collective-permute-start(bf16[8,4224]{1,0:T(8,128)(2,1)S(1)} %get-tuple-element.22.refs_0_), channel_id=1, source_target_pairs={{0,28},{1,29},{2,30},{3,31},{4,24},{5,25},{6,26},{7,27},{8,20},{9,... | collective-permute-start | bytes 202760 | tf_op jit(solution)/shard_map/ppermute | solution.py:337
  27.8 5.3 %collective-permute-start.12 = (bf16[8,4224]{1,0:T(8,128)(2,1)S(1)}, bf16[8,4224]{1,0:T(8,128)(2,1)S(1)}, u32[]{:S(2)}, u32[]{:S(2)}) collective-permute-start(bf16[8,4224]{1,0:T(8,128)(2,1)S(1)} %get-tuple-element.22.refs_0_), channel_id=1, source_target_pairs={{0,20},{1,21},{2,22},{3,23},{4,16},{5,17},{6,18},{7,19},{8,28},{9,... | collective-permute-start | bytes 202760 | tf_op jit(solution)/shard_map/ppermute | solution.py:337
  29.0 4.1 %collective-permute-start.11 = (bf16[8,4224]{1,0:T(8,128)(2,1)S(1)}, bf16[8,4224]{1,0:T(8,128)(2,1)S(1)}, u32[]{:S(2)}, u32[]{:S(2)}) collective-permute-start(bf16[8,4224]{1,0:T(8,128)(2,1)S(1)} %get-tuple-element.22.refs_0_), channel_id=1, source_target_pairs={{0,12},{1,13},{2,14},{3,15},{4,8},{5,9},{6,10},{7,11},{8,4},{9,5},... | collective-permute-start | bytes 202760 | tf_op jit(solution)/shard_map/ppermute | solution.py:337

commit v7 on v6

--- a/solution.py
+++ b/solution.py
@@ -260,10 +260,12 @@
     back_projected(core(mine_ref, kw_ref), core(other_ref, kw_other_ref), g_ref)
 
 
-def tree_sum(values):
-    while len(values) > 1:
-        values = [a + b for a, b in zip(values[::2], values[1::2])]
-    return values[0]
+def added(shares):
+    if len(shares) < 4:
+        return sum(shares[1:], shares[0])
+    own, near, swapped, far = shares
+    is_first = lax.rem(lax.axis_index("dp"), 2) == 0
+    return (own + jnp.where(is_first, near, swapped)) + (jnp.where(is_first, swapped, near) + far)
 
 
 def at_ends(tile, layers, base):
@@ -273,8 +275,8 @@
 def stepped(layers, base, wave_ref, cut_ref, g_refs):
     width = wave_ref.shape[1]
     gradients = [stacked(g, layers) for g in g_refs]
-    smooth_g, detail_g = (tree_sum([g[p] for g in gradients]) for p in range(2))
-    edge = tree_sum([g[:, width:].astype(F32) for g in g_refs])
+    smooth_g, detail_g = (added([g[p] for g in gradients]) for p in range(2))
+    edge = added([g[:, width:].astype(F32) for g in g_refs])
     ends = at_ends(edge, layers, base)
     lane = lanes_of(ends.shape)
     smooth_g += jnp.where(lane == 0, 0.25 * ends, jnp.where(lane == LANES - 1, -0.125 * ends, 0.0))
@@ -308,7 +310,7 @@
 def fifth_kernel(mine_ref, other_ref, kw_ref, kw_other_ref, *refs):
     *shares, g_ref, residual_ref = refs
     models, rows = residual_ref.shape
-    predicted = tree_sum([s[...] for s in shares])
+    predicted = added([s[...] for s in shares])
     first, second = predicted[:, :rows], predicted[:, rows : 2 * rows]
     is_first = lax.rem(lax.axis_index("dp"), 2) == 0
 
@@ -330,28 +332,35 @@
     return lax.ppermute(x, axis, [(i, i ^ distance) for i in range(lax.axis_size(axis))])
 
 
-def from_other_core(x, chips, vox):
+def from_other_core(x, *steps):
     n_vox = lax.axis_size("vox")
-    places = [(d, z) for d in range(lax.axis_size("dp")) for z in range(n_vox)]
-    route = [(d * n_vox + z, (d ^ (2 * chips + 1)) * n_vox + (z ^ vox)) for d, z in places]
+    route = []
+    for d in range(lax.axis_size("dp")):
+        chips, vox = steps[(d + 1) % 2 % len(steps)]
+        route += [(d * n_vox + z, (d ^ (2 * chips + 1)) * n_vox + (z ^ vox)) for z in range(n_vox)]
     return lax.ppermute(x, ("dp", "vox"), route)
 
 
-def shares_of(x, size, fetch):
+def shares_of(x, size, step):
     lowest = 1
-    while size > 4:
-        parts = [x] + [fetch(x, lowest * d) for d in range(1, 4)]
-        x = tree_sum([p.astype(F32) for p in parts]).astype(x.dtype)
+    while True:
+        near, middle, far = (step(lowest * n) for n in (1, 2, 3))
+        if size < 4:
+            return [x] + [from_other_core(x, near)] * (size - 1)
+        fetched = from_other_core(x, near, middle)
+        shares = [x, fetched, from_partner(fetched, "dp", 1), from_other_core(x, far)]
+        if size == 4:
+            return shares
+        x = added([s.astype(F32) for s in shares]).astype(x.dtype)
         lowest, size = lowest * 4, size // 4
-    return [x] + [fetch(x, lowest * d) for d in range(1, size)]
 
 
 def over_chips(x):
-    return shares_of(x, lax.axis_size("dp") // 2, lambda x, d: from_other_core(x, d, 0))
+    return shares_of(x, lax.axis_size("dp") // 2, lambda n: (n, 0))
 
 
 def over_vox(x):
-    return shares_of(x, lax.axis_size("vox"), lambda x, d: from_other_core(x, 0, d))
+    return shares_of(x, lax.axis_size("vox"), lambda n: (0, n))
 
 
 def call(kernel, out_shape, *args, scratch=(), space=pltpu.VMEM):
@@ -394,7 +403,7 @@
         space=pltpu.HBM,
     )
     block_other = from_partner(block, "dp", 1)
-    packets = [from_other_core(packet, 0, d) for d in range(1, n_vox)]
+    packets = [from_other_core(packet, (0, d)) for d in range(1, n_vox)]
     kw, kw_other = (call(functools.partial(applied_kernel, layers), k_shape, b) for b in (block, block_other))
     cut, cut_halo = call(
         functools.partial(spread_kernel, layers, rows),

time: 34 us -> 33.2 us (0.976)
  starting transfers between devices: 15.9 us -> 15.2 us
    ppermute x12 -> x9, starting transfers between devices: 15.2 us -> 13.4 us  [from_other_core(): return lax.ppermute(x, ('dp', 'vox'), route)]
    ppermute x2 -> x5, starting transfers between devices: 0.69 us -> 1.76 us  [from_partner(): lax.ppermute(x, axis, [(i, i ^ distance) for i in range(lax.axis_size(axi...]
    ppermute x12 -> x9, waiting for transfers between devices: 11.7 us -> 11.5 us  [from_other_core(): return lax.ppermute(x, ('dp', 'vox'), route)]
  transfers between devices with their start and end apart: 14 -> 14, of which waited for: 10 -> 8; matrix products, arithmetic and copies ran while one was open for 2% -> 2% of each run, Pallas kernels for 3% -> 3%
where the time goes in v7:
time: 33.2 us; the launch traced here: 33 us
  starting transfers between devices  15.2 us (46%)
  waiting for transfers between devices  12.1 us (36%)
  Pallas kernels  4.46 us (13%)
  between operations  0.7 us (2%)
  local copies, waits for them, and re-layouts  0.6 us (2%)
    ppermute x9, starting transfers between devices, from_other_core(): return lax.ppermute(x, ('dp', 'vox'), route)  13.4 us
    ppermute x9, waiting for transfers between devices, from_other_core(): return lax.ppermute(x, ('dp', 'vox'), route)  11.5 us
    pallas_call x9, Pallas kernels, call(): pl.pallas_call(kernel, out_shape=out_shape, in_specs=[pl.BlockSpec(memory...  4.46 us
    ppermute x5, starting transfers between devices, from_partner(): lax.ppermute(x, axis, [(i, i ^ distance) for i in range(lax.axis_size(axi...  1.76 us
  transfers between devices with their start and end apart: 14, of which 8 were waited for; matrix products, arithmetic and copies ran while one was open for 2% of the time, Pallas kernels for 3%

profile of v7, /device:TPU:0, one launch (start us, length us, event | category | flops | bytes accessed | tf_op | source)
XLA Modules:
  0.0 33.0 jit_solution(12922724422775130512)
XLA Ops:
  0.6 1.3 %shard_map.59 = (bf16[64,128]{1,0:T(8,128)(2,1)S(1)}, f32[8,4096]{1,0:T(8,128)S(1)}, bf16[64,4096]{1,0:T(8,128)(2,1)S(1)}) custom-call(f32[8,4096]{1,0:T(8,128)} %wave_hbm.1, bf16[48,4096]{1,0:T(8,128)(2,1)} %k_hbm.1, f32[8,48]{1,0:T(8,128)} %observed_hbm.1), custom_call_target="tpu_custom_call" | custom-call | tf_op jit(solution)/shard_map/pallas_call | solution.py:367
  2.0 0.5 %collective-permute-start = (bf16[64,4096]{1,0:T(8,128)(2,1)S(1)}, bf16[64,4096]{1,0:T(8,128)(2,1)S(1)}, u32[]{:S(2)}, u32[]{:S(2)}) collective-permute-start(bf16[64,4096]{1,0:T(8,128)(2,1)S(1)} %get-tuple-element.15.block_ref), channel_id=1, source_target_pairs={{0,4},{4,0},{8,12},{12,8},{16,20},{20,16},{24,28},{28,24},{1,5},{5... | collective-permute-start | bytes 1572872 | tf_op jit(solution)/shard_map/ppermute | solution.py:332
  2.5 4.7 %collective-permute-start.3 = (bf16[64,128]{1,0:T(8,128)(2,1)S(1)}, bf16[64,128]{1,0:T(8,128)(2,1)S(1)}, u32[]{:S(2)}, u32[]{:S(2)}) collective-permute-start(bf16[64,128]{1,0:T(8,128)(2,1)S(1)} %get-tuple-element.16), channel_id=1, source_target_pairs={{0,7},{1,6},{2,5},{3,4},{4,3},{5,2},{6,1},{7,0},{8,15},{9,14},{10,... | collective-permute-start | bytes 49160 | tf_op jit(solution)/shard_map/ppermute | solution.py:341
  7.2 0.0 collective-permute-start.2
  7.2 0.3 collective-permute-start.1
  7.5 1.1 %collective-permute-done.3.refs_3_ = bf16[64,128]{1,0:T(8,128)(2,1)S(1)} collective-permute-done((bf16[64,128]{1,0:T(8,128)(2,1)S(1)}, bf16[64,128]{1,0:T(8,128)(2,1)S(1)}, u32[]{:S(2)}, u32[]{:S(2)}) %collective-permute-start.3) | collective-permute-done | bytes 16416 | tf_op jit(solution)/shard_map/ppermute | solution.py:341
  8.7 2.6 %collective-permute-done.2.refs_2_ = bf16[64,128]{1,0:T(8,128)(2,1)S(1)} collective-permute-done((bf16[64,128]{1,0:T(8,128)(2,1)S(1)}, bf16[64,128]{1,0:T(8,128)(2,1)S(1)}, u32[]{:S(2)}, u32[]{:S(2)}) %collective-permute-start.2) | collective-permute-done | bytes 16416 | tf_op jit(solution)/shard_map/ppermute | solution.py:341
  11.3 0.0 collective-permute-done.1.refs_1_
  11.3 0.0 collective-permute-done.refs_0_.block_ref.block_other_ref
  11.3 0.2 shard_map.61
  11.5 0.2 collective-permute-start.4
  11.7 0.3 shard_map.62.kw_ref
  11.9 0.3 shard_map.63.kw_other_ref
  12.2 0.0 copy-start
  12.2 0.6 %collective-permute-done.4.mine_ref = f32[64,128]{1,0:T(8,128)S(1)} collective-permute-done((f32[64,128]{1,0:T(8,128)S(1)}, f32[64,128]{1,0:T(8,128)S(1)}, u32[]{:S(2)}, u32[]{:S(2)}) %collective-permute-start.4) | collective-permute-done | bytes 32800 | tf_op jit(solution)/shard_map/ppermute | solution.py:332
  12.8 0.2 shard_map.64.refs_0_
  13.0 1.3 %collective-permute-start.5 = (bf16[8,4224]{1,0:T(8,128)(2,1)S(1)}, bf16[8,4224]{1,0:T(8,128)(2,1)S(1)}, u32[]{:S(2)}, u32[]{:S(2)}) collective-permute-start(bf16[8,4224]{1,0:T(8,128)(2,1)S(1)} %shard_map.64.refs_0_), channel_id=1, source_target_pairs={{0,20},{1,21},{2,22},{3,23},{4,8},{5,9},{6,10},{7,11},{8,28},{9,29... | collective-permute-start | bytes 202760 | tf_op jit(solution)/shard_map/ppermute | solution.py:341
  14.4 1.4 %collective-permute-start.7 = (bf16[8,4224]{1,0:T(8,128)(2,1)S(1)}, bf16[8,4224]{1,0:T(8,128)(2,1)S(1)}, u32[]{:S(2)}, u32[]{:S(2)}) collective-permute-start(bf16[8,4224]{1,0:T(8,128)(2,1)S(1)} %shard_map.64.refs_0_), channel_id=1, source_target_pairs={{0,28},{1,29},{2,30},{3,31},{4,24},{5,25},{6,26},{7,27},{8,20},{9,... | collective-permute-start | bytes 202760 | tf_op jit(solution)/shard_map/ppermute | solution.py:341
  15.8 1.0 %collective-permute-done.5.refs_1_ = bf16[8,4224]{1,0:T(8,128)(2,1)S(1)} collective-permute-done((bf16[8,4224]{1,0:T(8,128)(2,1)S(1)}, bf16[8,4224]{1,0:T(8,128)(2,1)S(1)}, u32[]{:S(2)}, u32[]{:S(2)}) %collective-permute-start.5) | collective-permute-done | bytes 67616 | tf_op jit(solution)/shard_map/ppermute | solution.py:341
  16.8 0.2 collective-permute-start.6
  16.9 0.0 copy-done
  16.9 0.4 %shard_map.60 = (f32[8,4096]{1,0:T(8,128)S(1)}, f32[8,128]{1,0:T(8,128)S(1)}) custom-call(f32[8,2,16]{2,1,0:T(2,128)S(1)} %bitcast.1), custom_call_target="tpu_custom_call" | custom-call | tf_op jit(solution)/shard_map/pallas_call | solution.py:367
  17.3 1.9 %collective-permute-done.7.refs_3_ = bf16[8,4224]{1,0:T(8,128)(2,1)S(1)} collective-permute-done((bf16[8,4224]{1,0:T(8,128)(2,1)S(1)}, bf16[8,4224]{1,0:T(8,128)(2,1)S(1)}, u32[]{:S(2)}, u32[]{:S(2)}) %collective-permute-start.7) | collective-permute-done | bytes 67616 | tf_op jit(solution)/shard_map/ppermute | solution.py:341
  19.3 0.0 collective-permute-done.6.refs_2_
  19.3 0.6 %shard_map.65 = (f32[8,4096]{1,0:T(8,128)S(1)}, f32[8,128]{1,0:T(8,128)S(1)}) custom-call(f32[8,4096]{1,0:T(8,128)S(1)} %get-tuple-element.13.wave_ref, f32[8,4096]{1,0:T(8,128)S(1)} %get-tuple-element.14.cut_ref, f32[8,128]{1,0:T(8,128)S(1)} %get-tuple-element.17.halo_ref, f32[8,128]{1,0:T(8,128)S(1)} %get-tuple-element.18.cut_halo_ref, ...), custom_call_target="tpu_custom_call" | custom-call | tf_op jit(solution)/shard_map/pallas_call | solution.py:367
  19.9 1.9 %collective-permute-start.8 = (f32[8,128]{1,0:T(8,128)S(1)}, f32[8,128]{1,0:T(8,128)S(1)}, u32[]{:S(2)}, u32[]{:S(2)}) collective-permute-start(f32[8,128]{1,0:T(8,128)S(1)} %get-tuple-element.21.refs_0_), channel_id=1, source_target_pairs={{0,6},{1,7},{2,4},{3,5},{4,1},{5,0},{6,3},{7,2},{8,14},{9,15},{10,... | collective-permute-start | bytes 12296 | tf_op jit(solution)/shard_map/ppermute | solution.py:341
  21.8 1.4 %collective-permute-start.10 = (f32[8,128]{1,0:T(8,128)S(1)}, f32[8,128]{1,0:T(8,128)S(1)}, u32[]{:S(2)}, u32[]{:S(2)}) collective-permute-start(f32[8,128]{1,0:T(8,128)S(1)} %get-tuple-element.21.refs_0_), channel_id=1, source_target_pairs={{0,7},{1,6},{2,5},{3,4},{4,3},{5,2},{6,1},{7,0},{8,15},{9,14},{10,... | collective-permute-start | bytes 12296 | tf_op jit(solution)/shard_map/ppermute | solution.py:341
  23.2 0.0 collective-permute-done.8.refs_1_
  23.2 0.9 %collective-permute-start.9 = (f32[8,128]{1,0:T(8,128)S(1)}, f32[8,128]{1,0:T(8,128)S(1)}, u32[]{:S(2)}, u32[]{:S(2)}) collective-permute-start(f32[8,128]{1,0:T(8,128)S(1)} %collective-permute-done.8.refs_1_), channel_id=1, source_target_pairs={{0,4},{4,0},{8,12},{12,8},{16,20},{20,16},{24,28},{28,24},{1,5},{5... | collective-permute-start | bytes 12296 | tf_op jit(solution)/shard_map/ppermute | solution.py:332
  24.1 2.5 %collective-permute-done.10.refs_3_ = f32[8,128]{1,0:T(8,128)S(1)} collective-permute-done((f32[8,128]{1,0:T(8,128)S(1)}, f32[8,128]{1,0:T(8,128)S(1)}, u32[]{:S(2)}, u32[]{:S(2)}) %collective-permute-start.10) | collective-permute-done | bytes 4128 | tf_op jit(solution)/shard_map/ppermute | solution.py:341
  26.6 0.0 collective-permute-done.9.refs_2_
  26.6 0.4 %shard_map.66 = (bf16[8,4224]{1,0:T(8,128)(2,1)S(1)}, f32[8,48]{1,0:T(8,128)S(1)}) custom-call(f32[64,128]{1,0:T(8,128)S(1)} %collective-permute-done.4.mine_ref, f32[64,128]{1,0:T(8,128)S(1)} %get-tuple-element.19.other_ref, bf16[48,4096]{1,0:T(8,128)(2,1)S(1)} %shard_map.62.kw_ref, bf16[48,4096]{1,0:T(8,128)(2,1)S(1)} %shard_map.63.kw_other_ref, ...), custom_call_target="tpu_custom_call" | custom-call | tf_op jit(solution)/shard_map/pallas_call | solution.py:367
  27.0 0.1 collective-permute-start.11
  27.0 2.3 %collective-permute-start.13 = (bf16[8,4224]{1,0:T(8,128)(2,1)S(1)}, bf16[8,4224]{1,0:T(8,128)(2,1)S(1)}, u32[]{:S(2)}, u32[]{:S(2)}) collective-permute-start(bf16[8,4224]{1,0:T(8,128)(2,1)S(1)} %get-tuple-element.22.refs_0_), channel_id=1, source_target_pairs={{0,28},{1,29},{2,30},{3,31},{4,24},{5,25},{6,26},{7,27},{8,20},{9,... | collective-permute-start | bytes 202760 | tf_op jit(solution)/shard_map/ppermute | solution.py:341
  29.3 1.4 %collective-permute-done.11.refs_1_ = bf16[8,4224]{1,0:T(8,128)(2,1)S(1)} collective-permute-done((bf16[8,4224]{1,0:T(8,128)(2,1)S(1)}, bf16[8,4224]{1,0:T(8,128)(2,1)S(1)}, u32[]{:S(2)}, u32[]{:S(2)}) %collective-permute-start.11) | collective-permute-done | bytes 67616 | tf_op jit(solution)/shard_map/ppermute | solution.py:341
  30.7 0.0 collective-permute-start.12
  30.7 0.6 %copy.6 = f32[8,48]{1,0:T(8,128)} copy(f32[8,48]{1,0:T(8,128)S(1)} %get-tuple-element.25) | data formatting | bytes 3072
  31.3 0.9 %collective-permute-done.13.refs_3_ = bf16[8,4224]{1,0:T(8,128)(2,1)S(1)} collective-permute-done((bf16[8,4224]{1,0:T(8,128)(2,1)S(1)}, bf16[8,4224]{1,0:T(8,128)(2,1)S(1)}, u32[]{:S(2)}, u32[]{:S(2)}) %collective-permute-start.13) | collective-permute-done | bytes 67616 | tf_op jit(solution)/shard_map/ppermute | solution.py:341
  32.2 0.0 collective-permute-done.12.refs_2_
  32.2 0.8 %shard_map.67 = f32[8,4096]{1,0:T(8,128)} custom-call(f32[8,4096]{1,0:T(8,128)S(1)} %get-tuple-element.20.wave_ref, f32[8,4096]{1,0:T(8,128)S(1)} %get-tuple-element.14.cut_ref, bf16[8,4224]{1,0:T(8,128)(2,1)S(1)} %get-tuple-element.22.refs_0_, bf16[8,4224]{1,0:T(8,128)(2,1)S(1)} %collective-permute-done.11.refs_1_, ...), custom_call_target="tpu_custom_call" | custom-call | tf_op jit(solution)/shard_map/pallas_call | solution.py:367
Async XLA Ops:
  2.0 9.3 %collective-permute-start = (bf16[64,4096]{1,0:T(8,128)(2,1)S(1)}, bf16[64,4096]{1,0:T(8,128)(2,1)S(1)}, u32[]{:S(2)}, u32[]{:S(2)}) collective-permute-start(bf16[64,4096]{1,0:T(8,128)(2,1)S(1)} %get-tuple-element.15.block_ref), channel_id=1, source_target_pairs={{0,4},{4,0},{8,12},{12,8},{16,20},{20,16},{24,28},{28,24},{1,5},{5... | collective-permute-start | bytes 1572872 | tf_op jit(solution)/shard_map/ppermute | solution.py:332
  2.5 6.2 %collective-permute-start.3 = (bf16[64,128]{1,0:T(8,128)(2,1)S(1)}, bf16[64,128]{1,0:T(8,128)(2,1)S(1)}, u32[]{:S(2)}, u32[]{:S(2)}) collective-permute-start(bf16[64,128]{1,0:T(8,128)(2,1)S(1)} %get-tuple-element.16), channel_id=1, source_target_pairs={{0,7},{1,6},{2,5},{3,4},{4,3},{5,2},{6,1},{7,0},{8,15},{9,14},{10,... | collective-permute-start | bytes 49160 | tf_op jit(solution)/shard_map/ppermute | solution.py:341
  7.2 4.1 %collective-permute-start.2 = (bf16[64,128]{1,0:T(8,128)(2,1)S(1)}, bf16[64,128]{1,0:T(8,128)(2,1)S(1)}, u32[]{:S(2)}, u32[]{:S(2)}) collective-permute-start(bf16[64,128]{1,0:T(8,128)(2,1)S(1)} %get-tuple-element.16), channel_id=1, source_target_pairs={{0,6},{1,7},{2,4},{3,5},{4,2},{5,3},{6,0},{7,1},{8,14},{9,15},{10,... | collective-permute-start | bytes 49160 | tf_op jit(solution)/shard_map/ppermute | solution.py:341
  7.2 4.1 %collective-permute-start.1 = (bf16[64,128]{1,0:T(8,128)(2,1)S(1)}, bf16[64,128]{1,0:T(8,128)(2,1)S(1)}, u32[]{:S(2)}, u32[]{:S(2)}) collective-permute-start(bf16[64,128]{1,0:T(8,128)(2,1)S(1)} %get-tuple-element.16), channel_id=1, source_target_pairs={{0,5},{1,4},{2,7},{3,6},{4,1},{5,0},{6,3},{7,2},{8,13},{9,12},{10,... | collective-permute-start | bytes 49160 | tf_op jit(solution)/shard_map/ppermute | solution.py:341
  11.5 1.3 %collective-permute-start.4 = (f32[64,128]{1,0:T(8,128)S(1)}, f32[64,128]{1,0:T(8,128)S(1)}, u32[]{:S(2)}, u32[]{:S(2)}) collective-permute-start(f32[64,128]{1,0:T(8,128)S(1)} %get-tuple-element.19.other_ref), channel_id=1, source_target_pairs={{0,4},{4,0},{8,12},{12,8},{16,20},{20,16},{24,28},{28,24},{1,5},{5... | collective-permute-start | bytes 98312 | tf_op jit(solution)/shard_map/ppermute | solution.py:332
  12.2 4.7 %copy-start = (f32[8,16,2]{1,2,0:T(2,128)S(1)}, f32[8,16,2]{1,2,0:T(2,128)}, u32[]{:S(2)}) copy-start(f32[8,16,2]{1,2,0:T(2,128)} %param.7) | copy-start | bytes 3076
  13.0 3.8 %collective-permute-start.5 = (bf16[8,4224]{1,0:T(8,128)(2,1)S(1)}, bf16[8,4224]{1,0:T(8,128)(2,1)S(1)}, u32[]{:S(2)}, u32[]{:S(2)}) collective-permute-start(bf16[8,4224]{1,0:T(8,128)(2,1)S(1)} %shard_map.64.refs_0_), channel_id=1, source_target_pairs={{0,20},{1,21},{2,22},{3,23},{4,8},{5,9},{6,10},{7,11},{8,28},{9,29... | collective-permute-start | bytes 202760 | tf_op jit(solution)/shard_map/ppermute | solution.py:341
  14.4 4.9 %collective-permute-start.7 = (bf16[8,4224]{1,0:T(8,128)(2,1)S(1)}, bf16[8,4224]{1,0:T(8,128)(2,1)S(1)}, u32[]{:S(2)}, u32[]{:S(2)}) collective-permute-start(bf16[8,4224]{1,0:T(8,128)(2,1)S(1)} %shard_map.64.refs_0_), channel_id=1, source_target_pairs={{0,28},{1,29},{2,30},{3,31},{4,24},{5,25},{6,26},{7,27},{8,20},{9,... | collective-permute-start | bytes 202760 | tf_op jit(solution)/shard_map/ppermute | solution.py:341
  16.8 2.5 %collective-permute-start.6 = (bf16[8,4224]{1,0:T(8,128)(2,1)S(1)}, bf16[8,4224]{1,0:T(8,128)(2,1)S(1)}, u32[]{:S(2)}, u32[]{:S(2)}) collective-permute-start(bf16[8,4224]{1,0:T(8,128)(2,1)S(1)} %collective-permute-done.5.refs_1_), channel_id=1, source_target_pairs={{0,4},{4,0},{8,12},{12,8},{16,20},{20,16},{24,28},{28,24},{1,5},{5... | collective-permute-start | bytes 202760 | tf_op jit(solution)/shard_map/ppermute | solution.py:332
  19.9 3.3 %collective-permute-start.8 = (f32[8,128]{1,0:T(8,128)S(1)}, f32[8,128]{1,0:T(8,128)S(1)}, u32[]{:S(2)}, u32[]{:S(2)}) collective-permute-start(f32[8,128]{1,0:T(8,128)S(1)} %get-tuple-element.21.refs_0_), channel_id=1, source_target_pairs={{0,6},{1,7},{2,4},{3,5},{4,1},{5,0},{6,3},{7,2},{8,14},{9,15},{10,... | collective-permute-start | bytes 12296 | tf_op jit(solution)/shard_map/ppermute | solution.py:341
  21.8 4.8 %collective-permute-start.10 = (f32[8,128]{1,0:T(8,128)S(1)}, f32[8,128]{1,0:T(8,128)S(1)}, u32[]{:S(2)}, u32[]{:S(2)}) collective-permute-start(f32[8,128]{1,0:T(8,128)S(1)} %get-tuple-element.21.refs_0_), channel_id=1, source_target_pairs={{0,7},{1,6},{2,5},{3,4},{4,3},{5,2},{6,1},{7,0},{8,15},{9,14},{10,... | collective-permute-start | bytes 12296 | tf_op jit(solution)/shard_map/ppermute | solution.py:341
  23.2 3.4 %collective-permute-start.9 = (f32[8,128]{1,0:T(8,128)S(1)}, f32[8,128]{1,0:T(8,128)S(1)}, u32[]{:S(2)}, u32[]{:S(2)}) collective-permute-start(f32[8,128]{1,0:T(8,128)S(1)} %collective-permute-done.8.refs_1_), channel_id=1, source_target_pairs={{0,4},{4,0},{8,12},{12,8},{16,20},{20,16},{24,28},{28,24},{1,5},{5... | collective-permute-start | bytes 12296 | tf_op jit(solution)/shard_map/ppermute | solution.py:332
  27.0 3.8 %collective-permute-start.11 = (bf16[8,4224]{1,0:T(8,128)(2,1)S(1)}, bf16[8,4224]{1,0:T(8,128)(2,1)S(1)}, u32[]{:S(2)}, u32[]{:S(2)}) collective-permute-start(bf16[8,4224]{1,0:T(8,128)(2,1)S(1)} %get-tuple-element.22.refs_0_), channel_id=1, source_target_pairs={{0,20},{1,21},{2,22},{3,23},{4,8},{5,9},{6,10},{7,11},{8,28},{9,29... | collective-permute-start | bytes 202760 | tf_op jit(solution)/shard_map/ppermute | solution.py:341
  27.0 5.2 %collective-permute-start.13 = (bf16[8,4224]{1,0:T(8,128)(2,1)S(1)}, bf16[8,4224]{1,0:T(8,128)(2,1)S(1)}, u32[]{:S(2)}, u32[]{:S(2)}) collective-permute-start(bf16[8,4224]{1,0:T(8,128)(2,1)S(1)} %get-tuple-element.22.refs_0_), channel_id=1, source_target_pairs={{0,28},{1,29},{2,30},{3,31},{4,24},{5,25},{6,26},{7,27},{8,20},{9,... | collective-permute-start | bytes 202760 | tf_op jit(solution)/shard_map/ppermute | solution.py:341
  30.7 1.5 %collective-permute-start.12 = (bf16[8,4224]{1,0:T(8,128)(2,1)S(1)}, bf16[8,4224]{1,0:T(8,128)(2,1)S(1)}, u32[]{:S(2)}, u32[]{:S(2)}) collective-permute-start(bf16[8,4224]{1,0:T(8,128)(2,1)S(1)} %collective-permute-done.11.refs_1_), channel_id=1, source_target_pairs={{0,4},{4,0},{8,12},{12,8},{16,20},{20,16},{24,28},{28,24},{1,5},{5... | collective-permute-start | bytes 202760 | tf_op jit(solution)/shard_map/ppermute | solution.py:332

commit v8 on v7

--- a/solution.py
+++ b/solution.py
@@ -260,12 +260,14 @@
     back_projected(core(mine_ref, kw_ref), core(other_ref, kw_other_ref), g_ref)
 
 
-def added(shares):
+def added(shares, swapped=False):
     if len(shares) < 4:
         return sum(shares[1:], shares[0])
-    own, near, swapped, far = shares
-    is_first = lax.rem(lax.axis_index("dp"), 2) == 0
-    return (own + jnp.where(is_first, near, swapped)) + (jnp.where(is_first, swapped, near) + far)
+    own, near, middle, far = shares
+    if swapped:
+        is_first = lax.rem(lax.axis_index("dp"), 2) == 0
+        near, middle = jnp.where(is_first, near, middle), jnp.where(is_first, middle, near)
+    return (own + near) + (middle + far)
 
 
 def at_ends(tile, layers, base):
@@ -275,8 +277,8 @@
 def stepped(layers, base, wave_ref, cut_ref, g_refs):
     width = wave_ref.shape[1]
     gradients = [stacked(g, layers) for g in g_refs]
-    smooth_g, detail_g = (added([g[p] for g in gradients]) for p in range(2))
-    edge = added([g[:, width:].astype(F32) for g in g_refs])
+    smooth_g, detail_g = (added([g[p] for g in gradients], True) for p in range(2))
+    edge = added([g[:, width:].astype(F32) for g in g_refs], True)
     ends = at_ends(edge, layers, base)
     lane = lanes_of(ends.shape)
     smooth_g += jnp.where(lane == 0, 0.25 * ends, jnp.where(lane == LANES - 1, -0.125 * ends, 0.0))
@@ -341,26 +343,31 @@
     return lax.ppermute(x, ("dp", "vox"), route)
 
 
-def shares_of(x, size, step):
+def all_shares(x, step):
+    return [x] + [from_other_core(x, step(n)) for n in (1, 2, 3)]
+
+
+def swapped_shares(x, step):
+    fetched = from_other_core(x, step(1), step(2))
+    return [x, fetched, from_partner(fetched, "dp", 1), from_other_core(x, step(3))]
+
+
+def shares_over(x, size, step, four, **how):
     lowest = 1
-    while True:
-        near, middle, far = (step(lowest * n) for n in (1, 2, 3))
-        if size < 4:
-            return [x] + [from_other_core(x, near)] * (size - 1)
-        fetched = from_other_core(x, near, middle)
-        shares = [x, fetched, from_partner(fetched, "dp", 1), from_other_core(x, far)]
-        if size == 4:
-            return shares
-        x = added([s.astype(F32) for s in shares]).astype(x.dtype)
+    while size > 4:
+        x = added([s.astype(F32) for s in four(x, lambda n: step(lowest * n))], **how).astype(x.dtype)
         lowest, size = lowest * 4, size // 4
+    if size == 4:
+        return four(x, lambda n: step(lowest * n))
+    return [x] + [from_other_core(x, step(lowest))] * (size - 1)
 
 
 def over_chips(x):
-    return shares_of(x, lax.axis_size("dp") // 2, lambda n: (n, 0))
+    return shares_over(x, lax.axis_size("dp") // 2, lambda n: (n, 0), swapped_shares, swapped=True)
 
 
 def over_vox(x):
-    return shares_of(x, lax.axis_size("vox"), lambda n: (0, n))
+    return shares_over(x, lax.axis_size("vox"), lambda n: (0, n), all_shares)
 
 
 def call(kernel, out_shape, *args, scratch=(), space=pltpu.VMEM):

time: 33.2 us -> 32 us (0.964)
  waiting for transfers between devices: 12.1 us -> 10.7 us
    ppermute x9 -> x10, waiting for transfers between devices: 11.5 us -> 10.1 us  [from_other_core(): return lax.ppermute(x, ('dp', 'vox'), route)]
    ppermute x9 -> x10, starting transfers between devices: 13.4 us -> 14.3 us  [from_other_core(): return lax.ppermute(x, ('dp', 'vox'), route)]
    ppermute x5 -> x4, starting transfers between devices: 1.76 us -> 1.12 us  [from_partner(): lax.ppermute(x, axis, [(i, i ^ distance) for i in range(lax.axis_size(axi...]
  transfers between devices with their start and end apart: 14 -> 14, of which waited for: 8 -> 9; matrix products, arithmetic and copies ran while one was open for 2% -> 2% of each run, Pallas kernels for 3% -> 3%
where the time goes in v8:
time: 32 us; the launch traced here: 31.9 us
  starting transfers between devices  15.4 us (48%)
  waiting for transfers between devices  10.7 us (33%)
  Pallas kernels  4.46 us (14%)
  between operations  0.69 us (2%)
  local copies, waits for them, and re-layouts  0.6 us (2%)
    ppermute x10, starting transfers between devices, from_other_core(): return lax.ppermute(x, ('dp', 'vox'), route)  14.3 us
    ppermute x10, waiting for transfers between devices, from_other_core(): return lax.ppermute(x, ('dp', 'vox'), route)  10.1 us
    pallas_call x9, Pallas kernels, call(): pl.pallas_call(kernel, out_shape=out_shape, in_specs=[pl.BlockSpec(memory...  4.46 us
    ppermute x4, starting transfers between devices, from_partner(): lax.ppermute(x, axis, [(i, i ^ distance) for i in range(lax.axis_size(axi...  1.12 us
  transfers between devices with their start and end apart: 14, of which 9 were waited for; matrix products, arithmetic and copies ran while one was open for 2% of the time, Pallas kernels for 3%

profile of v8, /device:TPU:0, one launch (start us, length us, event | category | flops | bytes accessed | tf_op | source)
XLA Modules:
  0.0 31.9 jit_solution(14401688922773388092)
XLA Ops:
  0.6 1.3 %shard_map.59 = (bf16[64,128]{1,0:T(8,128)(2,1)S(1)}, f32[8,4096]{1,0:T(8,128)S(1)}, bf16[64,4096]{1,0:T(8,128)(2,1)S(1)}) custom-call(f32[8,4096]{1,0:T(8,128)} %wave_hbm.1, bf16[48,4096]{1,0:T(8,128)(2,1)} %k_hbm.1, f32[8,48]{1,0:T(8,128)} %observed_hbm.1), custom_call_target="tpu_custom_call" | custom-call | tf_op jit(solution)/shard_map/pallas_call | solution.py:374
  2.0 0.5 %collective-permute-start = (bf16[64,4096]{1,0:T(8,128)(2,1)S(1)}, bf16[64,4096]{1,0:T(8,128)(2,1)S(1)}, u32[]{:S(2)}, u32[]{:S(2)}) collective-permute-start(bf16[64,4096]{1,0:T(8,128)(2,1)S(1)} %get-tuple-element.15.block_ref), channel_id=1, source_target_pairs={{0,4},{4,0},{8,12},{12,8},{16,20},{20,16},{24,28},{28,24},{1,5},{5... | collective-permute-start | bytes 1572872 | tf_op jit(solution)/shard_map/ppermute | solution.py:334
  2.5 4.7 %collective-permute-start.3 = (bf16[64,128]{1,0:T(8,128)(2,1)S(1)}, bf16[64,128]{1,0:T(8,128)(2,1)S(1)}, u32[]{:S(2)}, u32[]{:S(2)}) collective-permute-start(bf16[64,128]{1,0:T(8,128)(2,1)S(1)} %get-tuple-element.16), channel_id=1, source_target_pairs={{0,7},{1,6},{2,5},{3,4},{4,3},{5,2},{6,1},{7,0},{8,15},{9,14},{10,... | collective-permute-start | bytes 49160 | tf_op jit(solution)/shard_map/ppermute | solution.py:343
  7.2 0.0 collective-permute-start.2
  7.2 0.3 collective-permute-start.1
  7.5 1.1 %collective-permute-done.3.refs_3_ = bf16[64,128]{1,0:T(8,128)(2,1)S(1)} collective-permute-done((bf16[64,128]{1,0:T(8,128)(2,1)S(1)}, bf16[64,128]{1,0:T(8,128)(2,1)S(1)}, u32[]{:S(2)}, u32[]{:S(2)}) %collective-permute-start.3) | collective-permute-done | bytes 16416 | tf_op jit(solution)/shard_map/ppermute | solution.py:343
  8.7 2.6 %collective-permute-done.2.refs_2_ = bf16[64,128]{1,0:T(8,128)(2,1)S(1)} collective-permute-done((bf16[64,128]{1,0:T(8,128)(2,1)S(1)}, bf16[64,128]{1,0:T(8,128)(2,1)S(1)}, u32[]{:S(2)}, u32[]{:S(2)}) %collective-permute-start.2) | collective-permute-done | bytes 16416 | tf_op jit(solution)/shard_map/ppermute | solution.py:343
  11.3 0.0 collective-permute-done.1.refs_1_
  11.3 0.0 collective-permute-done.refs_0_.block_ref.block_other_ref
  11.3 0.2 shard_map.61
  11.5 0.2 collective-permute-start.4
  11.7 0.3 shard_map.62.kw_ref
  11.9 0.3 shard_map.63.kw_other_ref
  12.2 0.0 copy-start
  12.2 0.6 %collective-permute-done.4.mine_ref = f32[64,128]{1,0:T(8,128)S(1)} collective-permute-done((f32[64,128]{1,0:T(8,128)S(1)}, f32[64,128]{1,0:T(8,128)S(1)}, u32[]{:S(2)}, u32[]{:S(2)}) %collective-permute-start.4) | collective-permute-done | bytes 32800 | tf_op jit(solution)/shard_map/ppermute | solution.py:334
  12.8 0.2 shard_map.64.refs_0_
  13.0 1.3 %collective-permute-start.5 = (bf16[8,4224]{1,0:T(8,128)(2,1)S(1)}, bf16[8,4224]{1,0:T(8,128)(2,1)S(1)}, u32[]{:S(2)}, u32[]{:S(2)}) collective-permute-start(bf16[8,4224]{1,0:T(8,128)(2,1)S(1)} %shard_map.64.refs_0_), channel_id=1, source_target_pairs={{0,20},{1,21},{2,22},{3,23},{4,8},{5,9},{6,10},{7,11},{8,28},{9,29... | collective-permute-start | bytes 202760 | tf_op jit(solution)/shard_map/ppermute | solution.py:343
  14.4 1.4 %collective-permute-start.7 = (bf16[8,4224]{1,0:T(8,128)(2,1)S(1)}, bf16[8,4224]{1,0:T(8,128)(2,1)S(1)}, u32[]{:S(2)}, u32[]{:S(2)}) collective-permute-start(bf16[8,4224]{1,0:T(8,128)(2,1)S(1)} %shard_map.64.refs_0_), channel_id=1, source_target_pairs={{0,28},{1,29},{2,30},{3,31},{4,24},{5,25},{6,26},{7,27},{8,20},{9,... | collective-permute-start | bytes 202760 | tf_op jit(solution)/shard_map/ppermute | solution.py:343
  15.8 1.0 %collective-permute-done.5.refs_1_ = bf16[8,4224]{1,0:T(8,128)(2,1)S(1)} collective-permute-done((bf16[8,4224]{1,0:T(8,128)(2,1)S(1)}, bf16[8,4224]{1,0:T(8,128)(2,1)S(1)}, u32[]{:S(2)}, u32[]{:S(2)}) %collective-permute-start.5) | collective-permute-done | bytes 67616 | tf_op jit(solution)/shard_map/ppermute | solution.py:343
  16.8 0.2 collective-permute-start.6
  16.9 0.0 copy-done
  16.9 0.4 %shard_map.60 = (f32[8,4096]{1,0:T(8,128)S(1)}, f32[8,128]{1,0:T(8,128)S(1)}) custom-call(f32[8,2,16]{2,1,0:T(2,128)S(1)} %bitcast.1), custom_call_target="tpu_custom_call" | custom-call | tf_op jit(solution)/shard_map/pallas_call | solution.py:374
  17.3 1.9 %collective-permute-done.7.refs_3_ = bf16[8,4224]{1,0:T(8,128)(2,1)S(1)} collective-permute-done((bf16[8,4224]{1,0:T(8,128)(2,1)S(1)}, bf16[8,4224]{1,0:T(8,128)(2,1)S(1)}, u32[]{:S(2)}, u32[]{:S(2)}) %collective-permute-start.7) | collective-permute-done | bytes 67616 | tf_op jit(solution)/shard_map/ppermute | solution.py:343
  19.3 0.0 collective-permute-done.6.refs_2_
  19.3 0.6 %shard_map.65 = (f32[8,4096]{1,0:T(8,128)S(1)}, f32[8,128]{1,0:T(8,128)S(1)}) custom-call(f32[8,4096]{1,0:T(8,128)S(1)} %get-tuple-element.13.wave_ref, f32[8,4096]{1,0:T(8,128)S(1)} %get-tuple-element.14.cut_ref, f32[8,128]{1,0:T(8,128)S(1)} %get-tuple-element.17.halo_ref, f32[8,128]{1,0:T(8,128)S(1)} %get-tuple-element.18.cut_halo_ref, ...), custom_call_target="tpu_custom_call" | custom-call | tf_op jit(solution)/shard_map/pallas_call | solution.py:374
  19.9 1.6 %collective-permute-start.10 = (f32[8,128]{1,0:T(8,128)S(1)}, f32[8,128]{1,0:T(8,128)S(1)}, u32[]{:S(2)}, u32[]{:S(2)}) collective-permute-start(f32[8,128]{1,0:T(8,128)S(1)} %get-tuple-element.21.refs_0_), channel_id=1, source_target_pairs={{0,7},{1,6},{2,5},{3,4},{4,3},{5,2},{6,1},{7,0},{8,15},{9,14},{10,... | collective-permute-start | bytes 12296 | tf_op jit(solution)/shard_map/ppermute | solution.py:343
  21.5 0.3 collective-permute-start.9
  21.8 2.1 %collective-permute-start.8 = (f32[8,128]{1,0:T(8,128)S(1)}, f32[8,128]{1,0:T(8,128)S(1)}, u32[]{:S(2)}, u32[]{:S(2)}) collective-permute-start(f32[8,128]{1,0:T(8,128)S(1)} %get-tuple-element.21.refs_0_), channel_id=1, source_target_pairs={{0,5},{1,4},{2,7},{3,6},{4,1},{5,0},{6,3},{7,2},{8,13},{9,12},{10,... | collective-permute-start | bytes 12296 | tf_op jit(solution)/shard_map/ppermute | solution.py:343
  23.9 0.9 %collective-permute-done.10.refs_3_ = f32[8,128]{1,0:T(8,128)S(1)} collective-permute-done((f32[8,128]{1,0:T(8,128)S(1)}, f32[8,128]{1,0:T(8,128)S(1)}, u32[]{:S(2)}, u32[]{:S(2)}) %collective-permute-start.10) | collective-permute-done | bytes 4128 | tf_op jit(solution)/shard_map/ppermute | solution.py:343
  24.8 0.6 %collective-permute-done.9.refs_2_ = f32[8,128]{1,0:T(8,128)S(1)} collective-permute-done((f32[8,128]{1,0:T(8,128)S(1)}, f32[8,128]{1,0:T(8,128)S(1)}, u32[]{:S(2)}, u32[]{:S(2)}) %collective-permute-start.9) | collective-permute-done | bytes 4128 | tf_op jit(solution)/shard_map/ppermute | solution.py:343
  25.4 0.0 collective-permute-done.8.refs_1_
  25.4 0.4 %shard_map.66 = (bf16[8,4224]{1,0:T(8,128)(2,1)S(1)}, f32[8,48]{1,0:T(8,128)S(1)}) custom-call(f32[64,128]{1,0:T(8,128)S(1)} %collective-permute-done.4.mine_ref, f32[64,128]{1,0:T(8,128)S(1)} %get-tuple-element.19.other_ref, bf16[48,4096]{1,0:T(8,128)(2,1)S(1)} %shard_map.62.kw_ref, bf16[48,4096]{1,0:T(8,128)(2,1)S(1)} %shard_map.63.kw_other_ref, ...), custom_call_target="tpu_custom_call" | custom-call | tf_op jit(solution)/shard_map/pallas_call | solution.py:374
  25.8 0.6 %collective-permute-start.11 = (bf16[8,4224]{1,0:T(8,128)(2,1)S(1)}, bf16[8,4224]{1,0:T(8,128)(2,1)S(1)}, u32[]{:S(2)}, u32[]{:S(2)}) collective-permute-start(bf16[8,4224]{1,0:T(8,128)(2,1)S(1)} %get-tuple-element.22.refs_0_), channel_id=1, source_target_pairs={{0,20},{1,21},{2,22},{3,23},{4,8},{5,9},{6,10},{7,11},{8,28},{9,29... | collective-permute-start | bytes 202760 | tf_op jit(solution)/shard_map/ppermute | solution.py:343
  26.4 1.9 %collective-permute-start.13 = (bf16[8,4224]{1,0:T(8,128)(2,1)S(1)}, bf16[8,4224]{1,0:T(8,128)(2,1)S(1)}, u32[]{:S(2)}, u32[]{:S(2)}) collective-permute-start(bf16[8,4224]{1,0:T(8,128)(2,1)S(1)} %get-tuple-element.22.refs_0_), channel_id=1, source_target_pairs={{0,28},{1,29},{2,30},{3,31},{4,24},{5,25},{6,26},{7,27},{8,20},{9,... | collective-permute-start | bytes 202760 | tf_op jit(solution)/shard_map/ppermute | solution.py:343
  28.3 1.2 %collective-permute-done.11.refs_1_ = bf16[8,4224]{1,0:T(8,128)(2,1)S(1)} collective-permute-done((bf16[8,4224]{1,0:T(8,128)(2,1)S(1)}, bf16[8,4224]{1,0:T(8,128)(2,1)S(1)}, u32[]{:S(2)}, u32[]{:S(2)}) %collective-permute-start.11) | collective-permute-done | bytes 67616 | tf_op jit(solution)/shard_map/ppermute | solution.py:343
  29.5 0.3 collective-permute-start.12
  29.8 0.6 %copy.6 = f32[8,48]{1,0:T(8,128)} copy(f32[8,48]{1,0:T(8,128)S(1)} %get-tuple-element.25) | data formatting | bytes 3072
  30.4 0.7 %collective-permute-done.13.refs_3_ = bf16[8,4224]{1,0:T(8,128)(2,1)S(1)} collective-permute-done((bf16[8,4224]{1,0:T(8,128)(2,1)S(1)}, bf16[8,4224]{1,0:T(8,128)(2,1)S(1)}, u32[]{:S(2)}, u32[]{:S(2)}) %collective-permute-start.13) | collective-permute-done | bytes 67616 | tf_op jit(solution)/shard_map/ppermute | solution.py:343
  31.1 0.0 collective-permute-done.12.refs_2_
  31.1 0.8 %shard_map.67 = f32[8,4096]{1,0:T(8,128)} custom-call(f32[8,4096]{1,0:T(8,128)S(1)} %get-tuple-element.20.wave_ref, f32[8,4096]{1,0:T(8,128)S(1)} %get-tuple-element.14.cut_ref, bf16[8,4224]{1,0:T(8,128)(2,1)S(1)} %get-tuple-element.22.refs_0_, bf16[8,4224]{1,0:T(8,128)(2,1)S(1)} %collective-permute-done.11.refs_1_, ...), custom_call_target="tpu_custom_call" | custom-call | tf_op jit(solution)/shard_map/pallas_call | solution.py:374
Async XLA Ops:
  2.0 9.3 %collective-permute-start = (bf16[64,4096]{1,0:T(8,128)(2,1)S(1)}, bf16[64,4096]{1,0:T(8,128)(2,1)S(1)}, u32[]{:S(2)}, u32[]{:S(2)}) collective-permute-start(bf16[64,4096]{1,0:T(8,128)(2,1)S(1)} %get-tuple-element.15.block_ref), channel_id=1, source_target_pairs={{0,4},{4,0},{8,12},{12,8},{16,20},{20,16},{24,28},{28,24},{1,5},{5... | collective-permute-start | bytes 1572872 | tf_op jit(solution)/shard_map/ppermute | solution.py:334
  2.5 6.2 %collective-permute-start.3 = (bf16[64,128]{1,0:T(8,128)(2,1)S(1)}, bf16[64,128]{1,0:T(8,128)(2,1)S(1)}, u32[]{:S(2)}, u32[]{:S(2)}) collective-permute-start(bf16[64,128]{1,0:T(8,128)(2,1)S(1)} %get-tuple-element.16), channel_id=1, source_target_pairs={{0,7},{1,6},{2,5},{3,4},{4,3},{5,2},{6,1},{7,0},{8,15},{9,14},{10,... | collective-permute-start | bytes 49160 | tf_op jit(solution)/shard_map/ppermute | solution.py:343
  7.2 4.1 %collective-permute-start.2 = (bf16[64,128]{1,0:T(8,128)(2,1)S(1)}, bf16[64,128]{1,0:T(8,128)(2,1)S(1)}, u32[]{:S(2)}, u32[]{:S(2)}) collective-permute-start(bf16[64,128]{1,0:T(8,128)(2,1)S(1)} %get-tuple-element.16), channel_id=1, source_target_pairs={{0,6},{1,7},{2,4},{3,5},{4,2},{5,3},{6,0},{7,1},{8,14},{9,15},{10,... | collective-permute-start | bytes 49160 | tf_op jit(solution)/shard_map/ppermute | solution.py:343
  7.2 4.1 %collective-permute-start.1 = (bf16[64,128]{1,0:T(8,128)(2,1)S(1)}, bf16[64,128]{1,0:T(8,128)(2,1)S(1)}, u32[]{:S(2)}, u32[]{:S(2)}) collective-permute-start(bf16[64,128]{1,0:T(8,128)(2,1)S(1)} %get-tuple-element.16), channel_id=1, source_target_pairs={{0,5},{1,4},{2,7},{3,6},{4,1},{5,0},{6,3},{7,2},{8,13},{9,12},{10,... | collective-permute-start | bytes 49160 | tf_op jit(solution)/shard_map/ppermute | solution.py:343
  11.5 1.3 %collective-permute-start.4 = (f32[64,128]{1,0:T(8,128)S(1)}, f32[64,128]{1,0:T(8,128)S(1)}, u32[]{:S(2)}, u32[]{:S(2)}) collective-permute-start(f32[64,128]{1,0:T(8,128)S(1)} %get-tuple-element.19.other_ref), channel_id=1, source_target_pairs={{0,4},{4,0},{8,12},{12,8},{16,20},{20,16},{24,28},{28,24},{1,5},{5... | collective-permute-start | bytes 98312 | tf_op jit(solution)/shard_map/ppermute | solution.py:334
  12.2 4.7 %copy-start = (f32[8,16,2]{1,2,0:T(2,128)S(1)}, f32[8,16,2]{1,2,0:T(2,128)}, u32[]{:S(2)}) copy-start(f32[8,16,2]{1,2,0:T(2,128)} %param.7) | copy-start | bytes 3076
  13.0 3.8 %collective-permute-start.5 = (bf16[8,4224]{1,0:T(8,128)(2,1)S(1)}, bf16[8,4224]{1,0:T(8,128)(2,1)S(1)}, u32[]{:S(2)}, u32[]{:S(2)}) collective-permute-start(bf16[8,4224]{1,0:T(8,128)(2,1)S(1)} %shard_map.64.refs_0_), channel_id=1, source_target_pairs={{0,20},{1,21},{2,22},{3,23},{4,8},{5,9},{6,10},{7,11},{8,28},{9,29... | collective-permute-start | bytes 202760 | tf_op jit(solution)/shard_map/ppermute | solution.py:343
  14.4 4.9 %collective-permute-start.7 = (bf16[8,4224]{1,0:T(8,128)(2,1)S(1)}, bf16[8,4224]{1,0:T(8,128)(2,1)S(1)}, u32[]{:S(2)}, u32[]{:S(2)}) collective-permute-start(bf16[8,4224]{1,0:T(8,128)(2,1)S(1)} %shard_map.64.refs_0_), channel_id=1, source_target_pairs={{0,28},{1,29},{2,30},{3,31},{4,24},{5,25},{6,26},{7,27},{8,20},{9,... | collective-permute-start | bytes 202760 | tf_op jit(solution)/shard_map/ppermute | solution.py:343
  16.8 2.5 %collective-permute-start.6 = (bf16[8,4224]{1,0:T(8,128)(2,1)S(1)}, bf16[8,4224]{1,0:T(8,128)(2,1)S(1)}, u32[]{:S(2)}, u32[]{:S(2)}) collective-permute-start(bf16[8,4224]{1,0:T(8,128)(2,1)S(1)} %collective-permute-done.5.refs_1_), channel_id=1, source_target_pairs={{0,4},{4,0},{8,12},{12,8},{16,20},{20,16},{24,28},{28,24},{1,5},{5... | collective-permute-start | bytes 202760 | tf_op jit(solution)/shard_map/ppermute | solution.py:334
  19.9 4.8 %collective-permute-start.10 = (f32[8,128]{1,0:T(8,128)S(1)}, f32[8,128]{1,0:T(8,128)S(1)}, u32[]{:S(2)}, u32[]{:S(2)}) collective-permute-start(f32[8,128]{1,0:T(8,128)S(1)} %get-tuple-element.21.refs_0_), channel_id=1, source_target_pairs={{0,7},{1,6},{2,5},{3,4},{4,3},{5,2},{6,1},{7,0},{8,15},{9,14},{10,... | collective-permute-start | bytes 12296 | tf_op jit(solution)/shard_map/ppermute | solution.py:343
  21.5 3.9 %collective-permute-start.9 = (f32[8,128]{1,0:T(8,128)S(1)}, f32[8,128]{1,0:T(8,128)S(1)}, u32[]{:S(2)}, u32[]{:S(2)}) collective-permute-start(f32[8,128]{1,0:T(8,128)S(1)} %get-tuple-element.21.refs_0_), channel_id=1, source_target_pairs={{0,6},{1,7},{2,4},{3,5},{4,2},{5,3},{6,0},{7,1},{8,14},{9,15},{10,... | collective-permute-start | bytes 12296 | tf_op jit(solution)/shard_map/ppermute | solution.py:343
  21.8 3.6 %collective-permute-start.8 = (f32[8,128]{1,0:T(8,128)S(1)}, f32[8,128]{1,0:T(8,128)S(1)}, u32[]{:S(2)}, u32[]{:S(2)}) collective-permute-start(f32[8,128]{1,0:T(8,128)S(1)} %get-tuple-element.21.refs_0_), channel_id=1, source_target_pairs={{0,5},{1,4},{2,7},{3,6},{4,1},{5,0},{6,3},{7,2},{8,13},{9,12},{10,... | collective-permute-start | bytes 12296 | tf_op jit(solution)/shard_map/ppermute | solution.py:343
  25.8 3.8 %collective-permute-start.11 = (bf16[8,4224]{1,0:T(8,128)(2,1)S(1)}, bf16[8,4224]{1,0:T(8,128)(2,1)S(1)}, u32[]{:S(2)}, u32[]{:S(2)}) collective-permute-start(bf16[8,4224]{1,0:T(8,128)(2,1)S(1)} %get-tuple-element.22.refs_0_), channel_id=1, source_target_pairs={{0,20},{1,21},{2,22},{3,23},{4,8},{5,9},{6,10},{7,11},{8,28},{9,29... | collective-permute-start | bytes 202760 | tf_op jit(solution)/shard_map/ppermute | solution.py:343
  26.4 4.7 %collective-permute-start.13 = (bf16[8,4224]{1,0:T(8,128)(2,1)S(1)}, bf16[8,4224]{1,0:T(8,128)(2,1)S(1)}, u32[]{:S(2)}, u32[]{:S(2)}) collective-permute-start(bf16[8,4224]{1,0:T(8,128)(2,1)S(1)} %get-tuple-element.22.refs_0_), channel_id=1, source_target_pairs={{0,28},{1,29},{2,30},{3,31},{4,24},{5,25},{6,26},{7,27},{8,20},{9,... | collective-permute-start | bytes 202760 | tf_op jit(solution)/shard_map/ppermute | solution.py:343
  29.5 1.6 %collective-permute-start.12 = (bf16[8,4224]{1,0:T(8,128)(2,1)S(1)}, bf16[8,4224]{1,0:T(8,128)(2,1)S(1)}, u32[]{:S(2)}, u32[]{:S(2)}) collective-permute-start(bf16[8,4224]{1,0:T(8,128)(2,1)S(1)} %collective-permute-done.11.refs_1_), channel_id=1, source_target_pairs={{0,4},{4,0},{8,12},{12,8},{16,20},{20,16},{24,28},{28,24},{1,5},{5... | collective-permute-start | bytes 202760 | tf_op jit(solution)/shard_map/ppermute | solution.py:334

commit v9 on v8

--- a/solution.py
+++ b/solution.py
@@ -129,9 +129,25 @@
         block_ref[rows:, i * LANES : (i + 1) * LANES] = part
 
 
-def applied_kernel(layers, block_ref, kw_ref):
-    rows = kw_ref.shape[0]
-    kw_ref[...] = unstacked(*forward_wave(*stacked(block_ref.at[:rows], layers)), rows).astype(BF16)
+def on_first_core():
+    return lax.rem(lax.axis_index("dp"), 2) == 0
+
+
+def applied_kernel(layers, rows, block_ref, other_ref, kw_ref):
+    core = lax.rem(lax.axis_index("dp"), 2)
+    kw_ref[2 * rows :, :] = jnp.zeros((kw_ref.shape[0] - 2 * rows, kw_ref.shape[1]), BF16)
+    for which, source in ((core, block_ref), (1 - core, other_ref)):
+        waves = forward_wave(*stacked(source.at[:rows], layers))
+        kw_ref[pl.ds(pl.multiple_of(which * rows, 16), rows), :] = unstacked(*waves, rows).astype(BF16)
+
+
+def transposing_kernel(rows, block_ref, other_ref, kt_ref):
+    is_first = on_first_core()
+    rest = jnp.zeros((LANES - 2 * rows, LANES), F32)
+    for start in range(0, kt_ref.shape[0], LANES):
+        mine, other = (ref[:rows, start : start + LANES].astype(F32) for ref in (block_ref, other_ref))
+        both = [jnp.where(is_first, mine, other), jnp.where(is_first, other, mine), rest]
+        kt_ref[start : start + LANES, :] = jnp.concatenate(both, axis=0).T.astype(BF16)
 
 
 def spread_kernel(layers, base, threshold_ref, cut_ref, cut_halo_ref):
@@ -223,41 +239,25 @@
     )
 
 
-def in_core_order(mine, other, work):
-    core = lax.rem(lax.axis_index("dp"), 2)
-
-    @pl.when(core == 0)
-    def _():
-        work(mine, other)
-
-    @pl.when(core == 1)
-    def _():
-        work(other, mine)
-
-
-def back_projected(mine, other, g_ref):
-    width = mine[1].shape[1]
-
-    def work(*cores):
-        sent = [residual.astype(BF16) for residual, _, _ in cores]
-        g_ref[:, :width] = sum(
-            jnp.dot(r, k[...], preferred_element_type=F32) for r, (_, k, _) in zip(sent, cores)
-        ).astype(BF16)
-        g_ref[:, width:] = sum(
-            jnp.dot(r, h[...].astype(BF16), preferred_element_type=F32) for r, (_, _, h) in zip(sent, cores)
-        ).astype(BF16)
-
-    in_core_order(mine, other, work)
-
-
-def third_kernel(mine_ref, other_ref, kw_ref, kw_other_ref, g_ref):
-    rows = kw_ref.shape[0]
+def back_projected(residual, kw_ref, columns, g_ref):
+    width = kw_ref.shape[1]
+    sent = residual.astype(BF16)
+    g_ref[:, :width] = jnp.dot(sent, kw_ref[...], preferred_element_type=F32).astype(BF16)
+    g_ref[:, width:] = jnp.dot(sent, columns, preferred_element_type=F32).astype(BF16)
+
+
+def third_kernel(mine_ref, other_ref, kw_ref, g_ref, columns_ref, observed_ref):
     models = g_ref.shape[0]
-
-    def core(ref, k):
-        return ref[rows : rows + models, :rows], k, ref.at[:rows]
-
-    back_projected(core(mine_ref, kw_ref), core(other_ref, kw_other_ref), g_ref)
+    rows = mine_ref.shape[0] - 2 * models
+    is_first = on_first_core()
+    mine, other = mine_ref[...], other_ref[...]
+    first, second = jnp.where(is_first, mine, other), jnp.where(is_first, other, mine)
+    rest = jnp.zeros((LANES - 2 * rows, LANES), F32)
+    columns = jnp.concatenate([first[:rows], second[:rows], rest], axis=0).astype(BF16)
+    columns_ref[...] = columns
+    below = first[rows:] + turned(second[rows:], rows)
+    observed_ref[...] = below[models:]
+    back_projected(below[:models], kw_ref, columns, g_ref)
 
 
 def added(shares, swapped=False):
@@ -265,7 +265,7 @@
         return sum(shares[1:], shares[0])
     own, near, middle, far = shares
     if swapped:
-        is_first = lax.rem(lax.axis_index("dp"), 2) == 0
+        is_first = on_first_core()
         near, middle = jnp.where(is_first, near, middle), jnp.where(is_first, middle, near)
     return (own + near) + (middle + far)
 
@@ -274,60 +274,48 @@
     return jnp.concatenate([turned(tile, -(base + KINDS * layer + 1)) for layer in range(layers)], axis=0)
 
 
-def stepped(layers, base, wave_ref, cut_ref, g_refs):
-    width = wave_ref.shape[1]
+def halo_gradient(g_refs):
+    return added([g[:, g.shape[1] - LANES :].astype(F32) for g in g_refs], True)
+
+
+def stepped(layers, base, wave_ref, cut_ref, g_refs, edge):
     gradients = [stacked(g, layers) for g in g_refs]
     smooth_g, detail_g = (added([g[p] for g in gradients], True) for p in range(2))
-    edge = added([g[:, width:].astype(F32) for g in g_refs], True)
     ends = at_ends(edge, layers, base)
     lane = lanes_of(ends.shape)
     smooth_g += jnp.where(lane == 0, 0.25 * ends, jnp.where(lane == LANES - 1, -0.125 * ends, 0.0))
     detail_g += jnp.where(lane == LANES - 1, -0.5 * ends, 0.0)
-    smooth, detail = (
+    return tuple(
         shrink(w + step_size * g, cut)
         for w, g, cut in zip(stacked(wave_ref, layers), (smooth_g, detail_g), stacked(cut_ref, layers))
     )
-    return smooth, detail, edge
-
-
-def fourth_kernel(layers, base, wave_ref, cut_ref, halo_ref, cut_halo_ref, block_ref, block_other_ref, *refs):
+
+
+def fourth_kernel(layers, base, wave_ref, cut_ref, halo_ref, cut_halo_ref, kt_ref, *refs):
     *g_refs, new_ref, pred_ref = refs
     models = wave_ref.shape[0]
-    rows = base
-    smooth, detail, edge = stepped(layers, base, wave_ref, cut_ref, g_refs)
+    edge = halo_gradient(g_refs)
+    smooth, detail = stepped(layers, base, wave_ref, cut_ref, g_refs, edge)
     new_ref[...] = unstacked(smooth, detail, models)
     halo = shrink(halo_ref[...] + step_size * edge, cut_halo_ref[...])
     next_even = turned(halo, E_NEXT - S_NEXT) - 0.25 * (turned(halo, E_NEXT - D_LAST) + turned(halo, E_NEXT - D_NEXT))
     ends = at_ends(by_kind(lanes_of(halo.shape), base, next_even, halo), layers, base)
     model = unstacked(*inverse_wave(smooth, detail, ends), models).astype(BF16)
-    pred_ref[...] = jnp.zeros_like(pred_ref)
-
-    def work(first, second):
-        pred_ref[:, :rows] = nt_dot(model, first[:rows, :])
-        pred_ref[:, rows : 2 * rows] = nt_dot(model, second[:rows, :])
-
-    in_core_order(block_ref, block_other_ref, work)
-
-
-def fifth_kernel(mine_ref, other_ref, kw_ref, kw_other_ref, *refs):
+    pred_ref[...] = jnp.dot(model, kt_ref[...], preferred_element_type=F32)
+
+
+def fifth_kernel(kw_ref, columns_ref, observed_ref, *refs):
     *shares, g_ref, residual_ref = refs
-    models, rows = residual_ref.shape
-    predicted = added([s[...] for s in shares])
-    first, second = predicted[:, :rows], predicted[:, rows : 2 * rows]
-    is_first = lax.rem(lax.axis_index("dp"), 2) == 0
-
-    def core(ref, k, predicted):
-        return ref[rows + models :, :rows] - predicted, k, ref.at[:rows]
-
-    mine = core(mine_ref, kw_ref, jnp.where(is_first, first, second))
-    residual_ref[...] = mine[0]
-    back_projected(mine, core(other_ref, kw_other_ref, jnp.where(is_first, second, first)), g_ref)
+    rows = residual_ref.shape[1]
+    residual = observed_ref[...] - added([s[...] for s in shares])
+    back_projected(residual, kw_ref, columns_ref[...], g_ref)
+    residual_ref[...] = jnp.where(on_first_core(), residual, turned(residual, -rows))[:, :rows]
 
 
 def sixth_kernel(layers, base, wave_ref, cut_ref, *refs):
     *g_refs, new_ref = refs
-    smooth, detail, _ = stepped(layers, base, wave_ref, cut_ref, g_refs)
-    new_ref[...] = unstacked(smooth, detail, wave_ref.shape[0])
+    waves = stepped(layers, base, wave_ref, cut_ref, g_refs, halo_gradient(g_refs))
+    new_ref[...] = unstacked(*waves, wave_ref.shape[0])
 
 
 def from_partner(x, axis, distance):
@@ -390,7 +378,7 @@
     assert width == 2 * layers * LANES and rows + KINDS * layers <= LANES and 2 * rows <= LANES
     assert packet_rows % (2 * models) == 0 and packet_rows // (2 * models) + 2 <= 2 * layers
     g_shape = pltpu.VMEM((models, width + LANES), BF16)
-    k_shape = pltpu.VMEM((rows, width), BF16)
+    tile_shape = pltpu.VMEM((models, LANES), F32)
 
     packet, wavelets, block = call(
         functools.partial(first_kernel, layers),
@@ -411,39 +399,40 @@
     )
     block_other = from_partner(block, "dp", 1)
     packets = [from_other_core(packet, (0, d)) for d in range(1, n_vox)]
-    kw, kw_other = (call(functools.partial(applied_kernel, layers), k_shape, b) for b in (block, block_other))
+    kw = call(functools.partial(applied_kernel, layers, rows), pltpu.VMEM((LANES, width), BF16), block, block_other)
+    kt = call(functools.partial(transposing_kernel, rows), pltpu.VMEM((width, LANES), BF16), block, block_other)
     cut, cut_halo = call(
         functools.partial(spread_kernel, layers, rows),
-        (pltpu.VMEM((models, width), F32), pltpu.VMEM((models, LANES), F32)),
+        (pltpu.VMEM((models, width), F32), tile_shape),
         jnp.swapaxes(threshold, 1, 2),
     )
     other, halo = call(
         functools.partial(second_kernel, layers, n_vox, models),
-        (pltpu.VMEM((packet_rows, LANES), F32), pltpu.VMEM((models, LANES), F32)),
+        (pltpu.VMEM((packet_rows, LANES), F32), tile_shape),
         block_other,
         *packets,
         scratch=[pltpu.VMEM((n_vox, packet_rows, LANES), BF16)],
     )
     mine = from_partner(other, "dp", 1)
-    g = call(third_kernel, g_shape, mine, other, kw, kw_other)
+    g, columns, observed = call(
+        third_kernel, (g_shape, pltpu.VMEM((LANES, LANES), BF16), tile_shape), mine, other, kw
+    )
     wavelets, predicted = call(
         functools.partial(fourth_kernel, layers, rows),
-        (pltpu.VMEM((models, width), F32), pltpu.VMEM((models, LANES), F32)),
+        (pltpu.VMEM((models, width), F32), tile_shape),
         wavelets,
         cut,
         halo,
         cut_halo,
-        block,
-        block_other,
+        kt,
         *over_chips(g),
     )
     g, residual = call(
         fifth_kernel,
         (g_shape, pltpu.VMEM((models, rows), F32)),
-        mine,
-        other,
         kw,
-        kw_other,
+        columns,
+        observed,
         *over_vox(predicted),
     )
     coefficients = call(

time: 32 us -> 31.9 us (level)
    ppermute x10, waiting for transfers between devices: 10.1 us -> 9.75 us  [from_other_core(): return lax.ppermute(x, ('dp', 'vox'), route)]
  transfers between devices with their start and end apart: 14 -> 14, of which waited for: 9 -> 9; matrix products, arithmetic and copies ran while one was open for 2% -> 2% of each run, Pallas kernels for 3% -> 4%
where the time goes in v9:
time: 31.9 us; the launch traced here: 31.7 us
  starting transfers between devices  15.4 us (48%)
  waiting for transfers between devices  10.4 us (33%)
  Pallas kernels  4.63 us (15%)
  between operations  0.68 us (2%)
  local copies, waits for them, and re-layouts  0.6 us (2%)
    ppermute x10, starting transfers between devices, from_other_core(): return lax.ppermute(x, ('dp', 'vox'), route)  14.3 us
    ppermute x10, waiting for transfers between devices, from_other_core(): return lax.ppermute(x, ('dp', 'vox'), route)  9.75 us
    pallas_call x9, Pallas kernels, call(): pl.pallas_call(kernel, out_shape=out_shape, in_specs=[pl.BlockSpec(memory...  4.63 us
    ppermute x4, starting transfers between devices, from_partner(): lax.ppermute(x, axis, [(i, i ^ distance) for i in range(lax.axis_size(axi...  1.12 us
    ppermute x4, waiting for transfers between devices, from_partner(): lax.ppermute(x, axis, [(i, i ^ distance) for i in range(lax.axis_size(axi...  0.65 us
  transfers between devices with their start and end apart: 14, of which 9 were waited for; matrix products, arithmetic and copies ran while one was open for 2% of the time, Pallas kernels for 4%

profile of v9, /device:TPU:0, one launch (start us, length us, event | category | flops | bytes accessed | tf_op | source)
XLA Modules:
  0.0 31.7 jit_solution(11179128710497534266)
XLA Ops:
  0.6 1.3 %shard_map.59 = (bf16[64,128]{1,0:T(8,128)(2,1)S(1)}, f32[8,4096]{1,0:T(8,128)S(1)}, bf16[64,4096]{1,0:T(8,128)(2,1)S(1)}) custom-call(f32[8,4096]{1,0:T(8,128)} %wave_hbm.1, bf16[48,4096]{1,0:T(8,128)(2,1)} %k_hbm.1, f32[8,48]{1,0:T(8,128)} %observed_hbm.1), custom_call_target="tpu_custom_call" | custom-call | tf_op jit(solution)/shard_map/pallas_call | solution.py:362
  2.0 0.5 %collective-permute-start = (bf16[64,4096]{1,0:T(8,128)(2,1)S(1)}, bf16[64,4096]{1,0:T(8,128)(2,1)S(1)}, u32[]{:S(2)}, u32[]{:S(2)}) collective-permute-start(bf16[64,4096]{1,0:T(8,128)(2,1)S(1)} %get-tuple-element.18.block_ref), channel_id=1, source_target_pairs={{0,4},{4,0},{8,12},{12,8},{16,20},{20,16},{24,28},{28,24},{1,5},{5... | collective-permute-start | bytes 1572872 | tf_op jit(solution)/shard_map/ppermute | solution.py:322
  2.5 4.7 %collective-permute-start.3 = (bf16[64,128]{1,0:T(8,128)(2,1)S(1)}, bf16[64,128]{1,0:T(8,128)(2,1)S(1)}, u32[]{:S(2)}, u32[]{:S(2)}) collective-permute-start(bf16[64,128]{1,0:T(8,128)(2,1)S(1)} %get-tuple-element.19), channel_id=1, source_target_pairs={{0,7},{1,6},{2,5},{3,4},{4,3},{5,2},{6,1},{7,0},{8,15},{9,14},{10,... | collective-permute-start | bytes 49160 | tf_op jit(solution)/shard_map/ppermute | solution.py:331
  7.2 0.0 collective-permute-start.2
  7.2 0.3 collective-permute-start.1
  7.5 1.1 %collective-permute-done.3.refs_3_ = bf16[64,128]{1,0:T(8,128)(2,1)S(1)} collective-permute-done((bf16[64,128]{1,0:T(8,128)(2,1)S(1)}, bf16[64,128]{1,0:T(8,128)(2,1)S(1)}, u32[]{:S(2)}, u32[]{:S(2)}) %collective-permute-start.3) | collective-permute-done | bytes 16416 | tf_op jit(solution)/shard_map/ppermute | solution.py:331
  8.7 2.6 %collective-permute-done.2.refs_2_ = bf16[64,128]{1,0:T(8,128)(2,1)S(1)} collective-permute-done((bf16[64,128]{1,0:T(8,128)(2,1)S(1)}, bf16[64,128]{1,0:T(8,128)(2,1)S(1)}, u32[]{:S(2)}, u32[]{:S(2)}) %collective-permute-start.2) | collective-permute-done | bytes 16416 | tf_op jit(solution)/shard_map/ppermute | solution.py:331
  11.3 0.0 collective-permute-done.1.refs_1_
  11.3 0.0 collective-permute-done.refs_0_.other_ref
  11.3 0.2 shard_map.61
  11.5 0.2 collective-permute-start.4
  11.7 0.5 %shard_map.63.kw_ref = bf16[128,4096]{1,0:T(8,128)(2,1)S(1)} custom-call(bf16[64,4096]{1,0:T(8,128)(2,1)S(1)} %get-tuple-element.18.block_ref, bf16[64,4096]{1,0:T(8,128)(2,1)S(1)} %collective-permute-done.refs_0_.other_ref), custom_call_target="tpu_custom_call" | custom-call | tf_op jit(solution)/shard_map/pallas_call | solution.py:362
  12.1 0.6 %collective-permute-done.4.mine_ref = f32[64,128]{1,0:T(8,128)S(1)} collective-permute-done((f32[64,128]{1,0:T(8,128)S(1)}, f32[64,128]{1,0:T(8,128)S(1)}, u32[]{:S(2)}, u32[]{:S(2)}) %collective-permute-start.4) | collective-permute-done | bytes 32800 | tf_op jit(solution)/shard_map/ppermute | solution.py:322
  12.8 0.0 copy-start
  12.8 0.3 shard_map.64
  13.1 1.3 %collective-permute-start.5 = (bf16[8,4224]{1,0:T(8,128)(2,1)S(1)}, bf16[8,4224]{1,0:T(8,128)(2,1)S(1)}, u32[]{:S(2)}, u32[]{:S(2)}) collective-permute-start(bf16[8,4224]{1,0:T(8,128)(2,1)S(1)} %get-tuple-element.23.refs_0_), channel_id=1, source_target_pairs={{0,20},{1,21},{2,22},{3,23},{4,8},{5,9},{6,10},{7,11},{8,28},{9,29... | collective-permute-start | bytes 202760 | tf_op jit(solution)/shard_map/ppermute | solution.py:331
  14.4 1.4 %collective-permute-start.7 = (bf16[8,4224]{1,0:T(8,128)(2,1)S(1)}, bf16[8,4224]{1,0:T(8,128)(2,1)S(1)}, u32[]{:S(2)}, u32[]{:S(2)}) collective-permute-start(bf16[8,4224]{1,0:T(8,128)(2,1)S(1)} %get-tuple-element.23.refs_0_), channel_id=1, source_target_pairs={{0,28},{1,29},{2,30},{3,31},{4,24},{5,25},{6,26},{7,27},{8,20},{9,... | collective-permute-start | bytes 202760 | tf_op jit(solution)/shard_map/ppermute | solution.py:331
  15.8 1.0 %collective-permute-done.5.refs_1_ = bf16[8,4224]{1,0:T(8,128)(2,1)S(1)} collective-permute-done((bf16[8,4224]{1,0:T(8,128)(2,1)S(1)}, bf16[8,4224]{1,0:T(8,128)(2,1)S(1)}, u32[]{:S(2)}, u32[]{:S(2)}) %collective-permute-start.5) | collective-permute-done | bytes 67616 | tf_op jit(solution)/shard_map/ppermute | solution.py:331
  16.8 0.2 collective-permute-start.6
  17.0 0.0 copy-done
  17.0 0.4 %shard_map.60 = (f32[8,4096]{1,0:T(8,128)S(1)}, f32[8,128]{1,0:T(8,128)S(1)}) custom-call(f32[8,2,16]{2,1,0:T(2,128)S(1)} %bitcast.1), custom_call_target="tpu_custom_call" | custom-call | tf_op jit(solution)/shard_map/pallas_call | solution.py:362
  17.4 0.4 %shard_map.62.kt_ref = bf16[4096,128]{1,0:T(8,128)(2,1)S(1)} custom-call(bf16[64,4096]{1,0:T(8,128)(2,1)S(1)} %get-tuple-element.18.block_ref, bf16[64,4096]{1,0:T(8,128)(2,1)S(1)} %collective-permute-done.refs_0_.other_ref), custom_call_target="tpu_custom_call" | custom-call | tf_op jit(solution)/shard_map/pallas_call | solution.py:362
  17.8 1.6 %collective-permute-done.7.refs_3_ = bf16[8,4224]{1,0:T(8,128)(2,1)S(1)} collective-permute-done((bf16[8,4224]{1,0:T(8,128)(2,1)S(1)}, bf16[8,4224]{1,0:T(8,128)(2,1)S(1)}, u32[]{:S(2)}, u32[]{:S(2)}) %collective-permute-start.7) | collective-permute-done | bytes 67616 | tf_op jit(solution)/shard_map/ppermute | solution.py:331
  19.3 0.0 collective-permute-done.6.refs_2_
  19.3 0.5 %shard_map.65 = (f32[8,4096]{1,0:T(8,128)S(1)}, f32[8,128]{1,0:T(8,128)S(1)}) custom-call(f32[8,4096]{1,0:T(8,128)S(1)} %get-tuple-element.16.wave_ref, f32[8,4096]{1,0:T(8,128)S(1)} %get-tuple-element.17.cut_ref, f32[8,128]{1,0:T(8,128)S(1)} %get-tuple-element.20.halo_ref, f32[8,128]{1,0:T(8,128)S(1)} %get-tuple-element.21.cut_halo_ref, ...), custom_call_target="tpu_custom_call" | custom-call | tf_op jit(solution)/shard_map/pallas_call | solution.py:362
  19.9 1.6 %collective-permute-start.10 = (f32[8,128]{1,0:T(8,128)S(1)}, f32[8,128]{1,0:T(8,128)S(1)}, u32[]{:S(2)}, u32[]{:S(2)}) collective-permute-start(f32[8,128]{1,0:T(8,128)S(1)} %get-tuple-element.27.refs_0_), channel_id=1, source_target_pairs={{0,7},{1,6},{2,5},{3,4},{4,3},{5,2},{6,1},{7,0},{8,15},{9,14},{10,... | collective-permute-start | bytes 12296 | tf_op jit(solution)/shard_map/ppermute | solution.py:331
  21.5 0.4 %collective-permute-start.9 = (f32[8,128]{1,0:T(8,128)S(1)}, f32[8,128]{1,0:T(8,128)S(1)}, u32[]{:S(2)}, u32[]{:S(2)}) collective-permute-start(f32[8,128]{1,0:T(8,128)S(1)} %get-tuple-element.27.refs_0_), channel_id=1, source_target_pairs={{0,6},{1,7},{2,4},{3,5},{4,2},{5,3},{6,0},{7,1},{8,14},{9,15},{10,... | collective-permute-start | bytes 12296 | tf_op jit(solution)/shard_map/ppermute | solution.py:331
  21.8 2.1 %collective-permute-start.8 = (f32[8,128]{1,0:T(8,128)S(1)}, f32[8,128]{1,0:T(8,128)S(1)}, u32[]{:S(2)}, u32[]{:S(2)}) collective-permute-start(f32[8,128]{1,0:T(8,128)S(1)} %get-tuple-element.27.refs_0_), channel_id=1, source_target_pairs={{0,5},{1,4},{2,7},{3,6},{4,1},{5,0},{6,3},{7,2},{8,13},{9,12},{10,... | collective-permute-start | bytes 12296 | tf_op jit(solution)/shard_map/ppermute | solution.py:331
  23.9 0.9 %collective-permute-done.10.refs_3_ = f32[8,128]{1,0:T(8,128)S(1)} collective-permute-done((f32[8,128]{1,0:T(8,128)S(1)}, f32[8,128]{1,0:T(8,128)S(1)}, u32[]{:S(2)}, u32[]{:S(2)}) %collective-permute-start.10) | collective-permute-done | bytes 4128 | tf_op jit(solution)/shard_map/ppermute | solution.py:331
  24.8 0.6 %collective-permute-done.9.refs_2_ = f32[8,128]{1,0:T(8,128)S(1)} collective-permute-done((f32[8,128]{1,0:T(8,128)S(1)}, f32[8,128]{1,0:T(8,128)S(1)}, u32[]{:S(2)}, u32[]{:S(2)}) %collective-permute-start.9) | collective-permute-done | bytes 4128 | tf_op jit(solution)/shard_map/ppermute | solution.py:331
  25.4 0.0 collective-permute-done.8.refs_1_
  25.4 0.3 shard_map.66
  25.6 0.6 %collective-permute-start.11 = (bf16[8,4224]{1,0:T(8,128)(2,1)S(1)}, bf16[8,4224]{1,0:T(8,128)(2,1)S(1)}, u32[]{:S(2)}, u32[]{:S(2)}) collective-permute-start(bf16[8,4224]{1,0:T(8,128)(2,1)S(1)} %get-tuple-element.28.refs_0_), channel_id=1, source_target_pairs={{0,20},{1,21},{2,22},{3,23},{4,8},{5,9},{6,10},{7,11},{8,28},{9,29... | collective-permute-start | bytes 202760 | tf_op jit(solution)/shard_map/ppermute | solution.py:331
  26.2 1.9 %collective-permute-start.13 = (bf16[8,4224]{1,0:T(8,128)(2,1)S(1)}, bf16[8,4224]{1,0:T(8,128)(2,1)S(1)}, u32[]{:S(2)}, u32[]{:S(2)}) collective-permute-start(bf16[8,4224]{1,0:T(8,128)(2,1)S(1)} %get-tuple-element.28.refs_0_), channel_id=1, source_target_pairs={{0,28},{1,29},{2,30},{3,31},{4,24},{5,25},{6,26},{7,27},{8,20},{9,... | collective-permute-start | bytes 202760 | tf_op jit(solution)/shard_map/ppermute | solution.py:331
  28.2 1.2 %collective-permute-done.11.refs_1_ = bf16[8,4224]{1,0:T(8,128)(2,1)S(1)} collective-permute-done((bf16[8,4224]{1,0:T(8,128)(2,1)S(1)}, bf16[8,4224]{1,0:T(8,128)(2,1)S(1)}, u32[]{:S(2)}, u32[]{:S(2)}) %collective-permute-start.11) | collective-permute-done | bytes 67616 | tf_op jit(solution)/shard_map/ppermute | solution.py:331
  29.4 0.3 collective-permute-start.12
  29.7 0.6 %copy.6 = f32[8,48]{1,0:T(8,128)} copy(f32[8,48]{1,0:T(8,128)S(1)} %get-tuple-element.31) | data formatting | bytes 3072
  30.3 0.7 %collective-permute-done.13.refs_3_ = bf16[8,4224]{1,0:T(8,128)(2,1)S(1)} collective-permute-done((bf16[8,4224]{1,0:T(8,128)(2,1)S(1)}, bf16[8,4224]{1,0:T(8,128)(2,1)S(1)}, u32[]{:S(2)}, u32[]{:S(2)}) %collective-permute-start.13) | collective-permute-done | bytes 67616 | tf_op jit(solution)/shard_map/ppermute | solution.py:331
  30.9 0.0 collective-permute-done.12.refs_2_
  30.9 0.8 %shard_map.67 = f32[8,4096]{1,0:T(8,128)} custom-call(f32[8,4096]{1,0:T(8,128)S(1)} %get-tuple-element.24.wave_ref, f32[8,4096]{1,0:T(8,128)S(1)} %get-tuple-element.17.cut_ref, bf16[8,4224]{1,0:T(8,128)(2,1)S(1)} %get-tuple-element.28.refs_0_, bf16[8,4224]{1,0:T(8,128)(2,1)S(1)} %collective-permute-done.11.refs_1_, ...), custom_call_target="tpu_custom_call" | custom-call | tf_op jit(solution)/shard_map/pallas_call | solution.py:362
Async XLA Ops:
  2.0 9.3 %collective-permute-start = (bf16[64,4096]{1,0:T(8,128)(2,1)S(1)}, bf16[64,4096]{1,0:T(8,128)(2,1)S(1)}, u32[]{:S(2)}, u32[]{:S(2)}) collective-permute-start(bf16[64,4096]{1,0:T(8,128)(2,1)S(1)} %get-tuple-element.18.block_ref), channel_id=1, source_target_pairs={{0,4},{4,0},{8,12},{12,8},{16,20},{20,16},{24,28},{28,24},{1,5},{5... | collective-permute-start | bytes 1572872 | tf_op jit(solution)/shard_map/ppermute | solution.py:322
  2.5 6.2 %collective-permute-start.3 = (bf16[64,128]{1,0:T(8,128)(2,1)S(1)}, bf16[64,128]{1,0:T(8,128)(2,1)S(1)}, u32[]{:S(2)}, u32[]{:S(2)}) collective-permute-start(bf16[64,128]{1,0:T(8,128)(2,1)S(1)} %get-tuple-element.19), channel_id=1, source_target_pairs={{0,7},{1,6},{2,5},{3,4},{4,3},{5,2},{6,1},{7,0},{8,15},{9,14},{10,... | collective-permute-start | bytes 49160 | tf_op jit(solution)/shard_map/ppermute | solution.py:331
  7.2 4.1 %collective-permute-start.2 = (bf16[64,128]{1,0:T(8,128)(2,1)S(1)}, bf16[64,128]{1,0:T(8,128)(2,1)S(1)}, u32[]{:S(2)}, u32[]{:S(2)}) collective-permute-start(bf16[64,128]{1,0:T(8,128)(2,1)S(1)} %get-tuple-element.19), channel_id=1, source_target_pairs={{0,6},{1,7},{2,4},{3,5},{4,2},{5,3},{6,0},{7,1},{8,14},{9,15},{10,... | collective-permute-start | bytes 49160 | tf_op jit(solution)/shard_map/ppermute | solution.py:331
  7.2 4.1 %collective-permute-start.1 = (bf16[64,128]{1,0:T(8,128)(2,1)S(1)}, bf16[64,128]{1,0:T(8,128)(2,1)S(1)}, u32[]{:S(2)}, u32[]{:S(2)}) collective-permute-start(bf16[64,128]{1,0:T(8,128)(2,1)S(1)} %get-tuple-element.19), channel_id=1, source_target_pairs={{0,5},{1,4},{2,7},{3,6},{4,1},{5,0},{6,3},{7,2},{8,13},{9,12},{10,... | collective-permute-start | bytes 49160 | tf_op jit(solution)/shard_map/ppermute | solution.py:331
  11.5 1.3 %collective-permute-start.4 = (f32[64,128]{1,0:T(8,128)S(1)}, f32[64,128]{1,0:T(8,128)S(1)}, u32[]{:S(2)}, u32[]{:S(2)}) collective-permute-start(f32[64,128]{1,0:T(8,128)S(1)} %get-tuple-element.22.other_ref), channel_id=1, source_target_pairs={{0,4},{4,0},{8,12},{12,8},{16,20},{20,16},{24,28},{28,24},{1,5},{5... | collective-permute-start | bytes 98312 | tf_op jit(solution)/shard_map/ppermute | solution.py:322
  12.8 4.2 %copy-start = (f32[8,16,2]{1,2,0:T(2,128)S(1)}, f32[8,16,2]{1,2,0:T(2,128)}, u32[]{:S(2)}) copy-start(f32[8,16,2]{1,2,0:T(2,128)} %param.7) | copy-start | bytes 3076
  13.1 3.7 %collective-permute-start.5 = (bf16[8,4224]{1,0:T(8,128)(2,1)S(1)}, bf16[8,4224]{1,0:T(8,128)(2,1)S(1)}, u32[]{:S(2)}, u32[]{:S(2)}) collective-permute-start(bf16[8,4224]{1,0:T(8,128)(2,1)S(1)} %get-tuple-element.23.refs_0_), channel_id=1, source_target_pairs={{0,20},{1,21},{2,22},{3,23},{4,8},{5,9},{6,10},{7,11},{8,28},{9,29... | collective-permute-start | bytes 202760 | tf_op jit(solution)/shard_map/ppermute | solution.py:331
  14.4 4.9 %collective-permute-start.7 = (bf16[8,4224]{1,0:T(8,128)(2,1)S(1)}, bf16[8,4224]{1,0:T(8,128)(2,1)S(1)}, u32[]{:S(2)}, u32[]{:S(2)}) collective-permute-start(bf16[8,4224]{1,0:T(8,128)(2,1)S(1)} %get-tuple-element.23.refs_0_), channel_id=1, source_target_pairs={{0,28},{1,29},{2,30},{3,31},{4,24},{5,25},{6,26},{7,27},{8,20},{9,... | collective-permute-start | bytes 202760 | tf_op jit(solution)/shard_map/ppermute | solution.py:331
  16.8 2.5 %collective-permute-start.6 = (bf16[8,4224]{1,0:T(8,128)(2,1)S(1)}, bf16[8,4224]{1,0:T(8,128)(2,1)S(1)}, u32[]{:S(2)}, u32[]{:S(2)}) collective-permute-start(bf16[8,4224]{1,0:T(8,128)(2,1)S(1)} %collective-permute-done.5.refs_1_), channel_id=1, source_target_pairs={{0,4},{4,0},{8,12},{12,8},{16,20},{20,16},{24,28},{28,24},{1,5},{5... | collective-permute-start | bytes 202760 | tf_op jit(solution)/shard_map/ppermute | solution.py:322
  19.9 4.9 %collective-permute-start.10 = (f32[8,128]{1,0:T(8,128)S(1)}, f32[8,128]{1,0:T(8,128)S(1)}, u32[]{:S(2)}, u32[]{:S(2)}) collective-permute-start(f32[8,128]{1,0:T(8,128)S(1)} %get-tuple-element.27.refs_0_), channel_id=1, source_target_pairs={{0,7},{1,6},{2,5},{3,4},{4,3},{5,2},{6,1},{7,0},{8,15},{9,14},{10,... | collective-permute-start | bytes 12296 | tf_op jit(solution)/shard_map/ppermute | solution.py:331
  21.5 3.9 %collective-permute-start.9 = (f32[8,128]{1,0:T(8,128)S(1)}, f32[8,128]{1,0:T(8,128)S(1)}, u32[]{:S(2)}, u32[]{:S(2)}) collective-permute-start(f32[8,128]{1,0:T(8,128)S(1)} %get-tuple-element.27.refs_0_), channel_id=1, source_target_pairs={{0,6},{1,7},{2,4},{3,5},{4,2},{5,3},{6,0},{7,1},{8,14},{9,15},{10,... | collective-permute-start | bytes 12296 | tf_op jit(solution)/shard_map/ppermute | solution.py:331
  21.8 3.6 %collective-permute-start.8 = (f32[8,128]{1,0:T(8,128)S(1)}, f32[8,128]{1,0:T(8,128)S(1)}, u32[]{:S(2)}, u32[]{:S(2)}) collective-permute-start(f32[8,128]{1,0:T(8,128)S(1)} %get-tuple-element.27.refs_0_), channel_id=1, source_target_pairs={{0,5},{1,4},{2,7},{3,6},{4,1},{5,0},{6,3},{7,2},{8,13},{9,12},{10,... | collective-permute-start | bytes 12296 | tf_op jit(solution)/shard_map/ppermute | solution.py:331
  25.6 3.8 %collective-permute-start.11 = (bf16[8,4224]{1,0:T(8,128)(2,1)S(1)}, bf16[8,4224]{1,0:T(8,128)(2,1)S(1)}, u32[]{:S(2)}, u32[]{:S(2)}) collective-permute-start(bf16[8,4224]{1,0:T(8,128)(2,1)S(1)} %get-tuple-element.28.refs_0_), channel_id=1, source_target_pairs={{0,20},{1,21},{2,22},{3,23},{4,8},{5,9},{6,10},{7,11},{8,28},{9,29... | collective-permute-start | bytes 202760 | tf_op jit(solution)/shard_map/ppermute | solution.py:331
  26.2 4.7 %collective-permute-start.13 = (bf16[8,4224]{1,0:T(8,128)(2,1)S(1)}, bf16[8,4224]{1,0:T(8,128)(2,1)S(1)}, u32[]{:S(2)}, u32[]{:S(2)}) collective-permute-start(bf16[8,4224]{1,0:T(8,128)(2,1)S(1)} %get-tuple-element.28.refs_0_), channel_id=1, source_target_pairs={{0,28},{1,29},{2,30},{3,31},{4,24},{5,25},{6,26},{7,27},{8,20},{9,... | collective-permute-start | bytes 202760 | tf_op jit(solution)/shard_map/ppermute | solution.py:331
  29.4 1.5 %collective-permute-start.12 = (bf16[8,4224]{1,0:T(8,128)(2,1)S(1)}, bf16[8,4224]{1,0:T(8,128)(2,1)S(1)}, u32[]{:S(2)}, u32[]{:S(2)}) collective-permute-start(bf16[8,4224]{1,0:T(8,128)(2,1)S(1)} %collective-permute-done.11.refs_1_), channel_id=1, source_target_pairs={{0,4},{4,0},{8,12},{12,8},{16,20},{20,16},{24,28},{28,24},{1,5},{5... | collective-permute-start | bytes 202760 | tf_op jit(solution)/shard_map/ppermute | solution.py:322

commit v10 on v9

--- a/solution.py
+++ b/solution.py
@@ -260,14 +260,10 @@
     back_projected(below[:models], kw_ref, columns, g_ref)
 
 
-def added(shares, swapped=False):
-    if len(shares) < 4:
-        return sum(shares[1:], shares[0])
-    own, near, middle, far = shares
-    if swapped:
-        is_first = on_first_core()
-        near, middle = jnp.where(is_first, near, middle), jnp.where(is_first, middle, near)
-    return (own + near) + (middle + far)
+def added(shares):
+    while len(shares) > 1:
+        shares = [a + b for a, b in zip(shares[::2], shares[1::2])]
+    return shares[0]
 
 
 def at_ends(tile, layers, base):
@@ -275,12 +271,12 @@
 
 
 def halo_gradient(g_refs):
-    return added([g[:, g.shape[1] - LANES :].astype(F32) for g in g_refs], True)
+    return added([g[:, g.shape[1] - LANES :].astype(F32) for g in g_refs])
 
 
 def stepped(layers, base, wave_ref, cut_ref, g_refs, edge):
     gradients = [stacked(g, layers) for g in g_refs]
-    smooth_g, detail_g = (added([g[p] for g in gradients], True) for p in range(2))
+    smooth_g, detail_g = (added([g[p] for g in gradients]) for p in range(2))
     ends = at_ends(edge, layers, base)
     lane = lanes_of(ends.shape)
     smooth_g += jnp.where(lane == 0, 0.25 * ends, jnp.where(lane == LANES - 1, -0.125 * ends, 0.0))
@@ -306,10 +302,9 @@
 
 def fifth_kernel(kw_ref, columns_ref, observed_ref, *refs):
     *shares, g_ref, residual_ref = refs
-    rows = residual_ref.shape[1]
     residual = observed_ref[...] - added([s[...] for s in shares])
     back_projected(residual, kw_ref, columns_ref[...], g_ref)
-    residual_ref[...] = jnp.where(on_first_core(), residual, turned(residual, -rows))[:, :rows]
+    residual_ref[...] = residual
 
 
 def sixth_kernel(layers, base, wave_ref, cut_ref, *refs):
@@ -318,44 +313,53 @@
     new_ref[...] = unstacked(*waves, wave_ref.shape[0])
 
 
+def seventh_kernel(wave_ref, other_wave_ref, residual_ref, other_residual_ref, out_ref, own_ref):
+    rows = own_ref.shape[1]
+    is_first = on_first_core()
+    out_ref[...] = jnp.where(is_first, other_wave_ref[...], wave_ref[...])
+    own_ref[...] = jnp.where(is_first, residual_ref[...], turned(other_residual_ref[...], -rows))[:, :rows]
+
+
 def from_partner(x, axis, distance):
     return lax.ppermute(x, axis, [(i, i ^ distance) for i in range(lax.axis_size(axis))])
 
 
-def from_other_core(x, *steps):
+def from_other_core(x, vox):
+    n_vox = lax.axis_size("vox")
+    places = [(d, z) for d in range(lax.axis_size("dp")) for z in range(n_vox)]
+    return lax.ppermute(x, ("dp", "vox"), [(d * n_vox + z, (d ^ 1) * n_vox + (z ^ vox)) for d, z in places])
+
+
+def from_same_core(x, chips, vox):
+    n_vox = lax.axis_size("vox")
+    places = [(d, z) for d in range(lax.axis_size("dp")) for z in range(n_vox)]
+    return lax.ppermute(x, ("dp", "vox"), [(d * n_vox + z, (d ^ (2 * chips)) * n_vox + (z ^ vox)) for d, z in places])
+
+
+def handed_over(x, sender, chips, vox):
     n_vox = lax.axis_size("vox")
     route = []
     for d in range(lax.axis_size("dp")):
-        chips, vox = steps[(d + 1) % 2 % len(steps)]
-        route += [(d * n_vox + z, (d ^ (2 * chips + 1)) * n_vox + (z ^ vox)) for z in range(n_vox)]
+        away = (chips, vox) if d % 2 == sender else (0, 0)
+        route += [(d * n_vox + z, (d ^ 1 ^ (2 * away[0])) * n_vox + (z ^ away[1])) for z in range(n_vox)]
     return lax.ppermute(x, ("dp", "vox"), route)
 
 
-def all_shares(x, step):
-    return [x] + [from_other_core(x, step(n)) for n in (1, 2, 3)]
-
-
-def swapped_shares(x, step):
-    fetched = from_other_core(x, step(1), step(2))
-    return [x, fetched, from_partner(fetched, "dp", 1), from_other_core(x, step(3))]
-
-
-def shares_over(x, size, step, four, **how):
+def shares_over(x, size, step, sender):
     lowest = 1
     while size > 4:
-        x = added([s.astype(F32) for s in four(x, lambda n: step(lowest * n))], **how).astype(x.dtype)
+        fours = [x] + [from_same_core(x, *step(lowest * n)) for n in (1, 2, 3)]
+        x = added([f.astype(F32) for f in fours]).astype(x.dtype)
         lowest, size = lowest * 4, size // 4
-    if size == 4:
-        return four(x, lambda n: step(lowest * n))
-    return [x] + [from_other_core(x, step(lowest))] * (size - 1)
+    return [handed_over(x, sender, *step(lowest * n)) for n in range(size)]
 
 
 def over_chips(x):
-    return shares_over(x, lax.axis_size("dp") // 2, lambda n: (n, 0), swapped_shares, swapped=True)
+    return shares_over(x, lax.axis_size("dp") // 2, lambda n: (n, 0), 0)
 
 
 def over_vox(x):
-    return shares_over(x, lax.axis_size("vox"), lambda n: (0, n), all_shares)
+    return shares_over(x, lax.axis_size("vox"), lambda n: (0, n), 1)
 
 
 def call(kernel, out_shape, *args, scratch=(), space=pltpu.VMEM):
@@ -398,7 +402,7 @@
         space=pltpu.HBM,
     )
     block_other = from_partner(block, "dp", 1)
-    packets = [from_other_core(packet, (0, d)) for d in range(1, n_vox)]
+    packets = [from_other_core(packet, d) for d in range(1, n_vox)]
     kw = call(functools.partial(applied_kernel, layers, rows), pltpu.VMEM((LANES, width), BF16), block, block_other)
     kt = call(functools.partial(transposing_kernel, rows), pltpu.VMEM((width, LANES), BF16), block, block_other)
     cut, cut_halo = call(
@@ -427,22 +431,22 @@
         kt,
         *over_chips(g),
     )
-    g, residual = call(
-        fifth_kernel,
-        (g_shape, pltpu.VMEM((models, rows), F32)),
-        kw,
-        columns,
-        observed,
-        *over_vox(predicted),
-    )
+    g, residual = call(fifth_kernel, (g_shape, tile_shape), kw, columns, observed, *over_vox(predicted))
     coefficients = call(
         functools.partial(sixth_kernel, layers, rows),
-        jax.ShapeDtypeStruct((models, width), F32),
+        pltpu.VMEM((models, width), F32),
         wavelets,
         cut,
         *over_chips(g),
     )
-    return coefficients, residual
+    return call(
+        seventh_kernel,
+        (jax.ShapeDtypeStruct((models, width), F32), jax.ShapeDtypeStruct((models, rows), F32)),
+        coefficients,
+        from_partner(coefficients, "dp", 1),
+        residual,
+        from_partner(residual, "dp", 1),
+    )
 
 
 def solution(mesh):

time: 31.9 us -> 31.4 us (0.984)
  local copies, waits for them, and re-layouts: 0.6 us -> 0.01 us
    ppermute x4, starting transfers between devices: 1.12 us -> 2.48 us  [from_partner(): lax.ppermute(x, axis, [(i, i ^ distance) for i in range(lax.axis_size(axi...]
    ppermute x10 -> x15, starting transfers between devices: 14.3 us -> 13 us  [the longest x12 7.98 us: handed_over(): return lax.ppermute(x, ('dp', 'vox'), route)]
    ppermute x4, waiting for transfers between devices: 0.65 us -> 1.73 us  [from_partner(): lax.ppermute(x, axis, [(i, i ^ distance) for i in range(lax.axis_size(axi...]
    ppermute x10 -> x15, waiting for transfers between devices: 9.75 us -> 8.68 us  [the longest x12 4.93 us: handed_over(): return lax.ppermute(x, ('dp', 'vox'), route)]
    unnamed x3 -> x2, local copies, waits for them, and re-layouts: 0.6 us -> 0.01 us
    pallas_call x9 -> x10, Pallas kernels: 4.63 us -> 4.64 us  [call(): pl.pallas_call(kernel, out_shape=out_shape, in_specs=[pl.BlockSpec(memory...]
  transfers between devices with their start and end apart: 14 -> 19, of which waited for: 9 -> 12; matrix products, arithmetic and copies ran while one was open for 2% -> 0% of each run, Pallas kernels for 4% -> 4%
where the time goes in v10:
time: 31.4 us; the launch traced here: 31.3 us
  starting transfers between devices  15.5 us (49%)
  waiting for transfers between devices  10.4 us (33%)
  Pallas kernels  4.64 us (15%)
  between operations  0.7 us (2%)
    ppermute x12, starting transfers between devices, handed_over(): return lax.ppermute(x, ('dp', 'vox'), route)  7.98 us
    ppermute x3, starting transfers between devices, from_other_core(): lax.ppermute(x, ('dp', 'vox'), [(d * n_vox + z, (d ^ 1) * n_vox + (z ^ vo...  5.04 us
    ppermute x12, waiting for transfers between devices, handed_over(): return lax.ppermute(x, ('dp', 'vox'), route)  4.93 us
    pallas_call x10, Pallas kernels, call(): pl.pallas_call(kernel, out_shape=out_shape, in_specs=[pl.BlockSpec(memory...  4.64 us
    ppermute x3, waiting for transfers between devices, from_other_core(): lax.ppermute(x, ('dp', 'vox'), [(d * n_vox + z, (d ^ 1) * n_vox + (z ^ vo...  3.75 us
    ppermute x4, starting transfers between devices, from_partner(): lax.ppermute(x, axis, [(i, i ^ distance) for i in range(lax.axis_size(axi...  2.48 us
    ppermute x4, waiting for transfers between devices, from_partner(): lax.ppermute(x, axis, [(i, i ^ distance) for i in range(lax.axis_size(axi...  1.73 us
  transfers between devices with their start and end apart: 19, of which 12 were waited for; matrix products, arithmetic and copies ran while one was open for 0% of the time, Pallas kernels for 4%

profile of v10, /device:TPU:0, one launch (start us, length us, event | category | flops | bytes accessed | tf_op | source)
XLA Modules:
  0.0 31.3 jit_solution(15679443265911539063)
XLA Ops:
  0.6 1.3 %shard_map.59 = (bf16[64,128]{1,0:T(8,128)(2,1)S(1)}, f32[8,4096]{1,0:T(8,128)S(1)}, bf16[64,4096]{1,0:T(8,128)(2,1)S(1)}) custom-call(f32[8,4096]{1,0:T(8,128)} %wave_hbm.1, bf16[48,4096]{1,0:T(8,128)(2,1)} %k_hbm.1, f32[8,48]{1,0:T(8,128)} %observed_hbm.1), custom_call_target="tpu_custom_call" | custom-call | tf_op jit(solution)/shard_map/pallas_call | solution.py:366
  2.0 0.5 %collective-permute-start = (bf16[64,4096]{1,0:T(8,128)(2,1)S(1)}, bf16[64,4096]{1,0:T(8,128)(2,1)S(1)}, u32[]{:S(2)}, u32[]{:S(2)}) collective-permute-start(bf16[64,4096]{1,0:T(8,128)(2,1)S(1)} %get-tuple-element.18.block_ref), channel_id=1, source_target_pairs={{0,4},{4,0},{8,12},{12,8},{16,20},{20,16},{24,28},{28,24},{1,5},{5... | collective-permute-start | bytes 1572872 | tf_op jit(solution)/shard_map/ppermute | solution.py:324
  2.5 4.7 %collective-permute-start.3 = (bf16[64,128]{1,0:T(8,128)(2,1)S(1)}, bf16[64,128]{1,0:T(8,128)(2,1)S(1)}, u32[]{:S(2)}, u32[]{:S(2)}) collective-permute-start(bf16[64,128]{1,0:T(8,128)(2,1)S(1)} %get-tuple-element.19), channel_id=1, source_target_pairs={{0,7},{1,6},{2,5},{3,4},{4,3},{5,2},{6,1},{7,0},{8,15},{9,14},{10,... | collective-permute-start | bytes 49160 | tf_op jit(solution)/shard_map/ppermute | solution.py:330
  7.2 0.0 collective-permute-start.2
  7.2 0.3 collective-permute-start.1
  7.5 1.1 %collective-permute-done.3.refs_3_ = bf16[64,128]{1,0:T(8,128)(2,1)S(1)} collective-permute-done((bf16[64,128]{1,0:T(8,128)(2,1)S(1)}, bf16[64,128]{1,0:T(8,128)(2,1)S(1)}, u32[]{:S(2)}, u32[]{:S(2)}) %collective-permute-start.3) | collective-permute-done | bytes 16416 | tf_op jit(solution)/shard_map/ppermute | solution.py:330
  8.7 2.6 %collective-permute-done.2.refs_2_ = bf16[64,128]{1,0:T(8,128)(2,1)S(1)} collective-permute-done((bf16[64,128]{1,0:T(8,128)(2,1)S(1)}, bf16[64,128]{1,0:T(8,128)(2,1)S(1)}, u32[]{:S(2)}, u32[]{:S(2)}) %collective-permute-start.2) | collective-permute-done | bytes 16416 | tf_op jit(solution)/shard_map/ppermute | solution.py:330
  11.3 0.0 collective-permute-done.1.refs_1_
  11.3 0.0 collective-permute-done.refs_0_.other_ref
  11.3 0.2 shard_map.61
  11.5 0.2 collective-permute-start.4
  11.7 0.5 %shard_map.63.kw_ref = bf16[128,4096]{1,0:T(8,128)(2,1)S(1)} custom-call(bf16[64,4096]{1,0:T(8,128)(2,1)S(1)} %get-tuple-element.18.block_ref, bf16[64,4096]{1,0:T(8,128)(2,1)S(1)} %collective-permute-done.refs_0_.other_ref), custom_call_target="tpu_custom_call" | custom-call | tf_op jit(solution)/shard_map/pallas_call | solution.py:366
  12.1 0.6 %collective-permute-done.4.mine_ref = f32[64,128]{1,0:T(8,128)S(1)} collective-permute-done((f32[64,128]{1,0:T(8,128)S(1)}, f32[64,128]{1,0:T(8,128)S(1)}, u32[]{:S(2)}, u32[]{:S(2)}) %collective-permute-start.4) | collective-permute-done | bytes 32800 | tf_op jit(solution)/shard_map/ppermute | solution.py:324
  12.8 0.3 %shard_map.64 = (bf16[8,4224]{1,0:T(8,128)(2,1)S(1)}, bf16[128,128]{1,0:T(8,128)(2,1)S(1)}, f32[8,128]{1,0:T(8,128)S(1)}) custom-call(f32[64,128]{1,0:T(8,128)S(1)} %collective-permute-done.4.mine_ref, f32[64,128]{1,0:T(8,128)S(1)} %get-tuple-element.22.other_ref, bf16[128,4096]{1,0:T(8,128)(2,1)S(1)} %shard_map.63.kw_ref), custom_call_target="tpu_custom_call" | custom-call | tf_op jit(solution)/shard_map/pallas_call | solution.py:366
  13.1 2.2 %collective-permute-start.8 = (bf16[8,4224]{1,0:T(8,128)(2,1)S(1)}, bf16[8,4224]{1,0:T(8,128)(2,1)S(1)}, u32[]{:S(2)}, u32[]{:S(2)}) collective-permute-start(bf16[8,4224]{1,0:T(8,128)(2,1)S(1)} %get-tuple-element.23), channel_id=1, source_target_pairs={{0,28},{1,29},{2,30},{3,31},{4,0},{5,1},{6,2},{7,3},{8,20},{9,21},... | collective-permute-start | bytes 202760 | tf_op jit(solution)/shard_map/ppermute | solution.py:345
  15.3 0.0 collective-permute-start.7
  15.3 0.6 %collective-permute-start.6 = (bf16[8,4224]{1,0:T(8,128)(2,1)S(1)}, bf16[8,4224]{1,0:T(8,128)(2,1)S(1)}, u32[]{:S(2)}, u32[]{:S(2)}) collective-permute-start(bf16[8,4224]{1,0:T(8,128)(2,1)S(1)} %get-tuple-element.23), channel_id=1, source_target_pairs={{0,12},{1,13},{2,14},{3,15},{4,0},{5,1},{6,2},{7,3},{8,4},{9,5},{1... | collective-permute-start | bytes 202760 | tf_op jit(solution)/shard_map/ppermute | solution.py:345
  16.0 0.0 collective-permute-start.5
  16.0 0.4 %shard_map.60 = (f32[8,4096]{1,0:T(8,128)S(1)}, f32[8,128]{1,0:T(8,128)S(1)}) custom-call(f32[8,2,16]{2,1,0:T(2,128)S(1)} %bitcast.1), custom_call_target="tpu_custom_call" | custom-call | tf_op jit(solution)/shard_map/pallas_call | solution.py:366
  16.4 0.4 %shard_map.62.kt_ref = bf16[4096,128]{1,0:T(8,128)(2,1)S(1)} custom-call(bf16[64,4096]{1,0:T(8,128)(2,1)S(1)} %get-tuple-element.18.block_ref, bf16[64,4096]{1,0:T(8,128)(2,1)S(1)} %collective-permute-done.refs_0_.other_ref), custom_call_target="tpu_custom_call" | custom-call | tf_op jit(solution)/shard_map/pallas_call | solution.py:366
  16.8 0.5 %collective-permute-done.8.refs_3_ = bf16[8,4224]{1,0:T(8,128)(2,1)S(1)} collective-permute-done((bf16[8,4224]{1,0:T(8,128)(2,1)S(1)}, bf16[8,4224]{1,0:T(8,128)(2,1)S(1)}, u32[]{:S(2)}, u32[]{:S(2)}) %collective-permute-start.8) | collective-permute-done | bytes 67616 | tf_op jit(solution)/shard_map/ppermute | solution.py:345
  17.3 0.6 %collective-permute-done.7.refs_2_ = bf16[8,4224]{1,0:T(8,128)(2,1)S(1)} collective-permute-done((bf16[8,4224]{1,0:T(8,128)(2,1)S(1)}, bf16[8,4224]{1,0:T(8,128)(2,1)S(1)}, u32[]{:S(2)}, u32[]{:S(2)}) %collective-permute-start.7) | collective-permute-done | bytes 67616 | tf_op jit(solution)/shard_map/ppermute | solution.py:345
  17.8 0.1 collective-permute-done.6.refs_1_
  17.9 0.0 collective-permute-done.5.refs_0_
  17.9 0.5 %shard_map.65 = (f32[8,4096]{1,0:T(8,128)S(1)}, f32[8,128]{1,0:T(8,128)S(1)}) custom-call(f32[8,4096]{1,0:T(8,128)S(1)} %get-tuple-element.16.wave_ref, f32[8,4096]{1,0:T(8,128)S(1)} %get-tuple-element.17.cut_ref, f32[8,128]{1,0:T(8,128)S(1)} %get-tuple-element.20.halo_ref, f32[8,128]{1,0:T(8,128)S(1)} %get-tuple-element.21.cut_halo_ref, ...), custom_call_target="tpu_custom_call" | custom-call | tf_op jit(solution)/shard_map/pallas_call | solution.py:366
  18.5 1.7 %collective-permute-start.12 = (f32[8,128]{1,0:T(8,128)S(1)}, f32[8,128]{1,0:T(8,128)S(1)}, u32[]{:S(2)}, u32[]{:S(2)}) collective-permute-start(f32[8,128]{1,0:T(8,128)S(1)} %get-tuple-element.27), channel_id=1, source_target_pairs={{0,4},{1,5},{2,6},{3,7},{4,3},{5,2},{6,1},{7,0},{8,12},{9,13},{10,... | collective-permute-start | bytes 12296 | tf_op jit(solution)/shard_map/ppermute | solution.py:345
  20.2 0.1 collective-permute-start.11
  20.3 1.9 %collective-permute-start.10 = (f32[8,128]{1,0:T(8,128)S(1)}, f32[8,128]{1,0:T(8,128)S(1)}, u32[]{:S(2)}, u32[]{:S(2)}) collective-permute-start(f32[8,128]{1,0:T(8,128)S(1)} %get-tuple-element.27), channel_id=1, source_target_pairs={{0,4},{1,5},{2,6},{3,7},{4,1},{5,0},{6,3},{7,2},{8,12},{9,13},{10,... | collective-permute-start | bytes 12296 | tf_op jit(solution)/shard_map/ppermute | solution.py:345
  22.2 0.0 collective-permute-start.9
  22.2 1.1 %collective-permute-done.12.refs_3_ = f32[8,128]{1,0:T(8,128)S(1)} collective-permute-done((f32[8,128]{1,0:T(8,128)S(1)}, f32[8,128]{1,0:T(8,128)S(1)}, u32[]{:S(2)}, u32[]{:S(2)}) %collective-permute-start.12) | collective-permute-done | bytes 4128 | tf_op jit(solution)/shard_map/ppermute | solution.py:345
  23.3 0.7 %collective-permute-done.11.refs_2_ = f32[8,128]{1,0:T(8,128)S(1)} collective-permute-done((f32[8,128]{1,0:T(8,128)S(1)}, f32[8,128]{1,0:T(8,128)S(1)}, u32[]{:S(2)}, u32[]{:S(2)}) %collective-permute-start.11) | collective-permute-done | bytes 4128 | tf_op jit(solution)/shard_map/ppermute | solution.py:345
  24.1 0.0 collective-permute-done.10.refs_1_
  24.1 0.0 collective-permute-done.9.refs_0_
  24.1 0.3 shard_map.66
  24.3 0.0 collective-permute-start.16
  24.4 0.7 %collective-permute-start.15 = (bf16[8,4224]{1,0:T(8,128)(2,1)S(1)}, bf16[8,4224]{1,0:T(8,128)(2,1)S(1)}, u32[]{:S(2)}, u32[]{:S(2)}) collective-permute-start(bf16[8,4224]{1,0:T(8,128)(2,1)S(1)} %get-tuple-element.28), channel_id=1, source_target_pairs={{0,20},{1,21},{2,22},{3,23},{4,0},{5,1},{6,2},{7,3},{8,28},{9,29},... | collective-permute-start | bytes 202760 | tf_op jit(solution)/shard_map/ppermute | solution.py:345
  25.1 0.6 %collective-permute-start.14 = (bf16[8,4224]{1,0:T(8,128)(2,1)S(1)}, bf16[8,4224]{1,0:T(8,128)(2,1)S(1)}, u32[]{:S(2)}, u32[]{:S(2)}) collective-permute-start(bf16[8,4224]{1,0:T(8,128)(2,1)S(1)} %get-tuple-element.28), channel_id=1, source_target_pairs={{0,12},{1,13},{2,14},{3,15},{4,0},{5,1},{6,2},{7,3},{8,4},{9,5},{1... | collective-permute-start | bytes 202760 | tf_op jit(solution)/shard_map/ppermute | solution.py:345
  25.6 0.0 collective-permute-start.13
  25.6 0.7 %collective-permute-done.16.refs_3_ = bf16[8,4224]{1,0:T(8,128)(2,1)S(1)} collective-permute-done((bf16[8,4224]{1,0:T(8,128)(2,1)S(1)}, bf16[8,4224]{1,0:T(8,128)(2,1)S(1)}, u32[]{:S(2)}, u32[]{:S(2)}) %collective-permute-start.16) | collective-permute-done | bytes 67616 | tf_op jit(solution)/shard_map/ppermute | solution.py:345
  26.3 1.2 %collective-permute-done.15.refs_2_ = bf16[8,4224]{1,0:T(8,128)(2,1)S(1)} collective-permute-done((bf16[8,4224]{1,0:T(8,128)(2,1)S(1)}, bf16[8,4224]{1,0:T(8,128)(2,1)S(1)}, u32[]{:S(2)}, u32[]{:S(2)}) %collective-permute-start.15) | collective-permute-done | bytes 67616 | tf_op jit(solution)/shard_map/ppermute | solution.py:345
  27.5 0.1 collective-permute-done.14.refs_1_
  27.6 0.0 collective-permute-done.13.refs_0_
  27.6 0.1 shard_map.67.wave_ref
  27.7 1.7 %collective-permute-start.17 = (f32[8,4096]{1,0:T(8,128)S(1)}, f32[8,4096]{1,0:T(8,128)S(1)}, u32[]{:S(2)}, u32[]{:S(2)}) collective-permute-start(f32[8,4096]{1,0:T(8,128)S(1)} %shard_map.67.wave_ref), channel_id=1, source_target_pairs={{0,4},{4,0},{8,12},{12,8},{16,20},{20,16},{24,28},{28,24},{1,5},{5... | collective-permute-start | bytes 393224 | tf_op jit(solution)/shard_map/ppermute | solution.py:324
  29.4 0.1 collective-permute-start.18
  29.5 1.1 %collective-permute-done.18.other_residual_ref = f32[8,128]{1,0:T(8,128)S(1)} collective-permute-done((f32[8,128]{1,0:T(8,128)S(1)}, f32[8,128]{1,0:T(8,128)S(1)}, u32[]{:S(2)}, u32[]{:S(2)}) %collective-permute-start.18) | collective-permute-done | bytes 4128 | tf_op jit(solution)/shard_map/ppermute | solution.py:324
  30.6 0.0 collective-permute-done.17.other_wave_ref
  30.6 0.7 %shard_map.68 = (f32[8,4096]{1,0:T(8,128)}, f32[8,48]{1,0:T(8,128)}) custom-call(f32[8,4096]{1,0:T(8,128)S(1)} %shard_map.67.wave_ref, f32[8,4096]{1,0:T(8,128)S(1)} %collective-permute-done.17.other_wave_ref, f32[8,128]{1,0:T(8,128)S(1)} %get-tuple-element.29.residual_ref, f32[8,128]{1,0:T(8,128)S(1)} %collective-permute-done.18.other_residual_ref), custom_call_target="tpu_custom_call" | custom-call | tf_op jit(solution)/shard_map/pallas_call | solution.py:366
  (2 shorter events, 0.0 us)
Async XLA Ops:
  2.0 9.3 %collective-permute-start = (bf16[64,4096]{1,0:T(8,128)(2,1)S(1)}, bf16[64,4096]{1,0:T(8,128)(2,1)S(1)}, u32[]{:S(2)}, u32[]{:S(2)}) collective-permute-start(bf16[64,4096]{1,0:T(8,128)(2,1)S(1)} %get-tuple-element.18.block_ref), channel_id=1, source_target_pairs={{0,4},{4,0},{8,12},{12,8},{16,20},{20,16},{24,28},{28,24},{1,5},{5... | collective-permute-start | bytes 1572872 | tf_op jit(solution)/shard_map/ppermute | solution.py:324
  2.5 6.2 %collective-permute-start.3 = (bf16[64,128]{1,0:T(8,128)(2,1)S(1)}, bf16[64,128]{1,0:T(8,128)(2,1)S(1)}, u32[]{:S(2)}, u32[]{:S(2)}) collective-permute-start(bf16[64,128]{1,0:T(8,128)(2,1)S(1)} %get-tuple-element.19), channel_id=1, source_target_pairs={{0,7},{1,6},{2,5},{3,4},{4,3},{5,2},{6,1},{7,0},{8,15},{9,14},{10,... | collective-permute-start | bytes 49160 | tf_op jit(solution)/shard_map/ppermute | solution.py:330
  7.2 4.1 %collective-permute-start.2 = (bf16[64,128]{1,0:T(8,128)(2,1)S(1)}, bf16[64,128]{1,0:T(8,128)(2,1)S(1)}, u32[]{:S(2)}, u32[]{:S(2)}) collective-permute-start(bf16[64,128]{1,0:T(8,128)(2,1)S(1)} %get-tuple-element.19), channel_id=1, source_target_pairs={{0,6},{1,7},{2,4},{3,5},{4,2},{5,3},{6,0},{7,1},{8,14},{9,15},{10,... | collective-permute-start | bytes 49160 | tf_op jit(solution)/shard_map/ppermute | solution.py:330
  7.2 4.1 %collective-permute-start.1 = (bf16[64,128]{1,0:T(8,128)(2,1)S(1)}, bf16[64,128]{1,0:T(8,128)(2,1)S(1)}, u32[]{:S(2)}, u32[]{:S(2)}) collective-permute-start(bf16[64,128]{1,0:T(8,128)(2,1)S(1)} %get-tuple-element.19), channel_id=1, source_target_pairs={{0,5},{1,4},{2,7},{3,6},{4,1},{5,0},{6,3},{7,2},{8,13},{9,12},{10,... | collective-permute-start | bytes 49160 | tf_op jit(solution)/shard_map/ppermute | solution.py:330
  11.5 1.3 %collective-permute-start.4 = (f32[64,128]{1,0:T(8,128)S(1)}, f32[64,128]{1,0:T(8,128)S(1)}, u32[]{:S(2)}, u32[]{:S(2)}) collective-permute-start(f32[64,128]{1,0:T(8,128)S(1)} %get-tuple-element.22.other_ref), channel_id=1, source_target_pairs={{0,4},{4,0},{8,12},{12,8},{16,20},{20,16},{24,28},{28,24},{1,5},{5... | collective-permute-start | bytes 98312 | tf_op jit(solution)/shard_map/ppermute | solution.py:324
  12.8 3.2 %copy-start = (f32[8,16,2]{1,2,0:T(2,128)S(1)}, f32[8,16,2]{1,2,0:T(2,128)}, u32[]{:S(2)}) copy-start(f32[8,16,2]{1,2,0:T(2,128)} %param.7) | copy-start | bytes 3076
  13.1 4.2 %collective-permute-start.8 = (bf16[8,4224]{1,0:T(8,128)(2,1)S(1)}, bf16[8,4224]{1,0:T(8,128)(2,1)S(1)}, u32[]{:S(2)}, u32[]{:S(2)}) collective-permute-start(bf16[8,4224]{1,0:T(8,128)(2,1)S(1)} %get-tuple-element.23), channel_id=1, source_target_pairs={{0,28},{1,29},{2,30},{3,31},{4,0},{5,1},{6,2},{7,3},{8,20},{9,21},... | collective-permute-start | bytes 202760 | tf_op jit(solution)/shard_map/ppermute | solution.py:345
  15.3 2.5 %collective-permute-start.7 = (bf16[8,4224]{1,0:T(8,128)(2,1)S(1)}, bf16[8,4224]{1,0:T(8,128)(2,1)S(1)}, u32[]{:S(2)}, u32[]{:S(2)}) collective-permute-start(bf16[8,4224]{1,0:T(8,128)(2,1)S(1)} %get-tuple-element.23), channel_id=1, source_target_pairs={{0,20},{1,21},{2,22},{3,23},{4,0},{5,1},{6,2},{7,3},{8,28},{9,29},... | collective-permute-start | bytes 202760 | tf_op jit(solution)/shard_map/ppermute | solution.py:345
  15.3 2.6 %collective-permute-start.6 = (bf16[8,4224]{1,0:T(8,128)(2,1)S(1)}, bf16[8,4224]{1,0:T(8,128)(2,1)S(1)}, u32[]{:S(2)}, u32[]{:S(2)}) collective-permute-start(bf16[8,4224]{1,0:T(8,128)(2,1)S(1)} %get-tuple-element.23), channel_id=1, source_target_pairs={{0,12},{1,13},{2,14},{3,15},{4,0},{5,1},{6,2},{7,3},{8,4},{9,5},{1... | collective-permute-start | bytes 202760 | tf_op jit(solution)/shard_map/ppermute | solution.py:345
  16.0 1.9 %collective-permute-start.5 = (bf16[8,4224]{1,0:T(8,128)(2,1)S(1)}, bf16[8,4224]{1,0:T(8,128)(2,1)S(1)}, u32[]{:S(2)}, u32[]{:S(2)}) collective-permute-start(bf16[8,4224]{1,0:T(8,128)(2,1)S(1)} %get-tuple-element.23), channel_id=1, source_target_pairs={{0,4},{1,5},{2,6},{3,7},{4,0},{5,1},{6,2},{7,3},{8,12},{9,13},{10,... | collective-permute-start | bytes 202760 | tf_op jit(solution)/shard_map/ppermute | solution.py:345
  18.5 4.9 %collective-permute-start.12 = (f32[8,128]{1,0:T(8,128)S(1)}, f32[8,128]{1,0:T(8,128)S(1)}, u32[]{:S(2)}, u32[]{:S(2)}) collective-permute-start(f32[8,128]{1,0:T(8,128)S(1)} %get-tuple-element.27), channel_id=1, source_target_pairs={{0,4},{1,5},{2,6},{3,7},{4,3},{5,2},{6,1},{7,0},{8,12},{9,13},{10,... | collective-permute-start | bytes 12296 | tf_op jit(solution)/shard_map/ppermute | solution.py:345
  20.2 3.9 %collective-permute-start.11 = (f32[8,128]{1,0:T(8,128)S(1)}, f32[8,128]{1,0:T(8,128)S(1)}, u32[]{:S(2)}, u32[]{:S(2)}) collective-permute-start(f32[8,128]{1,0:T(8,128)S(1)} %get-tuple-element.27), channel_id=1, source_target_pairs={{0,4},{1,5},{2,6},{3,7},{4,2},{5,3},{6,0},{7,1},{8,12},{9,13},{10,... | collective-permute-start | bytes 12296 | tf_op jit(solution)/shard_map/ppermute | solution.py:345
  20.3 3.8 %collective-permute-start.10 = (f32[8,128]{1,0:T(8,128)S(1)}, f32[8,128]{1,0:T(8,128)S(1)}, u32[]{:S(2)}, u32[]{:S(2)}) collective-permute-start(f32[8,128]{1,0:T(8,128)S(1)} %get-tuple-element.27), channel_id=1, source_target_pairs={{0,4},{1,5},{2,6},{3,7},{4,1},{5,0},{6,3},{7,2},{8,12},{9,13},{10,... | collective-permute-start | bytes 12296 | tf_op jit(solution)/shard_map/ppermute | solution.py:345
  22.2 1.8 %collective-permute-start.9 = (f32[8,128]{1,0:T(8,128)S(1)}, f32[8,128]{1,0:T(8,128)S(1)}, u32[]{:S(2)}, u32[]{:S(2)}) collective-permute-start(f32[8,128]{1,0:T(8,128)S(1)} %get-tuple-element.27), channel_id=1, source_target_pairs={{0,4},{1,5},{2,6},{3,7},{4,0},{5,1},{6,2},{7,3},{8,12},{9,13},{10,... | collective-permute-start | bytes 12296 | tf_op jit(solution)/shard_map/ppermute | solution.py:345
  24.3 2.0 %collective-permute-start.16 = (bf16[8,4224]{1,0:T(8,128)(2,1)S(1)}, bf16[8,4224]{1,0:T(8,128)(2,1)S(1)}, u32[]{:S(2)}, u32[]{:S(2)}) collective-permute-start(bf16[8,4224]{1,0:T(8,128)(2,1)S(1)} %get-tuple-element.28), channel_id=1, source_target_pairs={{0,28},{1,29},{2,30},{3,31},{4,0},{5,1},{6,2},{7,3},{8,20},{9,21},... | collective-permute-start | bytes 202760 | tf_op jit(solution)/shard_map/ppermute | solution.py:345
  24.4 3.1 %collective-permute-start.15 = (bf16[8,4224]{1,0:T(8,128)(2,1)S(1)}, bf16[8,4224]{1,0:T(8,128)(2,1)S(1)}, u32[]{:S(2)}, u32[]{:S(2)}) collective-permute-start(bf16[8,4224]{1,0:T(8,128)(2,1)S(1)} %get-tuple-element.28), channel_id=1, source_target_pairs={{0,20},{1,21},{2,22},{3,23},{4,0},{5,1},{6,2},{7,3},{8,28},{9,29},... | collective-permute-start | bytes 202760 | tf_op jit(solution)/shard_map/ppermute | solution.py:345
  25.1 2.5 %collective-permute-start.14 = (bf16[8,4224]{1,0:T(8,128)(2,1)S(1)}, bf16[8,4224]{1,0:T(8,128)(2,1)S(1)}, u32[]{:S(2)}, u32[]{:S(2)}) collective-permute-start(bf16[8,4224]{1,0:T(8,128)(2,1)S(1)} %get-tuple-element.28), channel_id=1, source_target_pairs={{0,12},{1,13},{2,14},{3,15},{4,0},{5,1},{6,2},{7,3},{8,4},{9,5},{1... | collective-permute-start | bytes 202760 | tf_op jit(solution)/shard_map/ppermute | solution.py:345
  25.6 1.9 %collective-permute-start.13 = (bf16[8,4224]{1,0:T(8,128)(2,1)S(1)}, bf16[8,4224]{1,0:T(8,128)(2,1)S(1)}, u32[]{:S(2)}, u32[]{:S(2)}) collective-permute-start(bf16[8,4224]{1,0:T(8,128)(2,1)S(1)} %get-tuple-element.28), channel_id=1, source_target_pairs={{0,4},{1,5},{2,6},{3,7},{4,0},{5,1},{6,2},{7,3},{8,12},{9,13},{10,... | collective-permute-start | bytes 202760 | tf_op jit(solution)/shard_map/ppermute | solution.py:345
  27.7 2.9 %collective-permute-start.17 = (f32[8,4096]{1,0:T(8,128)S(1)}, f32[8,4096]{1,0:T(8,128)S(1)}, u32[]{:S(2)}, u32[]{:S(2)}) collective-permute-start(f32[8,4096]{1,0:T(8,128)S(1)} %shard_map.67.wave_ref), channel_id=1, source_target_pairs={{0,4},{4,0},{8,12},{12,8},{16,20},{20,16},{24,28},{28,24},{1,5},{5... | collective-permute-start | bytes 393224 | tf_op jit(solution)/shard_map/ppermute | solution.py:324
  29.4 1.2 %collective-permute-start.18 = (f32[8,128]{1,0:T(8,128)S(1)}, f32[8,128]{1,0:T(8,128)S(1)}, u32[]{:S(2)}, u32[]{:S(2)}) collective-permute-start(f32[8,128]{1,0:T(8,128)S(1)} %get-tuple-element.29.residual_ref), channel_id=1, source_target_pairs={{0,4},{4,0},{8,12},{12,8},{16,20},{20,16},{24,28},{28,24},{1,5},{5... | collective-permute-start | bytes 12296 | tf_op jit(solution)/shard_map/ppermute | solution.py:324

commit v11 on v10

--- a/solution.py
+++ b/solution.py
@@ -99,13 +99,13 @@
     return result
 
 
-def first_kernel(layers, wave_hbm, k_hbm, observed_hbm, packet_ref, wave_ref, block_ref, observed_ref, tile, arrived):
-    rows = k_hbm.shape[0]
+def first_kernel(layers, wave_hbm, k_hbm, observed_hbm, packet_ref, wave_ref, k_ref, observed_ref, tile, arrived):
+    rows = k_ref.shape[0]
     models = wave_ref.shape[0]
     loads = [
         pltpu.make_async_copy(source, target, arrived.at[i])
         for i, (source, target) in enumerate(
-            ((wave_hbm, wave_ref), (k_hbm, block_ref.at[:rows]), (observed_hbm, observed_ref))
+            ((wave_hbm, wave_ref), (k_hbm, k_ref), (observed_hbm, observed_ref))
         )
     ]
     for load in loads:
@@ -116,36 +116,51 @@
     tile[...] = edge_tile(lambda l: layer_tiles(wave_ref, l), layers, rows)
     loads[1].wait()
     loads[2].wait()
-    edges = edge_tile(lambda l: tuple(t[:rows].astype(F32) for t in layer_tiles(block_ref, l)), layers, rows)
+    edges = edge_tile(lambda l: tuple(t.astype(F32) for t in layer_tiles(k_ref, l)), layers, rows)
     packet_ref[:rows, :] = edges.astype(BF16)
-    tile[:, :rows] = nt_dot(model, block_ref[:rows, :])
-    packet_ref[rows:, :] = jnp.concatenate(pieces(tile[...], 2), axis=0).astype(BF16)
+    tile[:, :rows] = nt_dot(model, k_ref[...])
+    parts = pieces(tile[...], 2)
     tile[...] = jnp.zeros_like(tile)
     tile[:, :rows] = observed_ref[...]
-    below = pieces(tile[...], 3) + [jnp.zeros_like(tile)]
-    below = [jnp.concatenate(below[i : i + 2], axis=0).astype(BF16) for i in (0, 2)]
-    packed = [packet_ref[i : i + 2 * models, :] for i in range(0, packet_ref.shape[0], 2 * models)] + below
-    for i, part in enumerate(packed):
-        block_ref[rows:, i * LANES : (i + 1) * LANES] = part
+    parts += pieces(tile[...], 3) + [jnp.zeros_like(tile)]
+    packet_ref[rows:, :] = jnp.concatenate(parts, axis=0).astype(BF16)
+
+
+def joining_kernel(models, mine_ref, other_ref, k_in_ref, both_ref, observed_ref, k_ref):
+    del k_in_ref, k_ref
+    is_first = on_first_core()
+    mine, other = mine_ref[...].astype(F32), other_ref[...].astype(F32)
+    first, second = jnp.where(is_first, mine, other), jnp.where(is_first, other, mine)
+    end = mine.shape[0] - 4 * models
+    rows = end - 2 * models
+    both_ref[...] = jnp.concatenate([first[:end], second[:end]], axis=0).astype(BF16)
+
+    def observations(packet):
+        high, middle, low = (packet[i : i + models] for i in range(end, end + 3 * models, models))
+        return (high + middle) + low
+
+    observed_ref[...] = observations(first) + turned(observations(second), rows)
 
 
 def on_first_core():
     return lax.rem(lax.axis_index("dp"), 2) == 0
 
 
-def applied_kernel(layers, rows, block_ref, other_ref, kw_ref):
+def applied_kernel(layers, k_ref, k_other_ref, kw_ref):
     core = lax.rem(lax.axis_index("dp"), 2)
+    rows = k_ref.shape[0]
     kw_ref[2 * rows :, :] = jnp.zeros((kw_ref.shape[0] - 2 * rows, kw_ref.shape[1]), BF16)
-    for which, source in ((core, block_ref), (1 - core, other_ref)):
-        waves = forward_wave(*stacked(source.at[:rows], layers))
+    for which, source in ((core, k_ref), (1 - core, k_other_ref)):
+        waves = forward_wave(*stacked(source, layers))
         kw_ref[pl.ds(pl.multiple_of(which * rows, 16), rows), :] = unstacked(*waves, rows).astype(BF16)
 
 
-def transposing_kernel(rows, block_ref, other_ref, kt_ref):
+def transposing_kernel(k_ref, k_other_ref, kt_ref):
     is_first = on_first_core()
+    rows = k_ref.shape[0]
     rest = jnp.zeros((LANES - 2 * rows, LANES), F32)
     for start in range(0, kt_ref.shape[0], LANES):
-        mine, other = (ref[:rows, start : start + LANES].astype(F32) for ref in (block_ref, other_ref))
+        mine, other = (ref[:, start : start + LANES].astype(F32) for ref in (k_ref, k_other_ref))
         both = [jnp.where(is_first, mine, other), jnp.where(is_first, other, mine), rest]
         kt_ref[start : start + LANES, :] = jnp.concatenate(both, axis=0).T.astype(BF16)
 
@@ -167,36 +182,25 @@
     cut_halo_ref[...] = halo
 
 
-def second_kernel(layers, n_vox, models, *refs):
-    (block_ref, *packets, out_ref, halo_ref, held) = refs
-    rows = held.shape[1] - 2 * models
-    me = lax.axis_index("vox")
-    for distance, packet in enumerate(packets, 1):
-        held[me ^ distance] = packet[...]
-    chunks = held.shape[1] // (2 * models)
-    below = [block_ref[rows:, i * LANES : (i + 1) * LANES] for i in range(chunks + 2)]
-    for i in range(chunks):
-        held[me, i * 2 * models : (i + 1) * 2 * models] = below[i]
-    high, low = below[chunks].astype(F32), below[chunks + 1].astype(F32)
-    observed = ((high[:models] + high[models:]) + low[:models])[:, :rows]
-    left, right = lax.rem(me + n_vox - 1, n_vox), lax.rem(me + 1, n_vox)
-    lane = lanes_of((models, LANES))
-    inside = (lane >= rows) & (lane < rows + KINDS * layers)
-
-    def edge_values(which):
-        both = held[which, rows:, :].astype(F32)
-        return both[:models] + both[models:]
-
-    edge = [edge_values(z) for z in range(n_vox)]
-    terms, columns = [], []
-    for z in range(n_vox):
-        before, after = edge[z - 1], edge[(z + 1) % n_vox]
+def back_projected(residual, kw_ref, columns, g_ref):
+    width = kw_ref.shape[1]
+    sent = residual.astype(BF16)
+    g_ref[:, :width] = jnp.dot(sent, kw_ref[...], preferred_element_type=F32).astype(BF16)
+    g_ref[:, width:] = jnp.dot(sent, columns, preferred_element_type=F32).astype(BF16)
+
+
+def edge_terms(edge, base, layers):
+    lane = lanes_of(edge[0].shape)
+    inside = (lane >= base) & (lane < base + KINDS * layers)
+    terms = []
+    for z, own in enumerate(edge):
+        before, after = edge[z - 1], edge[(z + 1) % len(edge)]
         next_smooth = turned(after, O_LAST - E_FIRST)
         next_detail = turned(after, O_LAST - O_FIRST)
-        next_even = next_smooth - 0.25 * (edge[z] + next_detail)
+        next_even = next_smooth - 0.25 * (own + next_detail)
         term = by_kind(
             lane,
-            rows,
+            base,
             0.0,
             -0.25 * turned(before, E_FIRST - O_LAST),
             0.0,
@@ -204,60 +208,65 @@
             -0.125 * turned(before, O_FIRST - O_LAST),
         )
         terms.append(jnp.where(inside, term, 0.0).astype(BF16))
-        columns.append(held[z, :rows, :])
-    predicted = nt_dot(jnp.concatenate(terms, axis=1), jnp.concatenate(columns, axis=1))
-    shares = edge[0]
-    for z in range(1, n_vox):
-        shares = shares + edge[z]
-    predicted = predicted + shares[:, :rows]
-
-    before, own, after = (held[z, :rows, :].astype(F32) for z in (left, me, right))
+    return jnp.concatenate(terms, axis=1)
+
+
+def halo_columns(before, own, after, base):
+    lane = lanes_of(own.shape)
     details = by_kind(
-        lanes_of(own.shape),
-        rows,
+        lane,
+        base,
         0.0,
         0.0,
         0.0,
         own - 0.5 * (turned(own, O_LAST - E_LAST) + turned(after, O_LAST - E_FIRST)),
         after - 0.5 * (turned(after, O_FIRST - E_FIRST) + turned(after, O_FIRST - E_SECOND)),
     )
-    out_ref[:rows, :] = by_kind(
-        lanes_of(own.shape),
-        rows,
+    return by_kind(
+        lane,
+        base,
         turned(after, E_NEXT - E_FIRST),
         turned(before, D_BEFORE - O_LAST) - 0.5 * (turned(before, D_BEFORE - E_LAST) + own),
         turned(after, S_NEXT - E_FIRST) + 0.25 * (turned(details, S_NEXT - D_LAST) + turned(details, S_NEXT - D_NEXT)),
         details,
         details,
     )
-    out_ref[rows:, :] = jnp.zeros((2 * models, LANES), F32)
-    out_ref[rows : rows + models, :rows] = observed - predicted
-    out_ref[rows + models :, :rows] = observed
-    before, own, after = (edge_values(z) for z in (left, me, right))
+
+
+def second_kernel(layers, n_vox, observed_ref, kw_ref, *refs):
+    (*packets, g_ref, columns_ref, halo_ref, held, tile) = refs
+    models = observed_ref.shape[0]
+    size = held.shape[1] // 2
+    rows = size - 2 * models
+    me = lax.axis_index("vox")
+    for distance, packet in enumerate(reversed(packets)):
+        held[me ^ distance] = packet[...]
+    left, right = lax.rem(me + n_vox - 1, n_vox), lax.rem(me + 1, n_vox)
+    lane = lanes_of((models, LANES))
+
+    def values(which, core):
+        both = held[which, core * size + rows : (core + 1) * size, :].astype(F32)
+        return both[:models] + both[models:]
+
+    terms = edge_terms([values(z, 0) for z in range(n_vox)], rows, layers)
+    columns = []
+    tile[...] = jnp.zeros_like(tile)
+    for core in range(2):
+        edges = jnp.concatenate([held[z, core * size : core * size + rows, :] for z in range(n_vox)], axis=1)
+        shares = values(0, core)
+        for z in range(1, n_vox):
+            shares = shares + values(z, core)
+        tile[:, core * rows : (core + 1) * rows] = nt_dot(terms, edges) + shares[:, :rows]
+        around = [held[z, core * size : core * size + rows, :].astype(F32) for z in (left, me, right)]
+        columns.append(halo_columns(*around, rows))
+    columns.append(jnp.zeros((LANES - 2 * rows, LANES), F32))
+    columns = jnp.concatenate(columns, axis=0).astype(BF16)
+    columns_ref[...] = columns
+    back_projected(observed_ref[...] - tile[...], kw_ref, columns, g_ref)
+    before, own, after = (values(z, 0) for z in (left, me, right))
     halo_ref[...] = by_kind(
         lane, rows, 0.0, turned(before, D_BEFORE - O_LAST), turned(after, S_NEXT - E_FIRST), own, after
     )
-
-
-def back_projected(residual, kw_ref, columns, g_ref):
-    width = kw_ref.shape[1]
-    sent = residual.astype(BF16)
-    g_ref[:, :width] = jnp.dot(sent, kw_ref[...], preferred_element_type=F32).astype(BF16)
-    g_ref[:, width:] = jnp.dot(sent, columns, preferred_element_type=F32).astype(BF16)
-
-
-def third_kernel(mine_ref, other_ref, kw_ref, g_ref, columns_ref, observed_ref):
-    models = g_ref.shape[0]
-    rows = mine_ref.shape[0] - 2 * models
-    is_first = on_first_core()
-    mine, other = mine_ref[...], other_ref[...]
-    first, second = jnp.where(is_first, mine, other), jnp.where(is_first, other, mine)
-    rest = jnp.zeros((LANES - 2 * rows, LANES), F32)
-    columns = jnp.concatenate([first[:rows], second[:rows], rest], axis=0).astype(BF16)
-    columns_ref[...] = columns
-    below = first[rows:] + turned(second[rows:], rows)
-    observed_ref[...] = below[models:]
-    back_projected(below[:models], kw_ref, columns, g_ref)
 
 
 def added(shares):
@@ -324,12 +333,6 @@
     return lax.ppermute(x, axis, [(i, i ^ distance) for i in range(lax.axis_size(axis))])
 
 
-def from_other_core(x, vox):
-    n_vox = lax.axis_size("vox")
-    places = [(d, z) for d in range(lax.axis_size("dp")) for z in range(n_vox)]
-    return lax.ppermute(x, ("dp", "vox"), [(d * n_vox + z, (d ^ 1) * n_vox + (z ^ vox)) for d, z in places])
-
-
 def from_same_core(x, chips, vox):
     n_vox = lax.axis_size("vox")
     places = [(d, z) for d in range(lax.axis_size("dp")) for z in range(n_vox)]
@@ -351,7 +354,7 @@
         fours = [x] + [from_same_core(x, *step(lowest * n)) for n in (1, 2, 3)]
         x = added([f.astype(F32) for f in fours]).astype(x.dtype)
         lowest, size = lowest * 4, size // 4
-    return [handed_over(x, sender, *step(lowest * n)) for n in range(size)]
+    return [handed_over(x, sender, *step(lowest * n)) for n in reversed(range(size))]
 
 
 def over_chips(x):
@@ -362,13 +365,14 @@
     return shares_over(x, lax.axis_size("vox"), lambda n: (0, n), 1)
 
 
-def call(kernel, out_shape, *args, scratch=(), space=pltpu.VMEM):
+def call(kernel, out_shape, *args, scratch=(), space=pltpu.VMEM, aliases=None):
     return pl.pallas_call(
         kernel,
         out_shape=out_shape,
         in_specs=[pl.BlockSpec(memory_space=space)] * len(args),
         out_specs=jax.tree.map(lambda _: pl.BlockSpec(memory_space=pltpu.VMEM), out_shape),
         scratch_shapes=list(scratch),
+        input_output_aliases=aliases or {},
         compiler_params=pltpu.CompilerParams(vmem_limit_bytes=KERNEL_BYTES),
     )(*[pltpu.with_memory_space_constraint(arg, space) for arg in args])
 
@@ -378,60 +382,57 @@
     rows = kernels.shape[0]
     layers = threshold.shape[1]
     n_vox = lax.axis_size("vox")
-    packet_rows = rows + 2 * models
     assert width == 2 * layers * LANES and rows + KINDS * layers <= LANES and 2 * rows <= LANES
-    assert packet_rows % (2 * models) == 0 and packet_rows // (2 * models) + 2 <= 2 * layers
     g_shape = pltpu.VMEM((models, width + LANES), BF16)
+    k_shape = pltpu.VMEM((rows, width), BF16)
     tile_shape = pltpu.VMEM((models, LANES), F32)
-
-    packet, wavelets, block = call(
+    both_shape = pltpu.VMEM((2 * (rows + 2 * models), LANES), BF16)
+
+    packet, wavelets, k_mine = call(
         functools.partial(first_kernel, layers),
-        (
-            pltpu.VMEM((packet_rows, LANES), BF16),
-            pltpu.VMEM((models, width), F32),
-            pltpu.VMEM((rows + 2 * models, width), BF16),
-        ),
+        (pltpu.VMEM((rows + 6 * models, LANES), BF16), pltpu.VMEM((models, width), F32), k_shape),
         initial,
         kernels,
         observed,
-        scratch=[
-            pltpu.VMEM((models, rows), F32),
-            pltpu.VMEM((models, LANES), F32),
-            pltpu.SemaphoreType.DMA((3,)),
-        ],
+        scratch=[pltpu.VMEM((models, rows), F32), tile_shape, pltpu.SemaphoreType.DMA((3,))],
         space=pltpu.HBM,
     )
-    block_other = from_partner(block, "dp", 1)
-    packets = [from_other_core(packet, d) for d in range(1, n_vox)]
-    kw = call(functools.partial(applied_kernel, layers, rows), pltpu.VMEM((LANES, width), BF16), block, block_other)
-    kt = call(functools.partial(transposing_kernel, rows), pltpu.VMEM((width, LANES), BF16), block, block_other)
+    both, observed_both, k_mine = call(
+        functools.partial(joining_kernel, models),
+        (both_shape, tile_shape, k_shape),
+        packet,
+        from_partner(packet, "dp", 1),
+        k_mine,
+        aliases={2: 2},
+    )
+    k_other = from_partner(k_mine, "dp", 1)
+    packets = [handed_over(both, 1, 0, d) for d in reversed(range(1, n_vox))] + [both]
+    kw = call(functools.partial(applied_kernel, layers), pltpu.VMEM((LANES, width), BF16), k_mine, k_other)
+    kt = call(transposing_kernel, pltpu.VMEM((width, LANES), BF16), k_mine, k_other)
     cut, cut_halo = call(
         functools.partial(spread_kernel, layers, rows),
         (pltpu.VMEM((models, width), F32), tile_shape),
         jnp.swapaxes(threshold, 1, 2),
     )
-    other, halo = call(
-        functools.partial(second_kernel, layers, n_vox, models),
-        (pltpu.VMEM((packet_rows, LANES), F32), tile_shape),
-        block_other,
+    g, columns, halo = call(
+        functools.partial(second_kernel, layers, n_vox),
+        (g_shape, pltpu.VMEM((LANES, LANES), BF16), tile_shape),
+        observed_both,
+        kw,
         *packets,
-        scratch=[pltpu.VMEM((n_vox, packet_rows, LANES), BF16)],
-    )
-    mine = from_partner(other, "dp", 1)
-    g, columns, observed = call(
-        third_kernel, (g_shape, pltpu.VMEM((LANES, LANES), BF16), tile_shape), mine, other, kw
+        scratch=[pltpu.VMEM((n_vox, *both_shape.shape), BF16), tile_shape],
     )
     wavelets, predicted = call(
         functools.partial(fourth_kernel, layers, rows),
         (pltpu.VMEM((models, width), F32), tile_shape),
         wavelets,
         cut,
-        halo,
+        from_partner(halo, "dp", 1),
         cut_halo,
         kt,
         *over_chips(g),
     )
-    g, residual = call(fifth_kernel, (g_shape, tile_shape), kw, columns, observed, *over_vox(predicted))
+    g, residual = call(fifth_kernel, (g_shape, tile_shape), kw, columns, observed_both, *over_vox(predicted))
     coefficients = call(
         functools.partial(sixth_kernel, layers, rows),
         pltpu.VMEM((models, width), F32),

time: 31.4 us -> 29.1 us (0.927)
  starting transfers between devices: 15.5 us -> 14 us
  waiting for transfers between devices: 10.4 us -> 9.57 us
    ppermute x3 -> x0, starting transfers between devices: 5.04 us -> none  [from_other_core(): lax.ppermute(x, ('dp', 'vox'), [(d * n_vox + z, (d ^ 1) * n_vox + (z ^ vo...]
    ppermute x3 -> x0, waiting for transfers between devices: 3.75 us -> none  [from_other_core(): lax.ppermute(x, ('dp', 'vox'), [(d * n_vox + z, (d ^ 1) * n_vox + (z ^ vo...]
    ppermute x12 -> x15, starting transfers between devices: 7.98 us -> 11.5 us  [handed_over(): return lax.ppermute(x, ('dp', 'vox'), route)]
    ppermute x12 -> x15, waiting for transfers between devices: 4.93 us -> 7.26 us  [handed_over(): return lax.ppermute(x, ('dp', 'vox'), route)]
    ppermute x4 -> x5, waiting for transfers between devices: 1.73 us -> 2.31 us  [from_partner(): lax.ppermute(x, axis, [(i, i ^ distance) for i in range(lax.axis_size(axi...]
    ppermute x4 -> x5, starting transfers between devices: 2.48 us -> 2.5 us  [from_partner(): lax.ppermute(x, axis, [(i, i ^ distance) for i in range(lax.axis_size(axi...]
  transfers between devices with their start and end apart: 19 -> 20, of which waited for: 12 -> 10; matrix products, arithmetic and copies ran while one was open for 0% -> 0% of each run, Pallas kernels for 4% -> 4%
where the time goes in v11:
time: 29.1 us; the launch traced here: 29 us
  starting transfers between devices  14 us (48%)
  waiting for transfers between devices  9.57 us (33%)
  Pallas kernels  4.72 us (16%)
  between operations  0.7 us (2%)
    ppermute x15, starting transfers between devices, handed_over(): return lax.ppermute(x, ('dp', 'vox'), route)  11.5 us
    ppermute x15, waiting for transfers between devices, handed_over(): return lax.ppermute(x, ('dp', 'vox'), route)  7.26 us
    pallas_call x10, Pallas kernels, call(): pl.pallas_call(kernel, out_shape=out_shape, in_specs=[pl.BlockSpec(memory...  4.72 us
    ppermute x5, starting transfers between devices, from_partner(): lax.ppermute(x, axis, [(i, i ^ distance) for i in range(lax.axis_size(axi...  2.5 us
    ppermute x5, waiting for transfers between devices, from_partner(): lax.ppermute(x, axis, [(i, i ^ distance) for i in range(lax.axis_size(axi...  2.31 us
  transfers between devices with their start and end apart: 20, of which 10 were waited for; matrix products, arithmetic and copies ran while one was open for 0% of the time, Pallas kernels for 4%

profile of v11, /device:TPU:0, one launch (start us, length us, event | category | flops | bytes accessed | tf_op | source)
XLA Modules:
  0.0 29.0 jit_solution(17624910118368622229)
XLA Ops:
  0.6 1.3 %shard_map.59 = (bf16[96,128]{1,0:T(8,128)(2,1)S(1)}, f32[8,4096]{1,0:T(8,128)S(1)}, bf16[48,4096]{1,0:T(8,128)(2,1)S(1)}) custom-call(f32[8,4096]{1,0:T(8,128)} %wave_hbm.1, bf16[48,4096]{1,0:T(8,128)(2,1)} %k_hbm.1, f32[8,48]{1,0:T(8,128)} %observed_hbm.1), custom_call_target="tpu_custom_call" | custom-call | tf_op jit(solution)/shard_map/pallas_call | solution.py:369
  2.0 0.5 %collective-permute-start = (bf16[96,128]{1,0:T(8,128)(2,1)S(1)}, bf16[96,128]{1,0:T(8,128)(2,1)S(1)}, u32[]{:S(2)}, u32[]{:S(2)}) collective-permute-start(bf16[96,128]{1,0:T(8,128)(2,1)S(1)} %get-tuple-element.19.mine_ref), channel_id=1, source_target_pairs={{0,4},{4,0},{8,12},{12,8},{16,20},{20,16},{24,28},{28,24},{1,5},{5... | collective-permute-start | bytes 73736 | tf_op jit(solution)/shard_map/ppermute | solution.py:333
  2.5 0.8 %collective-permute-done.other_ref = bf16[96,128]{1,0:T(8,128)(2,1)S(1)} collective-permute-done((bf16[96,128]{1,0:T(8,128)(2,1)S(1)}, bf16[96,128]{1,0:T(8,128)(2,1)S(1)}, u32[]{:S(2)}, u32[]{:S(2)}) %collective-permute-start) | collective-permute-done | bytes 24608 | tf_op jit(solution)/shard_map/ppermute | solution.py:333
  3.3 0.1 shard_map.61
  3.4 0.3 %collective-permute-start.1 = (bf16[48,4096]{1,0:T(8,128)(2,1)S(1)}, bf16[48,4096]{1,0:T(8,128)(2,1)S(1)}, u32[]{:S(2)}, u32[]{:S(2)}) collective-permute-start(bf16[48,4096]{1,0:T(8,128)(2,1)S(1)} %get-tuple-element.22.k_ref), channel_id=1, source_target_pairs={{0,4},{4,0},{8,12},{12,8},{16,20},{20,16},{24,28},{28,24},{1,5},{5... | collective-permute-start | bytes 1179656 | tf_op jit(solution)/shard_map/ppermute | solution.py:333
  3.8 0.2 collective-permute-start.2
  3.9 4.7 %collective-permute-start.3 = (bf16[128,128]{1,0:T(8,128)(2,1)S(1)}, bf16[128,128]{1,0:T(8,128)(2,1)S(1)}, u32[]{:S(2)}, u32[]{:S(2)}) collective-permute-start(bf16[128,128]{1,0:T(8,128)(2,1)S(1)} %get-tuple-element.23.refs_3_), channel_id=1, source_target_pairs={{0,4},{1,5},{2,6},{3,7},{4,2},{5,3},{6,0},{7,1},{8,12},{9,13},{10,... | collective-permute-start | bytes 98312 | tf_op jit(solution)/shard_map/ppermute | solution.py:348
  8.7 0.0 collective-permute-start.4
  8.7 0.0 collective-permute-done.1.k_other_ref
  8.7 0.5 %shard_map.62.kw_ref = bf16[128,4096]{1,0:T(8,128)(2,1)S(1)} custom-call(bf16[48,4096]{1,0:T(8,128)(2,1)S(1)} %get-tuple-element.22.k_ref, bf16[48,4096]{1,0:T(8,128)(2,1)S(1)} %collective-permute-done.1.k_other_ref), custom_call_target="tpu_custom_call" | custom-call | tf_op jit(solution)/shard_map/pallas_call | solution.py:369
  9.1 1.0 %collective-permute-done.2.refs_0_ = bf16[128,128]{1,0:T(8,128)(2,1)S(1)} collective-permute-done((bf16[128,128]{1,0:T(8,128)(2,1)S(1)}, bf16[128,128]{1,0:T(8,128)(2,1)S(1)}, u32[]{:S(2)}, u32[]{:S(2)}) %collective-permute-start.2) | collective-permute-done | bytes 32800 | tf_op jit(solution)/shard_map/ppermute | solution.py:348
  10.1 0.0 collective-permute-done.3.refs_1_
  10.1 1.9 %collective-permute-done.4.refs_2_ = bf16[128,128]{1,0:T(8,128)(2,1)S(1)} collective-permute-done((bf16[128,128]{1,0:T(8,128)(2,1)S(1)}, bf16[128,128]{1,0:T(8,128)(2,1)S(1)}, u32[]{:S(2)}, u32[]{:S(2)}) %collective-permute-start.4) | collective-permute-done | bytes 32800 | tf_op jit(solution)/shard_map/ppermute | solution.py:348
  12.0 0.5 %shard_map.63 = (bf16[8,4224]{1,0:T(8,128)(2,1)S(1)}, bf16[128,128]{1,0:T(8,128)(2,1)S(1)}, f32[8,128]{1,0:T(8,128)S(1)}) custom-call(f32[8,128]{1,0:T(8,128)S(1)} %get-tuple-element.21.observed_ref, bf16[128,4096]{1,0:T(8,128)(2,1)S(1)} %shard_map.62.kw_ref, bf16[128,128]{1,0:T(8,128)(2,1)S(1)} %collective-permute-done.2.refs_0_, ...), custom_call_target="tpu_custom_call" | custom-call | tf_op jit(solution)/shard_map/pallas_call | solution.py:369
  12.5 0.4 %collective-permute-start.6 = (bf16[8,4224]{1,0:T(8,128)(2,1)S(1)}, bf16[8,4224]{1,0:T(8,128)(2,1)S(1)}, u32[]{:S(2)}, u32[]{:S(2)}) collective-permute-start(bf16[8,4224]{1,0:T(8,128)(2,1)S(1)} %get-tuple-element.26), channel_id=1, source_target_pairs={{0,28},{1,29},{2,30},{3,31},{4,0},{5,1},{6,2},{7,3},{8,20},{9,21},... | collective-permute-start | bytes 202760 | tf_op jit(solution)/shard_map/ppermute | solution.py:348
  12.9 1.3 %collective-permute-start.7 = (bf16[8,4224]{1,0:T(8,128)(2,1)S(1)}, bf16[8,4224]{1,0:T(8,128)(2,1)S(1)}, u32[]{:S(2)}, u32[]{:S(2)}) collective-permute-start(bf16[8,4224]{1,0:T(8,128)(2,1)S(1)} %get-tuple-element.26), channel_id=1, source_target_pairs={{0,20},{1,21},{2,22},{3,23},{4,0},{5,1},{6,2},{7,3},{8,28},{9,29},... | collective-permute-start | bytes 202760 | tf_op jit(solution)/shard_map/ppermute | solution.py:348
  14.2 0.0 collective-permute-start.8
  14.2 0.5 %collective-permute-start.9 = (bf16[8,4224]{1,0:T(8,128)(2,1)S(1)}, bf16[8,4224]{1,0:T(8,128)(2,1)S(1)}, u32[]{:S(2)}, u32[]{:S(2)}) collective-permute-start(bf16[8,4224]{1,0:T(8,128)(2,1)S(1)} %get-tuple-element.26), channel_id=1, source_target_pairs={{0,4},{1,5},{2,6},{3,7},{4,0},{5,1},{6,2},{7,3},{8,12},{9,13},{10,... | collective-permute-start | bytes 202760 | tf_op jit(solution)/shard_map/ppermute | solution.py:348
  14.7 0.0 collective-permute-start.5
  14.7 0.4 %shard_map.60 = (f32[8,4096]{1,0:T(8,128)S(1)}, f32[8,128]{1,0:T(8,128)S(1)}) custom-call(f32[8,2,16]{2,1,0:T(2,128)S(1)} %bitcast.1), custom_call_target="tpu_custom_call" | custom-call | tf_op jit(solution)/shard_map/pallas_call | solution.py:369
  15.1 0.4 %shard_map.64.kt_ref = bf16[4096,128]{1,0:T(8,128)(2,1)S(1)} custom-call(bf16[48,4096]{1,0:T(8,128)(2,1)S(1)} %get-tuple-element.22.k_ref, bf16[48,4096]{1,0:T(8,128)(2,1)S(1)} %collective-permute-done.1.k_other_ref), custom_call_target="tpu_custom_call" | custom-call | tf_op jit(solution)/shard_map/pallas_call | solution.py:369
  15.5 0.4 %collective-permute-done.5.halo_ref = f32[8,128]{1,0:T(8,128)S(1)} collective-permute-done((f32[8,128]{1,0:T(8,128)S(1)}, f32[8,128]{1,0:T(8,128)S(1)}, u32[]{:S(2)}, u32[]{:S(2)}) %collective-permute-start.5) | collective-permute-done | bytes 4128 | tf_op jit(solution)/shard_map/ppermute | solution.py:333
  15.9 0.0 collective-permute-done.6.refs_0_
  15.9 0.2 collective-permute-done.7.refs_1_
  16.1 0.0 collective-permute-done.8.refs_2_
  16.2 0.5 %shard_map.65 = (f32[8,4096]{1,0:T(8,128)S(1)}, f32[8,128]{1,0:T(8,128)S(1)}) custom-call(f32[8,4096]{1,0:T(8,128)S(1)} %get-tuple-element.17.wave_ref, f32[8,4096]{1,0:T(8,128)S(1)} %get-tuple-element.18.cut_ref, f32[8,128]{1,0:T(8,128)S(1)} %collective-permute-done.5.halo_ref, f32[8,128]{1,0:T(8,128)S(1)} %get-tuple-element.25.cut_halo_ref, ...), custom_call_target="tpu_custom_call" | custom-call | tf_op jit(solution)/shard_map/pallas_call | solution.py:369
  16.7 1.7 %collective-permute-start.10 = (f32[8,128]{1,0:T(8,128)S(1)}, f32[8,128]{1,0:T(8,128)S(1)}, u32[]{:S(2)}, u32[]{:S(2)}) collective-permute-start(f32[8,128]{1,0:T(8,128)S(1)} %get-tuple-element.29), channel_id=1, source_target_pairs={{0,4},{1,5},{2,6},{3,7},{4,3},{5,2},{6,1},{7,0},{8,12},{9,13},{10,... | collective-permute-start | bytes 12296 | tf_op jit(solution)/shard_map/ppermute | solution.py:348
  18.4 0.2 collective-permute-start.11
  18.5 1.1 %collective-permute-start.12 = (f32[8,128]{1,0:T(8,128)S(1)}, f32[8,128]{1,0:T(8,128)S(1)}, u32[]{:S(2)}, u32[]{:S(2)}) collective-permute-start(f32[8,128]{1,0:T(8,128)S(1)} %get-tuple-element.29), channel_id=1, source_target_pairs={{0,4},{1,5},{2,6},{3,7},{4,1},{5,0},{6,3},{7,2},{8,12},{9,13},{10,... | collective-permute-start | bytes 12296 | tf_op jit(solution)/shard_map/ppermute | solution.py:348
  19.6 0.0 collective-permute-start.13
  19.6 2.0 %collective-permute-done.10.refs_0_ = f32[8,128]{1,0:T(8,128)S(1)} collective-permute-done((f32[8,128]{1,0:T(8,128)S(1)}, f32[8,128]{1,0:T(8,128)S(1)}, u32[]{:S(2)}, u32[]{:S(2)}) %collective-permute-start.10) | collective-permute-done | bytes 4128 | tf_op jit(solution)/shard_map/ppermute | solution.py:348
  21.6 0.7 %collective-permute-done.11.refs_1_ = f32[8,128]{1,0:T(8,128)S(1)} collective-permute-done((f32[8,128]{1,0:T(8,128)S(1)}, f32[8,128]{1,0:T(8,128)S(1)}, u32[]{:S(2)}, u32[]{:S(2)}) %collective-permute-start.11) | collective-permute-done | bytes 4128 | tf_op jit(solution)/shard_map/ppermute | solution.py:348
  22.3 0.0 collective-permute-done.13.refs_3_
  22.3 0.3 shard_map.66
  22.5 0.0 collective-permute-start.14
  22.6 0.9 %collective-permute-start.15 = (bf16[8,4224]{1,0:T(8,128)(2,1)S(1)}, bf16[8,4224]{1,0:T(8,128)(2,1)S(1)}, u32[]{:S(2)}, u32[]{:S(2)}) collective-permute-start(bf16[8,4224]{1,0:T(8,128)(2,1)S(1)} %get-tuple-element.30), channel_id=1, source_target_pairs={{0,20},{1,21},{2,22},{3,23},{4,0},{5,1},{6,2},{7,3},{8,28},{9,29},... | collective-permute-start | bytes 202760 | tf_op jit(solution)/shard_map/ppermute | solution.py:348
  23.5 0.0 collective-permute-start.16
  23.5 0.5 %collective-permute-start.17 = (bf16[8,4224]{1,0:T(8,128)(2,1)S(1)}, bf16[8,4224]{1,0:T(8,128)(2,1)S(1)}, u32[]{:S(2)}, u32[]{:S(2)}) collective-permute-start(bf16[8,4224]{1,0:T(8,128)(2,1)S(1)} %get-tuple-element.30), channel_id=1, source_target_pairs={{0,4},{1,5},{2,6},{3,7},{4,0},{5,1},{6,2},{7,3},{8,12},{9,13},{10,... | collective-permute-start | bytes 202760 | tf_op jit(solution)/shard_map/ppermute | solution.py:348
  24.1 0.5 %collective-permute-done.14.refs_0_ = bf16[8,4224]{1,0:T(8,128)(2,1)S(1)} collective-permute-done((bf16[8,4224]{1,0:T(8,128)(2,1)S(1)}, bf16[8,4224]{1,0:T(8,128)(2,1)S(1)}, u32[]{:S(2)}, u32[]{:S(2)}) %collective-permute-start.14) | collective-permute-done | bytes 67616 | tf_op jit(solution)/shard_map/ppermute | solution.py:348
  24.5 1.0 %collective-permute-done.15.refs_1_ = bf16[8,4224]{1,0:T(8,128)(2,1)S(1)} collective-permute-done((bf16[8,4224]{1,0:T(8,128)(2,1)S(1)}, bf16[8,4224]{1,0:T(8,128)(2,1)S(1)}, u32[]{:S(2)}, u32[]{:S(2)}) %collective-permute-start.15) | collective-permute-done | bytes 67616 | tf_op jit(solution)/shard_map/ppermute | solution.py:348
  25.5 0.0 collective-permute-done.16.refs_2_
  25.5 0.0 collective-permute-done.17.refs_3_
  25.5 0.1 shard_map.67.wave_ref
  25.6 1.5 %collective-permute-start.18 = (f32[8,4096]{1,0:T(8,128)S(1)}, f32[8,4096]{1,0:T(8,128)S(1)}, u32[]{:S(2)}, u32[]{:S(2)}) collective-permute-start(f32[8,4096]{1,0:T(8,128)S(1)} %shard_map.67.wave_ref), channel_id=1, source_target_pairs={{0,4},{4,0},{8,12},{12,8},{16,20},{20,16},{24,28},{28,24},{1,5},{5... | collective-permute-start | bytes 393224 | tf_op jit(solution)/shard_map/ppermute | solution.py:333
  27.1 0.1 collective-permute-start.19
  27.2 1.1 %collective-permute-done.19.other_residual_ref = f32[8,128]{1,0:T(8,128)S(1)} collective-permute-done((f32[8,128]{1,0:T(8,128)S(1)}, f32[8,128]{1,0:T(8,128)S(1)}, u32[]{:S(2)}, u32[]{:S(2)}) %collective-permute-start.19) | collective-permute-done | bytes 4128 | tf_op jit(solution)/shard_map/ppermute | solution.py:333
  28.3 0.0 collective-permute-done.18.other_wave_ref
  28.3 0.7 %shard_map.68 = (f32[8,4096]{1,0:T(8,128)}, f32[8,48]{1,0:T(8,128)}) custom-call(f32[8,4096]{1,0:T(8,128)S(1)} %shard_map.67.wave_ref, f32[8,4096]{1,0:T(8,128)S(1)} %collective-permute-done.18.other_wave_ref, f32[8,128]{1,0:T(8,128)S(1)} %get-tuple-element.31.residual_ref, f32[8,128]{1,0:T(8,128)S(1)} %collective-permute-done.19.other_residual_ref), custom_call_target="tpu_custom_call" | custom-call | tf_op jit(solution)/shard_map/pallas_call | solution.py:369
  (4 shorter events, 0.0 us)
Async XLA Ops:
  2.0 1.4 %collective-permute-start = (bf16[96,128]{1,0:T(8,128)(2,1)S(1)}, bf16[96,128]{1,0:T(8,128)(2,1)S(1)}, u32[]{:S(2)}, u32[]{:S(2)}) collective-permute-start(bf16[96,128]{1,0:T(8,128)(2,1)S(1)} %get-tuple-element.19.mine_ref), channel_id=1, source_target_pairs={{0,4},{4,0},{8,12},{12,8},{16,20},{20,16},{24,28},{28,24},{1,5},{5... | collective-permute-start | bytes 73736 | tf_op jit(solution)/shard_map/ppermute | solution.py:333
  3.4 5.2 %collective-permute-start.1 = (bf16[48,4096]{1,0:T(8,128)(2,1)S(1)}, bf16[48,4096]{1,0:T(8,128)(2,1)S(1)}, u32[]{:S(2)}, u32[]{:S(2)}) collective-permute-start(bf16[48,4096]{1,0:T(8,128)(2,1)S(1)} %get-tuple-element.22.k_ref), channel_id=1, source_target_pairs={{0,4},{4,0},{8,12},{12,8},{16,20},{20,16},{24,28},{28,24},{1,5},{5... | collective-permute-start | bytes 1179656 | tf_op jit(solution)/shard_map/ppermute | solution.py:333
  3.8 6.3 %collective-permute-start.2 = (bf16[128,128]{1,0:T(8,128)(2,1)S(1)}, bf16[128,128]{1,0:T(8,128)(2,1)S(1)}, u32[]{:S(2)}, u32[]{:S(2)}) collective-permute-start(bf16[128,128]{1,0:T(8,128)(2,1)S(1)} %get-tuple-element.23.refs_3_), channel_id=1, source_target_pairs={{0,4},{1,5},{2,6},{3,7},{4,3},{5,2},{6,1},{7,0},{8,12},{9,13},{10,... | collective-permute-start | bytes 98312 | tf_op jit(solution)/shard_map/ppermute | solution.py:348
  3.9 6.1 %collective-permute-start.3 = (bf16[128,128]{1,0:T(8,128)(2,1)S(1)}, bf16[128,128]{1,0:T(8,128)(2,1)S(1)}, u32[]{:S(2)}, u32[]{:S(2)}) collective-permute-start(bf16[128,128]{1,0:T(8,128)(2,1)S(1)} %get-tuple-element.23.refs_3_), channel_id=1, source_target_pairs={{0,4},{1,5},{2,6},{3,7},{4,2},{5,3},{6,0},{7,1},{8,12},{9,13},{10,... | collective-permute-start | bytes 98312 | tf_op jit(solution)/shard_map/ppermute | solution.py:348
  8.7 3.3 %collective-permute-start.4 = (bf16[128,128]{1,0:T(8,128)(2,1)S(1)}, bf16[128,128]{1,0:T(8,128)(2,1)S(1)}, u32[]{:S(2)}, u32[]{:S(2)}) collective-permute-start(bf16[128,128]{1,0:T(8,128)(2,1)S(1)} %get-tuple-element.23.refs_3_), channel_id=1, source_target_pairs={{0,4},{1,5},{2,6},{3,7},{4,1},{5,0},{6,3},{7,2},{8,12},{9,13},{10,... | collective-permute-start | bytes 98312 | tf_op jit(solution)/shard_map/ppermute | solution.py:348
  12.0 2.7 %copy-start = (f32[8,16,2]{1,2,0:T(2,128)S(1)}, f32[8,16,2]{1,2,0:T(2,128)}, u32[]{:S(2)}) copy-start(f32[8,16,2]{1,2,0:T(2,128)} %param.7) | copy-start | bytes 3076
  12.5 3.3 %collective-permute-start.6 = (bf16[8,4224]{1,0:T(8,128)(2,1)S(1)}, bf16[8,4224]{1,0:T(8,128)(2,1)S(1)}, u32[]{:S(2)}, u32[]{:S(2)}) collective-permute-start(bf16[8,4224]{1,0:T(8,128)(2,1)S(1)} %get-tuple-element.26), channel_id=1, source_target_pairs={{0,28},{1,29},{2,30},{3,31},{4,0},{5,1},{6,2},{7,3},{8,20},{9,21},... | collective-permute-start | bytes 202760 | tf_op jit(solution)/shard_map/ppermute | solution.py:348
  12.9 3.2 %collective-permute-start.7 = (bf16[8,4224]{1,0:T(8,128)(2,1)S(1)}, bf16[8,4224]{1,0:T(8,128)(2,1)S(1)}, u32[]{:S(2)}, u32[]{:S(2)}) collective-permute-start(bf16[8,4224]{1,0:T(8,128)(2,1)S(1)} %get-tuple-element.26), channel_id=1, source_target_pairs={{0,20},{1,21},{2,22},{3,23},{4,0},{5,1},{6,2},{7,3},{8,28},{9,29},... | collective-permute-start | bytes 202760 | tf_op jit(solution)/shard_map/ppermute | solution.py:348
  14.2 2.0 %collective-permute-start.8 = (bf16[8,4224]{1,0:T(8,128)(2,1)S(1)}, bf16[8,4224]{1,0:T(8,128)(2,1)S(1)}, u32[]{:S(2)}, u32[]{:S(2)}) collective-permute-start(bf16[8,4224]{1,0:T(8,128)(2,1)S(1)} %get-tuple-element.26), channel_id=1, source_target_pairs={{0,12},{1,13},{2,14},{3,15},{4,0},{5,1},{6,2},{7,3},{8,4},{9,5},{1... | collective-permute-start | bytes 202760 | tf_op jit(solution)/shard_map/ppermute | solution.py:348
  14.2 1.9 %collective-permute-start.9 = (bf16[8,4224]{1,0:T(8,128)(2,1)S(1)}, bf16[8,4224]{1,0:T(8,128)(2,1)S(1)}, u32[]{:S(2)}, u32[]{:S(2)}) collective-permute-start(bf16[8,4224]{1,0:T(8,128)(2,1)S(1)} %get-tuple-element.26), channel_id=1, source_target_pairs={{0,4},{1,5},{2,6},{3,7},{4,0},{5,1},{6,2},{7,3},{8,12},{9,13},{10,... | collective-permute-start | bytes 202760 | tf_op jit(solution)/shard_map/ppermute | solution.py:348
  14.7 1.2 %collective-permute-start.5 = (f32[8,128]{1,0:T(8,128)S(1)}, f32[8,128]{1,0:T(8,128)S(1)}, u32[]{:S(2)}, u32[]{:S(2)}) collective-permute-start(f32[8,128]{1,0:T(8,128)S(1)} %get-tuple-element.24), channel_id=1, source_target_pairs={{0,4},{4,0},{8,12},{12,8},{16,20},{20,16},{24,28},{28,24},{1,5},{5... | collective-permute-start | bytes 12296 | tf_op jit(solution)/shard_map/ppermute | solution.py:333
  16.7 4.9 %collective-permute-start.10 = (f32[8,128]{1,0:T(8,128)S(1)}, f32[8,128]{1,0:T(8,128)S(1)}, u32[]{:S(2)}, u32[]{:S(2)}) collective-permute-start(f32[8,128]{1,0:T(8,128)S(1)} %get-tuple-element.29), channel_id=1, source_target_pairs={{0,4},{1,5},{2,6},{3,7},{4,3},{5,2},{6,1},{7,0},{8,12},{9,13},{10,... | collective-permute-start | bytes 12296 | tf_op jit(solution)/shard_map/ppermute | solution.py:348
  18.4 3.9 %collective-permute-start.11 = (f32[8,128]{1,0:T(8,128)S(1)}, f32[8,128]{1,0:T(8,128)S(1)}, u32[]{:S(2)}, u32[]{:S(2)}) collective-permute-start(f32[8,128]{1,0:T(8,128)S(1)} %get-tuple-element.29), channel_id=1, source_target_pairs={{0,4},{1,5},{2,6},{3,7},{4,2},{5,3},{6,0},{7,1},{8,12},{9,13},{10,... | collective-permute-start | bytes 12296 | tf_op jit(solution)/shard_map/ppermute | solution.py:348
  18.5 3.7 %collective-permute-start.12 = (f32[8,128]{1,0:T(8,128)S(1)}, f32[8,128]{1,0:T(8,128)S(1)}, u32[]{:S(2)}, u32[]{:S(2)}) collective-permute-start(f32[8,128]{1,0:T(8,128)S(1)} %get-tuple-element.29), channel_id=1, source_target_pairs={{0,4},{1,5},{2,6},{3,7},{4,1},{5,0},{6,3},{7,2},{8,12},{9,13},{10,... | collective-permute-start | bytes 12296 | tf_op jit(solution)/shard_map/ppermute | solution.py:348
  19.6 2.7 %collective-permute-start.13 = (f32[8,128]{1,0:T(8,128)S(1)}, f32[8,128]{1,0:T(8,128)S(1)}, u32[]{:S(2)}, u32[]{:S(2)}) collective-permute-start(f32[8,128]{1,0:T(8,128)S(1)} %get-tuple-element.29), channel_id=1, source_target_pairs={{0,4},{1,5},{2,6},{3,7},{4,0},{5,1},{6,2},{7,3},{8,12},{9,13},{10,... | collective-permute-start | bytes 12296 | tf_op jit(solution)/shard_map/ppermute | solution.py:348
  22.5 2.0 %collective-permute-start.14 = (bf16[8,4224]{1,0:T(8,128)(2,1)S(1)}, bf16[8,4224]{1,0:T(8,128)(2,1)S(1)}, u32[]{:S(2)}, u32[]{:S(2)}) collective-permute-start(bf16[8,4224]{1,0:T(8,128)(2,1)S(1)} %get-tuple-element.30), channel_id=1, source_target_pairs={{0,28},{1,29},{2,30},{3,31},{4,0},{5,1},{6,2},{7,3},{8,20},{9,21},... | collective-permute-start | bytes 202760 | tf_op jit(solution)/shard_map/ppermute | solution.py:348
  22.6 2.9 %collective-permute-start.15 = (bf16[8,4224]{1,0:T(8,128)(2,1)S(1)}, bf16[8,4224]{1,0:T(8,128)(2,1)S(1)}, u32[]{:S(2)}, u32[]{:S(2)}) collective-permute-start(bf16[8,4224]{1,0:T(8,128)(2,1)S(1)} %get-tuple-element.30), channel_id=1, source_target_pairs={{0,20},{1,21},{2,22},{3,23},{4,0},{5,1},{6,2},{7,3},{8,28},{9,29},... | collective-permute-start | bytes 202760 | tf_op jit(solution)/shard_map/ppermute | solution.py:348
  23.5 1.9 %collective-permute-start.16 = (bf16[8,4224]{1,0:T(8,128)(2,1)S(1)}, bf16[8,4224]{1,0:T(8,128)(2,1)S(1)}, u32[]{:S(2)}, u32[]{:S(2)}) collective-permute-start(bf16[8,4224]{1,0:T(8,128)(2,1)S(1)} %get-tuple-element.30), channel_id=1, source_target_pairs={{0,12},{1,13},{2,14},{3,15},{4,0},{5,1},{6,2},{7,3},{8,4},{9,5},{1... | collective-permute-start | bytes 202760 | tf_op jit(solution)/shard_map/ppermute | solution.py:348
  23.5 1.9 %collective-permute-start.17 = (bf16[8,4224]{1,0:T(8,128)(2,1)S(1)}, bf16[8,4224]{1,0:T(8,128)(2,1)S(1)}, u32[]{:S(2)}, u32[]{:S(2)}) collective-permute-start(bf16[8,4224]{1,0:T(8,128)(2,1)S(1)} %get-tuple-element.30), channel_id=1, source_target_pairs={{0,4},{1,5},{2,6},{3,7},{4,0},{5,1},{6,2},{7,3},{8,12},{9,13},{10,... | collective-permute-start | bytes 202760 | tf_op jit(solution)/shard_map/ppermute | solution.py:348
  25.6 2.7 %collective-permute-start.18 = (f32[8,4096]{1,0:T(8,128)S(1)}, f32[8,4096]{1,0:T(8,128)S(1)}, u32[]{:S(2)}, u32[]{:S(2)}) collective-permute-start(f32[8,4096]{1,0:T(8,128)S(1)} %shard_map.67.wave_ref), channel_id=1, source_target_pairs={{0,4},{4,0},{8,12},{12,8},{16,20},{20,16},{24,28},{28,24},{1,5},{5... | collective-permute-start | bytes 393224 | tf_op jit(solution)/shard_map/ppermute | solution.py:333
  27.1 1.2 %collective-permute-start.19 = (f32[8,128]{1,0:T(8,128)S(1)}, f32[8,128]{1,0:T(8,128)S(1)}, u32[]{:S(2)}, u32[]{:S(2)}) collective-permute-start(f32[8,128]{1,0:T(8,128)S(1)} %get-tuple-element.31.residual_ref), channel_id=1, source_target_pairs={{0,4},{4,0},{8,12},{12,8},{16,20},{20,16},{24,28},{28,24},{1,5},{5... | collective-permute-start | bytes 12296 | tf_op jit(solution)/shard_map/ppermute | solution.py:333

commit v12 on v11

--- a/solution.py
+++ b/solution.py
@@ -233,13 +233,13 @@
     )
 
 
-def second_kernel(layers, n_vox, observed_ref, kw_ref, *refs):
+def second_kernel(layers, n_vox, distances, observed_ref, kw_ref, *refs):
     (*packets, g_ref, columns_ref, halo_ref, held, tile) = refs
     models = observed_ref.shape[0]
     size = held.shape[1] // 2
     rows = size - 2 * models
     me = lax.axis_index("vox")
-    for distance, packet in enumerate(reversed(packets)):
+    for distance, packet in zip(distances, packets):
         held[me ^ distance] = packet[...]
     left, right = lax.rem(me + n_vox - 1, n_vox), lax.rem(me + 1, n_vox)
     lane = lanes_of((models, LANES))
@@ -406,7 +406,8 @@
         aliases={2: 2},
     )
     k_other = from_partner(k_mine, "dp", 1)
-    packets = [handed_over(both, 1, 0, d) for d in reversed(range(1, n_vox))] + [both]
+    distances = sorted(range(1, n_vox), key=lambda d: (d != n_vox // 2, -d))
+    packets = [handed_over(both, 1, 0, d) for d in distances] + [both]
     kw = call(functools.partial(applied_kernel, layers), pltpu.VMEM((LANES, width), BF16), k_mine, k_other)
     kt = call(transposing_kernel, pltpu.VMEM((width, LANES), BF16), k_mine, k_other)
     cut, cut_halo = call(
@@ -415,7 +416,7 @@
         jnp.swapaxes(threshold, 1, 2),
     )
     g, columns, halo = call(
-        functools.partial(second_kernel, layers, n_vox),
+        functools.partial(second_kernel, layers, n_vox, distances + [0]),
         (g_shape, pltpu.VMEM((LANES, LANES), BF16), tile_shape),
         observed_both,
         kw,

time: 29.1 us -> 28.8 us (0.990)
  waiting for transfers between devices: 9.57 us -> 8.37 us
  starting transfers between devices: 14 us -> 14.8 us
    ppermute x15, starting transfers between devices: 11.5 us -> 12.6 us  [handed_over(): return lax.ppermute(x, ('dp', 'vox'), route)]
    ppermute x15, waiting for transfers between devices: 7.26 us -> 6.37 us  [handed_over(): return lax.ppermute(x, ('dp', 'vox'), route)]
    ppermute x5, waiting for transfers between devices: 2.31 us -> 2.01 us  [from_partner(): lax.ppermute(x, axis, [(i, i ^ distance) for i in range(lax.axis_size(axi...]
  transfers between devices with their start and end apart: 20 -> 20, of which waited for: 10 -> 11; matrix products, arithmetic and copies ran while one was open for 0% -> 0% of each run, Pallas kernels for 4% -> 4%
where the time goes in v12:
time: 28.8 us; the launch traced here: 28.6 us
  starting transfers between devices  14.8 us (51%)
  waiting for transfers between devices  8.37 us (29%)
  Pallas kernels  4.72 us (16%)
  between operations  0.71 us (2%)
    ppermute x15, starting transfers between devices, handed_over(): return lax.ppermute(x, ('dp', 'vox'), route)  12.6 us
    ppermute x15, waiting for transfers between devices, handed_over(): return lax.ppermute(x, ('dp', 'vox'), route)  6.37 us
    pallas_call x10, Pallas kernels, call(): pl.pallas_call(kernel, out_shape=out_shape, in_specs=[pl.BlockSpec(memory...  4.72 us
    ppermute x5, starting transfers between devices, from_partner(): lax.ppermute(x, axis, [(i, i ^ distance) for i in range(lax.axis_size(axi...  2.27 us
    ppermute x5, waiting for transfers between devices, from_partner(): lax.ppermute(x, axis, [(i, i ^ distance) for i in range(lax.axis_size(axi...  2.01 us
  transfers between devices with their start and end apart: 20, of which 11 were waited for; matrix products, arithmetic and copies ran while one was open for 0% of the time, Pallas kernels for 4%

profile of v12, /device:TPU:0, one launch (start us, length us, event | category | flops | bytes accessed | tf_op | source)
XLA Modules:
  0.0 28.6 jit_solution(3528592628672923409)
XLA Ops:
  0.6 1.3 %shard_map.59 = (bf16[96,128]{1,0:T(8,128)(2,1)S(1)}, f32[8,4096]{1,0:T(8,128)S(1)}, bf16[48,4096]{1,0:T(8,128)(2,1)S(1)}) custom-call(f32[8,4096]{1,0:T(8,128)} %wave_hbm.1, bf16[48,4096]{1,0:T(8,128)(2,1)} %k_hbm.1, f32[8,48]{1,0:T(8,128)} %observed_hbm.1), custom_call_target="tpu_custom_call" | custom-call | tf_op jit(solution)/shard_map/pallas_call | solution.py:369
  2.0 0.5 %collective-permute-start = (bf16[96,128]{1,0:T(8,128)(2,1)S(1)}, bf16[96,128]{1,0:T(8,128)(2,1)S(1)}, u32[]{:S(2)}, u32[]{:S(2)}) collective-permute-start(bf16[96,128]{1,0:T(8,128)(2,1)S(1)} %get-tuple-element.19.mine_ref), channel_id=1, source_target_pairs={{0,4},{4,0},{8,12},{12,8},{16,20},{20,16},{24,28},{28,24},{1,5},{5... | collective-permute-start | bytes 73736 | tf_op jit(solution)/shard_map/ppermute | solution.py:333
  2.5 0.8 %collective-permute-done.other_ref = bf16[96,128]{1,0:T(8,128)(2,1)S(1)} collective-permute-done((bf16[96,128]{1,0:T(8,128)(2,1)S(1)}, bf16[96,128]{1,0:T(8,128)(2,1)S(1)}, u32[]{:S(2)}, u32[]{:S(2)}) %collective-permute-start) | collective-permute-done | bytes 24608 | tf_op jit(solution)/shard_map/ppermute | solution.py:333
  3.3 0.1 shard_map.61
  3.4 0.3 %collective-permute-start.1 = (bf16[48,4096]{1,0:T(8,128)(2,1)S(1)}, bf16[48,4096]{1,0:T(8,128)(2,1)S(1)}, u32[]{:S(2)}, u32[]{:S(2)}) collective-permute-start(bf16[48,4096]{1,0:T(8,128)(2,1)S(1)} %get-tuple-element.22.k_ref), channel_id=1, source_target_pairs={{0,4},{4,0},{8,12},{12,8},{16,20},{20,16},{24,28},{28,24},{1,5},{5... | collective-permute-start | bytes 1179656 | tf_op jit(solution)/shard_map/ppermute | solution.py:333
  3.8 0.2 collective-permute-start.2
  3.9 3.7 %collective-permute-start.3 = (bf16[128,128]{1,0:T(8,128)(2,1)S(1)}, bf16[128,128]{1,0:T(8,128)(2,1)S(1)}, u32[]{:S(2)}, u32[]{:S(2)}) collective-permute-start(bf16[128,128]{1,0:T(8,128)(2,1)S(1)} %get-tuple-element.23.refs_3_), channel_id=1, source_target_pairs={{0,4},{1,5},{2,6},{3,7},{4,3},{5,2},{6,1},{7,0},{8,12},{9,13},{10,... | collective-permute-start | bytes 98312 | tf_op jit(solution)/shard_map/ppermute | solution.py:348
  7.6 1.4 %collective-permute-start.4 = (bf16[128,128]{1,0:T(8,128)(2,1)S(1)}, bf16[128,128]{1,0:T(8,128)(2,1)S(1)}, u32[]{:S(2)}, u32[]{:S(2)}) collective-permute-start(bf16[128,128]{1,0:T(8,128)(2,1)S(1)} %get-tuple-element.23.refs_3_), channel_id=1, source_target_pairs={{0,4},{1,5},{2,6},{3,7},{4,1},{5,0},{6,3},{7,2},{8,12},{9,13},{10,... | collective-permute-start | bytes 98312 | tf_op jit(solution)/shard_map/ppermute | solution.py:348
  9.0 0.0 collective-permute-done.1.k_other_ref
  9.0 0.5 %shard_map.62.kw_ref = bf16[128,4096]{1,0:T(8,128)(2,1)S(1)} custom-call(bf16[48,4096]{1,0:T(8,128)(2,1)S(1)} %get-tuple-element.22.k_ref, bf16[48,4096]{1,0:T(8,128)(2,1)S(1)} %collective-permute-done.1.k_other_ref), custom_call_target="tpu_custom_call" | custom-call | tf_op jit(solution)/shard_map/pallas_call | solution.py:369
  9.5 0.0 collective-permute-done.2.refs_0_
  9.5 1.1 %collective-permute-done.3.refs_1_ = bf16[128,128]{1,0:T(8,128)(2,1)S(1)} collective-permute-done((bf16[128,128]{1,0:T(8,128)(2,1)S(1)}, bf16[128,128]{1,0:T(8,128)(2,1)S(1)}, u32[]{:S(2)}, u32[]{:S(2)}) %collective-permute-start.3) | collective-permute-done | bytes 32800 | tf_op jit(solution)/shard_map/ppermute | solution.py:348
  10.5 0.4 %collective-permute-done.4.refs_2_ = bf16[128,128]{1,0:T(8,128)(2,1)S(1)} collective-permute-done((bf16[128,128]{1,0:T(8,128)(2,1)S(1)}, bf16[128,128]{1,0:T(8,128)(2,1)S(1)}, u32[]{:S(2)}, u32[]{:S(2)}) %collective-permute-start.4) | collective-permute-done | bytes 32800 | tf_op jit(solution)/shard_map/ppermute | solution.py:348
  11.0 0.5 %shard_map.63 = (bf16[8,4224]{1,0:T(8,128)(2,1)S(1)}, bf16[128,128]{1,0:T(8,128)(2,1)S(1)}, f32[8,128]{1,0:T(8,128)S(1)}) custom-call(f32[8,128]{1,0:T(8,128)S(1)} %get-tuple-element.21.observed_ref, bf16[128,4096]{1,0:T(8,128)(2,1)S(1)} %shard_map.62.kw_ref, bf16[128,128]{1,0:T(8,128)(2,1)S(1)} %collective-permute-done.2.refs_0_, ...), custom_call_target="tpu_custom_call" | custom-call | tf_op jit(solution)/shard_map/pallas_call | solution.py:369
  11.5 1.5 %collective-permute-start.6 = (bf16[8,4224]{1,0:T(8,128)(2,1)S(1)}, bf16[8,4224]{1,0:T(8,128)(2,1)S(1)}, u32[]{:S(2)}, u32[]{:S(2)}) collective-permute-start(bf16[8,4224]{1,0:T(8,128)(2,1)S(1)} %get-tuple-element.26), channel_id=1, source_target_pairs={{0,28},{1,29},{2,30},{3,31},{4,0},{5,1},{6,2},{7,3},{8,20},{9,21},... | collective-permute-start | bytes 202760 | tf_op jit(solution)/shard_map/ppermute | solution.py:348
  13.0 0.2 collective-permute-start.7
  13.2 0.4 %collective-permute-start.8 = (bf16[8,4224]{1,0:T(8,128)(2,1)S(1)}, bf16[8,4224]{1,0:T(8,128)(2,1)S(1)}, u32[]{:S(2)}, u32[]{:S(2)}) collective-permute-start(bf16[8,4224]{1,0:T(8,128)(2,1)S(1)} %get-tuple-element.26), channel_id=1, source_target_pairs={{0,12},{1,13},{2,14},{3,15},{4,0},{5,1},{6,2},{7,3},{8,4},{9,5},{1... | collective-permute-start | bytes 202760 | tf_op jit(solution)/shard_map/ppermute | solution.py:348
  13.6 0.1 collective-permute-start.9
  13.7 0.4 %collective-permute-start.5 = (f32[8,128]{1,0:T(8,128)S(1)}, f32[8,128]{1,0:T(8,128)S(1)}, u32[]{:S(2)}, u32[]{:S(2)}) collective-permute-start(f32[8,128]{1,0:T(8,128)S(1)} %get-tuple-element.24), channel_id=1, source_target_pairs={{0,4},{4,0},{8,12},{12,8},{16,20},{20,16},{24,28},{28,24},{1,5},{5... | collective-permute-start | bytes 12296 | tf_op jit(solution)/shard_map/ppermute | solution.py:333
  14.1 0.4 %shard_map.60 = (f32[8,4096]{1,0:T(8,128)S(1)}, f32[8,128]{1,0:T(8,128)S(1)}) custom-call(f32[8,2,16]{2,1,0:T(2,128)S(1)} %bitcast.1), custom_call_target="tpu_custom_call" | custom-call | tf_op jit(solution)/shard_map/pallas_call | solution.py:369
  14.5 0.4 %shard_map.64.kt_ref = bf16[4096,128]{1,0:T(8,128)(2,1)S(1)} custom-call(bf16[48,4096]{1,0:T(8,128)(2,1)S(1)} %get-tuple-element.22.k_ref, bf16[48,4096]{1,0:T(8,128)(2,1)S(1)} %collective-permute-done.1.k_other_ref), custom_call_target="tpu_custom_call" | custom-call | tf_op jit(solution)/shard_map/pallas_call | solution.py:369
  14.9 0.1 collective-permute-done.5.halo_ref
  15.0 0.0 collective-permute-done.6.refs_0_
  15.0 0.5 %collective-permute-done.7.refs_1_ = bf16[8,4224]{1,0:T(8,128)(2,1)S(1)} collective-permute-done((bf16[8,4224]{1,0:T(8,128)(2,1)S(1)}, bf16[8,4224]{1,0:T(8,128)(2,1)S(1)}, u32[]{:S(2)}, u32[]{:S(2)}) %collective-permute-start.7) | collective-permute-done | bytes 67616 | tf_op jit(solution)/shard_map/ppermute | solution.py:348
  15.5 0.1 collective-permute-done.8.refs_2_
  15.6 0.5 %shard_map.65 = (f32[8,4096]{1,0:T(8,128)S(1)}, f32[8,128]{1,0:T(8,128)S(1)}) custom-call(f32[8,4096]{1,0:T(8,128)S(1)} %get-tuple-element.17.wave_ref, f32[8,4096]{1,0:T(8,128)S(1)} %get-tuple-element.18.cut_ref, f32[8,128]{1,0:T(8,128)S(1)} %collective-permute-done.5.halo_ref, f32[8,128]{1,0:T(8,128)S(1)} %get-tuple-element.25.cut_halo_ref, ...), custom_call_target="tpu_custom_call" | custom-call | tf_op jit(solution)/shard_map/pallas_call | solution.py:369
  16.1 1.7 %collective-permute-start.10 = (f32[8,128]{1,0:T(8,128)S(1)}, f32[8,128]{1,0:T(8,128)S(1)}, u32[]{:S(2)}, u32[]{:S(2)}) collective-permute-start(f32[8,128]{1,0:T(8,128)S(1)} %get-tuple-element.29), channel_id=1, source_target_pairs={{0,4},{1,5},{2,6},{3,7},{4,3},{5,2},{6,1},{7,0},{8,12},{9,13},{10,... | collective-permute-start | bytes 12296 | tf_op jit(solution)/shard_map/ppermute | solution.py:348
  17.8 1.1 %collective-permute-start.11 = (f32[8,128]{1,0:T(8,128)S(1)}, f32[8,128]{1,0:T(8,128)S(1)}, u32[]{:S(2)}, u32[]{:S(2)}) collective-permute-start(f32[8,128]{1,0:T(8,128)S(1)} %get-tuple-element.29), channel_id=1, source_target_pairs={{0,4},{1,5},{2,6},{3,7},{4,2},{5,3},{6,0},{7,1},{8,12},{9,13},{10,... | collective-permute-start | bytes 12296 | tf_op jit(solution)/shard_map/ppermute | solution.py:348
  18.9 0.1 collective-permute-start.12
  18.9 0.2 collective-permute-start.13
  19.1 2.2 %collective-permute-done.10.refs_0_ = f32[8,128]{1,0:T(8,128)S(1)} collective-permute-done((f32[8,128]{1,0:T(8,128)S(1)}, f32[8,128]{1,0:T(8,128)S(1)}, u32[]{:S(2)}, u32[]{:S(2)}) %collective-permute-start.10) | collective-permute-done | bytes 4128 | tf_op jit(solution)/shard_map/ppermute | solution.py:348
  21.3 0.4 %collective-permute-done.11.refs_1_ = f32[8,128]{1,0:T(8,128)S(1)} collective-permute-done((f32[8,128]{1,0:T(8,128)S(1)}, f32[8,128]{1,0:T(8,128)S(1)}, u32[]{:S(2)}, u32[]{:S(2)}) %collective-permute-start.11) | collective-permute-done | bytes 4128 | tf_op jit(solution)/shard_map/ppermute | solution.py:348
  21.7 0.2 collective-permute-done.12.refs_2_
  22.0 0.0 collective-permute-done.13.refs_3_
  22.0 0.3 shard_map.66
  22.2 0.0 collective-permute-start.14
  22.3 1.6 %collective-permute-start.15 = (bf16[8,4224]{1,0:T(8,128)(2,1)S(1)}, bf16[8,4224]{1,0:T(8,128)(2,1)S(1)}, u32[]{:S(2)}, u32[]{:S(2)}) collective-permute-start(bf16[8,4224]{1,0:T(8,128)(2,1)S(1)} %get-tuple-element.30), channel_id=1, source_target_pairs={{0,20},{1,21},{2,22},{3,23},{4,0},{5,1},{6,2},{7,3},{8,28},{9,29},... | collective-permute-start | bytes 202760 | tf_op jit(solution)/shard_map/ppermute | solution.py:348
  23.9 0.0 collective-permute-start.16
  23.9 0.5 %collective-permute-start.17 = (bf16[8,4224]{1,0:T(8,128)(2,1)S(1)}, bf16[8,4224]{1,0:T(8,128)(2,1)S(1)}, u32[]{:S(2)}, u32[]{:S(2)}) collective-permute-start(bf16[8,4224]{1,0:T(8,128)(2,1)S(1)} %get-tuple-element.30), channel_id=1, source_target_pairs={{0,4},{1,5},{2,6},{3,7},{4,0},{5,1},{6,2},{7,3},{8,12},{9,13},{10,... | collective-permute-start | bytes 202760 | tf_op jit(solution)/shard_map/ppermute | solution.py:348
  24.4 1.4 %collective-permute-done.15.refs_1_ = bf16[8,4224]{1,0:T(8,128)(2,1)S(1)} collective-permute-done((bf16[8,4224]{1,0:T(8,128)(2,1)S(1)}, bf16[8,4224]{1,0:T(8,128)(2,1)S(1)}, u32[]{:S(2)}, u32[]{:S(2)}) %collective-permute-start.15) | collective-permute-done | bytes 67616 | tf_op jit(solution)/shard_map/ppermute | solution.py:348
  25.8 0.0 collective-permute-done.16.refs_2_
  25.8 0.0 collective-permute-done.17.refs_3_
  25.8 0.1 shard_map.67.wave_ref
  25.9 0.9 %collective-permute-start.18 = (f32[8,4096]{1,0:T(8,128)S(1)}, f32[8,4096]{1,0:T(8,128)S(1)}, u32[]{:S(2)}, u32[]{:S(2)}) collective-permute-start(f32[8,4096]{1,0:T(8,128)S(1)} %shard_map.67.wave_ref), channel_id=1, source_target_pairs={{0,4},{4,0},{8,12},{12,8},{16,20},{20,16},{24,28},{28,24},{1,5},{5... | collective-permute-start | bytes 393224 | tf_op jit(solution)/shard_map/ppermute | solution.py:333
  26.8 0.1 collective-permute-start.19
  26.9 1.1 %collective-permute-done.19.other_residual_ref = f32[8,128]{1,0:T(8,128)S(1)} collective-permute-done((f32[8,128]{1,0:T(8,128)S(1)}, f32[8,128]{1,0:T(8,128)S(1)}, u32[]{:S(2)}, u32[]{:S(2)}) %collective-permute-start.19) | collective-permute-done | bytes 4128 | tf_op jit(solution)/shard_map/ppermute | solution.py:333
  28.0 0.0 collective-permute-done.18.other_wave_ref
  28.0 0.7 %shard_map.68 = (f32[8,4096]{1,0:T(8,128)}, f32[8,48]{1,0:T(8,128)}) custom-call(f32[8,4096]{1,0:T(8,128)S(1)} %shard_map.67.wave_ref, f32[8,4096]{1,0:T(8,128)S(1)} %collective-permute-done.18.other_wave_ref, f32[8,128]{1,0:T(8,128)S(1)} %get-tuple-element.31.residual_ref, f32[8,128]{1,0:T(8,128)S(1)} %collective-permute-done.19.other_residual_ref), custom_call_target="tpu_custom_call" | custom-call | tf_op jit(solution)/shard_map/pallas_call | solution.py:369
  (4 shorter events, 0.0 us)
Async XLA Ops:
  2.0 1.4 %collective-permute-start = (bf16[96,128]{1,0:T(8,128)(2,1)S(1)}, bf16[96,128]{1,0:T(8,128)(2,1)S(1)}, u32[]{:S(2)}, u32[]{:S(2)}) collective-permute-start(bf16[96,128]{1,0:T(8,128)(2,1)S(1)} %get-tuple-element.19.mine_ref), channel_id=1, source_target_pairs={{0,4},{4,0},{8,12},{12,8},{16,20},{20,16},{24,28},{28,24},{1,5},{5... | collective-permute-start | bytes 73736 | tf_op jit(solution)/shard_map/ppermute | solution.py:333
  3.4 5.6 %collective-permute-start.1 = (bf16[48,4096]{1,0:T(8,128)(2,1)S(1)}, bf16[48,4096]{1,0:T(8,128)(2,1)S(1)}, u32[]{:S(2)}, u32[]{:S(2)}) collective-permute-start(bf16[48,4096]{1,0:T(8,128)(2,1)S(1)} %get-tuple-element.22.k_ref), channel_id=1, source_target_pairs={{0,4},{4,0},{8,12},{12,8},{16,20},{20,16},{24,28},{28,24},{1,5},{5... | collective-permute-start | bytes 1179656 | tf_op jit(solution)/shard_map/ppermute | solution.py:333
  3.8 5.7 %collective-permute-start.2 = (bf16[128,128]{1,0:T(8,128)(2,1)S(1)}, bf16[128,128]{1,0:T(8,128)(2,1)S(1)}, u32[]{:S(2)}, u32[]{:S(2)}) collective-permute-start(bf16[128,128]{1,0:T(8,128)(2,1)S(1)} %get-tuple-element.23.refs_3_), channel_id=1, source_target_pairs={{0,4},{1,5},{2,6},{3,7},{4,2},{5,3},{6,0},{7,1},{8,12},{9,13},{10,... | collective-permute-start | bytes 98312 | tf_op jit(solution)/shard_map/ppermute | solution.py:348
  3.9 6.6 %collective-permute-start.3 = (bf16[128,128]{1,0:T(8,128)(2,1)S(1)}, bf16[128,128]{1,0:T(8,128)(2,1)S(1)}, u32[]{:S(2)}, u32[]{:S(2)}) collective-permute-start(bf16[128,128]{1,0:T(8,128)(2,1)S(1)} %get-tuple-element.23.refs_3_), channel_id=1, source_target_pairs={{0,4},{1,5},{2,6},{3,7},{4,3},{5,2},{6,1},{7,0},{8,12},{9,13},{10,... | collective-permute-start | bytes 98312 | tf_op jit(solution)/shard_map/ppermute | solution.py:348
  7.6 3.3 %collective-permute-start.4 = (bf16[128,128]{1,0:T(8,128)(2,1)S(1)}, bf16[128,128]{1,0:T(8,128)(2,1)S(1)}, u32[]{:S(2)}, u32[]{:S(2)}) collective-permute-start(bf16[128,128]{1,0:T(8,128)(2,1)S(1)} %get-tuple-element.23.refs_3_), channel_id=1, source_target_pairs={{0,4},{1,5},{2,6},{3,7},{4,1},{5,0},{6,3},{7,2},{8,12},{9,13},{10,... | collective-permute-start | bytes 98312 | tf_op jit(solution)/shard_map/ppermute | solution.py:348
  11.0 3.2 %copy-start = (f32[8,16,2]{1,2,0:T(2,128)S(1)}, f32[8,16,2]{1,2,0:T(2,128)}, u32[]{:S(2)}) copy-start(f32[8,16,2]{1,2,0:T(2,128)} %param.7) | copy-start | bytes 3076
  11.5 3.4 %collective-permute-start.6 = (bf16[8,4224]{1,0:T(8,128)(2,1)S(1)}, bf16[8,4224]{1,0:T(8,128)(2,1)S(1)}, u32[]{:S(2)}, u32[]{:S(2)}) collective-permute-start(bf16[8,4224]{1,0:T(8,128)(2,1)S(1)} %get-tuple-element.26), channel_id=1, source_target_pairs={{0,28},{1,29},{2,30},{3,31},{4,0},{5,1},{6,2},{7,3},{8,20},{9,21},... | collective-permute-start | bytes 202760 | tf_op jit(solution)/shard_map/ppermute | solution.py:348
  13.0 2.5 %collective-permute-start.7 = (bf16[8,4224]{1,0:T(8,128)(2,1)S(1)}, bf16[8,4224]{1,0:T(8,128)(2,1)S(1)}, u32[]{:S(2)}, u32[]{:S(2)}) collective-permute-start(bf16[8,4224]{1,0:T(8,128)(2,1)S(1)} %get-tuple-element.26), channel_id=1, source_target_pairs={{0,20},{1,21},{2,22},{3,23},{4,0},{5,1},{6,2},{7,3},{8,28},{9,29},... | collective-permute-start | bytes 202760 | tf_op jit(solution)/shard_map/ppermute | solution.py:348
  13.2 2.4 %collective-permute-start.8 = (bf16[8,4224]{1,0:T(8,128)(2,1)S(1)}, bf16[8,4224]{1,0:T(8,128)(2,1)S(1)}, u32[]{:S(2)}, u32[]{:S(2)}) collective-permute-start(bf16[8,4224]{1,0:T(8,128)(2,1)S(1)} %get-tuple-element.26), channel_id=1, source_target_pairs={{0,12},{1,13},{2,14},{3,15},{4,0},{5,1},{6,2},{7,3},{8,4},{9,5},{1... | collective-permute-start | bytes 202760 | tf_op jit(solution)/shard_map/ppermute | solution.py:348
  13.6 1.9 %collective-permute-start.9 = (bf16[8,4224]{1,0:T(8,128)(2,1)S(1)}, bf16[8,4224]{1,0:T(8,128)(2,1)S(1)}, u32[]{:S(2)}, u32[]{:S(2)}) collective-permute-start(bf16[8,4224]{1,0:T(8,128)(2,1)S(1)} %get-tuple-element.26), channel_id=1, source_target_pairs={{0,4},{1,5},{2,6},{3,7},{4,0},{5,1},{6,2},{7,3},{8,12},{9,13},{10,... | collective-permute-start | bytes 202760 | tf_op jit(solution)/shard_map/ppermute | solution.py:348
  13.7 1.3 %collective-permute-start.5 = (f32[8,128]{1,0:T(8,128)S(1)}, f32[8,128]{1,0:T(8,128)S(1)}, u32[]{:S(2)}, u32[]{:S(2)}) collective-permute-start(f32[8,128]{1,0:T(8,128)S(1)} %get-tuple-element.24), channel_id=1, source_target_pairs={{0,4},{4,0},{8,12},{12,8},{16,20},{20,16},{24,28},{28,24},{1,5},{5... | collective-permute-start | bytes 12296 | tf_op jit(solution)/shard_map/ppermute | solution.py:333
  16.1 5.2 %collective-permute-start.10 = (f32[8,128]{1,0:T(8,128)S(1)}, f32[8,128]{1,0:T(8,128)S(1)}, u32[]{:S(2)}, u32[]{:S(2)}) collective-permute-start(f32[8,128]{1,0:T(8,128)S(1)} %get-tuple-element.29), channel_id=1, source_target_pairs={{0,4},{1,5},{2,6},{3,7},{4,3},{5,2},{6,1},{7,0},{8,12},{9,13},{10,... | collective-permute-start | bytes 12296 | tf_op jit(solution)/shard_map/ppermute | solution.py:348
  17.8 3.9 %collective-permute-start.11 = (f32[8,128]{1,0:T(8,128)S(1)}, f32[8,128]{1,0:T(8,128)S(1)}, u32[]{:S(2)}, u32[]{:S(2)}) collective-permute-start(f32[8,128]{1,0:T(8,128)S(1)} %get-tuple-element.29), channel_id=1, source_target_pairs={{0,4},{1,5},{2,6},{3,7},{4,2},{5,3},{6,0},{7,1},{8,12},{9,13},{10,... | collective-permute-start | bytes 12296 | tf_op jit(solution)/shard_map/ppermute | solution.py:348
  18.9 3.1 %collective-permute-start.12 = (f32[8,128]{1,0:T(8,128)S(1)}, f32[8,128]{1,0:T(8,128)S(1)}, u32[]{:S(2)}, u32[]{:S(2)}) collective-permute-start(f32[8,128]{1,0:T(8,128)S(1)} %get-tuple-element.29), channel_id=1, source_target_pairs={{0,4},{1,5},{2,6},{3,7},{4,1},{5,0},{6,3},{7,2},{8,12},{9,13},{10,... | collective-permute-start | bytes 12296 | tf_op jit(solution)/shard_map/ppermute | solution.py:348
  18.9 3.0 %collective-permute-start.13 = (f32[8,128]{1,0:T(8,128)S(1)}, f32[8,128]{1,0:T(8,128)S(1)}, u32[]{:S(2)}, u32[]{:S(2)}) collective-permute-start(f32[8,128]{1,0:T(8,128)S(1)} %get-tuple-element.29), channel_id=1, source_target_pairs={{0,4},{1,5},{2,6},{3,7},{4,0},{5,1},{6,2},{7,3},{8,12},{9,13},{10,... | collective-permute-start | bytes 12296 | tf_op jit(solution)/shard_map/ppermute | solution.py:348
  22.2 2.1 %collective-permute-start.14 = (bf16[8,4224]{1,0:T(8,128)(2,1)S(1)}, bf16[8,4224]{1,0:T(8,128)(2,1)S(1)}, u32[]{:S(2)}, u32[]{:S(2)}) collective-permute-start(bf16[8,4224]{1,0:T(8,128)(2,1)S(1)} %get-tuple-element.30), channel_id=1, source_target_pairs={{0,28},{1,29},{2,30},{3,31},{4,0},{5,1},{6,2},{7,3},{8,20},{9,21},... | collective-permute-start | bytes 202760 | tf_op jit(solution)/shard_map/ppermute | solution.py:348
  22.3 3.5 %collective-permute-start.15 = (bf16[8,4224]{1,0:T(8,128)(2,1)S(1)}, bf16[8,4224]{1,0:T(8,128)(2,1)S(1)}, u32[]{:S(2)}, u32[]{:S(2)}) collective-permute-start(bf16[8,4224]{1,0:T(8,128)(2,1)S(1)} %get-tuple-element.30), channel_id=1, source_target_pairs={{0,20},{1,21},{2,22},{3,23},{4,0},{5,1},{6,2},{7,3},{8,28},{9,29},... | collective-permute-start | bytes 202760 | tf_op jit(solution)/shard_map/ppermute | solution.py:348
  23.9 1.9 %collective-permute-start.16 = (bf16[8,4224]{1,0:T(8,128)(2,1)S(1)}, bf16[8,4224]{1,0:T(8,128)(2,1)S(1)}, u32[]{:S(2)}, u32[]{:S(2)}) collective-permute-start(bf16[8,4224]{1,0:T(8,128)(2,1)S(1)} %get-tuple-element.30), channel_id=1, source_target_pairs={{0,12},{1,13},{2,14},{3,15},{4,0},{5,1},{6,2},{7,3},{8,4},{9,5},{1... | collective-permute-start | bytes 202760 | tf_op jit(solution)/shard_map/ppermute | solution.py:348
  23.9 1.9 %collective-permute-start.17 = (bf16[8,4224]{1,0:T(8,128)(2,1)S(1)}, bf16[8,4224]{1,0:T(8,128)(2,1)S(1)}, u32[]{:S(2)}, u32[]{:S(2)}) collective-permute-start(bf16[8,4224]{1,0:T(8,128)(2,1)S(1)} %get-tuple-element.30), channel_id=1, source_target_pairs={{0,4},{1,5},{2,6},{3,7},{4,0},{5,1},{6,2},{7,3},{8,12},{9,13},{10,... | collective-permute-start | bytes 202760 | tf_op jit(solution)/shard_map/ppermute | solution.py:348
  25.9 2.1 %collective-permute-start.18 = (f32[8,4096]{1,0:T(8,128)S(1)}, f32[8,4096]{1,0:T(8,128)S(1)}, u32[]{:S(2)}, u32[]{:S(2)}) collective-permute-start(f32[8,4096]{1,0:T(8,128)S(1)} %shard_map.67.wave_ref), channel_id=1, source_target_pairs={{0,4},{4,0},{8,12},{12,8},{16,20},{20,16},{24,28},{28,24},{1,5},{5... | collective-permute-start | bytes 393224 | tf_op jit(solution)/shard_map/ppermute | solution.py:333
  26.8 1.2 %collective-permute-start.19 = (f32[8,128]{1,0:T(8,128)S(1)}, f32[8,128]{1,0:T(8,128)S(1)}, u32[]{:S(2)}, u32[]{:S(2)}) collective-permute-start(f32[8,128]{1,0:T(8,128)S(1)} %get-tuple-element.31.residual_ref), channel_id=1, source_target_pairs={{0,4},{4,0},{8,12},{12,8},{16,20},{20,16},{24,28},{28,24},{1,5},{5... | collective-permute-start | bytes 12296 | tf_op jit(solution)/shard_map/ppermute | solution.py:333

commit v13 on v12

--- a/solution.py
+++ b/solution.py
@@ -234,7 +234,7 @@
 
 
 def second_kernel(layers, n_vox, distances, observed_ref, kw_ref, *refs):
-    (*packets, g_ref, columns_ref, halo_ref, held, tile) = refs
+    (*packets, g_ref, columns_ref, halo_ref, held) = refs
     models = observed_ref.shape[0]
     size = held.shape[1] // 2
     rows = size - 2 * models
@@ -249,20 +249,23 @@
         return both[:models] + both[models:]
 
     terms = edge_terms([values(z, 0) for z in range(n_vox)], rows, layers)
-    columns = []
-    tile[...] = jnp.zeros_like(tile)
+    edges, columns, shares = [], [], []
     for core in range(2):
-        edges = jnp.concatenate([held[z, core * size : core * size + rows, :] for z in range(n_vox)], axis=1)
-        shares = values(0, core)
+        edges.append(
+            jnp.concatenate([held[z, core * size : core * size + rows, :] for z in range(n_vox)], axis=1)
+        )
+        share = values(0, core)
         for z in range(1, n_vox):
-            shares = shares + values(z, core)
-        tile[:, core * rows : (core + 1) * rows] = nt_dot(terms, edges) + shares[:, :rows]
+            share = share + values(z, core)
+        shares.append(jnp.where(lane < rows, share, 0.0))
         around = [held[z, core * size : core * size + rows, :].astype(F32) for z in (left, me, right)]
         columns.append(halo_columns(*around, rows))
-    columns.append(jnp.zeros((LANES - 2 * rows, LANES), F32))
+    known = observed_ref[...] - (shares[0] + turned(shares[1], rows))
+    residual = known[:, : 2 * rows] - nt_dot(terms, jnp.concatenate(edges, axis=0))
     columns = jnp.concatenate(columns, axis=0).astype(BF16)
-    columns_ref[...] = columns
-    back_projected(observed_ref[...] - tile[...], kw_ref, columns, g_ref)
+    columns_ref[...] = jnp.zeros_like(columns_ref)
+    columns_ref[: 2 * rows, :] = columns
+    back_projected(residual, kw_ref.at[: 2 * rows], columns, g_ref)
     before, own, after = (values(z, 0) for z in (left, me, right))
     halo_ref[...] = by_kind(
         lane, rows, 0.0, turned(before, D_BEFORE - O_LAST), turned(after, S_NEXT - E_FIRST), own, after
@@ -316,8 +319,9 @@
     residual_ref[...] = residual
 
 
-def sixth_kernel(layers, base, wave_ref, cut_ref, *refs):
-    *g_refs, new_ref = refs
+def sixth_kernel(layers, base, residual_in_ref, wave_ref, cut_ref, *refs):
+    *g_refs, new_ref, residual_ref = refs
+    del residual_in_ref, residual_ref
     waves = stepped(layers, base, wave_ref, cut_ref, g_refs, halo_gradient(g_refs))
     new_ref[...] = unstacked(*waves, wave_ref.shape[0])
 
@@ -421,7 +425,7 @@
         observed_both,
         kw,
         *packets,
-        scratch=[pltpu.VMEM((n_vox, *both_shape.shape), BF16), tile_shape],
+        scratch=[pltpu.VMEM((n_vox, *both_shape.shape), BF16)],
     )
     wavelets, predicted = call(
         functools.partial(fourth_kernel, layers, rows),
@@ -434,12 +438,14 @@
         *over_chips(g),
     )
     g, residual = call(fifth_kernel, (g_shape, tile_shape), kw, columns, observed_both, *over_vox(predicted))
-    coefficients = call(
+    coefficients, residual_other = call(
         functools.partial(sixth_kernel, layers, rows),
-        pltpu.VMEM((models, width), F32),
+        (pltpu.VMEM((models, width), F32), tile_shape),
+        from_partner(residual, "dp", 1),
         wavelets,
         cut,
         *over_chips(g),
+        aliases={0: 1},
     )
     return call(
         seventh_kernel,
@@ -447,7 +453,7 @@
         coefficients,
         from_partner(coefficients, "dp", 1),
         residual,
-        from_partner(residual, "dp", 1),
+        residual_other,
     )
 
 

time: 28.8 us -> 28.5 us (0.990)
    ppermute x15, waiting for transfers between devices: 6.37 us -> 5.2 us  [handed_over(): return lax.ppermute(x, ('dp', 'vox'), route)]
    ppermute x5, waiting for transfers between devices: 2.01 us -> 3.06 us  [from_partner(): lax.ppermute(x, axis, [(i, i ^ distance) for i in range(lax.axis_size(axi...]
  transfers between devices with their start and end apart: 20 -> 20, of which waited for: 11 -> 12; matrix products, arithmetic and copies ran while one was open for 0% -> 0% of each run, Pallas kernels for 4% -> 4%
where the time goes in v13:
time: 28.5 us; the launch traced here: 28.4 us
  starting transfers between devices  14.8 us (52%)
  waiting for transfers between devices  8.26 us (29%)
  Pallas kernels  4.64 us (16%)
  between operations  0.71 us (2%)
    ppermute x15, starting transfers between devices, handed_over(): return lax.ppermute(x, ('dp', 'vox'), route)  12.6 us
    ppermute x15, waiting for transfers between devices, handed_over(): return lax.ppermute(x, ('dp', 'vox'), route)  5.2 us
    pallas_call x10, Pallas kernels, call(): pl.pallas_call(kernel, out_shape=out_shape, in_specs=[pl.BlockSpec(memory...  4.64 us
    ppermute x5, waiting for transfers between devices, from_partner(): lax.ppermute(x, axis, [(i, i ^ distance) for i in range(lax.axis_size(axi...  3.06 us
    ppermute x5, starting transfers between devices, from_partner(): lax.ppermute(x, axis, [(i, i ^ distance) for i in range(lax.axis_size(axi...  2.2 us
  transfers between devices with their start and end apart: 20, of which 12 were waited for; matrix products, arithmetic and copies ran while one was open for 0% of the time, Pallas kernels for 4%

profile of v13, /device:TPU:0, one launch (start us, length us, event | category | flops | bytes accessed | tf_op | source)
XLA Modules:
  0.0 28.4 jit_solution(2822652935587149965)
XLA Ops:
  0.6 1.3 %shard_map.59 = (bf16[96,128]{1,0:T(8,128)(2,1)S(1)}, f32[8,4096]{1,0:T(8,128)S(1)}, bf16[48,4096]{1,0:T(8,128)(2,1)S(1)}) custom-call(f32[8,4096]{1,0:T(8,128)} %wave_hbm.1, bf16[48,4096]{1,0:T(8,128)(2,1)} %k_hbm.1, f32[8,48]{1,0:T(8,128)} %observed_hbm.1), custom_call_target="tpu_custom_call" | custom-call | tf_op jit(solution)/shard_map/pallas_call | solution.py:373
  2.0 0.5 %collective-permute-start = (bf16[96,128]{1,0:T(8,128)(2,1)S(1)}, bf16[96,128]{1,0:T(8,128)(2,1)S(1)}, u32[]{:S(2)}, u32[]{:S(2)}) collective-permute-start(bf16[96,128]{1,0:T(8,128)(2,1)S(1)} %get-tuple-element.19.mine_ref), channel_id=1, source_target_pairs={{0,4},{4,0},{8,12},{12,8},{16,20},{20,16},{24,28},{28,24},{1,5},{5... | collective-permute-start | bytes 73736 | tf_op jit(solution)/shard_map/ppermute | solution.py:337
  2.5 0.8 %collective-permute-done.other_ref = bf16[96,128]{1,0:T(8,128)(2,1)S(1)} collective-permute-done((bf16[96,128]{1,0:T(8,128)(2,1)S(1)}, bf16[96,128]{1,0:T(8,128)(2,1)S(1)}, u32[]{:S(2)}, u32[]{:S(2)}) %collective-permute-start) | collective-permute-done | bytes 24608 | tf_op jit(solution)/shard_map/ppermute | solution.py:337
  3.3 0.1 shard_map.60
  3.4 0.3 %collective-permute-start.1 = (bf16[48,4096]{1,0:T(8,128)(2,1)S(1)}, bf16[48,4096]{1,0:T(8,128)(2,1)S(1)}, u32[]{:S(2)}, u32[]{:S(2)}) collective-permute-start(bf16[48,4096]{1,0:T(8,128)(2,1)S(1)} %get-tuple-element.21.k_ref), channel_id=1, source_target_pairs={{0,4},{4,0},{8,12},{12,8},{16,20},{20,16},{24,28},{28,24},{1,5},{5... | collective-permute-start | bytes 1179656 | tf_op jit(solution)/shard_map/ppermute | solution.py:337
  3.8 0.2 collective-permute-start.2
  3.9 3.7 %collective-permute-start.3 = (bf16[128,128]{1,0:T(8,128)(2,1)S(1)}, bf16[128,128]{1,0:T(8,128)(2,1)S(1)}, u32[]{:S(2)}, u32[]{:S(2)}) collective-permute-start(bf16[128,128]{1,0:T(8,128)(2,1)S(1)} %get-tuple-element.23.refs_3_), channel_id=1, source_target_pairs={{0,4},{1,5},{2,6},{3,7},{4,3},{5,2},{6,1},{7,0},{8,12},{9,13},{10,... | collective-permute-start | bytes 98312 | tf_op jit(solution)/shard_map/ppermute | solution.py:352
  7.6 1.4 %collective-permute-start.4 = (bf16[128,128]{1,0:T(8,128)(2,1)S(1)}, bf16[128,128]{1,0:T(8,128)(2,1)S(1)}, u32[]{:S(2)}, u32[]{:S(2)}) collective-permute-start(bf16[128,128]{1,0:T(8,128)(2,1)S(1)} %get-tuple-element.23.refs_3_), channel_id=1, source_target_pairs={{0,4},{1,5},{2,6},{3,7},{4,1},{5,0},{6,3},{7,2},{8,12},{9,13},{10,... | collective-permute-start | bytes 98312 | tf_op jit(solution)/shard_map/ppermute | solution.py:352
  9.0 0.0 collective-permute-done.1.k_other_ref
  9.0 0.5 %shard_map.61.kw_ref = bf16[128,4096]{1,0:T(8,128)(2,1)S(1)} custom-call(bf16[48,4096]{1,0:T(8,128)(2,1)S(1)} %get-tuple-element.21.k_ref, bf16[48,4096]{1,0:T(8,128)(2,1)S(1)} %collective-permute-done.1.k_other_ref), custom_call_target="tpu_custom_call" | custom-call | tf_op jit(solution)/shard_map/pallas_call | solution.py:373
  9.5 0.0 collective-permute-done.2.refs_0_
  9.5 1.1 %collective-permute-done.3.refs_1_ = bf16[128,128]{1,0:T(8,128)(2,1)S(1)} collective-permute-done((bf16[128,128]{1,0:T(8,128)(2,1)S(1)}, bf16[128,128]{1,0:T(8,128)(2,1)S(1)}, u32[]{:S(2)}, u32[]{:S(2)}) %collective-permute-start.3) | collective-permute-done | bytes 32800 | tf_op jit(solution)/shard_map/ppermute | solution.py:352
  10.5 0.4 %collective-permute-done.4.refs_2_ = bf16[128,128]{1,0:T(8,128)(2,1)S(1)} collective-permute-done((bf16[128,128]{1,0:T(8,128)(2,1)S(1)}, bf16[128,128]{1,0:T(8,128)(2,1)S(1)}, u32[]{:S(2)}, u32[]{:S(2)}) %collective-permute-start.4) | collective-permute-done | bytes 32800 | tf_op jit(solution)/shard_map/ppermute | solution.py:352
  11.0 0.5 %shard_map.62 = (bf16[8,4224]{1,0:T(8,128)(2,1)S(1)}, bf16[128,128]{1,0:T(8,128)(2,1)S(1)}, f32[8,128]{1,0:T(8,128)S(1)}) custom-call(f32[8,128]{1,0:T(8,128)S(1)} %get-tuple-element.22.observed_ref, bf16[128,4096]{1,0:T(8,128)(2,1)S(1)} %shard_map.61.kw_ref, bf16[128,128]{1,0:T(8,128)(2,1)S(1)} %collective-permute-done.2.refs_0_, ...), custom_call_target="tpu_custom_call" | custom-call | tf_op jit(solution)/shard_map/pallas_call | solution.py:373
  11.4 1.5 %collective-permute-start.6 = (bf16[8,4224]{1,0:T(8,128)(2,1)S(1)}, bf16[8,4224]{1,0:T(8,128)(2,1)S(1)}, u32[]{:S(2)}, u32[]{:S(2)}) collective-permute-start(bf16[8,4224]{1,0:T(8,128)(2,1)S(1)} %get-tuple-element.29), channel_id=1, source_target_pairs={{0,28},{1,29},{2,30},{3,31},{4,0},{5,1},{6,2},{7,3},{8,20},{9,21},... | collective-permute-start | bytes 202760 | tf_op jit(solution)/shard_map/ppermute | solution.py:352
  12.9 0.2 collective-permute-start.7
  13.1 0.4 %collective-permute-start.8 = (bf16[8,4224]{1,0:T(8,128)(2,1)S(1)}, bf16[8,4224]{1,0:T(8,128)(2,1)S(1)}, u32[]{:S(2)}, u32[]{:S(2)}) collective-permute-start(bf16[8,4224]{1,0:T(8,128)(2,1)S(1)} %get-tuple-element.29), channel_id=1, source_target_pairs={{0,12},{1,13},{2,14},{3,15},{4,0},{5,1},{6,2},{7,3},{8,4},{9,5},{1... | collective-permute-start | bytes 202760 | tf_op jit(solution)/shard_map/ppermute | solution.py:352
  13.6 0.1 collective-permute-start.9
  13.6 0.4 %collective-permute-start.5 = (f32[8,128]{1,0:T(8,128)S(1)}, f32[8,128]{1,0:T(8,128)S(1)}, u32[]{:S(2)}, u32[]{:S(2)}) collective-permute-start(f32[8,128]{1,0:T(8,128)S(1)} %get-tuple-element.27), channel_id=1, source_target_pairs={{0,4},{4,0},{8,12},{12,8},{16,20},{20,16},{24,28},{28,24},{1,5},{5... | collective-permute-start | bytes 12296 | tf_op jit(solution)/shard_map/ppermute | solution.py:337
  14.1 0.4 %shard_map.63 = (f32[8,4096]{1,0:T(8,128)S(1)}, f32[8,128]{1,0:T(8,128)S(1)}) custom-call(f32[8,2,16]{2,1,0:T(2,128)S(1)} %bitcast.1), custom_call_target="tpu_custom_call" | custom-call | tf_op jit(solution)/shard_map/pallas_call | solution.py:373
  14.4 0.4 %shard_map.64.kt_ref = bf16[4096,128]{1,0:T(8,128)(2,1)S(1)} custom-call(bf16[48,4096]{1,0:T(8,128)(2,1)S(1)} %get-tuple-element.21.k_ref, bf16[48,4096]{1,0:T(8,128)(2,1)S(1)} %collective-permute-done.1.k_other_ref), custom_call_target="tpu_custom_call" | custom-call | tf_op jit(solution)/shard_map/pallas_call | solution.py:373
  14.8 0.1 collective-permute-done.5.halo_ref
  14.9 0.0 collective-permute-done.6.refs_0_
  14.9 0.5 %collective-permute-done.7.refs_1_ = bf16[8,4224]{1,0:T(8,128)(2,1)S(1)} collective-permute-done((bf16[8,4224]{1,0:T(8,128)(2,1)S(1)}, bf16[8,4224]{1,0:T(8,128)(2,1)S(1)}, u32[]{:S(2)}, u32[]{:S(2)}) %collective-permute-start.7) | collective-permute-done | bytes 67616 | tf_op jit(solution)/shard_map/ppermute | solution.py:352
  15.4 0.1 collective-permute-done.8.refs_2_
  15.5 0.5 %shard_map.65 = (f32[8,4096]{1,0:T(8,128)S(1)}, f32[8,128]{1,0:T(8,128)S(1)}) custom-call(f32[8,4096]{1,0:T(8,128)S(1)} %get-tuple-element.25.wave_ref, f32[8,4096]{1,0:T(8,128)S(1)} %get-tuple-element.26.cut_ref, f32[8,128]{1,0:T(8,128)S(1)} %collective-permute-done.5.halo_ref, f32[8,128]{1,0:T(8,128)S(1)} %get-tuple-element.28.cut_halo_ref, ...), custom_call_target="tpu_custom_call" | custom-call | tf_op jit(solution)/shard_map/pallas_call | solution.py:373
  16.0 1.7 %collective-permute-start.10 = (f32[8,128]{1,0:T(8,128)S(1)}, f32[8,128]{1,0:T(8,128)S(1)}, u32[]{:S(2)}, u32[]{:S(2)}) collective-permute-start(f32[8,128]{1,0:T(8,128)S(1)} %get-tuple-element.30), channel_id=1, source_target_pairs={{0,4},{1,5},{2,6},{3,7},{4,3},{5,2},{6,1},{7,0},{8,12},{9,13},{10,... | collective-permute-start | bytes 12296 | tf_op jit(solution)/shard_map/ppermute | solution.py:352
  17.7 1.1 %collective-permute-start.11 = (f32[8,128]{1,0:T(8,128)S(1)}, f32[8,128]{1,0:T(8,128)S(1)}, u32[]{:S(2)}, u32[]{:S(2)}) collective-permute-start(f32[8,128]{1,0:T(8,128)S(1)} %get-tuple-element.30), channel_id=1, source_target_pairs={{0,4},{1,5},{2,6},{3,7},{4,2},{5,3},{6,0},{7,1},{8,12},{9,13},{10,... | collective-permute-start | bytes 12296 | tf_op jit(solution)/shard_map/ppermute | solution.py:352
  18.8 0.1 collective-permute-start.12
  18.9 0.2 collective-permute-start.13
  19.1 2.2 %collective-permute-done.10.refs_0_ = f32[8,128]{1,0:T(8,128)S(1)} collective-permute-done((f32[8,128]{1,0:T(8,128)S(1)}, f32[8,128]{1,0:T(8,128)S(1)}, u32[]{:S(2)}, u32[]{:S(2)}) %collective-permute-start.10) | collective-permute-done | bytes 4128 | tf_op jit(solution)/shard_map/ppermute | solution.py:352
  21.2 0.4 %collective-permute-done.11.refs_1_ = f32[8,128]{1,0:T(8,128)S(1)} collective-permute-done((f32[8,128]{1,0:T(8,128)S(1)}, f32[8,128]{1,0:T(8,128)S(1)}, u32[]{:S(2)}, u32[]{:S(2)}) %collective-permute-start.11) | collective-permute-done | bytes 4128 | tf_op jit(solution)/shard_map/ppermute | solution.py:352
  21.6 0.2 collective-permute-done.12.refs_2_
  21.9 0.0 collective-permute-done.13.refs_3_
  21.9 0.3 shard_map.66
  22.2 0.0 collective-permute-start.15
  22.2 1.6 %collective-permute-start.16 = (bf16[8,4224]{1,0:T(8,128)(2,1)S(1)}, bf16[8,4224]{1,0:T(8,128)(2,1)S(1)}, u32[]{:S(2)}, u32[]{:S(2)}) collective-permute-start(bf16[8,4224]{1,0:T(8,128)(2,1)S(1)} %get-tuple-element.33), channel_id=1, source_target_pairs={{0,20},{1,21},{2,22},{3,23},{4,0},{5,1},{6,2},{7,3},{8,28},{9,29},... | collective-permute-start | bytes 202760 | tf_op jit(solution)/shard_map/ppermute | solution.py:352
  23.8 0.0 collective-permute-start.17
  23.8 0.5 %collective-permute-start.18 = (bf16[8,4224]{1,0:T(8,128)(2,1)S(1)}, bf16[8,4224]{1,0:T(8,128)(2,1)S(1)}, u32[]{:S(2)}, u32[]{:S(2)}) collective-permute-start(bf16[8,4224]{1,0:T(8,128)(2,1)S(1)} %get-tuple-element.33), channel_id=1, source_target_pairs={{0,4},{1,5},{2,6},{3,7},{4,0},{5,1},{6,2},{7,3},{8,12},{9,13},{10,... | collective-permute-start | bytes 202760 | tf_op jit(solution)/shard_map/ppermute | solution.py:352
  24.3 0.0 collective-permute-start.14
  24.3 1.2 %collective-permute-done.14.residual_in_ref = f32[8,128]{1,0:T(8,128)S(1)} collective-permute-done((f32[8,128]{1,0:T(8,128)S(1)}, f32[8,128]{1,0:T(8,128)S(1)}, u32[]{:S(2)}, u32[]{:S(2)}) %collective-permute-start.14) | collective-permute-done | bytes 4128 | tf_op jit(solution)/shard_map/ppermute | solution.py:337
  25.5 0.2 collective-permute-done.16.refs_1_
  25.7 0.0 collective-permute-done.17.refs_2_
  25.7 0.0 collective-permute-done.18.refs_3_
  25.7 0.1 shard_map.67
  25.8 0.9 %collective-permute-start.19 = (f32[8,4096]{1,0:T(8,128)S(1)}, f32[8,4096]{1,0:T(8,128)S(1)}, u32[]{:S(2)}, u32[]{:S(2)}) collective-permute-start(f32[8,4096]{1,0:T(8,128)S(1)} %get-tuple-element.34.wave_ref), channel_id=1, source_target_pairs={{0,4},{4,0},{8,12},{12,8},{16,20},{20,16},{24,28},{28,24},{1,5},{5... | collective-permute-start | bytes 393224 | tf_op jit(solution)/shard_map/ppermute | solution.py:337
  26.7 1.0 %collective-permute-done.19.other_wave_ref = f32[8,4096]{1,0:T(8,128)S(1)} collective-permute-done((f32[8,4096]{1,0:T(8,128)S(1)}, f32[8,4096]{1,0:T(8,128)S(1)}, u32[]{:S(2)}, u32[]{:S(2)}) %collective-permute-start.19) | collective-permute-done | bytes 131104 | tf_op jit(solution)/shard_map/ppermute | solution.py:337
  27.7 0.7 %shard_map.68 = (f32[8,4096]{1,0:T(8,128)}, f32[8,48]{1,0:T(8,128)}) custom-call(f32[8,4096]{1,0:T(8,128)S(1)} %get-tuple-element.34.wave_ref, f32[8,4096]{1,0:T(8,128)S(1)} %collective-permute-done.19.other_wave_ref, f32[8,128]{1,0:T(8,128)S(1)} %get-tuple-element.31.residual_ref, f32[8,128]{1,0:T(8,128)S(1)} %get-tuple-element.35.other_residual_ref), custom_call_target="tpu_custom_call" | custom-call | tf_op jit(solution)/shard_map/pallas_call | solution.py:373
  (4 shorter events, 0.0 us)
Async XLA Ops:
  2.0 1.4 %collective-permute-start = (bf16[96,128]{1,0:T(8,128)(2,1)S(1)}, bf16[96,128]{1,0:T(8,128)(2,1)S(1)}, u32[]{:S(2)}, u32[]{:S(2)}) collective-permute-start(bf16[96,128]{1,0:T(8,128)(2,1)S(1)} %get-tuple-element.19.mine_ref), channel_id=1, source_target_pairs={{0,4},{4,0},{8,12},{12,8},{16,20},{20,16},{24,28},{28,24},{1,5},{5... | collective-permute-start | bytes 73736 | tf_op jit(solution)/shard_map/ppermute | solution.py:337
  3.4 5.6 %collective-permute-start.1 = (bf16[48,4096]{1,0:T(8,128)(2,1)S(1)}, bf16[48,4096]{1,0:T(8,128)(2,1)S(1)}, u32[]{:S(2)}, u32[]{:S(2)}) collective-permute-start(bf16[48,4096]{1,0:T(8,128)(2,1)S(1)} %get-tuple-element.21.k_ref), channel_id=1, source_target_pairs={{0,4},{4,0},{8,12},{12,8},{16,20},{20,16},{24,28},{28,24},{1,5},{5... | collective-permute-start | bytes 1179656 | tf_op jit(solution)/shard_map/ppermute | solution.py:337
  3.8 5.7 %collective-permute-start.2 = (bf16[128,128]{1,0:T(8,128)(2,1)S(1)}, bf16[128,128]{1,0:T(8,128)(2,1)S(1)}, u32[]{:S(2)}, u32[]{:S(2)}) collective-permute-start(bf16[128,128]{1,0:T(8,128)(2,1)S(1)} %get-tuple-element.23.refs_3_), channel_id=1, source_target_pairs={{0,4},{1,5},{2,6},{3,7},{4,2},{5,3},{6,0},{7,1},{8,12},{9,13},{10,... | collective-permute-start | bytes 98312 | tf_op jit(solution)/shard_map/ppermute | solution.py:352
  3.9 6.6 %collective-permute-start.3 = (bf16[128,128]{1,0:T(8,128)(2,1)S(1)}, bf16[128,128]{1,0:T(8,128)(2,1)S(1)}, u32[]{:S(2)}, u32[]{:S(2)}) collective-permute-start(bf16[128,128]{1,0:T(8,128)(2,1)S(1)} %get-tuple-element.23.refs_3_), channel_id=1, source_target_pairs={{0,4},{1,5},{2,6},{3,7},{4,3},{5,2},{6,1},{7,0},{8,12},{9,13},{10,... | collective-permute-start | bytes 98312 | tf_op jit(solution)/shard_map/ppermute | solution.py:352
  7.6 3.3 %collective-permute-start.4 = (bf16[128,128]{1,0:T(8,128)(2,1)S(1)}, bf16[128,128]{1,0:T(8,128)(2,1)S(1)}, u32[]{:S(2)}, u32[]{:S(2)}) collective-permute-start(bf16[128,128]{1,0:T(8,128)(2,1)S(1)} %get-tuple-element.23.refs_3_), channel_id=1, source_target_pairs={{0,4},{1,5},{2,6},{3,7},{4,1},{5,0},{6,3},{7,2},{8,12},{9,13},{10,... | collective-permute-start | bytes 98312 | tf_op jit(solution)/shard_map/ppermute | solution.py:352
  11.0 3.1 %copy-start = (f32[8,16,2]{1,2,0:T(2,128)S(1)}, f32[8,16,2]{1,2,0:T(2,128)}, u32[]{:S(2)}) copy-start(f32[8,16,2]{1,2,0:T(2,128)} %param.7) | copy-start | bytes 3076
  11.4 3.5 %collective-permute-start.6 = (bf16[8,4224]{1,0:T(8,128)(2,1)S(1)}, bf16[8,4224]{1,0:T(8,128)(2,1)S(1)}, u32[]{:S(2)}, u32[]{:S(2)}) collective-permute-start(bf16[8,4224]{1,0:T(8,128)(2,1)S(1)} %get-tuple-element.29), channel_id=1, source_target_pairs={{0,28},{1,29},{2,30},{3,31},{4,0},{5,1},{6,2},{7,3},{8,20},{9,21},... | collective-permute-start | bytes 202760 | tf_op jit(solution)/shard_map/ppermute | solution.py:352
  12.9 2.5 %collective-permute-start.7 = (bf16[8,4224]{1,0:T(8,128)(2,1)S(1)}, bf16[8,4224]{1,0:T(8,128)(2,1)S(1)}, u32[]{:S(2)}, u32[]{:S(2)}) collective-permute-start(bf16[8,4224]{1,0:T(8,128)(2,1)S(1)} %get-tuple-element.29), channel_id=1, source_target_pairs={{0,20},{1,21},{2,22},{3,23},{4,0},{5,1},{6,2},{7,3},{8,28},{9,29},... | collective-permute-start | bytes 202760 | tf_op jit(solution)/shard_map/ppermute | solution.py:352
  13.1 2.4 %collective-permute-start.8 = (bf16[8,4224]{1,0:T(8,128)(2,1)S(1)}, bf16[8,4224]{1,0:T(8,128)(2,1)S(1)}, u32[]{:S(2)}, u32[]{:S(2)}) collective-permute-start(bf16[8,4224]{1,0:T(8,128)(2,1)S(1)} %get-tuple-element.29), channel_id=1, source_target_pairs={{0,12},{1,13},{2,14},{3,15},{4,0},{5,1},{6,2},{7,3},{8,4},{9,5},{1... | collective-permute-start | bytes 202760 | tf_op jit(solution)/shard_map/ppermute | solution.py:352
  13.6 1.9 %collective-permute-start.9 = (bf16[8,4224]{1,0:T(8,128)(2,1)S(1)}, bf16[8,4224]{1,0:T(8,128)(2,1)S(1)}, u32[]{:S(2)}, u32[]{:S(2)}) collective-permute-start(bf16[8,4224]{1,0:T(8,128)(2,1)S(1)} %get-tuple-element.29), channel_id=1, source_target_pairs={{0,4},{1,5},{2,6},{3,7},{4,0},{5,1},{6,2},{7,3},{8,12},{9,13},{10,... | collective-permute-start | bytes 202760 | tf_op jit(solution)/shard_map/ppermute | solution.py:352
  13.6 1.3 %collective-permute-start.5 = (f32[8,128]{1,0:T(8,128)S(1)}, f32[8,128]{1,0:T(8,128)S(1)}, u32[]{:S(2)}, u32[]{:S(2)}) collective-permute-start(f32[8,128]{1,0:T(8,128)S(1)} %get-tuple-element.27), channel_id=1, source_target_pairs={{0,4},{4,0},{8,12},{12,8},{16,20},{20,16},{24,28},{28,24},{1,5},{5... | collective-permute-start | bytes 12296 | tf_op jit(solution)/shard_map/ppermute | solution.py:337
  16.0 5.2 %collective-permute-start.10 = (f32[8,128]{1,0:T(8,128)S(1)}, f32[8,128]{1,0:T(8,128)S(1)}, u32[]{:S(2)}, u32[]{:S(2)}) collective-permute-start(f32[8,128]{1,0:T(8,128)S(1)} %get-tuple-element.30), channel_id=1, source_target_pairs={{0,4},{1,5},{2,6},{3,7},{4,3},{5,2},{6,1},{7,0},{8,12},{9,13},{10,... | collective-permute-start | bytes 12296 | tf_op jit(solution)/shard_map/ppermute | solution.py:352
  17.7 3.9 %collective-permute-start.11 = (f32[8,128]{1,0:T(8,128)S(1)}, f32[8,128]{1,0:T(8,128)S(1)}, u32[]{:S(2)}, u32[]{:S(2)}) collective-permute-start(f32[8,128]{1,0:T(8,128)S(1)} %get-tuple-element.30), channel_id=1, source_target_pairs={{0,4},{1,5},{2,6},{3,7},{4,2},{5,3},{6,0},{7,1},{8,12},{9,13},{10,... | collective-permute-start | bytes 12296 | tf_op jit(solution)/shard_map/ppermute | solution.py:352
  18.8 3.1 %collective-permute-start.12 = (f32[8,128]{1,0:T(8,128)S(1)}, f32[8,128]{1,0:T(8,128)S(1)}, u32[]{:S(2)}, u32[]{:S(2)}) collective-permute-start(f32[8,128]{1,0:T(8,128)S(1)} %get-tuple-element.30), channel_id=1, source_target_pairs={{0,4},{1,5},{2,6},{3,7},{4,1},{5,0},{6,3},{7,2},{8,12},{9,13},{10,... | collective-permute-start | bytes 12296 | tf_op jit(solution)/shard_map/ppermute | solution.py:352
  18.9 3.0 %collective-permute-start.13 = (f32[8,128]{1,0:T(8,128)S(1)}, f32[8,128]{1,0:T(8,128)S(1)}, u32[]{:S(2)}, u32[]{:S(2)}) collective-permute-start(f32[8,128]{1,0:T(8,128)S(1)} %get-tuple-element.30), channel_id=1, source_target_pairs={{0,4},{1,5},{2,6},{3,7},{4,0},{5,1},{6,2},{7,3},{8,12},{9,13},{10,... | collective-permute-start | bytes 12296 | tf_op jit(solution)/shard_map/ppermute | solution.py:352
  22.2 3.3 %collective-permute-start.15 = (bf16[8,4224]{1,0:T(8,128)(2,1)S(1)}, bf16[8,4224]{1,0:T(8,128)(2,1)S(1)}, u32[]{:S(2)}, u32[]{:S(2)}) collective-permute-start(bf16[8,4224]{1,0:T(8,128)(2,1)S(1)} %get-tuple-element.33), channel_id=1, source_target_pairs={{0,28},{1,29},{2,30},{3,31},{4,0},{5,1},{6,2},{7,3},{8,20},{9,21},... | collective-permute-start | bytes 202760 | tf_op jit(solution)/shard_map/ppermute | solution.py:352
  22.2 3.5 %collective-permute-start.16 = (bf16[8,4224]{1,0:T(8,128)(2,1)S(1)}, bf16[8,4224]{1,0:T(8,128)(2,1)S(1)}, u32[]{:S(2)}, u32[]{:S(2)}) collective-permute-start(bf16[8,4224]{1,0:T(8,128)(2,1)S(1)} %get-tuple-element.33), channel_id=1, source_target_pairs={{0,20},{1,21},{2,22},{3,23},{4,0},{5,1},{6,2},{7,3},{8,28},{9,29},... | collective-permute-start | bytes 202760 | tf_op jit(solution)/shard_map/ppermute | solution.py:352
  23.8 1.9 %collective-permute-start.17 = (bf16[8,4224]{1,0:T(8,128)(2,1)S(1)}, bf16[8,4224]{1,0:T(8,128)(2,1)S(1)}, u32[]{:S(2)}, u32[]{:S(2)}) collective-permute-start(bf16[8,4224]{1,0:T(8,128)(2,1)S(1)} %get-tuple-element.33), channel_id=1, source_target_pairs={{0,12},{1,13},{2,14},{3,15},{4,0},{5,1},{6,2},{7,3},{8,4},{9,5},{1... | collective-permute-start | bytes 202760 | tf_op jit(solution)/shard_map/ppermute | solution.py:352
  23.8 1.9 %collective-permute-start.18 = (bf16[8,4224]{1,0:T(8,128)(2,1)S(1)}, bf16[8,4224]{1,0:T(8,128)(2,1)S(1)}, u32[]{:S(2)}, u32[]{:S(2)}) collective-permute-start(bf16[8,4224]{1,0:T(8,128)(2,1)S(1)} %get-tuple-element.33), channel_id=1, source_target_pairs={{0,4},{1,5},{2,6},{3,7},{4,0},{5,1},{6,2},{7,3},{8,12},{9,13},{10,... | collective-permute-start | bytes 202760 | tf_op jit(solution)/shard_map/ppermute | solution.py:352
  24.3 1.2 %collective-permute-start.14 = (f32[8,128]{1,0:T(8,128)S(1)}, f32[8,128]{1,0:T(8,128)S(1)}, u32[]{:S(2)}, u32[]{:S(2)}) collective-permute-start(f32[8,128]{1,0:T(8,128)S(1)} %get-tuple-element.31.residual_ref), channel_id=1, source_target_pairs={{0,4},{4,0},{8,12},{12,8},{16,20},{20,16},{24,28},{28,24},{1,5},{5... | collective-permute-start | bytes 12296 | tf_op jit(solution)/shard_map/ppermute | solution.py:337
  25.8 1.9 %collective-permute-start.19 = (f32[8,4096]{1,0:T(8,128)S(1)}, f32[8,4096]{1,0:T(8,128)S(1)}, u32[]{:S(2)}, u32[]{:S(2)}) collective-permute-start(f32[8,4096]{1,0:T(8,128)S(1)} %get-tuple-element.34.wave_ref), channel_id=1, source_target_pairs={{0,4},{4,0},{8,12},{12,8},{16,20},{20,16},{24,28},{28,24},{1,5},{5... | collective-permute-start | bytes 393224 | tf_op jit(solution)/shard_map/ppermute | solution.py:337

commit v14 on v13

--- a/solution.py
+++ b/solution.py
@@ -108,8 +108,8 @@
             ((wave_hbm, wave_ref), (k_hbm, k_ref), (observed_hbm, observed_ref))
         )
     ]
-    for load in loads:
-        load.start()
+    for load, priority in zip(loads, (0, 1, 0)):
+        load.start(priority=priority)
     loads[0].wait()
     even, odd = inverse_wave(*stacked(wave_ref, layers), 0.0)
     model = unstacked(even, odd, models).astype(BF16)

time: 28.5 us -> 28.6 us (level)
  no operation moved by 1% of the time
where the time goes in v14:
time: 28.6 us; the launch traced here: 28.4 us
  starting transfers between devices  14.8 us (52%)
  waiting for transfers between devices  8.27 us (29%)
  Pallas kernels  4.65 us (16%)
  between operations  0.71 us (2%)
    ppermute x15, starting transfers between devices, handed_over(): return lax.ppermute(x, ('dp', 'vox'), route)  12.6 us
    ppermute x15, waiting for transfers between devices, handed_over(): return lax.ppermute(x, ('dp', 'vox'), route)  5.2 us
    pallas_call x10, Pallas kernels, call(): pl.pallas_call(kernel, out_shape=out_shape, in_specs=[pl.BlockSpec(memory...  4.65 us
    ppermute x5, waiting for transfers between devices, from_partner(): lax.ppermute(x, axis, [(i, i ^ distance) for i in range(lax.axis_size(axi...  3.06 us
    ppermute x5, starting transfers between devices, from_partner(): lax.ppermute(x, axis, [(i, i ^ distance) for i in range(lax.axis_size(axi...  2.19 us
  transfers between devices with their start and end apart: 20, of which 12 were waited for; matrix products, arithmetic and copies ran while one was open for 0% of the time, Pallas kernels for 4%

profile of v14, /device:TPU:0, one launch (start us, length us, event | category | flops | bytes accessed | tf_op | source)
XLA Modules:
  0.0 28.4 jit_solution(18350302837719226618)
XLA Ops:
  0.6 1.3 %shard_map.59 = (bf16[96,128]{1,0:T(8,128)(2,1)S(1)}, f32[8,4096]{1,0:T(8,128)S(1)}, bf16[48,4096]{1,0:T(8,128)(2,1)S(1)}) custom-call(f32[8,4096]{1,0:T(8,128)} %wave_hbm.1, bf16[48,4096]{1,0:T(8,128)(2,1)} %k_hbm.1, f32[8,48]{1,0:T(8,128)} %observed_hbm.1), custom_call_target="tpu_custom_call" | custom-call | tf_op jit(solution)/shard_map/pallas_call | solution.py:373
  2.0 0.5 %collective-permute-start = (bf16[96,128]{1,0:T(8,128)(2,1)S(1)}, bf16[96,128]{1,0:T(8,128)(2,1)S(1)}, u32[]{:S(2)}, u32[]{:S(2)}) collective-permute-start(bf16[96,128]{1,0:T(8,128)(2,1)S(1)} %get-tuple-element.19.mine_ref), channel_id=1, source_target_pairs={{0,4},{4,0},{8,12},{12,8},{16,20},{20,16},{24,28},{28,24},{1,5},{5... | collective-permute-start | bytes 73736 | tf_op jit(solution)/shard_map/ppermute | solution.py:337
  2.5 0.8 %collective-permute-done.other_ref = bf16[96,128]{1,0:T(8,128)(2,1)S(1)} collective-permute-done((bf16[96,128]{1,0:T(8,128)(2,1)S(1)}, bf16[96,128]{1,0:T(8,128)(2,1)S(1)}, u32[]{:S(2)}, u32[]{:S(2)}) %collective-permute-start) | collective-permute-done | bytes 24608 | tf_op jit(solution)/shard_map/ppermute | solution.py:337
  3.4 0.1 shard_map.60
  3.4 0.3 %collective-permute-start.1 = (bf16[48,4096]{1,0:T(8,128)(2,1)S(1)}, bf16[48,4096]{1,0:T(8,128)(2,1)S(1)}, u32[]{:S(2)}, u32[]{:S(2)}) collective-permute-start(bf16[48,4096]{1,0:T(8,128)(2,1)S(1)} %get-tuple-element.21.k_ref), channel_id=1, source_target_pairs={{0,4},{4,0},{8,12},{12,8},{16,20},{20,16},{24,28},{28,24},{1,5},{5... | collective-permute-start | bytes 1179656 | tf_op jit(solution)/shard_map/ppermute | solution.py:337
  3.8 0.2 collective-permute-start.2
  3.9 3.7 %collective-permute-start.3 = (bf16[128,128]{1,0:T(8,128)(2,1)S(1)}, bf16[128,128]{1,0:T(8,128)(2,1)S(1)}, u32[]{:S(2)}, u32[]{:S(2)}) collective-permute-start(bf16[128,128]{1,0:T(8,128)(2,1)S(1)} %get-tuple-element.23.refs_3_), channel_id=1, source_target_pairs={{0,4},{1,5},{2,6},{3,7},{4,3},{5,2},{6,1},{7,0},{8,12},{9,13},{10,... | collective-permute-start | bytes 98312 | tf_op jit(solution)/shard_map/ppermute | solution.py:352
  7.6 1.4 %collective-permute-start.4 = (bf16[128,128]{1,0:T(8,128)(2,1)S(1)}, bf16[128,128]{1,0:T(8,128)(2,1)S(1)}, u32[]{:S(2)}, u32[]{:S(2)}) collective-permute-start(bf16[128,128]{1,0:T(8,128)(2,1)S(1)} %get-tuple-element.23.refs_3_), channel_id=1, source_target_pairs={{0,4},{1,5},{2,6},{3,7},{4,1},{5,0},{6,3},{7,2},{8,12},{9,13},{10,... | collective-permute-start | bytes 98312 | tf_op jit(solution)/shard_map/ppermute | solution.py:352
  9.0 0.0 collective-permute-done.1.k_other_ref
  9.0 0.5 %shard_map.61.kw_ref = bf16[128,4096]{1,0:T(8,128)(2,1)S(1)} custom-call(bf16[48,4096]{1,0:T(8,128)(2,1)S(1)} %get-tuple-element.21.k_ref, bf16[48,4096]{1,0:T(8,128)(2,1)S(1)} %collective-permute-done.1.k_other_ref), custom_call_target="tpu_custom_call" | custom-call | tf_op jit(solution)/shard_map/pallas_call | solution.py:373
  9.5 0.0 collective-permute-done.2.refs_0_
  9.5 1.1 %collective-permute-done.3.refs_1_ = bf16[128,128]{1,0:T(8,128)(2,1)S(1)} collective-permute-done((bf16[128,128]{1,0:T(8,128)(2,1)S(1)}, bf16[128,128]{1,0:T(8,128)(2,1)S(1)}, u32[]{:S(2)}, u32[]{:S(2)}) %collective-permute-start.3) | collective-permute-done | bytes 32800 | tf_op jit(solution)/shard_map/ppermute | solution.py:352
  10.5 0.4 %collective-permute-done.4.refs_2_ = bf16[128,128]{1,0:T(8,128)(2,1)S(1)} collective-permute-done((bf16[128,128]{1,0:T(8,128)(2,1)S(1)}, bf16[128,128]{1,0:T(8,128)(2,1)S(1)}, u32[]{:S(2)}, u32[]{:S(2)}) %collective-permute-start.4) | collective-permute-done | bytes 32800 | tf_op jit(solution)/shard_map/ppermute | solution.py:352
  11.0 0.5 %shard_map.62 = (bf16[8,4224]{1,0:T(8,128)(2,1)S(1)}, bf16[128,128]{1,0:T(8,128)(2,1)S(1)}, f32[8,128]{1,0:T(8,128)S(1)}) custom-call(f32[8,128]{1,0:T(8,128)S(1)} %get-tuple-element.22.observed_ref, bf16[128,4096]{1,0:T(8,128)(2,1)S(1)} %shard_map.61.kw_ref, bf16[128,128]{1,0:T(8,128)(2,1)S(1)} %collective-permute-done.2.refs_0_, ...), custom_call_target="tpu_custom_call" | custom-call | tf_op jit(solution)/shard_map/pallas_call | solution.py:373
  11.4 1.5 %collective-permute-start.6 = (bf16[8,4224]{1,0:T(8,128)(2,1)S(1)}, bf16[8,4224]{1,0:T(8,128)(2,1)S(1)}, u32[]{:S(2)}, u32[]{:S(2)}) collective-permute-start(bf16[8,4224]{1,0:T(8,128)(2,1)S(1)} %get-tuple-element.29), channel_id=1, source_target_pairs={{0,28},{1,29},{2,30},{3,31},{4,0},{5,1},{6,2},{7,3},{8,20},{9,21},... | collective-permute-start | bytes 202760 | tf_op jit(solution)/shard_map/ppermute | solution.py:352
  12.9 0.2 collective-permute-start.7
  13.1 0.4 %collective-permute-start.8 = (bf16[8,4224]{1,0:T(8,128)(2,1)S(1)}, bf16[8,4224]{1,0:T(8,128)(2,1)S(1)}, u32[]{:S(2)}, u32[]{:S(2)}) collective-permute-start(bf16[8,4224]{1,0:T(8,128)(2,1)S(1)} %get-tuple-element.29), channel_id=1, source_target_pairs={{0,12},{1,13},{2,14},{3,15},{4,0},{5,1},{6,2},{7,3},{8,4},{9,5},{1... | collective-permute-start | bytes 202760 | tf_op jit(solution)/shard_map/ppermute | solution.py:352
  13.6 0.1 collective-permute-start.9
  13.6 0.4 %collective-permute-start.5 = (f32[8,128]{1,0:T(8,128)S(1)}, f32[8,128]{1,0:T(8,128)S(1)}, u32[]{:S(2)}, u32[]{:S(2)}) collective-permute-start(f32[8,128]{1,0:T(8,128)S(1)} %get-tuple-element.27), channel_id=1, source_target_pairs={{0,4},{4,0},{8,12},{12,8},{16,20},{20,16},{24,28},{28,24},{1,5},{5... | collective-permute-start | bytes 12296 | tf_op jit(solution)/shard_map/ppermute | solution.py:337
  14.1 0.4 %shard_map.63 = (f32[8,4096]{1,0:T(8,128)S(1)}, f32[8,128]{1,0:T(8,128)S(1)}) custom-call(f32[8,2,16]{2,1,0:T(2,128)S(1)} %bitcast.1), custom_call_target="tpu_custom_call" | custom-call | tf_op jit(solution)/shard_map/pallas_call | solution.py:373
  14.4 0.4 %shard_map.64.kt_ref = bf16[4096,128]{1,0:T(8,128)(2,1)S(1)} custom-call(bf16[48,4096]{1,0:T(8,128)(2,1)S(1)} %get-tuple-element.21.k_ref, bf16[48,4096]{1,0:T(8,128)(2,1)S(1)} %collective-permute-done.1.k_other_ref), custom_call_target="tpu_custom_call" | custom-call | tf_op jit(solution)/shard_map/pallas_call | solution.py:373
  14.8 0.1 collective-permute-done.5.halo_ref
  14.9 0.5 %collective-permute-done.7.refs_1_ = bf16[8,4224]{1,0:T(8,128)(2,1)S(1)} collective-permute-done((bf16[8,4224]{1,0:T(8,128)(2,1)S(1)}, bf16[8,4224]{1,0:T(8,128)(2,1)S(1)}, u32[]{:S(2)}, u32[]{:S(2)}) %collective-permute-start.7) | collective-permute-done | bytes 67616 | tf_op jit(solution)/shard_map/ppermute | solution.py:352
  15.4 0.1 collective-permute-done.8.refs_2_
  15.5 0.0 collective-permute-done.9.refs_3_
  15.5 0.5 %shard_map.65 = (f32[8,4096]{1,0:T(8,128)S(1)}, f32[8,128]{1,0:T(8,128)S(1)}) custom-call(f32[8,4096]{1,0:T(8,128)S(1)} %get-tuple-element.25.wave_ref, f32[8,4096]{1,0:T(8,128)S(1)} %get-tuple-element.26.cut_ref, f32[8,128]{1,0:T(8,128)S(1)} %collective-permute-done.5.halo_ref, f32[8,128]{1,0:T(8,128)S(1)} %get-tuple-element.28.cut_halo_ref, ...), custom_call_target="tpu_custom_call" | custom-call | tf_op jit(solution)/shard_map/pallas_call | solution.py:373
  16.0 1.7 %collective-permute-start.10 = (f32[8,128]{1,0:T(8,128)S(1)}, f32[8,128]{1,0:T(8,128)S(1)}, u32[]{:S(2)}, u32[]{:S(2)}) collective-permute-start(f32[8,128]{1,0:T(8,128)S(1)} %get-tuple-element.30), channel_id=1, source_target_pairs={{0,4},{1,5},{2,6},{3,7},{4,3},{5,2},{6,1},{7,0},{8,12},{9,13},{10,... | collective-permute-start | bytes 12296 | tf_op jit(solution)/shard_map/ppermute | solution.py:352
  17.7 1.1 %collective-permute-start.11 = (f32[8,128]{1,0:T(8,128)S(1)}, f32[8,128]{1,0:T(8,128)S(1)}, u32[]{:S(2)}, u32[]{:S(2)}) collective-permute-start(f32[8,128]{1,0:T(8,128)S(1)} %get-tuple-element.30), channel_id=1, source_target_pairs={{0,4},{1,5},{2,6},{3,7},{4,2},{5,3},{6,0},{7,1},{8,12},{9,13},{10,... | collective-permute-start | bytes 12296 | tf_op jit(solution)/shard_map/ppermute | solution.py:352
  18.8 0.1 collective-permute-start.12
  18.9 0.2 collective-permute-start.13
  19.1 2.2 %collective-permute-done.10.refs_0_ = f32[8,128]{1,0:T(8,128)S(1)} collective-permute-done((f32[8,128]{1,0:T(8,128)S(1)}, f32[8,128]{1,0:T(8,128)S(1)}, u32[]{:S(2)}, u32[]{:S(2)}) %collective-permute-start.10) | collective-permute-done | bytes 4128 | tf_op jit(solution)/shard_map/ppermute | solution.py:352
  21.2 0.4 %collective-permute-done.11.refs_1_ = f32[8,128]{1,0:T(8,128)S(1)} collective-permute-done((f32[8,128]{1,0:T(8,128)S(1)}, f32[8,128]{1,0:T(8,128)S(1)}, u32[]{:S(2)}, u32[]{:S(2)}) %collective-permute-start.11) | collective-permute-done | bytes 4128 | tf_op jit(solution)/shard_map/ppermute | solution.py:352
  21.7 0.2 collective-permute-done.12.refs_2_
  21.9 0.3 shard_map.66
  22.2 0.0 collective-permute-start.15
  22.2 1.6 %collective-permute-start.16 = (bf16[8,4224]{1,0:T(8,128)(2,1)S(1)}, bf16[8,4224]{1,0:T(8,128)(2,1)S(1)}, u32[]{:S(2)}, u32[]{:S(2)}) collective-permute-start(bf16[8,4224]{1,0:T(8,128)(2,1)S(1)} %get-tuple-element.33), channel_id=1, source_target_pairs={{0,20},{1,21},{2,22},{3,23},{4,0},{5,1},{6,2},{7,3},{8,28},{9,29},... | collective-permute-start | bytes 202760 | tf_op jit(solution)/shard_map/ppermute | solution.py:352
  23.8 0.0 collective-permute-start.17
  23.8 0.5 %collective-permute-start.18 = (bf16[8,4224]{1,0:T(8,128)(2,1)S(1)}, bf16[8,4224]{1,0:T(8,128)(2,1)S(1)}, u32[]{:S(2)}, u32[]{:S(2)}) collective-permute-start(bf16[8,4224]{1,0:T(8,128)(2,1)S(1)} %get-tuple-element.33), channel_id=1, source_target_pairs={{0,4},{1,5},{2,6},{3,7},{4,0},{5,1},{6,2},{7,3},{8,12},{9,13},{10,... | collective-permute-start | bytes 202760 | tf_op jit(solution)/shard_map/ppermute | solution.py:352
  24.3 0.0 collective-permute-start.14
  24.3 1.2 %collective-permute-done.14.residual_in_ref = f32[8,128]{1,0:T(8,128)S(1)} collective-permute-done((f32[8,128]{1,0:T(8,128)S(1)}, f32[8,128]{1,0:T(8,128)S(1)}, u32[]{:S(2)}, u32[]{:S(2)}) %collective-permute-start.14) | collective-permute-done | bytes 4128 | tf_op jit(solution)/shard_map/ppermute | solution.py:337
  25.5 0.0 collective-permute-done.15.refs_0_
  25.5 0.2 collective-permute-done.16.refs_1_
  25.7 0.0 collective-permute-done.17.refs_2_
  25.7 0.0 collective-permute-done.18.refs_3_
  25.7 0.1 shard_map.67
  25.9 0.9 %collective-permute-start.19 = (f32[8,4096]{1,0:T(8,128)S(1)}, f32[8,4096]{1,0:T(8,128)S(1)}, u32[]{:S(2)}, u32[]{:S(2)}) collective-permute-start(f32[8,4096]{1,0:T(8,128)S(1)} %get-tuple-element.34.wave_ref), channel_id=1, source_target_pairs={{0,4},{4,0},{8,12},{12,8},{16,20},{20,16},{24,28},{28,24},{1,5},{5... | collective-permute-start | bytes 393224 | tf_op jit(solution)/shard_map/ppermute | solution.py:337
  26.7 1.0 %collective-permute-done.19.other_wave_ref = f32[8,4096]{1,0:T(8,128)S(1)} collective-permute-done((f32[8,4096]{1,0:T(8,128)S(1)}, f32[8,4096]{1,0:T(8,128)S(1)}, u32[]{:S(2)}, u32[]{:S(2)}) %collective-permute-start.19) | collective-permute-done | bytes 131104 | tf_op jit(solution)/shard_map/ppermute | solution.py:337
  27.7 0.7 %shard_map.68 = (f32[8,4096]{1,0:T(8,128)}, f32[8,48]{1,0:T(8,128)}) custom-call(f32[8,4096]{1,0:T(8,128)S(1)} %get-tuple-element.34.wave_ref, f32[8,4096]{1,0:T(8,128)S(1)} %collective-permute-done.19.other_wave_ref, f32[8,128]{1,0:T(8,128)S(1)} %get-tuple-element.31.residual_ref, f32[8,128]{1,0:T(8,128)S(1)} %get-tuple-element.35.other_residual_ref), custom_call_target="tpu_custom_call" | custom-call | tf_op jit(solution)/shard_map/pallas_call | solution.py:373
  (4 shorter events, 0.0 us)
Async XLA Ops:
  2.0 1.4 %collective-permute-start = (bf16[96,128]{1,0:T(8,128)(2,1)S(1)}, bf16[96,128]{1,0:T(8,128)(2,1)S(1)}, u32[]{:S(2)}, u32[]{:S(2)}) collective-permute-start(bf16[96,128]{1,0:T(8,128)(2,1)S(1)} %get-tuple-element.19.mine_ref), channel_id=1, source_target_pairs={{0,4},{4,0},{8,12},{12,8},{16,20},{20,16},{24,28},{28,24},{1,5},{5... | collective-permute-start | bytes 73736 | tf_op jit(solution)/shard_map/ppermute | solution.py:337
  3.4 5.6 %collective-permute-start.1 = (bf16[48,4096]{1,0:T(8,128)(2,1)S(1)}, bf16[48,4096]{1,0:T(8,128)(2,1)S(1)}, u32[]{:S(2)}, u32[]{:S(2)}) collective-permute-start(bf16[48,4096]{1,0:T(8,128)(2,1)S(1)} %get-tuple-element.21.k_ref), channel_id=1, source_target_pairs={{0,4},{4,0},{8,12},{12,8},{16,20},{20,16},{24,28},{28,24},{1,5},{5... | collective-permute-start | bytes 1179656 | tf_op jit(solution)/shard_map/ppermute | solution.py:337
  3.8 5.7 %collective-permute-start.2 = (bf16[128,128]{1,0:T(8,128)(2,1)S(1)}, bf16[128,128]{1,0:T(8,128)(2,1)S(1)}, u32[]{:S(2)}, u32[]{:S(2)}) collective-permute-start(bf16[128,128]{1,0:T(8,128)(2,1)S(1)} %get-tuple-element.23.refs_3_), channel_id=1, source_target_pairs={{0,4},{1,5},{2,6},{3,7},{4,2},{5,3},{6,0},{7,1},{8,12},{9,13},{10,... | collective-permute-start | bytes 98312 | tf_op jit(solution)/shard_map/ppermute | solution.py:352
  3.9 6.6 %collective-permute-start.3 = (bf16[128,128]{1,0:T(8,128)(2,1)S(1)}, bf16[128,128]{1,0:T(8,128)(2,1)S(1)}, u32[]{:S(2)}, u32[]{:S(2)}) collective-permute-start(bf16[128,128]{1,0:T(8,128)(2,1)S(1)} %get-tuple-element.23.refs_3_), channel_id=1, source_target_pairs={{0,4},{1,5},{2,6},{3,7},{4,3},{5,2},{6,1},{7,0},{8,12},{9,13},{10,... | collective-permute-start | bytes 98312 | tf_op jit(solution)/shard_map/ppermute | solution.py:352
  7.6 3.3 %collective-permute-start.4 = (bf16[128,128]{1,0:T(8,128)(2,1)S(1)}, bf16[128,128]{1,0:T(8,128)(2,1)S(1)}, u32[]{:S(2)}, u32[]{:S(2)}) collective-permute-start(bf16[128,128]{1,0:T(8,128)(2,1)S(1)} %get-tuple-element.23.refs_3_), channel_id=1, source_target_pairs={{0,4},{1,5},{2,6},{3,7},{4,1},{5,0},{6,3},{7,2},{8,12},{9,13},{10,... | collective-permute-start | bytes 98312 | tf_op jit(solution)/shard_map/ppermute | solution.py:352
  11.0 3.1 %copy-start = (f32[8,16,2]{1,2,0:T(2,128)S(1)}, f32[8,16,2]{1,2,0:T(2,128)}, u32[]{:S(2)}) copy-start(f32[8,16,2]{1,2,0:T(2,128)} %param.7) | copy-start | bytes 3076
  11.4 3.5 %collective-permute-start.6 = (bf16[8,4224]{1,0:T(8,128)(2,1)S(1)}, bf16[8,4224]{1,0:T(8,128)(2,1)S(1)}, u32[]{:S(2)}, u32[]{:S(2)}) collective-permute-start(bf16[8,4224]{1,0:T(8,128)(2,1)S(1)} %get-tuple-element.29), channel_id=1, source_target_pairs={{0,28},{1,29},{2,30},{3,31},{4,0},{5,1},{6,2},{7,3},{8,20},{9,21},... | collective-permute-start | bytes 202760 | tf_op jit(solution)/shard_map/ppermute | solution.py:352
  12.9 2.5 %collective-permute-start.7 = (bf16[8,4224]{1,0:T(8,128)(2,1)S(1)}, bf16[8,4224]{1,0:T(8,128)(2,1)S(1)}, u32[]{:S(2)}, u32[]{:S(2)}) collective-permute-start(bf16[8,4224]{1,0:T(8,128)(2,1)S(1)} %get-tuple-element.29), channel_id=1, source_target_pairs={{0,20},{1,21},{2,22},{3,23},{4,0},{5,1},{6,2},{7,3},{8,28},{9,29},... | collective-permute-start | bytes 202760 | tf_op jit(solution)/shard_map/ppermute | solution.py:352
  13.1 2.4 %collective-permute-start.8 = (bf16[8,4224]{1,0:T(8,128)(2,1)S(1)}, bf16[8,4224]{1,0:T(8,128)(2,1)S(1)}, u32[]{:S(2)}, u32[]{:S(2)}) collective-permute-start(bf16[8,4224]{1,0:T(8,128)(2,1)S(1)} %get-tuple-element.29), channel_id=1, source_target_pairs={{0,12},{1,13},{2,14},{3,15},{4,0},{5,1},{6,2},{7,3},{8,4},{9,5},{1... | collective-permute-start | bytes 202760 | tf_op jit(solution)/shard_map/ppermute | solution.py:352
  13.6 1.9 %collective-permute-start.9 = (bf16[8,4224]{1,0:T(8,128)(2,1)S(1)}, bf16[8,4224]{1,0:T(8,128)(2,1)S(1)}, u32[]{:S(2)}, u32[]{:S(2)}) collective-permute-start(bf16[8,4224]{1,0:T(8,128)(2,1)S(1)} %get-tuple-element.29), channel_id=1, source_target_pairs={{0,4},{1,5},{2,6},{3,7},{4,0},{5,1},{6,2},{7,3},{8,12},{9,13},{10,... | collective-permute-start | bytes 202760 | tf_op jit(solution)/shard_map/ppermute | solution.py:352
  13.6 1.3 %collective-permute-start.5 = (f32[8,128]{1,0:T(8,128)S(1)}, f32[8,128]{1,0:T(8,128)S(1)}, u32[]{:S(2)}, u32[]{:S(2)}) collective-permute-start(f32[8,128]{1,0:T(8,128)S(1)} %get-tuple-element.27), channel_id=1, source_target_pairs={{0,4},{4,0},{8,12},{12,8},{16,20},{20,16},{24,28},{28,24},{1,5},{5... | collective-permute-start | bytes 12296 | tf_op jit(solution)/shard_map/ppermute | solution.py:337
  16.0 5.2 %collective-permute-start.10 = (f32[8,128]{1,0:T(8,128)S(1)}, f32[8,128]{1,0:T(8,128)S(1)}, u32[]{:S(2)}, u32[]{:S(2)}) collective-permute-start(f32[8,128]{1,0:T(8,128)S(1)} %get-tuple-element.30), channel_id=1, source_target_pairs={{0,4},{1,5},{2,6},{3,7},{4,3},{5,2},{6,1},{7,0},{8,12},{9,13},{10,... | collective-permute-start | bytes 12296 | tf_op jit(solution)/shard_map/ppermute | solution.py:352
  17.7 3.9 %collective-permute-start.11 = (f32[8,128]{1,0:T(8,128)S(1)}, f32[8,128]{1,0:T(8,128)S(1)}, u32[]{:S(2)}, u32[]{:S(2)}) collective-permute-start(f32[8,128]{1,0:T(8,128)S(1)} %get-tuple-element.30), channel_id=1, source_target_pairs={{0,4},{1,5},{2,6},{3,7},{4,2},{5,3},{6,0},{7,1},{8,12},{9,13},{10,... | collective-permute-start | bytes 12296 | tf_op jit(solution)/shard_map/ppermute | solution.py:352
  18.8 3.1 %collective-permute-start.12 = (f32[8,128]{1,0:T(8,128)S(1)}, f32[8,128]{1,0:T(8,128)S(1)}, u32[]{:S(2)}, u32[]{:S(2)}) collective-permute-start(f32[8,128]{1,0:T(8,128)S(1)} %get-tuple-element.30), channel_id=1, source_target_pairs={{0,4},{1,5},{2,6},{3,7},{4,1},{5,0},{6,3},{7,2},{8,12},{9,13},{10,... | collective-permute-start | bytes 12296 | tf_op jit(solution)/shard_map/ppermute | solution.py:352
  18.9 3.0 %collective-permute-start.13 = (f32[8,128]{1,0:T(8,128)S(1)}, f32[8,128]{1,0:T(8,128)S(1)}, u32[]{:S(2)}, u32[]{:S(2)}) collective-permute-start(f32[8,128]{1,0:T(8,128)S(1)} %get-tuple-element.30), channel_id=1, source_target_pairs={{0,4},{1,5},{2,6},{3,7},{4,0},{5,1},{6,2},{7,3},{8,12},{9,13},{10,... | collective-permute-start | bytes 12296 | tf_op jit(solution)/shard_map/ppermute | solution.py:352
  22.2 3.3 %collective-permute-start.15 = (bf16[8,4224]{1,0:T(8,128)(2,1)S(1)}, bf16[8,4224]{1,0:T(8,128)(2,1)S(1)}, u32[]{:S(2)}, u32[]{:S(2)}) collective-permute-start(bf16[8,4224]{1,0:T(8,128)(2,1)S(1)} %get-tuple-element.33), channel_id=1, source_target_pairs={{0,28},{1,29},{2,30},{3,31},{4,0},{5,1},{6,2},{7,3},{8,20},{9,21},... | collective-permute-start | bytes 202760 | tf_op jit(solution)/shard_map/ppermute | solution.py:352
  22.2 3.5 %collective-permute-start.16 = (bf16[8,4224]{1,0:T(8,128)(2,1)S(1)}, bf16[8,4224]{1,0:T(8,128)(2,1)S(1)}, u32[]{:S(2)}, u32[]{:S(2)}) collective-permute-start(bf16[8,4224]{1,0:T(8,128)(2,1)S(1)} %get-tuple-element.33), channel_id=1, source_target_pairs={{0,20},{1,21},{2,22},{3,23},{4,0},{5,1},{6,2},{7,3},{8,28},{9,29},... | collective-permute-start | bytes 202760 | tf_op jit(solution)/shard_map/ppermute | solution.py:352
  23.8 1.9 %collective-permute-start.17 = (bf16[8,4224]{1,0:T(8,128)(2,1)S(1)}, bf16[8,4224]{1,0:T(8,128)(2,1)S(1)}, u32[]{:S(2)}, u32[]{:S(2)}) collective-permute-start(bf16[8,4224]{1,0:T(8,128)(2,1)S(1)} %get-tuple-element.33), channel_id=1, source_target_pairs={{0,12},{1,13},{2,14},{3,15},{4,0},{5,1},{6,2},{7,3},{8,4},{9,5},{1... | collective-permute-start | bytes 202760 | tf_op jit(solution)/shard_map/ppermute | solution.py:352
  23.8 1.9 %collective-permute-start.18 = (bf16[8,4224]{1,0:T(8,128)(2,1)S(1)}, bf16[8,4224]{1,0:T(8,128)(2,1)S(1)}, u32[]{:S(2)}, u32[]{:S(2)}) collective-permute-start(bf16[8,4224]{1,0:T(8,128)(2,1)S(1)} %get-tuple-element.33), channel_id=1, source_target_pairs={{0,4},{1,5},{2,6},{3,7},{4,0},{5,1},{6,2},{7,3},{8,12},{9,13},{10,... | collective-permute-start | bytes 202760 | tf_op jit(solution)/shard_map/ppermute | solution.py:352
  24.3 1.2 %collective-permute-start.14 = (f32[8,128]{1,0:T(8,128)S(1)}, f32[8,128]{1,0:T(8,128)S(1)}, u32[]{:S(2)}, u32[]{:S(2)}) collective-permute-start(f32[8,128]{1,0:T(8,128)S(1)} %get-tuple-element.31.residual_ref), channel_id=1, source_target_pairs={{0,4},{4,0},{8,12},{12,8},{16,20},{20,16},{24,28},{28,24},{1,5},{5... | collective-permute-start | bytes 12296 | tf_op jit(solution)/shard_map/ppermute | solution.py:337
  25.9 1.9 %collective-permute-start.19 = (f32[8,4096]{1,0:T(8,128)S(1)}, f32[8,4096]{1,0:T(8,128)S(1)}, u32[]{:S(2)}, u32[]{:S(2)}) collective-permute-start(f32[8,4096]{1,0:T(8,128)S(1)} %get-tuple-element.34.wave_ref), channel_id=1, source_target_pairs={{0,4},{4,0},{8,12},{12,8},{16,20},{20,16},{24,28},{28,24},{1,5},{5... | collective-permute-start | bytes 393224 | tf_op jit(solution)/shard_map/ppermute | solution.py:337
